TPU v7x, 32 devices: a whole 2x2x4 slice. The times are simulated.
32 devices in a mesh: dp: 8 (over y, x, core), sp: 4 (over z).
Axes of the slice: x: 2, y: 2, z: 4, core: 2. Of those that a mesh axis runs over, the one named last changes fastest.
Arguments:
- tokens: bfloat16 [16, 1024, 1024], P('dp', 'sp'), may hold values from -6 to 6
- timestep: int32 [16], P('dp'), may hold values from 0 to 4999
- segment_ids: int32 [16, 1024], P('dp', 'sp'), may hold values from 0 to 1023, as said below
- cotangent: bfloat16 [16, 1024, 1024], P('dp', 'sp'), may hold values from -6 to 6
- time_weight: bfloat16 [1024, 1024], P(('dp', 'sp')), may hold values from -0.1875 to 0.1875
- qkv_weight: bfloat16 [1024, 3072], P(('dp', 'sp')), may hold values from -0.1875 to 0.1875
- qv_bias: bfloat16 [2048], P(('dp', 'sp')), may hold values from -3 to 3
- out_weight: bfloat16 [1024, 1024], P(('dp', 'sp')), may hold values from -0.75 to 0.75
- out_bias: bfloat16 [1024], P(('dp', 'sp')), may hold values from -3 to 3
- norm_gain: bfloat16 [1024], P(('dp', 'sp')), may hold values from 0.099609375 to 1.8984375
- norm_bias: bfloat16 [1024], P(('dp', 'sp')), may hold values from -3 to 3
- up_weight: bfloat16 [1024, 4096], P(('dp', 'sp')), may hold values from -0.1875 to 0.1875
- up_bias: bfloat16 [4096], P(('dp', 'sp')), may hold values from -3 to 3
- down_weight: bfloat16 [4096, 1024], P(('dp', 'sp')), may hold values from -0.09375 to 0.09375
- down_bias: bfloat16 [1024], P(('dp', 'sp')), may hold values from -3 to 3
- final_gain: bfloat16 [1024], P(('dp', 'sp')), may hold values from 0.099609375 to 1.8984375
- final_bias: bfloat16 [1024], P(('dp', 'sp')), may hold values from -3 to 3
Outputs:
- output: bfloat16 [16, 1024, 1024], P('dp', 'sp')
- input_grad: bfloat16 [16, 1024, 1024], P('dp', 'sp')
- grad_time_weight: float32 [1024, 1024], P(('dp', 'sp'))
- grad_qkv_weight: float32 [1024, 3072], P(('dp', 'sp'))
- grad_qv_bias: float32 [2048], P(('dp', 'sp'))
- grad_out_weight: float32 [1024, 1024], P(('dp', 'sp'))
- grad_out_bias: float32 [1024], P(('dp', 'sp'))
- grad_norm_gain: float32 [1024], P(('dp', 'sp'))
- grad_norm_bias: float32 [1024], P(('dp', 'sp'))
- grad_up_weight: float32 [1024, 4096], P(('dp', 'sp'))
- grad_up_bias: float32 [4096], P(('dp', 'sp'))
- grad_down_weight: float32 [4096, 1024], P(('dp', 'sp'))
- grad_down_bias: float32 [1024], P(('dp', 'sp'))
- grad_final_gain: float32 [1024], P(('dp', 'sp'))
- grad_final_bias: float32 [1024], P(('dp', 'sp'))
Inputs may be any that keep to these rules, and one draw needn't show every extreme that they name: `segment_ids`: each position's id is the position within its row at which its document begins; attention stays within one document of one row.
All inputs are finite; a program needn't handle non-finite values.
Results may differ from a plain program's by a relative error of at most 0.02.
Values may be sent and summed in bfloat16 or wider, within the bound.
No kernel may reach another device: no remote copies, remote signals or barrier semaphores. Data moves between devices by JAX's collectives and lax.ppermute only.
A program may use at most 256 MiB of HBM per device.

v0:
```python
import math

import jax
import jax.numpy as jnp
from jax import lax
from jax.sharding import PartitionSpec as P

HEADS = 16
HEAD_DIM = 64


EPSILON = 1e-05
INVERSE_ROOT_TWO = 1.0 / math.sqrt(2.0)
INVERSE_ROOT_TWO_PI = 1.0 / math.sqrt(2.0 * math.pi)


def time_features(stamps, model_width):
    halfway = model_width // 2
    frequency = jnp.exp(-math.log(10000.0) * jnp.arange(halfway, dtype=jnp.float32) / halfway)
    phases = stamps.astype(jnp.float32)[:, None] * frequency[None, :]
    return jnp.concatenate([jnp.sin(phases), jnp.cos(phases)], axis=1)


def layer_norm_parts(values, gain, offset):
    center = values - jnp.mean(values, axis=-1, keepdims=True)
    variance = jnp.mean(center * center, axis=-1, keepdims=True)
    inverse = lax.rsqrt(variance + EPSILON)
    normal_part = center * inverse
    return (normal_part * gain + offset, normal_part, inverse)


def layer_norm_back(upstream, normal_part, inverse, gain):
    scaled = upstream * gain
    return inverse * (
        scaled
        - jnp.mean(scaled, axis=-1, keepdims=True)
        - normal_part * jnp.mean(scaled * normal_part, axis=-1, keepdims=True)
    )


def gelu_slope(values):
    cumulative = 0.5 * (1.0 + lax.erf(values * INVERSE_ROOT_TWO))
    density = jnp.exp(-0.5 * values * values) * INVERSE_ROOT_TWO_PI
    return cumulative + values * density


def contract_rows(left, right):
    return lax.dot_general(
        left, right, (((0,), (0,)), ((), ())), preferred_element_type=jnp.float32
    )


def times_transposed(left, right):
    return lax.dot_general(
        left, right, (((1,), (1,)), ((), ())), preferred_element_type=jnp.float32
    )


def flatten_grads(grads):
    return tuple((grad.reshape(-1, 128) if grad.ndim == 2 else grad for grad in grads))


def restore_grads(shares, templates):
    return tuple((share.reshape(template.shape) for share, template in zip(shares, templates)))


def attention_forward(queries, keys_all, values_all, seg_full, query_block, scale):
    block_count = queries.shape[1] // query_block

    def one_block(index):
        start = index * query_block
        query_part = lax.dynamic_slice_in_dim(queries, start, query_block, 1)
        seg_part = lax.dynamic_slice_in_dim(seg_full, start, query_block, 1)
        scores = (
            jnp.einsum("rqhd,rkhd->rhqk", query_part, keys_all, preferred_element_type=jnp.float32)
            * scale
        )
        allowed = seg_part[:, None, :, None] == seg_full[:, None, None, :]
        scores = jnp.where(allowed, scores, -1e30)
        largest = jnp.max(scores, axis=-1, keepdims=True)
        exponent = jnp.exp(scores - largest)
        totals = jnp.sum(exponent, axis=-1, keepdims=True)
        probability = exponent / totals
        log_total = largest[..., 0] + jnp.log(totals[..., 0])
        mixed = jnp.einsum(
            "rhqk,rkhd->rqhd",
            probability.astype(jnp.bfloat16),
            values_all,
            preferred_element_type=jnp.float32,
        )
        return (mixed, log_total)

    mixed_blocks, log_totals = lax.map(one_block, jnp.arange(block_count, dtype=jnp.int32))
    mixed = jnp.moveaxis(mixed_blocks, 0, 1).reshape(queries.shape)
    return (mixed, log_totals)


def attention_backward(
    queries, keys_all, values_all, seg_full, grad_heads, log_totals, query_block, scale
):
    block_count = queries.shape[1] // query_block

    def one_block(carry, index):
        key_grad, value_grad = carry
        start = index * query_block
        query_part = lax.dynamic_slice_in_dim(queries, start, query_block, 1)
        seg_part = lax.dynamic_slice_in_dim(seg_full, start, query_block, 1)
        grad_part = lax.dynamic_slice_in_dim(grad_heads, start, query_block, 1)
        scores = (
            jnp.einsum("rqhd,rkhd->rhqk", query_part, keys_all, preferred_element_type=jnp.float32)
            * scale
        )
        allowed = seg_part[:, None, :, None] == seg_full[:, None, None, :]
        scores = jnp.where(allowed, scores, -1e30)
        probability = jnp.exp(scores - log_totals[index][..., None])
        dotted = jnp.einsum(
            "rqhd,rkhd->rhqk", grad_part, values_all, preferred_element_type=jnp.float32
        )
        center = jnp.sum(probability * dotted, axis=-1, keepdims=True)
        score_grad = (probability * (dotted - center)).astype(jnp.bfloat16)
        query_grad = (
            jnp.einsum("rhqk,rkhd->rqhd", score_grad, keys_all, preferred_element_type=jnp.float32)
            * scale
        )
        key_grad = (
            key_grad
            + jnp.einsum(
                "rhqk,rqhd->rkhd", score_grad, query_part, preferred_element_type=jnp.float32
            )
            * scale
        )
        value_grad = value_grad + jnp.einsum(
            "rhqk,rqhd->rkhd",
            probability.astype(jnp.bfloat16),
            grad_part,
            preferred_element_type=jnp.float32,
        )
        return ((key_grad, value_grad), query_grad)

    starting = (jnp.zeros(keys_all.shape, jnp.float32), jnp.zeros(values_all.shape, jnp.float32))
    (key_grad, value_grad), query_blocks = lax.scan(
        one_block, starting, jnp.arange(block_count, dtype=jnp.int32)
    )
    query_grad = jnp.moveaxis(query_blocks, 0, 1).reshape(queries.shape)
    return (query_grad, key_grad, value_grad)


def body(
    tokens,
    timestep,
    segment_ids,
    cotangent,
    time_weight,
    qkv_weight,
    qv_bias,
    out_weight,
    out_bias,
    norm_gain,
    norm_bias,
    up_weight,
    up_bias,
    down_weight,
    down_bias,
    final_gain,
    final_bias,
):
    shards = (
        time_weight,
        qkv_weight,
        qv_bias,
        out_weight,
        out_bias,
        norm_gain,
        norm_bias,
        up_weight,
        up_bias,
        down_weight,
        down_bias,
        final_gain,
        final_bias,
    )
    sp_count = lax.axis_size("sp")
    micro_count = max(2, sp_count // 2)
    rows_local, piece_len, model_width = tokens.shape
    rows_micro = rows_local // micro_count
    seq_len = piece_len * sp_count
    width_local = model_width // sp_count
    heads_local = HEADS // sp_count
    query_block = min(512, seq_len)
    scale = 1.0 / math.sqrt(HEAD_DIM)
    tok_count = rows_micro * piece_len
    owned = tuple((jnp.zeros(piece.shape, jnp.float32) for piece in shards))
    output_parts = []
    input_parts = []
    for micro in range(micro_count):
        first_row = micro * rows_micro
        block_tokens = tokens[first_row : first_row + rows_micro]
        block_cotangent = cotangent[first_row : first_row + rows_micro]
        block_segments = segment_ids[first_row : first_row + rows_micro]
        block_stamps = timestep[first_row : first_row + rows_micro]
        gathered = (
            lax.all_gather(shards[0], ("dp", "sp"), axis=0, tiled=True),
            lax.all_gather(shards[1], ("dp", "sp"), axis=0, tiled=True),
            lax.all_gather(shards[2], ("dp", "sp"), axis=0, tiled=True),
            lax.all_gather(shards[3], ("dp", "sp"), axis=0, tiled=True),
            lax.all_gather(shards[4], ("dp", "sp"), axis=0, tiled=True),
            lax.all_gather(shards[5], ("dp", "sp"), axis=0, tiled=True),
            lax.all_gather(shards[6], ("dp", "sp"), axis=0, tiled=True),
            lax.all_gather(shards[7], ("dp", "sp"), axis=0, tiled=True),
            lax.all_gather(shards[8], ("dp", "sp"), axis=0, tiled=True),
            lax.all_gather(shards[9], ("dp", "sp"), axis=0, tiled=True),
            lax.all_gather(shards[10], ("dp", "sp"), axis=0, tiled=True),
            lax.all_gather(shards[11], ("dp", "sp"), axis=0, tiled=True),
            lax.all_gather(shards[12], ("dp", "sp"), axis=0, tiled=True),
        )
        (
            time_full,
            qkv_full,
            qv_full,
            out_full,
            out_shift,
            first_gain,
            first_shift,
            up_full,
            up_shift,
            down_full,
            down_shift,
            second_gain,
            second_shift,
        ) = gathered
        features = time_features(block_stamps, model_width).astype(jnp.bfloat16)
        embedded = jnp.dot(features, time_full, preferred_element_type=jnp.float32)
        hidden = block_tokens.astype(jnp.float32) + embedded[:, None, :]
        hidden_flat = hidden.reshape(tok_count, model_width)
        hidden_low = hidden_flat.astype(jnp.bfloat16)
        qv_float = qv_full.astype(jnp.float32)
        qkv_shift = jnp.concatenate(
            [qv_float[:model_width], jnp.zeros((model_width,), jnp.float32), qv_float[model_width:]]
        )
        packed = jnp.dot(hidden_low, qkv_full, preferred_element_type=jnp.float32) + qkv_shift
        packed = packed.astype(jnp.bfloat16).reshape(rows_micro, piece_len, 3, model_width)
        seg_copies = jnp.broadcast_to(
            block_segments[:, :, None, None], (rows_micro, piece_len, 1, sp_count)
        )
        packed_heads, seg_heads = (
            lax.all_to_all(packed, "sp", split_axis=3, concat_axis=1, tiled=True),
            lax.all_to_all(seg_copies, "sp", split_axis=3, concat_axis=1, tiled=True),
        )
        seg_full = seg_heads[:, :, 0, 0]
        head_shape = (rows_micro, seq_len, heads_local, HEAD_DIM)
        queries = packed_heads[:, :, 0].reshape(head_shape)
        keys_all = packed_heads[:, :, 1].reshape(head_shape)
        values_all = packed_heads[:, :, 2].reshape(head_shape)
        mixed, log_totals = attention_forward(
            queries, keys_all, values_all, seg_full, query_block, scale
        )
        mixed_low = mixed.astype(jnp.bfloat16).reshape(rows_micro, seq_len, width_local)
        mixed_local = lax.all_to_all(mixed_low, "sp", split_axis=1, concat_axis=2, tiled=True)
        mixed_flat = mixed_local.reshape(tok_count, model_width)
        attended = jnp.dot(
            mixed_flat, out_full, preferred_element_type=jnp.float32
        ) + out_shift.astype(jnp.float32)
        first_gain_f = first_gain.astype(jnp.float32)
        normed, normal_one, inverse_one = layer_norm_parts(
            hidden_flat + attended, first_gain_f, first_shift.astype(jnp.float32)
        )
        normed_low = normed.astype(jnp.bfloat16)
        upward = jnp.dot(normed_low, up_full, preferred_element_type=jnp.float32) + up_shift.astype(
            jnp.float32
        )
        activated = jax.nn.gelu(upward, approximate=False).astype(jnp.bfloat16)
        downward = jnp.dot(
            activated, down_full, preferred_element_type=jnp.float32
        ) + down_shift.astype(jnp.float32)
        second_gain_f = second_gain.astype(jnp.float32)
        result, normal_two, inverse_two = layer_norm_parts(
            normed + downward, second_gain_f, second_shift.astype(jnp.float32)
        )
        output_parts.append(result.astype(jnp.bfloat16).reshape(rows_micro, piece_len, model_width))
        upstream = block_cotangent.reshape(tok_count, model_width).astype(jnp.float32)
        grad_second_gain = jnp.sum(upstream * normal_two, axis=0)
        grad_second_shift = jnp.sum(upstream, axis=0)
        resid_two = layer_norm_back(upstream, normal_two, inverse_two, second_gain_f)
        down_grad = resid_two.astype(jnp.bfloat16)
        grad_down_shift = jnp.sum(down_grad, axis=0, dtype=jnp.float32)
        grad_down_full = contract_rows(activated, down_grad)
        act_grad = times_transposed(down_grad, down_full)
        up_grad = (act_grad * gelu_slope(upward)).astype(jnp.bfloat16)
        grad_up_shift = jnp.sum(up_grad, axis=0, dtype=jnp.float32)
        grad_up_full = contract_rows(normed_low, up_grad)
        normed_grad = resid_two + times_transposed(up_grad, up_full)
        grad_first_gain = jnp.sum(normed_grad * normal_one, axis=0)
        grad_first_shift = jnp.sum(normed_grad, axis=0)
        resid_one = layer_norm_back(normed_grad, normal_one, inverse_one, first_gain_f)
        attended_grad = resid_one.astype(jnp.bfloat16)
        grad_out_shift = jnp.sum(attended_grad, axis=0, dtype=jnp.float32)
        grad_out_full = contract_rows(mixed_flat, attended_grad)
        mixed_grad = times_transposed(attended_grad, out_full).astype(jnp.bfloat16)
        mixed_grad = mixed_grad.reshape(rows_micro, piece_len, model_width)
        grad_heads = lax.all_to_all(
            mixed_grad, "sp", split_axis=2, concat_axis=1, tiled=True
        ).reshape(head_shape)
        query_grad, key_grad, value_grad = attention_backward(
            queries, keys_all, values_all, seg_full, grad_heads, log_totals, query_block, scale
        )
        packed_grad = jnp.stack([query_grad, key_grad, value_grad], axis=2)
        packed_grad = packed_grad.reshape(rows_micro, seq_len, 3, width_local).astype(jnp.bfloat16)
        packed_local = lax.all_to_all(packed_grad, "sp", split_axis=1, concat_axis=3, tiled=True)
        packed_flat = packed_local.reshape(tok_count, 3 * model_width)
        third_sums = jnp.sum(packed_flat, axis=0, dtype=jnp.float32)
        grad_qv_full = jnp.concatenate([third_sums[:model_width], third_sums[2 * model_width :]])
        grad_qkv_full = contract_rows(hidden_low, packed_flat)
        hidden_grad = resid_one + times_transposed(packed_flat, qkv_full)
        input_parts.append(
            hidden_grad.astype(jnp.bfloat16).reshape(rows_micro, piece_len, model_width)
        )
        embed_grad = jnp.sum(hidden_grad.reshape(rows_micro, piece_len, model_width), axis=1)
        grad_time_full = jnp.dot(
            features.astype(jnp.float32).T, embed_grad, precision=lax.Precision.HIGHEST
        )
        grads = (
            grad_time_full,
            grad_qkv_full,
            grad_qv_full,
            grad_out_full,
            grad_out_shift,
            grad_first_gain,
            grad_first_shift,
            grad_up_full,
            grad_up_shift,
            grad_down_full,
            grad_down_shift,
            grad_second_gain,
            grad_second_shift,
        )
        shares = lax.psum_scatter(
            flatten_grads(grads), ("dp", "sp"), scatter_dimension=0, tiled=True
        )
        owned = jax.tree.map(jnp.add, owned, restore_grads(shares, owned))
    output = jnp.concatenate(output_parts, axis=0)
    input_grad = jnp.concatenate(input_parts, axis=0)
    return (
        output,
        input_grad,
        owned[0],
        owned[1],
        owned[2],
        owned[3],
        owned[4],
        owned[5],
        owned[6],
        owned[7],
        owned[8],
        owned[9],
        owned[10],
        owned[11],
        owned[12],
    )


def solution(mesh):
    in_specs = (
        P("dp", "sp", None),
        P("dp"),
        P("dp", "sp"),
        P("dp", "sp", None),
        P(("dp", "sp"), None),
        P(("dp", "sp"), None),
        P(("dp", "sp")),
        P(("dp", "sp"), None),
        P(("dp", "sp")),
        P(("dp", "sp")),
        P(("dp", "sp")),
        P(("dp", "sp"), None),
        P(("dp", "sp")),
        P(("dp", "sp"), None),
        P(("dp", "sp")),
        P(("dp", "sp")),
        P(("dp", "sp")),
    )
    out_specs = (
        P("dp", "sp", None),
        P("dp", "sp", None),
        P(("dp", "sp"), None),
        P(("dp", "sp"), None),
        P(("dp", "sp")),
        P(("dp", "sp"), None),
        P(("dp", "sp")),
        P(("dp", "sp")),
        P(("dp", "sp")),
        P(("dp", "sp"), None),
        P(("dp", "sp")),
        P(("dp", "sp"), None),
        P(("dp", "sp")),
        P(("dp", "sp")),
        P(("dp", "sp")),
    )
    return jax.shard_map(body, mesh=mesh, in_specs=in_specs, out_specs=out_specs, check_vma=False)
```

profile of v0, /device:TPU:0, one launch (start us, length us, event | category | flops | bytes accessed | tf_op | source)
XLA Modules:
  0.0 1843.3 jit_solution(8675911827234323687)
XLA Ops:
  18.5 42.3 %all-reduce.16 = (bf16[2048]{0:T(1024)(128)(2,1)S(1)}, bf16[1024]{0:T(1024)(128)(2,1)}, bf16[1024]{0:T(1024)(128)(2,1)}, bf16[1024]{0:T(1024)(128)(2,1)}, bf16[1...) all-reduce(bf16[2048]{0:T(1024)(128)(2,1)S(1)} %dynamic-update-slic, ...), channel_id=1, replica_groups=mesh['dp'=8,'sp'=4] {'dp','sp'}, use_global_device_ids=true, to_apply=%add | all-reduce | flops 8192 | bytes 32768
  60.8 9.8 all-gather.7.cloned.1.call-done
  72.6 69.3 %all-gather.9.cloned.1.call-done = bf16[1024,3072]{1,0:T(8,128)(2,1)} async-done(((bf16[32,3072]{1,0:T(8,128)(2,1)}), bf16[1024,3072]{1,0:T(8,128)(2,1)}) %all-gather.9.cloned.1.call-update) | async-done | bytes 6291472 | tf_op jit(solution)/shard_map/all_gather | solution.py:203
  141.9 4.8 fusion.122
  157.7 5.7 fusion.123
  166.0 4.2 copy.161
  170.2 36.2 %all-to-all-done.1 = bf16[1,256,3,1024]{1,2,0,3:T(4,128)(2,1)S(1)} async-done(((bf16[1,256,3,1024]{1,2,0,3:T(4,128)(2,1)}), bf16[1,256,3,1024]{1,2,0,3:T(4,128)(2,1)S(1)}, u32[]{:S(2)}, u32[]{:S(2)}) %all-to-all-start.1) | async-done | bytes 1572896 | tf_op jit(solution)/shard_map/all_to_all | solution.py:246
  206.4 4.5 all-to-all-start.4
  214.6 51.6 %all-to-all-done.4 = bf16[1,256,3,1024]{1,2,0,3:T(4,128)(2,1)} async-done(((bf16[1,256,3,1024]{1,2,0,3:T(4,128)(2,1)}), bf16[1,256,3,1024]{1,2,0,3:T(4,128)(2,1)}, u32[]{:S(2)}, u32[]{:S(2)}) %all-to-all-start.4) | async-done | bytes 1572896 | tf_op jit(solution)/shard_map/all_to_all | solution.py:246
  276.4 5.0 all-to-all-start.3
  282.2 19.0 %while.54 = (s32[]{:T(128)}, bf16[2,1,512,4,64]{2,4,3,1,0:T(8,128)(2,1)}, f32[2,1,4,512]{3,2,1,0:T(4,128)S(1)}, s32[2]{0:T(128)S(1)}, s32[1,1024]{1,0:T(1,128)S(...) while((s32[]{:T(128)}, ...), condition=%wide.region_3.4_spmd, body=%wide.region_0.3_spmd.sunk | while | flops 562558976 | bytes 33368328 | solution.py:93
  304.8 3.9 reshape.869
  309.3 3.8 reduce.20
  317.9 5.4 all-to-all-start.2
  323.3 17.4 while.55
  345.1 4.8 reduce.21
  350.8 5.1 all-to-all-start.5
  355.9 77.1 %all-gather = bf16[32,1,128]{2,1,0:T(2,128)(2,1)S(1)} all-gather(bf16[1,1,128]{2,1,0:T(2,128)(2,1)S(1)} %bitcast.534), channel_id=1, replica_groups=mesh['dp'=8,'sp'=4] {'dp','sp'}, dimensions={0}, use_global_device_ids=true | all-gather | bytes 8448 | tf_op jit(solution)/shard_map/all_gather | solution.py:210
  451.9 15.7 fusion.96
  467.7 6.8 fusion.196
  474.9 11.7 fusion.99
  493.4 7.3 convert_reduce_fusion.1
  500.8 4.2 multiply_reduce_fusion.3
  505.0 6.7 convert_reduce_fusion
  511.7 6.6 convert_reduce_fusion.9
  525.4 5.6 reduce.22
  532.9 4.1 all-to-all-start.8
  544.1 5.6 reduce.23
  556.6 4.9 reshape.837
  561.6 5.2 all-to-all-start.6
  575.8 57.1 %while.57 = (s32[]{:T(128)}, f32[1,1024,4,64]{1,3,2,0:T(8,128)S(1)}, f32[1,1024,4,64]{1,3,2,0:T(8,128)}, bf16[2,1,512,4,64]{2,4,3,1,0:T(8,128)(2,1)}, s32[2]{0:T...) while((s32[]{:T(128)}, ...), condition=%wide.region_29.30_spmd.clone, body=%wide.region_27.29_spmd.clone.sunk | while | flops 1375598592 | bytes 129042952 | solution.py:141
  577.0 4.6 fusion.301
  584.0 5.8 multiply_reduce_fusion.15
  590.0 3.7 multiply_convert_fusion.5
  597.0 5.0 fusion.303
  605.6 4.6 fusion.301
  612.5 5.8 multiply_reduce_fusion.15
  618.6 3.7 multiply_convert_fusion.5
  625.6 5.0 fusion.303
  639.0 5.7 all-to-all-start.9
  653.8 57.0 %while.56 = (s32[]{:T(128)}, f32[1,1024,4,64]{1,3,2,0:T(8,128)S(1)}, f32[1,1024,4,64]{1,3,2,0:T(8,128)}, bf16[2,1,512,4,64]{2,4,3,1,0:T(8,128)(2,1)}, s32[2]{0:T...) while((s32[]{:T(128)}, ...), condition=%wide.region_22.23_spmd.clone, body=%wide.region_20.22_spmd.clone.sunk | while | flops 1375598592 | bytes 129042952 | solution.py:141
  655.0 4.6 fusion.289
  662.0 5.8 multiply_reduce_fusion.14
  675.0 5.0 fusion.291
  683.5 4.6 fusion.289
  690.5 5.8 multiply_reduce_fusion.14
  703.5 5.0 fusion.291
  716.9 5.1 all-to-all-start.7
  725.5 48.1 %all-to-all-done.7 = bf16[1,1024,3,256]{3,2,0,1:T(4,128)(2,1)} async-done(((bf16[1,1024,3,256]{3,2,0,1:T(4,128)(2,1)}), bf16[1,1024,3,256]{3,2,0,1:T(4,128)(2,1)}, u32[]{:S(2)}, u32[]{:S(2)}) %all-to-all-start.7) | async-done | bytes 1572896 | tf_op jit(solution)/shard_map/all_to_all | solution.py:308
  777.1 5.5 convolution_add_fusion.10
  782.6 5.8 fusion.190
  790.9 4.9 reshape.835
  800.3 6.4 convolution_add_fusion.2
  806.7 13.8 reshape.836
  821.2 4.4 fusion.183
  825.7 10.0 convolution_add_fusion.1
  835.7 18.0 reshape.838
  854.9 4.0 fusion.176
  858.9 10.1 convolution_add_fusion
  869.0 18.0 reshape.839
  891.7 40.6 %all-reduce.15 = (f32[2048]{0:T(1024)S(1)}, f32[1024]{0:T(1024)S(1)}, f32[1024]{0:T(1024)S(1)}, f32[1024]{0:T(1024)S(1)}, f32[4096]{0:T(1024)S(1)}, /*index=5*/f...) all-reduce(f32[2048]{0:T(1024)S(1)} %maximum_add_fusion, ...), channel_id=17, replica_groups=mesh['dp'=8,'sp'=4] {'dp','sp'}, use_global_device_ids=true, to_apply=%region_37.38.clone | all-reduce | flops 12288 | bytes 98304
  945.4 158.6 %reduce-scatter.8.cloned.1.call-done = f32[768,128]{1,0:T(8,128)} async-done(((f32[24576,128]{1,0:T(8,128)}), f32[768,128]{1,0:T(8,128)}) %reduce-scatter.8.cloned.1.call-update) | async-done | bytes 393232 | tf_op jit(solution)/shard_map/reduce_scatter | solution.py:336
  1105.8 364.0 %reduce-scatter.12.cloned.1.call-done = f32[1024,128]{1,0:T(8,128)} async-done(((f32[32768,128]{1,0:T(8,128)}), f32[1024,128]{1,0:T(8,128)}) %reduce-scatter.12.cloned.1.call-update) | async-done | bytes 524304 | tf_op jit(solution)/shard_map/reduce_scatter | solution.py:336
  1471.8 362.5 %reduce-scatter.14.cloned.1.call-done = f32[1024,128]{1,0:T(8,128)} async-done(((f32[32768,128]{1,0:T(8,128)}), f32[1024,128]{1,0:T(8,128)}) %reduce-scatter.14.cloned.1.call-update) | async-done | bytes 524304 | tf_op jit(solution)/shard_map/reduce_scatter | solution.py:336
  (500 shorter events, 240.0 us)
Async XLA Ops:
  7.2 63.4 %all-gather.7.cloned.1.call-start = ((), (), s32[]{:S(2)}) async-start(), calls=%async_computation.15 | async-start | bytes 2162688 | tf_op jit(solution)/shard_map/all_gather | solution.py:202
  7.9 134.0 %all-gather.9.cloned.1.call-start = ((), (), s32[]{:S(2)}) async-start(), calls=%async_computation.16 | async-start | bytes 6488064 | tf_op jit(solution)/shard_map/all_gather | solution.py:203
  8.7 437.3 %all-gather.11.cloned.1.call-start = ((), (), s32[]{:S(2)}) async-start(), calls=%async_computation.17 | async-start | bytes 2162688 | tf_op jit(solution)/shard_map/all_gather | solution.py:205
  9.4 442.5 %all-gather.13.cloned.1.call-start = ((), (), s32[]{:S(2)}) async-start(), calls=%async_computation.18 | async-start | bytes 8650752 | tf_op jit(solution)/shard_map/all_gather | solution.py:209
  72.6 69.4 %copy-start.59 = (f32[1,1024]{1,0:T(1,128)}, f32[1,1024]{1,0:T(1,128)S(1)}, u32[]{:S(2)}) copy-start(f32[1,1024]{1,0:T(1,128)S(1)} %fusion.199) | copy-start | bytes 12292
  147.4 10.3 copy-start.27
  150.1 56.3 %all-to-all-start.1 = ((bf16[1,256,3,1024]{1,2,0,3:T(4,128)(2,1)}), bf16[1,256,3,1024]{1,2,0,3:T(4,128)(2,1)S(1)}, u32[]{:S(2)}, u32[]{:S(2)}) async-start(bf16[1,256,3,1024]{1,2,0,3:T(4,128)(2,1)} %copy.151), calls=%async_computation.1 | async-start | bytes 4194304 | tf_op jit(solution)/shard_map/all_to_all | solution.py:246
  166.0 45.5 %copy-start.90 = (s32[2,256]{1,0:T(2,128)S(1)}, s32[2,256]{1,0:T(2,128)}, u32[]{:S(2)}) copy-start(s32[2,256]{1,0:T(2,128)} %param.27) | copy-start | bytes 6148
  206.4 59.8 %all-to-all-start.4 = ((bf16[1,256,3,1024]{1,2,0,3:T(4,128)(2,1)}), bf16[1,256,3,1024]{1,2,0,3:T(4,128)(2,1)}, u32[]{:S(2)}, u32[]{:S(2)}) async-start(bf16[1,256,3,1024]{1,2,0,3:T(4,128)(2,1)} %copy.161), calls=%async_computation.4 | async-start | bytes 4194304 | tf_op jit(solution)/shard_map/all_to_all | solution.py:246
  210.9 256.8 %all-gather.15.cloned.1.call-start = ((), (), s32[]{:S(2)}) async-start(), calls=%async_computation.19 | async-start | bytes 8650752 | tf_op jit(solution)/shard_map/all_gather | solution.py:211
  266.8 9.0 all-to-all-start
  276.4 41.5 %all-to-all-start.3 = ((s32[1,256,1,4]{1,2,0,3:T(1,128)}), s32[1,256,1,4]{1,2,0,3:T(1,128)S(1)}, u32[]{:S(2)}, u32[]{:S(2)}) async-start(s32[1,256,1,4]{1,2,0,3:T(1,128)} %broadcast_in_dim.71), calls=%async_computation.3 | async-start | bytes 8192 | tf_op jit(solution)/shard_map/all_to_all | solution.py:247
  301.2 11.9 copy-start.2
  301.2 11.9 copy-start.5
  301.2 11.9 copy-start.12
  301.2 11.9 copy-start.44
  301.2 11.9 copy-start.57
  317.9 32.9 %all-to-all-start.2 = ((bf16[4,2,32768]{2,1,0:T(2,128)(2,1)}), bf16[4,2,32768]{2,1,0:T(2,128)(2,1)S(1)}, u32[]{:S(2)}, u32[]{:S(2)}) async-start(bf16[4,2,32768]{2,1,0:T(2,128)(2,1)} %reshape.873), calls=%async_computation.2 | async-start | bytes 1048576 | tf_op jit(solution)/shard_map/all_to_all | solution.py:258
  341.6 14.4 copy-start.89
  341.6 14.4 copy-start.91
  341.6 91.5 %copy-start.88 = (bf16[1024]{0:T(1024)(128)(2,1)S(1)}, bf16[1024]{0:T(1024)(128)(2,1)}, u32[]{:S(2)}) copy-start(bf16[1024]{0:T(1024)(128)(2,1)} %get-tuple-element.480) | copy-start | bytes 6148
  341.6 91.5 %copy-start.87 = (bf16[1024]{0:T(1024)(128)(2,1)S(1)}, bf16[1024]{0:T(1024)(128)(2,1)}, u32[]{:S(2)}) copy-start(bf16[1024]{0:T(1024)(128)(2,1)} %get-tuple-element.481) | copy-start | bytes 6148
  341.6 91.6 %copy-start.86 = (bf16[1024]{0:T(1024)(128)(2,1)S(1)}, bf16[1024]{0:T(1024)(128)(2,1)}, u32[]{:S(2)}) copy-start(bf16[1024]{0:T(1024)(128)(2,1)} %get-tuple-element.482) | copy-start | bytes 6148
  341.6 91.6 %copy-start.85 = (bf16[1024]{0:T(1024)(128)(2,1)S(1)}, bf16[1024]{0:T(1024)(128)(2,1)}, u32[]{:S(2)}) copy-start(bf16[1024]{0:T(1024)(128)(2,1)} %get-tuple-element.485) | copy-start | bytes 6148
  341.6 91.6 %copy-start.84 = (bf16[1024]{0:T(1024)(128)(2,1)S(1)}, bf16[1024]{0:T(1024)(128)(2,1)}, u32[]{:S(2)}) copy-start(bf16[1024]{0:T(1024)(128)(2,1)} %get-tuple-element.484) | copy-start | bytes 6148
  350.8 90.0 %all-to-all-start.5 = ((bf16[4,2,32768]{2,1,0:T(2,128)(2,1)}), bf16[4,2,32768]{2,1,0:T(2,128)(2,1)S(1)}, u32[]{:S(2)}, u32[]{:S(2)}) async-start(bf16[4,2,32768]{2,1,0:T(2,128)(2,1)} %reshape.871), calls=%async_computation.5 | async-start | bytes 1048576 | tf_op jit(solution)/shard_map/all_to_all | solution.py:258
  433.1 53.5 %copy-start.52 = (f32[1024]{0:T(1024)}, f32[1024]{0:T(1024)S(1)}, u32[]{:S(2)}) copy-start(f32[1024]{0:T(1024)S(1)} %convert_element_type.247) | copy-start | bytes 12292
  433.1 85.1 %copy-start.50 = (f32[1024]{0:T(1024)}, f32[1024]{0:T(1024)S(1)}, u32[]{:S(2)}) copy-start(f32[1024]{0:T(1024)S(1)} %convert_element_type.246) | copy-start | bytes 12292
  433.2 12.8 copy-start.60
  442.6 7.2 copy-start.55
  448.8 62.8 %copy-start.64 = (f32[256]{0:T(256)}, f32[256]{0:T(256)S(1)}, u32[]{:S(2)}) copy-start(f32[256]{0:T(256)S(1)} %broadcast_multiply_fusion.11) | copy-start | bytes 3076
  450.7 67.6 %copy-start.62 = (f32[256]{0:T(256)}, f32[256]{0:T(256)S(1)}, u32[]{:S(2)}) copy-start(f32[256]{0:T(256)S(1)} %broadcast_multiply_fusion.9) | copy-start | bytes 3076
  451.9 59.8 %copy-start.77 = (f32[256]{0:T(256)}, f32[256]{0:T(256)S(1)}, u32[]{:S(2)}) copy-start(f32[256]{0:T(256)S(1)} %add_rsqrt_fusion.3) | copy-start | bytes 3076
  451.9 66.4 %copy-start.66 = (f32[256]{0:T(256)}, f32[256]{0:T(256)S(1)}, u32[]{:S(2)}) copy-start(f32[256]{0:T(256)S(1)} %add_rsqrt_fusion.1) | copy-start | bytes 3076
  467.7 7.1 copy-start.10
  467.7 7.1 copy-start.92
  467.7 18.9 %slice-start.4 = ((s8[8388608]{0:T(1024)(128)(4,1)}), s8[4194304]{0:T(1024)(128)(4,1)S(1)}, s32[]{:S(2)}) async-start(s8[8388608]{0:T(1024)(128)(4,1)} %bitcast.535), calls=%async_computation.29 | async-start | bytes 8388608
  474.8 11.8 slice-start.5
  493.4 7.3 copy-start.30
  493.4 18.3 copy-start.33
  493.4 7.3 copy-start.17
  511.7 6.6 copy-start.34
  511.7 8.6 copy-start.8
  532.9 28.7 %all-to-all-start.8 = ((bf16[4,2,32768]{2,1,0:T(2,128)(2,1)}), bf16[4,2,32768]{2,1,0:T(2,128)(2,1)}, u32[]{:S(2)}, u32[]{:S(2)}) async-start(bf16[4,2,32768]{2,1,0:T(2,128)(2,1)} %reshape.875), calls=%async_computation.8 | async-start | bytes 1048576 | tf_op jit(solution)/shard_map/all_to_all | solution.py:300
  537.0 402.3 %reduce-scatter.10.cloned.1.call-start = ((), (), s32[]{:S(2)}) async-start(), calls=%async_computation.22 | async-start | bytes 4325376 | tf_op jit(solution)/shard_map/reduce_scatter | solution.py:336
  561.6 77.5 %all-to-all-start.6 = ((bf16[4,2,32768]{2,1,0:T(2,128)(2,1)}), bf16[4,2,32768]{2,1,0:T(2,128)(2,1)}, u32[]{:S(2)}, u32[]{:S(2)}) async-start(bf16[4,2,32768]{2,1,0:T(2,128)(2,1)} %reshape.877), calls=%async_computation.6 | async-start | bytes 1048576 | tf_op jit(solution)/shard_map/all_to_all | solution.py:300
  584.0 6.0 slice-start.1
  612.5 6.1 slice-start.1
  639.0 14.7 copy-start.3
  639.0 14.7 copy-start.4
  639.0 14.7 copy-start.6
  639.0 14.7 copy-start.13
  639.0 14.7 copy-start.45
  639.0 14.7 copy-start.58
  639.0 77.8 %all-to-all-start.9 = ((bf16[1,1024,3,256]{3,2,0,1:T(4,128)(2,1)}), bf16[1,1024,3,256]{3,2,0,1:T(4,128)(2,1)}, u32[]{:S(2)}, u32[]{:S(2)}) async-start(bf16[1,1024,3,256]{3,2,0,1:T(4,128)(2,1)} %copy.179), calls=%async_computation.9 | async-start | bytes 4194304 | tf_op jit(solution)/shard_map/all_to_all | solution.py:308
  661.9 6.0 slice-start.3
  690.5 6.0 slice-start.3
  716.9 56.8 %all-to-all-start.7 = ((bf16[1,1024,3,256]{3,2,0,1:T(4,128)(2,1)}), bf16[1,1024,3,256]{3,2,0,1:T(4,128)(2,1)}, u32[]{:S(2)}, u32[]{:S(2)}) async-start(bf16[1,1024,3,256]{3,2,0,1:T(4,128)(2,1)} %copy.173), calls=%async_computation.7 | async-start | bytes 4194304 | tf_op jit(solution)/shard_map/all_to_all | solution.py:308
  722.0 221.8 %reduce-scatter.6.cloned.1.call-start = ((), (), s32[]{:S(2)}) async-start(), calls=%async_computation.20 | async-start | bytes 4325376 | tf_op jit(solution)/shard_map/reduce_scatter | solution.py:336
  775.4 7.1 copy-start.14
  782.6 5.8 copy-start.75
  795.9 308.1 %reduce-scatter.8.cloned.1.call-start = ((), (), s32[]{:S(2)}) async-start(), calls=%async_computation.21 | async-start | bytes 12976128 | tf_op jit(solution)/shard_map/reduce_scatter | solution.py:336
  820.6 649.2 %reduce-scatter.12.cloned.1.call-start = ((), (), s32[]{:S(2)}) async-start(), calls=%async_computation.23 | async-start | bytes 17301504 | tf_op jit(solution)/shard_map/reduce_scatter | solution.py:336
  853.7 980.6 %reduce-scatter.14.cloned.1.call-start = ((), (), s32[]{:S(2)}) async-start(), calls=%async_computation.24 | async-start | bytes 17301504 | tf_op jit(solution)/shard_map/reduce_scatter | solution.py:336
  (74 other events, 212.5 us)
Sparse Core Ops, SparseCore 0:
  10.9 59.6 all-gather.6
  73.5 68.3 all-gather.8
  144.9 84.7 all-gather.10
  232.4 88.9 all-gather.12
  324.2 84.4 all-gather.14
  561.7 183.6 reduce-scatter.9
  796.0 147.7 reduce-scatter.5
  949.8 154.1 reduce-scatter.7
  1106.4 363.3 reduce-scatter.11
  1472.1 362.1 reduce-scatter.13
where the time goes:
time: 1860 us; the launch traced here: 1840 us
  waiting for transfers between devices  1110 us (60%)
  matrix products  238 us (13%)
  local copies, waits for them, and re-layouts  194 us (10%)
  blocking collectives  160 us (9%)
  other arithmetic  66.4 us (4%)
  starting transfers between devices  47.6 us (3%)
    reduce_scatter x5, waiting for transfers between devices, body(): lax.psum_scatter(flatten_grads(grads), ('dp', 'sp'), scatter_dimension=0,...  888 us
    all_to_all x2, waiting for transfers between devices, body(): lax.all_to_all(packed, 'sp', split_axis=3, concat_axis=1, tiled=True)  87.8 us
    unnamed x2, blocking collectives  82.9 us
    all_gather x1, blocking collectives, body(): lax.all_gather(shards[8], ('dp', 'sp'), axis=0, tiled=True)  77.1 us
    all_gather x1, waiting for transfers between devices, body(): lax.all_gather(shards[1], ('dp', 'sp'), axis=0, tiled=True)  69.3 us
    add x10, local copies, waits for them, and re-layouts, body(): owned = jax.tree.map(jnp.add, owned, restore_grads(shares, owned))  68.5 us
    all_to_all x2, waiting for transfers between devices, body(): lax.all_to_all(packed_grad, 'sp', split_axis=1, concat_axis=3, tiled=True)  48.1 us
    unnamed x205, local copies, waits for them, and re-layouts  43 us
  transfers between devices with their start and end apart: 20, of which 10 were waited for; matrix products, arithmetic and copies ran while one was open for 23% of the time, Pallas kernels for 0%

commit v1 on v0

--- a/solution.py
+++ b/solution.py
@@ -3,6 +3,8 @@
 import jax
 import jax.numpy as jnp
 from jax import lax
+from jax.experimental import pallas as pl
+from jax.experimental.pallas import tpu as pltpu
 from jax.sharding import PartitionSpec as P
 
 HEADS = 16
@@ -358,6 +360,968 @@
     )
 
 
+AXES = ("dp", "sp")
+BF = jnp.bfloat16
+F32 = jnp.float32
+NT = (((1,), (1,)), ((), ()))
+TN = (((0,), (0,)), ((), ()))
+NN = (((1,), (0,)), ((), ()))
+VMEM_LIMIT = 48 * 1024 * 1024
+CHIP_SLOTS = ((0, 0, 0), (0, 0, 1), (0, 1, 0), (0, 1, 1), (1, 0, 0), (1, 0, 1), (1, 1, 0), (1, 1, 1))
+
+
+def dot(left, right, dims=NN):
+    return lax.dot_general(left, right, dims, preferred_element_type=F32)
+
+
+def device_perm(target):
+    pairs = []
+    for y in range(2):
+        for x in range(2):
+            for c in range(2):
+                for z in range(4):
+                    ty, tx, tc, tz = target(y, x, c, z)
+                    source = ((y * 2 + x) * 2 + c) * 4 + z
+                    pairs.append((source, ((ty * 2 + tx) * 2 + tc) * 4 + tz))
+    return pairs
+
+
+PAIR = device_perm(lambda y, x, c, z: (y, x, 1 - c, z))
+ALONG_X = device_perm(lambda y, x, c, z: (y, 1 - x, c, z))
+ALONG_Y = device_perm(lambda y, x, c, z: (1 - y, x, c, z))
+DIAGONAL = device_perm(lambda y, x, c, z: (1 - y, 1 - x, c, z))
+SHIFT_Z = [device_perm(lambda y, x, c, z, k=k: (y, x, c, (z + k) % 4)) for k in range(4)]
+ROW_OUT = [device_perm(lambda y, x, c, z, k=k: (y, x, z // 2, c * 2 + (z + k) % 2)) for k in range(2)]
+ROW_BACK = [[(t, s) for s, t in pairs] for pairs in ROW_OUT]
+
+
+def send(value, pairs):
+    return lax.ppermute(value, AXES, pairs)
+
+
+def gather_pieces(shard):
+    near = [shard] + [send(shard, SHIFT_Z[k]) for k in (1, 2, 3)]
+    first, second = jnp.stack(near[:2]), jnp.stack(near[2:])
+    first_x, second_y = send(first, ALONG_X), send(second, ALONG_Y)
+    first_y, second_x = send(first, ALONG_Y), send(second, ALONG_X)
+    first_xy, second_xy = send(first_x, ALONG_Y), send(second_y, ALONG_X)
+    return [first, first_x, first_y, first_xy, second, second_x, second_y, second_xy]
+
+
+def scatter_pieces(first_keep, first_send, second_keep, second_send):
+    add = lambda a, b: (a.astype(F32) + b.astype(F32)).astype(BF)
+    from_y, from_x = send(first_send, ALONG_Y), send(second_send, ALONG_X)
+    to_x = add(first_keep[1], from_y[1])
+    to_y = add(second_keep[1], from_x[1])
+    from_x, from_y, mine_first, mine_second = (
+        send(to_x, ALONG_X),
+        send(to_y, ALONG_Y),
+        add(first_keep[0], from_y[0]),
+        add(second_keep[0], from_x[0]),
+    )
+    far = [
+        send(add(mine_first[1], from_x[1]), SHIFT_Z[1]),
+        send(add(mine_second[0], from_y[0]), SHIFT_Z[2]),
+        send(add(mine_second[1], from_y[1]), SHIFT_Z[3]),
+    ]
+    total = mine_first[0].astype(F32) + from_x[0].astype(F32)
+    return total + far[0].astype(F32) + far[1].astype(F32) + far[2].astype(F32)
+
+
+def place(meta, slot, j):
+    half, y_rel, x_rel = CHIP_SLOTS[slot]
+    y = lax.rem(meta[0] + y_rel, 2)
+    x = lax.rem(meta[1] + x_rel, 2)
+    z = lax.rem(meta[3] + 4 - (2 * half + j), 4)
+    return y * 2 + x, z
+
+
+def load_all(copies):
+    for copy in copies:
+        copy.start()
+    for copy in copies:
+        copy.wait()
+
+
+def load_split_rows(meta, refs, base, blocks, weight, sem):
+    copies = []
+    for slot, ref in enumerate(refs):
+        for j in range(2):
+            chip, z = place(meta, slot, j)
+            for other in range(2):
+                core = lax.rem(meta[2] + other, 2)
+                row = pl.multiple_of((chip * 2 + core) * 128 + z * 32, 32)
+                copies.append(
+                    pltpu.make_async_copy(
+                        ref.at[j, pl.ds(base + other * blocks, blocks)],
+                        weight.at[:, pl.ds(row, 32), :],
+                        sem.at[(slot * 2 + j) * 2 + other],
+                    )
+                )
+    return copies
+
+
+def load_own_rows(meta, refs, base, blocks, rows, weight, sem):
+    copies = []
+    for slot, ref in enumerate(refs):
+        for j in range(2):
+            chip, z = place(meta, slot, j)
+            row = pl.multiple_of((chip * 4 + z) * rows, 32)
+            copies.append(
+                pltpu.make_async_copy(
+                    ref.at[j, pl.ds(base, blocks)],
+                    weight.at[:, pl.ds(row, rows), :],
+                    sem.at[slot * 2 + j],
+                )
+            )
+    return copies
+
+
+def kernel_call(kernel, meta, operands, in_specs, out_specs, out_shape, scratch=(), grid=(4,), flops=0, moved=0, exps=0):
+    return pl.pallas_call(
+        kernel,
+        grid_spec=pltpu.PrefetchScalarGridSpec(
+            num_scalar_prefetch=1,
+            grid=grid,
+            in_specs=in_specs,
+            out_specs=out_specs,
+            scratch_shapes=list(scratch),
+        ),
+        out_shape=out_shape,
+        compiler_params=pltpu.CompilerParams(vmem_limit_bytes=VMEM_LIMIT),
+        cost_estimate=pl.CostEstimate(flops=flops, bytes_accessed=moved, transcendentals=exps),
+    )(meta, *operands)
+
+
+HBM = pl.BlockSpec(memory_space=pl.ANY)
+
+
+def spec(shape, index):
+    return pl.BlockSpec(shape, index)
+
+
+def whole(shape):
+    return pl.BlockSpec(shape, lambda i, m: (0,) * len(shape))
+
+
+def shaped(shape, kind):
+    return jax.ShapeDtypeStruct(shape, kind)
+
+
+def low_block(i):
+    return jnp.minimum(i, 1)
+
+
+def high_block(i):
+    return jnp.maximum(i - 2, 0)
+
+
+def turned(i):
+    return lax.rem(i + 2, 4)
+
+
+def project_qkv(meta, own, other, embedded, shift, pieces):
+    def kernel(m, own_ref, other_ref, emb_ref, shift_ref, *rest):
+        refs, (hidden_ref, out_ref, weight, sem) = rest[:8], rest[8:]
+        i = pl.program_id(0)
+
+        @pl.when(i == 0)
+        def _():
+            load_all(load_split_rows(m, refs, 0, 3, weight, sem))
+
+        tokens = jnp.where(i < 2, own_ref[...].astype(F32), other_ref[...].astype(F32))
+        hidden = (tokens + emb_ref[...]).astype(BF)
+        hidden_ref[...] = hidden
+        for t in range(3):
+            out_ref[t] = (dot(hidden, weight[t]) + shift_ref[t : t + 1, :]).astype(BF)
+
+    return kernel_call(
+        kernel,
+        meta,
+        (own, other, embedded, shift, *pieces),
+        [
+            spec((256, 1024), lambda i, m: (low_block(i), 0)),
+            spec((256, 1024), lambda i, m: (high_block(i), 0)),
+            whole((1, 1024)),
+            whole((3, 512)),
+        ]
+        + [HBM] * 8,
+        [spec((256, 1024), lambda i, m: (i, 0)), spec((3, 256, 512), lambda i, m: (0, i, 0))],
+        [shaped((1024, 1024), BF), shaped((3, 1024, 512), BF)],
+        [pltpu.VMEM((3, 1024, 512), BF), pltpu.SemaphoreType.DMA((32,))],
+        flops=2 * 1024 * 1024 * 1536,
+        moved=10 << 20,
+    )
+
+
+def head_lanes(h, kind):
+    lane = lax.broadcasted_iota(jnp.int32, (1, 128), 1)
+    return jnp.where(lane // HEAD_DIM == h, 1.0, 0.0).astype(kind)
+
+
+def attend(meta, qkv, seg_column, seg_row):
+    def kernel(m, q_ref, k_ref, v_ref, column_ref, row_ref, out_ref, lse_ref):
+        keys, values = k_ref[0], v_ref[0]
+        for block in range(4):
+            rows = pl.ds(block * 256, 256)
+            queries = q_ref[0, rows, :] * jnp.asarray(0.125, BF)
+            allowed = column_ref[rows, :] == row_ref[...]
+            mixed = jnp.zeros((256, 128), F32)
+            for h in range(2):
+                lanes = head_lanes(h, BF)
+                scores = jnp.where(allowed, dot(queries * lanes, keys, NT), -1e30)
+                largest = jnp.max(scores, axis=1, keepdims=True)
+                exponent = jnp.exp(scores - largest)
+                total = jnp.sum(exponent, axis=1, keepdims=True)
+                mixed += dot(exponent.astype(BF), values * lanes) / total
+                lse = jnp.broadcast_to(largest + jnp.log(total), (256, 128))
+                lse_ref[0, h : h + 1, rows] = jnp.transpose(lse)[0:1, :]
+            out_ref[rows, :] = mixed.astype(BF)
+
+    part = lambda t: spec((1, 1024, 128), lambda i, m: (t, 0, i))
+    return kernel_call(
+        kernel,
+        meta,
+        (qkv, qkv, qkv, seg_column, seg_row),
+        [part(0), part(1), part(2), whole((1024, 1)), whole((1, 1024))],
+        [spec((1024, 128), lambda i, m: (0, i)), spec((1, 8, 1024), lambda i, m: (i, 0, 0))],
+        [shaped((1024, 512), BF), shaped((4, 8, 1024), F32)],
+        flops=8 * 4 * 1024 * 1024 * 256,
+        moved=5 << 20,
+        exps=8 << 20,
+    )
+
+
+def attend_back(meta, qkv, out, grad, lse, seg_column, seg_row):
+    def kernel(m, q_ref, k_ref, v_ref, out_ref, grad_ref, lse_ref, column_ref, row_ref, d_ref, sum_ref, dq):
+        queries, upstream = q_ref[0], grad_ref[...]
+        product = out_ref[...].astype(F32) * upstream.astype(F32)
+        row = lax.broadcasted_iota(jnp.int32, (8, 128), 0)
+        lane = lax.broadcasted_iota(jnp.int32, (8, 128), 1)
+        picked = jnp.where(lane // HEAD_DIM == row, 1.0, 0.0).astype(F32)
+        center = lax.dot_general(picked, product, NT, precision=lax.Precision.HIGHEST, preferred_element_type=F32)
+        dq[...] = jnp.zeros_like(dq)
+        value_sum = jnp.zeros((1, 128), F32)
+        for block in range(4):
+            rows = pl.ds(block * 256, 256)
+            keys, values = k_ref[0, rows, :], v_ref[0, rows, :]
+            allowed = column_ref[rows, :] == row_ref[...]
+            dk = jnp.zeros((256, 128), F32)
+            dv = jnp.zeros((256, 128), F32)
+            for h in range(2):
+                lanes = head_lanes(h, BF)
+                keys_h = keys * lanes
+                scores = dot(keys_h * jnp.asarray(0.125, BF), queries, NT)
+                prob = jnp.where(allowed, jnp.exp(scores - lse_ref[0, h : h + 1, :]), 0.0)
+                dp = dot(values * lanes, upstream, NT)
+                ds = (prob * (dp - center[h : h + 1, :])).astype(BF)
+                dv += dot(prob.astype(BF), upstream * lanes)
+                dk += dot(ds, queries * lanes)
+                dq[...] += dot(ds, keys_h, TN)
+            dv = dv.astype(BF)
+            d_ref[1, rows, :] = (dk * 0.125).astype(BF)
+            d_ref[2, rows, :] = dv
+            value_sum += jnp.sum(dv.astype(F32), axis=0, keepdims=True)
+        final = (dq[...] * 0.125).astype(BF)
+        d_ref[0] = final
+        sum_ref[0:1, :] = jnp.sum(final.astype(F32), axis=0, keepdims=True)
+        sum_ref[1:2, :] = value_sum
+
+    part = lambda t: spec((1, 1024, 128), lambda i, m: (t, 0, i))
+    heads = spec((1024, 128), lambda i, m: (0, i))
+    return kernel_call(
+        kernel,
+        meta,
+        (qkv, qkv, qkv, out, grad, lse, seg_column, seg_row),
+        [part(0), part(1), part(2), heads, heads, spec((1, 8, 1024), lambda i, m: (i, 0, 0)), whole((1024, 1)), whole((1, 1024))],
+        [spec((3, 1024, 128), lambda i, m: (0, 0, i)), spec((8, 128), lambda i, m: (0, i))],
+        [shaped((3, 1024, 512), BF), shaped((8, 512), F32)],
+        [pltpu.VMEM((1024, 128), F32)],
+        flops=8 * 10 * 1024 * 1024 * 256,
+        moved=8 << 20,
+        exps=8 << 20,
+    )
+
+
+def project_out(meta, mixed, pieces):
+    def kernel(m, x_ref, *rest):
+        refs, (send_ref, own_ref, weight, sem) = rest[:8], rest[8:]
+        i = pl.program_id(0)
+
+        @pl.when(i == 0)
+        def _():
+            load_all(load_own_rows(m, refs, 0, 2, 32, weight, sem))
+
+        for b in range(2):
+            columns = pl.ds(b * 512, 512)
+            result = dot(x_ref[...], weight[b])
+
+            @pl.when(i < 2)
+            def _():
+                send_ref[:, columns] = result.astype(BF)
+
+            @pl.when(i >= 2)
+            def _():
+                own_ref[:, columns] = result
+
+    return kernel_call(
+        kernel,
+        meta,
+        (mixed, *pieces),
+        [spec((256, 512), lambda i, m: (turned(i), 0))] + [HBM] * 8,
+        [spec((256, 1024), lambda i, m: (low_block(i), 0)), spec((256, 1024), lambda i, m: (high_block(i), 0))],
+        [shaped((512, 1024), BF), shaped((512, 1024), F32)],
+        [pltpu.VMEM((2, 512, 512), BF), pltpu.SemaphoreType.DMA((16,))],
+        flops=2 * 1024 * 1024 * 512,
+        moved=6 << 20,
+    )
+
+
+def normal_parts(values):
+    center = values - jnp.mean(values, axis=-1, keepdims=True)
+    inverse = lax.rsqrt(jnp.mean(center * center, axis=-1, keepdims=True) + EPSILON)
+    return center * inverse, inverse
+
+
+def normal_back(upstream, normal_part, inverse, gain):
+    scaled = upstream * gain
+    return inverse * (
+        scaled
+        - jnp.mean(scaled, axis=-1, keepdims=True)
+        - normal_part * jnp.mean(scaled * normal_part, axis=-1, keepdims=True)
+    )
+
+
+ROWS128 = lambda i, m: (i, 0)
+
+
+def first_norm(meta, tokens, embedded, own, received, vectors):
+    def kernel(m, tok_ref, emb_ref, own_ref, recv_ref, vec_ref, normal_ref, inverse_ref, low_ref):
+        hidden = tok_ref[...].astype(F32) + emb_ref[...]
+        attended = own_ref[...] + recv_ref[...].astype(F32) + vec_ref[0:1, :]
+        normal_part, inverse = normal_parts(hidden + attended)
+        normal_ref[...] = normal_part
+        inverse_ref[...] = jnp.broadcast_to(inverse, (128, 128))
+        low_ref[...] = (normal_part * vec_ref[1:2, :] + vec_ref[2:3, :]).astype(BF)
+
+    block = spec((128, 1024), ROWS128)
+    return kernel_call(
+        kernel,
+        meta,
+        (tokens, embedded, own, received, vectors),
+        [block, whole((1, 1024)), block, block, whole((8, 1024))],
+        [block, spec((128, 128), ROWS128), block],
+        [shaped((512, 1024), F32), shaped((512, 128), F32), shaped((512, 1024), BF)],
+        flops=512 * 1024 * 12,
+        moved=8 << 20,
+    )
+
+
+def expand(meta, own, other, shift, pieces):
+    def kernel(m, own_ref, other_ref, shift_ref, *rest):
+        refs, (act_ref, slope_ref, weight, sem) = rest[:8], rest[8:]
+        i = pl.program_id(0)
+
+        @pl.when(i == 0)
+        def _():
+            load_all(load_split_rows(m, refs, 2, 4, weight, sem))
+
+        x = jnp.where(i < 2, own_ref[...].astype(F32), other_ref[...].astype(F32)).astype(BF)
+        for b in range(4):
+            columns = pl.ds(b * 512, 512)
+            u = dot(x, weight[b]) + shift_ref[:, columns]
+            cumulative = 0.5 * (1.0 + lax.erf(u * INVERSE_ROOT_TWO))
+            act_ref[:, columns] = (u * cumulative).astype(BF)
+            density = jnp.exp(-0.5 * u * u) * INVERSE_ROOT_TWO_PI
+            slope_ref[:, columns] = (cumulative + u * density).astype(BF)
+
+    return kernel_call(
+        kernel,
+        meta,
+        (own, other, shift, *pieces),
+        [
+            spec((256, 1024), lambda i, m: (low_block(i), 0)),
+            spec((256, 1024), lambda i, m: (high_block(i), 0)),
+            whole((1, 2048)),
+        ]
+        + [HBM] * 8,
+        [spec((256, 2048), ROWS128), spec((256, 2048), ROWS128)],
+        [shaped((1024, 2048), BF), shaped((1024, 2048), BF)],
+        [pltpu.VMEM((4, 1024, 512), BF), pltpu.SemaphoreType.DMA((32,))],
+        flops=2 * 1024 * 1024 * 2048,
+        moved=14 << 20,
+        exps=4 << 20,
+    )
+
+
+def contract(meta, activated, pieces):
+    def kernel(m, x_ref, *rest):
+        refs, (send_ref, own_ref, weight, sem) = rest[:8], rest[8:]
+        i = pl.program_id(0)
+
+        @pl.when(i == 0)
+        def _():
+            load_all(load_own_rows(m, refs, 0, 2, 128, weight, sem))
+
+        for b in range(2):
+            columns = pl.ds(b * 512, 512)
+            result = dot(x_ref[...], weight[b])
+
+            @pl.when(i < 2)
+            def _():
+                send_ref[:, columns] = result.astype(BF)
+
+            @pl.when(i >= 2)
+            def _():
+                own_ref[:, columns] = result
+
+    return kernel_call(
+        kernel,
+        meta,
+        (activated, *pieces),
+        [spec((256, 2048), lambda i, m: (turned(i), 0))] + [HBM] * 8,
+        [spec((256, 1024), lambda i, m: (low_block(i), 0)), spec((256, 1024), lambda i, m: (high_block(i), 0))],
+        [shaped((512, 1024), BF), shaped((512, 1024), F32)],
+        [pltpu.VMEM((2, 2048, 512), BF), pltpu.SemaphoreType.DMA((16,))],
+        flops=2 * 1024 * 1024 * 2048,
+        moved=11 << 20,
+    )
+
+
+def row_sums(sum_ref, i, rows):
+    @pl.when(i == 0)
+    def _():
+        sum_ref[...] = jnp.zeros_like(sum_ref)
+
+    for n, value in enumerate(rows):
+        sum_ref[n : n + 1, :] += jnp.sum(value, axis=0, keepdims=True)
+
+
+def second_norm(meta, normal_one, own, received, cotangent, vectors):
+    def kernel(m, normal_ref, own_ref, recv_ref, cot_ref, vec_ref, out_ref, resid_ref, low_ref, sum_ref):
+        normed = normal_ref[...] * vec_ref[1:2, :] + vec_ref[2:3, :]
+        downward = own_ref[...] + recv_ref[...].astype(F32) + vec_ref[3:4, :]
+        normal_part, inverse = normal_parts(normed + downward)
+        out_ref[...] = (normal_part * vec_ref[4:5, :] + vec_ref[5:6, :]).astype(BF)
+        upstream = cot_ref[...].astype(F32)
+        resid = normal_back(upstream, normal_part, inverse, vec_ref[4:5, :])
+        resid_ref[...] = resid
+        low = resid.astype(BF)
+        low_ref[...] = low
+        row_sums(sum_ref, pl.program_id(0), (upstream * normal_part, upstream, low.astype(F32)))
+
+    block = spec((128, 1024), ROWS128)
+    return kernel_call(
+        kernel,
+        meta,
+        (normal_one, own, received, cotangent, vectors),
+        [block, block, block, block, whole((8, 1024))],
+        [block, block, block, whole((8, 1024))],
+        [shaped((512, 1024), BF), shaped((512, 1024), F32), shaped((512, 1024), BF), shaped((8, 1024), F32)],
+        flops=512 * 1024 * 30,
+        moved=10 << 20,
+    )
+
+
+def feed_back(meta, own, other, slope, down_pieces, up_pieces):
+    def kernel(m, own_ref, other_ref, slope_ref, *rest):
+        down_refs, up_refs = rest[:8], rest[8:16]
+        du_ref, send_ref, mine_ref, sum_ref, down, up, down_sem, up_sem = rest[16:]
+        i = pl.program_id(0)
+
+        @pl.when(i == 0)
+        def _():
+            load_all(
+                load_own_rows(m, down_refs, 0, 2, 128, down, down_sem)
+                + load_split_rows(m, up_refs, 2, 4, up, up_sem)
+            )
+            sum_ref[...] = jnp.zeros_like(sum_ref)
+
+        df = jnp.where(i < 2, other_ref[...].astype(F32), own_ref[...].astype(F32)).astype(BF)
+        total = jnp.zeros((256, 1024), F32)
+        for b in range(4):
+            rows = pl.ds(b * 512, 512)
+            act = dot(df[:, :512], down[0, rows, :], NT) + dot(df[:, 512:], down[1, rows, :], NT)
+            du = (act * slope_ref[:, rows].astype(F32)).astype(BF)
+            du_ref[:, rows] = du
+            sum_ref[0:1, rows] += jnp.sum(du.astype(F32), axis=0, keepdims=True)
+            total += dot(du, up[b], NT)
+
+        @pl.when(i < 2)
+        def _():
+            send_ref[...] = total.astype(BF)
+
+        @pl.when(i >= 2)
+        def _():
+            mine_ref[...] = total
+
+    return kernel_call(
+        kernel,
+        meta,
+        (own, other, slope, *down_pieces, *up_pieces),
+        [
+            spec((256, 1024), lambda i, m: (high_block(i), 0)),
+            spec((256, 1024), lambda i, m: (low_block(i), 0)),
+            spec((256, 2048), lambda i, m: (turned(i), 0)),
+        ]
+        + [HBM] * 16,
+        [
+            spec((256, 2048), lambda i, m: (turned(i), 0)),
+            spec((256, 1024), lambda i, m: (low_block(i), 0)),
+            spec((256, 1024), lambda i, m: (high_block(i), 0)),
+            whole((8, 2048)),
+        ],
+        [shaped((1024, 2048), BF), shaped((512, 1024), BF), shaped((512, 1024), F32), shaped((8, 2048), F32)],
+        [
+            pltpu.VMEM((2, 2048, 512), BF),
+            pltpu.VMEM((4, 1024, 512), BF),
+            pltpu.SemaphoreType.DMA((16,)),
+            pltpu.SemaphoreType.DMA((32,)),
+        ],
+        flops=4 * 1024 * 1024 * 2048,
+        moved=22 << 20,
+    )
+
+
+def first_norm_back(meta, resid, own, received, normal_one, inverse_one, vectors):
+    def kernel(m, resid_ref, own_ref, recv_ref, normal_ref, inverse_ref, vec_ref, out_ref, low_ref, sum_ref):
+        upstream = resid_ref[...] + own_ref[...] + recv_ref[...].astype(F32)
+        normal_part = normal_ref[...]
+        resid_one = normal_back(upstream, normal_part, inverse_ref[:, 0:1], vec_ref[1:2, :])
+        out_ref[...] = resid_one
+        low = resid_one.astype(BF)
+        low_ref[...] = low
+        row_sums(sum_ref, pl.program_id(0), (upstream * normal_part, upstream, low.astype(F32)))
+
+    block = spec((128, 1024), ROWS128)
+    return kernel_call(
+        kernel,
+        meta,
+        (resid, own, received, normal_one, inverse_one, vectors),
+        [block, block, block, block, spec((128, 128), ROWS128), whole((8, 1024))],
+        [block, block, whole((8, 1024))],
+        [shaped((512, 1024), F32), shaped((512, 1024), BF), shaped((8, 1024), F32)],
+        flops=512 * 1024 * 20,
+        moved=10 << 20,
+    )
+
+
+def output_back(meta, own, other, pieces):
+    def kernel(m, own_ref, other_ref, *rest):
+        refs, (out_ref, weight, sem) = rest[:8], rest[8:]
+        i = pl.program_id(0)
+
+        @pl.when(i == 0)
+        def _():
+            load_all(load_own_rows(m, refs, 0, 2, 32, weight, sem))
+
+        da = jnp.where(i < 2, own_ref[...].astype(F32), other_ref[...].astype(F32)).astype(BF)
+        out_ref[...] = (dot(da[:, :512], weight[0], NT) + dot(da[:, 512:], weight[1], NT)).astype(BF)
+
+    return kernel_call(
+        kernel,
+        meta,
+        (own, other, *pieces),
+        [
+            spec((256, 1024), lambda i, m: (low_block(i), 0)),
+            spec((256, 1024), lambda i, m: (high_block(i), 0)),
+        ]
+        + [HBM] * 8,
+        spec((256, 512), ROWS128),
+        shaped((1024, 512), BF),
+        [pltpu.VMEM((2, 512, 512), BF), pltpu.SemaphoreType.DMA((16,))],
+        flops=2 * 1024 * 1024 * 512,
+        moved=4 << 20,
+    )
+
+
+def rel_chip(s, m):
+    return lax.rem(m[0] + s // 2, 2) * 2 + lax.rem(m[1] + lax.rem(s, 2), 2)
+
+
+def piece_outputs(blocks, rows):
+    shape = (2, 2, blocks, rows, 512)
+    return [HBM] * 4, [shaped(shape, BF)] * 4
+
+
+def push(s, outs, copy_for):
+    first_keep, first_send, second_keep, second_send = outs
+    slots = (
+        ((first_keep, 0), (second_keep, 0)),
+        ((first_keep, 1), (second_send, 0)),
+        ((first_send, 0), (second_keep, 1)),
+        ((first_send, 1), (second_send, 1)),
+    )
+    for n, (first, second) in enumerate(slots):
+
+        @pl.when(s == n)
+        def _(n=n, first=first, second=second):
+            for k in range(4):
+                ref, at = (first, second)[k // 2]
+                for copy in copy_for(n, k, ref.at[at, k % 2]):
+                    copy.start()
+
+    @pl.when(s == 3)
+    def _():
+        for n, (first, second) in enumerate(slots):
+            for k in range(4):
+                ref, at = (first, second)[k // 2]
+                for copy in copy_for(n, k, ref.at[at, k % 2]):
+                    copy.wait()
+
+
+def weigh_down(meta, activated, own, other):
+    def kernel(m, x_ref, own_ref, other_ref, *rest):
+        outs, (stage, sem) = rest[:4], rest[4:]
+        s = pl.program_id(0)
+        x = x_ref[...]
+        for b in range(2):
+            columns = pl.ds(b * 512, 512)
+            stage[s, b] = (dot(x[:512], own_ref[:, columns], TN) + dot(x[512:], other_ref[:, columns], TN)).astype(BF)
+
+        def copy_for(n, k, target):
+            row = pl.multiple_of(lax.rem(m[3] + k, 4) * 128, 128)
+            return [pltpu.make_async_copy(stage.at[n, :, pl.ds(row, 128), :], target, sem.at[n * 4 + k])]
+
+        push(s, outs, copy_for)
+
+    out_specs, out_shape = piece_outputs(2, 128)
+    return kernel_call(
+        kernel,
+        meta,
+        (activated, own, other),
+        [spec((1024, 512), lambda s, m: (0, rel_chip(s, m))), whole((512, 1024)), whole((512, 1024))],
+        out_specs,
+        out_shape,
+        [pltpu.VMEM((4, 2, 512, 512), BF), pltpu.SemaphoreType.DMA((16,))],
+        flops=2 * 1024 * 1024 * 2048,
+        moved=10 << 20,
+    )
+
+
+def weigh_up_out(meta, normed_own, normed_other, du, mixed, da_own, da_other):
+    def kernel(m, own_ref, other_ref, du_ref, mixed_ref, da_own_ref, da_other_ref, *rest):
+        outs, (up, out, sem) = rest[:4], rest[4:]
+        s = pl.program_id(0)
+        x = mixed_ref[...]
+        for b in range(2):
+            columns = pl.ds(b * 512, 512)
+            out[s, b] = (dot(x[:512], da_own_ref[:, columns], TN) + dot(x[512:], da_other_ref[:, columns], TN)).astype(BF)
+        for b in range(4):
+            columns = pl.ds(b * 512, 512)
+            up[s, b] = (dot(own_ref[...], du_ref[:512, columns], TN) + dot(other_ref[...], du_ref[512:, columns], TN)).astype(BF)
+
+        def copy_for(n, k, target):
+            z = lax.rem(m[3] + k, 4)
+            copies = [
+                pltpu.make_async_copy(
+                    out.at[n, :, pl.ds(pl.multiple_of(z * 32, 32), 32), :],
+                    target.at[pl.ds(0, 2)],
+                    sem.at[(n * 4 + k) * 3],
+                )
+            ]
+            for rel in range(2):
+                row = pl.multiple_of(lax.rem(m[2] + rel, 2) * 128 + z * 32, 32)
+                copies.append(
+                    pltpu.make_async_copy(
+                        up.at[n, :, pl.ds(row, 32), :],
+                        target.at[pl.ds(2 + rel * 4, 4)],
+                        sem.at[(n * 4 + k) * 3 + 1 + rel],
+                    )
+                )
+            return copies
+
+        push(s, outs, copy_for)
+
+    out_specs, out_shape = piece_outputs(10, 32)
+    return kernel_call(
+        kernel,
+        meta,
+        (normed_own, normed_other, du, mixed, da_own, da_other),
+        [
+            spec((512, 256), lambda s, m: (0, rel_chip(s, m))),
+            spec((512, 256), lambda s, m: (0, rel_chip(s, m))),
+            whole((1024, 2048)),
+            spec((1024, 128), lambda s, m: (0, rel_chip(s, m))),
+            whole((512, 1024)),
+            whole((512, 1024)),
+        ],
+        out_specs,
+        out_shape,
+        [pltpu.VMEM((4, 4, 256, 512), BF), pltpu.VMEM((4, 2, 128, 512), BF), pltpu.SemaphoreType.DMA((48,))],
+        flops=2 * 1024 * 1024 * 2560,
+        moved=15 << 20,
+    )
+
+
+def weigh_qkv(meta, hidden, dqkv):
+    def kernel(m, x_ref, d_ref, *rest):
+        outs, (stage, sem) = rest[:4], rest[4:]
+        s = pl.program_id(0)
+        for t in range(3):
+            stage[s, t] = dot(x_ref[...], d_ref[t], TN).astype(BF)
+
+        def copy_for(n, k, target):
+            copies = []
+            for rel in range(2):
+                row = pl.multiple_of(lax.rem(m[2] + rel, 2) * 128 + lax.rem(m[3] + k, 4) * 32, 32)
+                copies.append(
+                    pltpu.make_async_copy(
+                        stage.at[n, :, pl.ds(row, 32), :],
+                        target.at[pl.ds(rel * 3, 3)],
+                        sem.at[(n * 4 + k) * 2 + rel],
+                    )
+                )
+            return copies
+
+        push(s, outs, copy_for)
+
+    out_specs, out_shape = piece_outputs(6, 32)
+    return kernel_call(
+        kernel,
+        meta,
+        (hidden, dqkv),
+        [spec((1024, 256), lambda s, m: (0, rel_chip(s, m))), whole((3, 1024, 512))],
+        out_specs,
+        out_shape,
+        [pltpu.VMEM((4, 3, 256, 512), BF), pltpu.SemaphoreType.DMA((32,))],
+        flops=2 * 1024 * 1024 * 1536,
+        moved=8 << 20,
+    )
+
+
+def qkv_back(meta, dqkv, pieces):
+    def kernel(m, d_ref, *rest):
+        refs, (send_ref, own_ref, weight, sem) = rest[:8], rest[8:]
+        i = pl.program_id(0)
+
+        @pl.when(i == 0)
+        def _():
+            load_all(load_split_rows(m, refs, 0, 3, weight, sem))
+
+        total = dot(d_ref[0], weight[0], NT) + dot(d_ref[1], weight[1], NT) + dot(d_ref[2], weight[2], NT)
+
+        @pl.when(i < 2)
+        def _():
+            send_ref[...] = total.astype(BF)
+
+        @pl.when(i >= 2)
+        def _():
+            own_ref[...] = total
+
+    return kernel_call(
+        kernel,
+        meta,
+        (dqkv, *pieces),
+        [spec((3, 256, 512), lambda i, m: (0, turned(i), 0))] + [HBM] * 8,
+        [spec((256, 1024), lambda i, m: (low_block(i), 0)), spec((256, 1024), lambda i, m: (high_block(i), 0))],
+        [shaped((512, 1024), BF), shaped((512, 1024), F32)],
+        [pltpu.VMEM((3, 1024, 512), BF), pltpu.SemaphoreType.DMA((32,))],
+        flops=2 * 1024 * 1024 * 1536,
+        moved=9 << 20,
+    )
+
+
+def last_sum(meta, resid, own, received):
+    def kernel(m, resid_ref, own_ref, recv_ref, out_ref, sum_ref):
+        total = resid_ref[...] + own_ref[...] + recv_ref[...].astype(F32)
+        out_ref[...] = total.astype(BF)
+        row_sums(sum_ref, pl.program_id(0), (total,))
+
+    block = spec((128, 1024), ROWS128)
+    return kernel_call(
+        kernel,
+        meta,
+        (resid, own, received),
+        [block, block, block],
+        [block, whole((8, 1024))],
+        [shaped((512, 1024), BF), shaped((8, 1024), F32)],
+        flops=512 * 1024 * 4,
+        moved=6 << 20,
+    )
+
+
+VECTOR_SIZES = (64, 32, 32, 32, 128, 32, 32, 32)
+
+
+def split_vectors(packed):
+    parts, start = [], 0
+    for size in VECTOR_SIZES:
+        parts.append(packed[:, start : start + size])
+        start += size
+    return parts
+
+
+def chip_body(
+    tokens,
+    timestep,
+    segment_ids,
+    cotangent,
+    time_weight,
+    qkv_weight,
+    qv_bias,
+    out_weight,
+    out_bias,
+    norm_gain,
+    norm_bias,
+    up_weight,
+    up_bias,
+    down_weight,
+    down_bias,
+    final_gain,
+    final_bias,
+):
+    dp, z = lax.axis_index("dp"), lax.axis_index("sp")
+    y, x, c = dp // 4, (dp // 2) % 2, dp % 2
+    meta = jnp.stack([y, x, c, z]).astype(jnp.int32)
+    pick = lambda value, index, axis: lax.dynamic_index_in_dim(value, index, axis, keepdims=False)
+
+    qkv_split = qkv_weight.reshape(32, 3, 4, 2, 128)
+    up_split = up_weight.reshape(32, 4, 2, 512)
+    qkv_half = lambda core: pick(qkv_split, core, 3).reshape(32, 3, 512).transpose(1, 0, 2)
+    up_half = lambda core: pick(up_split, core, 2).transpose(1, 0, 2)
+    qkv_shard = jnp.concatenate([qkv_half(c), send(qkv_half(1 - c), PAIR)])
+    out_shard = out_weight.reshape(32, 2, 512).transpose(1, 0, 2)
+    mid_shard = jnp.concatenate([out_shard, up_half(c), send(up_half(1 - c), PAIR)])
+    down_shard = down_weight.reshape(128, 2, 512).transpose(1, 0, 2)
+    qkv_pieces = gather_pieces(qkv_shard)
+    mid_pieces = gather_pieces(mid_shard)
+    down_pieces = gather_pieces(down_shard)
+
+    stamps = timestep.astype(jnp.int32)
+    small = jnp.concatenate(
+        [qv_bias, out_bias, norm_gain, norm_bias, up_bias, down_bias, final_gain, final_bias]
+        + [(stamps // 64).astype(BF), (stamps % 64).astype(BF)]
+    )[None]
+    small = jnp.concatenate([small, send(small, PAIR)])
+    small = jnp.stack([small] + [send(small, SHIFT_Z[k]) for k in (1, 2, 3)])
+    small = jnp.stack([small] + [send(small, pairs) for pairs in (ALONG_X, ALONG_Y, DIAGONAL)])
+    small = small.reshape(32, -1)
+    natural = jnp.arange(32, dtype=jnp.int32)
+    ny, nx, nc, nz = natural // 16, (natural // 8) % 2, (natural // 4) % 2, natural % 4
+    source = (((ny ^ y) * 2 + (nx ^ x)) * 4 + (z + 4 - nz) % 4) * 2 + (nc ^ c)
+    order = (source[:, None] == natural[None, :]).astype(BF)
+    small = jnp.dot(order, small, preferred_element_type=F32)
+    full = [part.reshape(1, -1) for part in split_vectors(small)]
+    qv_full, out_shift, first_gain, first_shift, up_full, down_shift, second_gain, second_shift = full
+    blank = jnp.zeros((2, 1024), F32)
+    vectors = jnp.concatenate([out_shift, first_gain, first_shift, down_shift, second_gain, second_shift, blank])
+    qv_mine = pick(qv_full.reshape(2, 4, 2, 128), c, 2).reshape(2, 512)
+    qkv_shift = jnp.stack([qv_mine[0], jnp.zeros((512,), F32), qv_mine[1]])
+    up_shift = pick(up_full.reshape(4, 2, 512), c, 1).reshape(1, 2048)
+
+    all_stamps = (small[::4, 384:386] * 64.0 + small[::4, 386:388]).reshape(16)
+    column = (dp * 4 + z) * 32 + jnp.arange(32, dtype=jnp.int32)
+    frequency = jnp.exp(-math.log(10000.0) * (column % 512).astype(F32) / 512)
+    rel = jnp.arange(16, dtype=jnp.int32)
+    rel_row = ((rel // 8) ^ y) * 8 + (((rel // 4) % 2) ^ x) * 4
+
+    def features_for(rows):
+        phases = all_stamps[rows][:, None] * frequency[None, :]
+        return jnp.where(column[None, :] < 512, jnp.sin(phases), jnp.cos(phases)).astype(BF)
+
+    terms = jnp.dot(features_for(rel_row + (rel + z) % 4), time_weight, preferred_element_type=F32)
+    terms = (terms + send(terms, PAIR)).reshape(4, 4, 1024)
+    terms = terms[0] + send(terms[1], ALONG_X) + send(terms[2], ALONG_Y) + send(terms[3], DIAGONAL)
+    embedded = terms[0:1]
+    for k in (1, 2, 3):
+        embedded = embedded + send(terms[k : k + 1], SHIFT_Z[k])
+
+    def take_rows(value):
+        return jnp.concatenate([send(pick(value, (z + k) % 2, 0), ROW_OUT[k]) for k in range(2)])
+
+    def give_rows(value):
+        parts = [send(value[k * 256 : (k + 1) * 256], ROW_BACK[k]) for k in range(2)]
+        swapped = (z % 2) == 1
+        return jnp.stack([jnp.where(swapped, parts[1], parts[0]), jnp.where(swapped, parts[0], parts[1])])
+
+    own_tokens = take_rows(tokens)
+    own_segments = take_rows(segment_ids)
+    other_tokens = send(own_tokens, PAIR)
+    segments = jnp.concatenate([own_segments, send(own_segments, PAIR)])
+    seg_column, seg_row = segments[:, None], segments[None, :]
+    own_cotangent = take_rows(cotangent)
+
+    hidden, qkv = project_qkv(meta, own_tokens, other_tokens, embedded, qkv_shift, qkv_pieces)
+    mixed, lse = attend(meta, qkv, seg_column, seg_row)
+    away, mine = project_out(meta, mixed, mid_pieces)
+    normal_one, inverse_one, normed = first_norm(meta, own_tokens, embedded, mine, send(away, PAIR), vectors)
+    normed_other = send(normed, PAIR)
+    activated, slope = expand(meta, normed, normed_other, up_shift, mid_pieces)
+    away, mine = contract(meta, activated, down_pieces)
+    result, resid_two, df, sums_two = second_norm(meta, normal_one, mine, send(away, PAIR), own_cotangent, vectors)
+    output = give_rows(result)
+
+    df_other = send(df, PAIR)
+    down_share = scatter_pieces(*weigh_down(meta, activated, df, df_other))
+    du, away, mine, up_sums = feed_back(meta, df, df_other, slope, down_pieces, mid_pieces)
+    resid_one, da, sums_one = first_norm_back(meta, resid_two, mine, send(away, PAIR), normal_one, inverse_one, vectors)
+    da_other = send(da, PAIR)
+    dout = output_back(meta, da, da_other, mid_pieces)
+    mid_share = scatter_pieces(*weigh_up_out(meta, normed, normed_other, du, mixed, da, da_other))
+    dqkv, qv_sums = attend_back(meta, qkv, mixed, dout, lse, seg_column, seg_row)
+    qkv_share = scatter_pieces(*weigh_qkv(meta, hidden, dqkv))
+    away, mine = qkv_back(meta, dqkv, qkv_pieces)
+    input_low, embed_sums = last_sum(meta, resid_one, mine, send(away, PAIR))
+    input_grad = give_rows(input_low)
+
+    def both_halves(own, received):
+        return jnp.where(c == 0, jnp.stack([own, received], axis=-2), jnp.stack([received, own], axis=-2))
+
+    grad_down = down_share.transpose(1, 0, 2).reshape(128, 1024)
+    grad_out = mid_share[:2].transpose(1, 0, 2).reshape(32, 1024)
+    grad_up = both_halves(mid_share[2:6], send(mid_share[6:], PAIR))
+    grad_up = grad_up.transpose(1, 0, 2, 3).reshape(32, 4096)
+    split = lambda share: share.reshape(3, 32, 4, 128)
+    grad_qkv = both_halves(split(qkv_share[:3]), split(send(qkv_share[3:], PAIR)))
+    grad_qkv = grad_qkv.transpose(1, 0, 2, 3, 4).reshape(32, 3072)
+
+    core_lane = (jnp.arange(2) == c).astype(F32)
+    spread = lambda sums, width: (sums.reshape(-1, 1, width) * core_lane[None, :, None]).reshape(32, -1)
+    grads = jnp.concatenate(
+        [
+            spread(qv_sums[0:2], 128),
+            sums_one[2].reshape(32, 32),
+            sums_one[0].reshape(32, 32),
+            sums_one[1].reshape(32, 32),
+            spread(up_sums[0:1], 512),
+            sums_two[2].reshape(32, 32),
+            sums_two[0].reshape(32, 32),
+            sums_two[1].reshape(32, 32),
+        ],
+        axis=1,
+    ).reshape(4, 2, 4, 384)
+    grads = pick(grads, c, 1) + send(pick(grads, 1 - c, 1), PAIR)
+    rel_order = ((rel_row + (rel + z) % 4)[:, None] == rel[None, :]).astype(F32)
+    grads = jnp.dot(rel_order, grads.reshape(16, 384), precision=lax.Precision.HIGHEST).reshape(4, 4, 384)
+    grads = grads[0] + send(grads[1], ALONG_X) + send(grads[2], ALONG_Y) + send(grads[3], DIAGONAL)
+    total = grads[0:1]
+    for k in (1, 2, 3):
+        total = total + send(grads[k : k + 1], SHIFT_Z[k])
+    small_grads = [part.reshape(-1) for part in split_vectors(total)]
+
+    sums = embed_sums[0:1]
+    sums = sums + send(sums, PAIR)
+    sums = jnp.concatenate([sums] + [send(sums, SHIFT_Z[k]) for k in (1, 2, 3)])
+    sums = jnp.concatenate([sums] + [send(sums, pairs) for pairs in (ALONG_X, ALONG_Y, DIAGONAL)])
+    features = features_for(rel_row + (z + 4 - rel % 4) % 4).astype(F32)
+    grad_time = jnp.dot(features.T, sums, precision=lax.Precision.HIGHEST)
+
+    return (
+        output,
+        input_grad,
+        grad_time,
+        grad_qkv,
+        small_grads[0],
+        grad_out,
+        *small_grads[1:4],
+        grad_up,
+        small_grads[4],
+        grad_down,
+        *small_grads[5:],
+    )
+
+
 def solution(mesh):
     in_specs = (
         P("dp", "sp", None),
@@ -395,4 +1359,5 @@
         P(("dp", "sp")),
         P(("dp", "sp")),
     )
-    return jax.shard_map(body, mesh=mesh, in_specs=in_specs, out_specs=out_specs, check_vma=False)
+    plan = chip_body if dict(mesh.shape) == {"dp": 8, "sp": 4} else body
+    return jax.shard_map(plan, mesh=mesh, in_specs=in_specs, out_specs=out_specs, check_vma=False)

time: 1860 us -> 636 us (0.34)
  the two profiles are of different devices: /device:TPU:0 before, /device:TPU:27 now
where the time goes in v1:
time: 636 us; the launch traced here: 630 us
  waiting for transfers between devices  235 us (37%)
  Pallas kernels  173 us (27%)
  starting transfers between devices  137 us (22%)
  local copies, waits for them, and re-layouts  55.3 us (9%)
  other arithmetic  24.4 us (4%)
    ppermute x99, waiting for transfers between devices, send(): return lax.ppermute(value, AXES, pairs)  235 us
    pallas_call x16, Pallas kernels, kernel_call(): pl.pallas_call(kernel, grid_spec=pltpu.PrefetchScalarGridSpec(num_scalar_...  173 us
    ppermute x99, starting transfers between devices, send(): return lax.ppermute(value, AXES, pairs)  137 us
    unnamed x176, local copies, waits for them, and re-layouts  27 us
    convert_element_type x12, other arithmetic, scatter_pieces(): add = lambda a, b: (a.astype(F32) + b.astype(F32)).astype(BF)  13.8 us
  transfers between devices with their start and end apart: 99, of which 28 were waited for; matrix products, arithmetic and copies ran while one was open for 9% of the time, Pallas kernels for 16%

profile of v1, /device:TPU:27, one launch (start us, length us, event | category | flops | bytes accessed | tf_op | source)
XLA Modules:
  0.0 629.7 jit_solution(14726772560054223104)
XLA Ops:
  8.7 1.9 collective-permute-start.3
  12.2 9.0 %collective-permute-done.4 = bf16[2,388]{1,0:T(2,128)(2,1)S(1)} collective-permute-done((bf16[2,388]{1,0:T(2,128)(2,1)S(1)}, bf16[2,388]{1,0:T(2,128)(2,1)S(1)}, u32[]{:S(2)}, u32[]{:S(2)}) %collective-permute-start.4) | collective-permute-done | bytes 1584 | tf_op jit(solution)/shard_map/ppermute | solution.py:399
  32.8 2.0 collective-permute-start.30
  37.7 1.8 collective-permute-start.18
  39.6 20.2 %collective-permute-done.22 = bf16[6,32,512]{2,1,0:T(8,128)(2,1)S(1)} collective-permute-done((bf16[6,32,512]{2,1,0:T(8,128)(2,1)S(1)}, bf16[6,32,512]{2,1,0:T(8,128)(2,1)S(1)}, u32[]{:S(2)}, u32[]{:S(2)}) %collective-permute-start.22) | collective-permute-done | bytes 196640 | tf_op jit(solution)/shard_map/ppermute | solution.py:399
  59.9 4.1 collective-permute-start.13
  64.2 2.4 collective-permute-start.14
  67.8 3.2 collective-permute-start.31
  71.8 16.3 %collective-permute-done.14 = f32[1,1024]{1,0:T(1,128)S(1)} collective-permute-done((f32[1,1024]{1,0:T(1,128)S(1)}, f32[1,1024]{1,0:T(1,128)S(1)}, u32[]{:S(2)}, u32[]{:S(2)}) %collective-permute-start.14) | collective-permute-done | bytes 4128 | tf_op jit(solution)/shard_map/ppermute | solution.py:399
  92.4 6.0 collective-permute-done.25.rest_6_
  101.2 6.5 %collective-permute-done.24.rest_5_ = bf16[2,6,32,512]{3,2,1,0:T(8,128)(2,1)} collective-permute-done((bf16[2,6,32,512]{3,2,1,0:T(8,128)(2,1)S(1)}, bf16[2,6,32,512]{3,2,1,0:T(8,128)(2,1)}, u32[]{:S(2)}, u32[]{:S(2)}) %collective-permute-start.24) | collective-permute-done | bytes 393248 | tf_op jit(solution)/shard_map/ppermute | solution.py:399
  109.2 20.9 %collective-permute-done.26.rest_7_ = bf16[2,6,32,512]{3,2,1,0:T(8,128)(2,1)S(1)} collective-permute-done((bf16[2,6,32,512]{3,2,1,0:T(8,128)(2,1)}, bf16[2,6,32,512]{3,2,1,0:T(8,128)(2,1)S(1)}, u32[]{:S(2)}, u32[]{:S(2)}) %collective-permute-start.26) | collective-permute-done | bytes 393248 | tf_op jit(solution)/shard_map/ppermute | solution.py:399
  135.0 9.3 %shard_map.280 = (bf16[1024,1024]{1,0:T(8,128)(2,1)}, bf16[3,1024,512]{2,1,0:T(8,128)(2,1)}) custom-call(s32[4]{0:T(128)S(1)} %pad_add_fusion.1.m, bf16[512,1024]{1,0:T(8,128)(2,1)} %constant_dynamic-update-slice_fusion.own_ref.tok_ref, bf16[512,1024]{1,0:T(8,128)(2,1)} %collective-permute-done.16.other_ref, f32[1,1024]{1,0:T(1,128)S(1)} %fusion.55.emb_ref, ...), custom_call_target="tpu_custom_call" | custom-call | flops 3221225472 | bytes 10485760 | tf_op jit(solution)/shard_map/pallas_call | solution.py:481
  144.3 1.9 copy-done.43
  146.2 19.3 %shard_map.281 = (bf16[1024,512]{1,0:T(8,128)(2,1)S(1)}, f32[4,8,1024]{2,1,0:T(8,128)S(1)}) custom-call(s32[4]{0:T(128)S(1)} %pad_add_fusion.1.m, bf16[3,1024,512]{2,1,0:T(8,128)(2,1)S(1)} %copy-done.43, bf16[3,1024,512]{2,1,0:T(8,128)(2,1)S(1)} %copy-done.43, bf16[3,1024,512]{2,1,0:T(8,128)(2,1)S(1)} %copy-done.43, s32[1024,1]{1,0:T(8,128)S(1)} %copy-done.26, ...), custom_call_target="tpu_custom_call" | custom-call | flops 8589934592 | bytes 5242880 | tf_op jit(solution)/shard_map/pallas_call | solution.py:481
  166.6 7.0 %shard_map.282 = (bf16[512,1024]{1,0:T(8,128)(2,1)}, f32[512,1024]{1,0:T(8,128)}) custom-call(s32[4]{0:T(128)S(1)} %pad_add_fusion.1.m, bf16[1024,512]{1,0:T(8,128)(2,1)} %copy-done.20, bf16[2,10,32,512]{3,2,1,0:T(8,128)(2,1)S(1)} %pad_maximum_fusion.3.rest_0_.rest_8_, bf16[2,10,32,512]{3,2,1,0:T(8,128)(2,1)S(1)} %collective-permute-done.32.rest_1_.rest_9_, ...), custom_call_target="tpu_custom_call" | custom-call | flops 1073741824 | bytes 6291456 | tf_op jit(solution)/shard_map/pallas_call | solution.py:481
  173.7 2.9 collective-permute-start.40
  176.6 1.8 copy.47
  178.3 1.8 copy.48
  181.7 5.0 shard_map.283
  188.7 3.9 collective-permute-start.42
  192.7 5.1 collective-permute-done.46
  197.7 1.9 pad_maximum_fusion.6.rest_4_
  200.4 2.8 collective-permute-done.42
  206.6 6.4 %collective-permute-done.49.rest_6_ = bf16[2,2,128,512]{3,2,1,0:T(8,128)(2,1)} collective-permute-done((bf16[2,2,128,512]{3,2,1,0:T(8,128)(2,1)}, bf16[2,2,128,512]{3,2,1,0:T(8,128)(2,1)}, u32[]{:S(2)}, u32[]{:S(2)}) %collective-permute-start.49) | collective-permute-done | bytes 524320 | tf_op jit(solution)/shard_map/ppermute | solution.py:399
  214.2 3.3 collective-permute-done.43.rest_1_
  222.1 12.4 %shard_map.284 = (bf16[1024,2048]{1,0:T(8,128)(2,1)}, bf16[1024,2048]{1,0:T(8,128)(2,1)}) custom-call(s32[4]{0:T(128)S(1)} %pad_add_fusion.1.m, bf16[512,1024]{1,0:T(8,128)(2,1)} %get-tuple-element.62.own_ref, bf16[512,1024]{1,0:T(8,128)(2,1)} %collective-permute-done.41.other_ref, f32[1,2048]{1,0:T(1,128)S(1)} %bitcast.244, ...), custom_call_target="tpu_custom_call" | custom-call | flops 4294967296 | bytes 14680064 | tf_op jit(solution)/shard_map/pallas_call | solution.py:481
  234.5 5.4 collective-permute-done.50.rest_7_
  239.9 11.2 %shard_map.285 = (bf16[512,1024]{1,0:T(8,128)(2,1)S(1)}, f32[512,1024]{1,0:T(8,128)}) custom-call(s32[4]{0:T(128)S(1)} %pad_add_fusion.1.m, bf16[1024,2048]{1,0:T(8,128)(2,1)} %get-tuple-element.63.x_ref, bf16[2,2,128,512]{3,2,1,0:T(8,128)(2,1)} %pad_maximum_fusion.5.rest_0_, bf16[2,2,128,512]{3,2,1,0:T(8,128)(2,1)} %collective-permute-done.43.rest_1_, ...), custom_call_target="tpu_custom_call" | custom-call | flops 4294967296 | bytes 11534336 | tf_op jit(solution)/shard_map/pallas_call | solution.py:481
  253.2 2.3 collective-permute-start.53
  255.5 9.1 %collective-permute-done.53 = bf16[256,1024]{1,0:T(8,128)(2,1)S(1)} collective-permute-done((bf16[256,1024]{1,0:T(8,128)(2,1)S(1)}, bf16[256,1024]{1,0:T(8,128)(2,1)S(1)}, u32[]{:S(2)}, u32[]{:S(2)}) %collective-permute-start.53) | collective-permute-done | bytes 524320 | tf_op jit(solution)/shard_map/ppermute | solution.py:399
  264.7 5.8 shard_map.286
  270.4 12.6 %collective-permute-start.56 = (bf16[512,1024]{1,0:T(8,128)(2,1)S(1)}, bf16[512,1024]{1,0:T(8,128)(2,1)}, u32[]{:S(2)}, u32[]{:S(2)}) collective-permute-start(bf16[512,1024]{1,0:T(8,128)(2,1)S(1)} %get-tuple-element.68.own_ref), channel_id=1, source_target_pairs={{0,4},{1,5},{2,6},{3,7},{4,0},{5,1},{6,2},{7,3},{8,12},{9,13},{10,... | collective-permute-start | bytes 3145736 | tf_op jit(solution)/shard_map/ppermute | solution.py:399
  287.6 8.8 %shard_map.295 = (bf16[2,2,2,128,512]{4,3,2,1,0:T(8,128)(2,1)S(1)}, bf16[2,2,2,128,512]{4,3,2,1,0:T(8,128)(2,1)}, bf16[2,2,2,128,512]{4,3,2,1,0:T(8,128)(2,1)S(1)}, bf16[2,2,2,128,512]{4,3,2,1,0:T(8,128)(2,1)}) custom-call(s32[4]{0:T(128)S(1)} %pad_add_fusion.1.m, bf16[1024,2048]{1,0:T(8,128)(2,1)} %get-tuple-element.63.x_ref, ...), custom_call_target="tpu_custom_call" | custom-call | flops 4294967296 | bytes 10485760 | tf_op jit(solution)/shard_map/pallas_call | solution.py:481
  299.9 18.4 %shard_map.287 = (bf16[1024,2048]{1,0:T(8,128)(2,1)}, bf16[512,1024]{1,0:T(8,128)(2,1)}, f32[512,1024]{1,0:T(8,128)}, f32[8,2048]{1,0:T(8,128)S(1)}) custom-call(s32[4]{0:T(128)S(1)} %pad_add_fusion.1.m, bf16[512,1024]{1,0:T(8,128)(2,1)} %copy-done.36, bf16[512,1024]{1,0:T(8,128)(2,1)} %collective-permute-done.56.other_ref, ...), custom_call_target="tpu_custom_call" | custom-call | flops 8589934592 | bytes 23068672 | tf_op jit(solution)/shard_map/pallas_call | solution.py:481
  321.6 5.8 collective-permute-start.54
  333.9 3.6 collective-permute-done.54
  338.7 5.5 shard_map.288
  345.5 11.8 %collective-permute-start.58 = (bf16[512,1024]{1,0:T(8,128)(2,1)}, bf16[512,1024]{1,0:T(8,128)(2,1)}, u32[]{:S(2)}, u32[]{:S(2)}) collective-permute-start(bf16[512,1024]{1,0:T(8,128)(2,1)} %get-tuple-element.74.own_ref.da_own_ref), channel_id=1, source_target_pairs={{0,4},{1,5},{2,6},{3,7},{4,0},{5,1},{6,2},{7,3},{8,12},{9,13},{10,... | collective-permute-start | bytes 3145736 | tf_op jit(solution)/shard_map/ppermute | solution.py:399
  362.0 4.5 collective-permute-done.94
  366.4 13.4 %collective-permute-done.97 = bf16[2,128,512]{2,1,0:T(8,128)(2,1)S(1)} collective-permute-done((bf16[2,128,512]{2,1,0:T(8,128)(2,1)}, bf16[2,128,512]{2,1,0:T(8,128)(2,1)S(1)}, u32[]{:S(2)}, u32[]{:S(2)}) %collective-permute-start.97) | collective-permute-done | bytes 262176 | tf_op jit(solution)/shard_map/ppermute | solution.py:399
  380.8 2.2 copy.53
  383.0 2.0 copy.54
  388.3 6.3 shard_map.289.grad_ref
  395.9 31.3 %shard_map.290 = (bf16[3,1024,512]{2,1,0:T(8,128)(2,1)S(1)}, f32[8,512]{1,0:T(8,128)S(1)}) custom-call(s32[4]{0:T(128)S(1)} %pad_add_fusion.1.m, bf16[3,1024,512]{2,1,0:T(8,128)(2,1)} %get-tuple-element.57.q_ref.k_ref.v_ref, bf16[3,1024,512]{2,1,0:T(8,128)(2,1)} %get-tuple-element.57.q_ref.k_ref.v_ref, ...), custom_call_target="tpu_custom_call" | custom-call | flops 21474836480 | bytes 8388608 | tf_op jit(solution)/shard_map/pallas_call | solution.py:481
  430.2 11.8 %shard_map.294 = (bf16[2,2,10,32,512]{4,3,2,1,0:T(8,128)(2,1)}, bf16[2,2,10,32,512]{4,3,2,1,0:T(8,128)(2,1)}, bf16[2,2,10,32,512]{4,3,2,1,0:T(8,128)(2,1)}, bf16[2,2,10,32,512]{4,3,2,1,0:T(8,128)(2,1)}) custom-call(s32[4]{0:T(128)S(1)} %pad_add_fusion.1.m, bf16[512,1024]{1,0:T(8,128)(2,1)} %get-tuple-element.62.own_ref, ...), custom_call_target="tpu_custom_call" | custom-call | flops 5368709120 | bytes 15728640 | tf_op jit(solution)/shard_map/pallas_call | solution.py:481
  444.1 2.5 collective-permute-start.80
  447.6 9.3 %shard_map.291 = (bf16[512,1024]{1,0:T(8,128)(2,1)S(1)}, f32[512,1024]{1,0:T(8,128)}) custom-call(s32[4]{0:T(128)S(1)} %pad_add_fusion.1.m, bf16[3,1024,512]{2,1,0:T(8,128)(2,1)} %copy-done.42, bf16[2,6,32,512]{3,2,1,0:T(8,128)(2,1)S(1)} %copy-done.33, bf16[2,6,32,512]{3,2,1,0:T(8,128)(2,1)} %collective-permute-done.19.rest_1_, ...), custom_call_target="tpu_custom_call" | custom-call | flops 3221225472 | bytes 9437184 | tf_op jit(solution)/shard_map/pallas_call | solution.py:481
  458.1 15.0 %collective-permute-done.79 = f32[4,384]{1,0:T(4,128)S(1)} collective-permute-done((f32[4,384]{1,0:T(4,128)S(1)}, f32[4,384]{1,0:T(4,128)S(1)}, u32[]{:S(2)}, u32[]{:S(2)}) %collective-permute-start.79) | collective-permute-done | bytes 6176 | tf_op jit(solution)/shard_map/ppermute | solution.py:399
  473.4 3.3 collective-permute-start.82
  478.1 8.7 %shard_map.293 = (bf16[2,2,6,32,512]{4,3,2,1,0:T(8,128)(2,1)S(1)}, bf16[2,2,6,32,512]{4,3,2,1,0:T(8,128)(2,1)S(1)}, bf16[2,2,6,32,512]{4,3,2,1,0:T(8,128)(2,1)S(1)}, bf16[2,2,6,32,512]{4,3,2,1,0:T(8,128)(2,1)S(1)}) custom-call(s32[4]{0:T(128)S(1)} %pad_add_fusion.1.m, bf16[1024,1024]{1,0:T(8,128)(2,1)S(1)} %copy-done.44, bf16[3,1024,512]{2,1,0:T(8,128)(2,1)} %copy-done.42), custom_call_target="tpu_custom_call" | custom-call | flops 3221225472 | bytes 8388608 | tf_op jit(solution)/shard_map/pallas_call | solution.py:481
  489.6 3.0 shard_map.292
  492.7 2.2 collective-permute-start.62
  497.4 7.0 %collective-permute-done.69 = bf16[2,2,6,32,512]{4,3,2,1,0:T(8,128)(2,1)S(1)} collective-permute-done((bf16[2,2,6,32,512]{4,3,2,1,0:T(8,128)(2,1)S(1)}, bf16[2,2,6,32,512]{4,3,2,1,0:T(8,128)(2,1)S(1)}, u32[]{:S(2)}, u32[]{:S(2)}) %collective-permute-start.69) | collective-permute-done | bytes 786464 | tf_op jit(solution)/shard_map/ppermute | solution.py:399
  506.5 2.1 collective-permute-done.65
  511.2 30.7 %collective-permute-done.66 = f32[4,1024]{1,0:T(4,128)S(1)} collective-permute-done((f32[4,1024]{1,0:T(4,128)S(1)}, f32[4,1024]{1,0:T(4,128)S(1)}, u32[]{:S(2)}, u32[]{:S(2)}) %collective-permute-start.66) | collective-permute-done | bytes 16416 | tf_op jit(solution)/shard_map/ppermute | solution.py:399
  548.0 7.3 %collective-permute-start.71 = (bf16[6,32,512]{2,1,0:T(8,128)(2,1)S(1)}, bf16[6,32,512]{2,1,0:T(8,128)(2,1)S(1)}, u32[]{:S(2)}, u32[]{:S(2)}) collective-permute-start(bf16[6,32,512]{2,1,0:T(8,128)(2,1)S(1)} %fusion.36), channel_id=1, source_target_pairs={{0,1},{1,2},{2,3},{3,0},{4,5},{5,6},{6,7},{7,4},{8,9},{9,10},{10,1... | collective-permute-start | bytes 589832 | tf_op jit(solution)/shard_map/ppermute | solution.py:399
  555.8 2.7 add_convert_fusion.3
  558.6 2.6 add_convert_fusion.1
  561.6 5.4 collective-permute-start.61
  566.9 19.2 %collective-permute-done.74 = bf16[6,32,512]{2,1,0:T(8,128)(2,1)S(1)} collective-permute-done((bf16[6,32,512]{2,1,0:T(8,128)(2,1)S(1)}, bf16[6,32,512]{2,1,0:T(8,128)(2,1)S(1)}, u32[]{:S(2)}, u32[]{:S(2)}) %collective-permute-start.74) | collective-permute-done | bytes 196640 | tf_op jit(solution)/shard_map/ppermute | solution.py:399
  590.5 5.4 collective-permute-done.88
  597.0 4.6 collective-permute-start.90
  605.0 18.9 %collective-permute-done.89 = bf16[10,32,512]{2,1,0:T(8,128)(2,1)S(1)} collective-permute-done((bf16[10,32,512]{2,1,0:T(8,128)(2,1)}, bf16[10,32,512]{2,1,0:T(8,128)(2,1)S(1)}, u32[]{:S(2)}, u32[]{:S(2)}) %collective-permute-start.89) | collective-permute-done | bytes 327712 | tf_op jit(solution)/shard_map/ppermute | solution.py:399
  (467 shorter events, 126.6 us)
Async XLA Ops:
  2.5 32.6 %collective-permute-start.17 = (bf16[3,32,512]{2,1,0:T(8,128)(2,1)S(1)}, bf16[3,32,512]{2,1,0:T(8,128)(2,1)S(1)}, u32[]{:S(2)}, u32[]{:S(2)}) collective-permute-start(bf16[3,32,512]{2,1,0:T(8,128)(2,1)S(1)} %bitcast.267), channel_id=1, source_target_pairs={{0,4},{1,5},{2,6},{3,7},{4,0},{5,1},{6,2},{7,3},{8,12},{9,13},{10,... | collective-permute-start | bytes 294920 | tf_op jit(solution)/shard_map/ppermute | solution.py:399
  4.3 59.9 %collective-permute-start = (bf16[256,1024]{1,0:T(8,128)(2,1)}, bf16[256,1024]{1,0:T(8,128)(2,1)S(1)}, u32[]{:S(2)}, u32[]{:S(2)}) collective-permute-start(bf16[256,1024]{1,0:T(8,128)(2,1)} %get-tuple-element.147), channel_id=1, source_target_pairs={{0,0},{1,1},{2,4},{3,5},{4,2},{5,3},{6,6},{7,7},{8,8},{9,9},{10,12... | collective-permute-start | bytes 1572872 | tf_op jit(solution)/shard_map/ppermute | solution.py:399
  32.7 35.1 %collective-permute-start.1 = (bf16[256,1024]{1,0:T(8,128)(2,1)}, bf16[256,1024]{1,0:T(8,128)(2,1)S(1)}, u32[]{:S(2)}, u32[]{:S(2)}) collective-permute-start(bf16[256,1024]{1,0:T(8,128)(2,1)} %get-tuple-element.146), channel_id=1, source_target_pairs={{0,1},{1,0},{2,5},{3,4},{4,3},{5,2},{6,7},{7,6},{8,9},{9,8},{10,13... | collective-permute-start | bytes 1572872 | tf_op jit(solution)/shard_map/ppermute | solution.py:399
  35.1 24.8 %collective-permute-start.22 = (bf16[6,32,512]{2,1,0:T(8,128)(2,1)S(1)}, bf16[6,32,512]{2,1,0:T(8,128)(2,1)S(1)}, u32[]{:S(2)}, u32[]{:S(2)}) collective-permute-start(bf16[6,32,512]{2,1,0:T(8,128)(2,1)S(1)} %get-tuple-element.159), channel_id=1, source_target_pairs={{0,2},{1,3},{2,0},{3,1},{4,6},{5,7},{6,4},{7,5},{8,10},{9,11},{10,... | collective-permute-start | bytes 589832 | tf_op jit(solution)/shard_map/ppermute | solution.py:399
  36.2 23.6 %collective-permute-start.23 = (bf16[6,32,512]{2,1,0:T(8,128)(2,1)S(1)}, bf16[6,32,512]{2,1,0:T(8,128)(2,1)S(1)}, u32[]{:S(2)}, u32[]{:S(2)}) collective-permute-start(bf16[6,32,512]{2,1,0:T(8,128)(2,1)S(1)} %get-tuple-element.159), channel_id=1, source_target_pairs={{0,3},{1,0},{2,1},{3,2},{4,7},{5,4},{6,5},{7,6},{8,11},{9,8},{10,9... | collective-permute-start | bytes 589832 | tf_op jit(solution)/shard_map/ppermute | solution.py:399
  37.7 26.3 %collective-permute-start.18 = (bf16[6,32,512]{2,1,0:T(8,128)(2,1)S(1)}, bf16[6,32,512]{2,1,0:T(8,128)(2,1)S(1)}, u32[]{:S(2)}, u32[]{:S(2)}) collective-permute-start(bf16[6,32,512]{2,1,0:T(8,128)(2,1)S(1)} %get-tuple-element.159), channel_id=1, source_target_pairs={{0,1},{1,2},{2,3},{3,0},{4,5},{5,6},{6,7},{7,4},{8,9},{9,10},{10,1... | collective-permute-start | bytes 589832 | tf_op jit(solution)/shard_map/ppermute | solution.py:399
  64.1 25.8 %collective-permute-start.35 = (bf16[10,32,512]{2,1,0:T(8,128)(2,1)S(1)}, bf16[10,32,512]{2,1,0:T(8,128)(2,1)S(1)}, u32[]{:S(2)}, u32[]{:S(2)}) collective-permute-start(bf16[10,32,512]{2,1,0:T(8,128)(2,1)S(1)} %get-tuple-element.155), channel_id=1, source_target_pairs={{0,2},{1,3},{2,0},{3,1},{4,6},{5,7},{6,4},{7,5},{8,10},{9,11},{10,... | collective-permute-start | bytes 983048 | tf_op jit(solution)/shard_map/ppermute | solution.py:399
  64.2 23.9 %collective-permute-start.14 = (f32[1,1024]{1,0:T(1,128)S(1)}, f32[1,1024]{1,0:T(1,128)S(1)}, u32[]{:S(2)}, u32[]{:S(2)}) collective-permute-start(f32[1,1024]{1,0:T(1,128)S(1)} %get-tuple-element.176), channel_id=1, source_target_pairs={{0,2},{1,3},{2,0},{3,1},{4,6},{5,7},{6,4},{7,5},{8,10},{9,11},{10,... | collective-permute-start | bytes 12296 | tf_op jit(solution)/shard_map/ppermute | solution.py:399
  67.5 21.9 %collective-permute-start.15 = (f32[1,1024]{1,0:T(1,128)S(1)}, f32[1,1024]{1,0:T(1,128)S(1)}, u32[]{:S(2)}, u32[]{:S(2)}) collective-permute-start(f32[1,1024]{1,0:T(1,128)S(1)} %get-tuple-element.175), channel_id=1, source_target_pairs={{0,3},{1,0},{2,1},{3,2},{4,7},{5,4},{6,5},{7,6},{8,11},{9,8},{10,9... | collective-permute-start | bytes 12296 | tf_op jit(solution)/shard_map/ppermute | solution.py:399
  67.5 23.5 %collective-permute-start.36 = (bf16[10,32,512]{2,1,0:T(8,128)(2,1)S(1)}, bf16[10,32,512]{2,1,0:T(8,128)(2,1)S(1)}, u32[]{:S(2)}, u32[]{:S(2)}) collective-permute-start(bf16[10,32,512]{2,1,0:T(8,128)(2,1)S(1)} %get-tuple-element.155), channel_id=1, source_target_pairs={{0,3},{1,0},{2,1},{3,2},{4,7},{5,4},{6,5},{7,6},{8,11},{9,8},{10,9... | collective-permute-start | bytes 983048 | tf_op jit(solution)/shard_map/ppermute | solution.py:399
  67.8 24.2 %collective-permute-start.31 = (bf16[10,32,512]{2,1,0:T(8,128)(2,1)S(1)}, bf16[10,32,512]{2,1,0:T(8,128)(2,1)S(1)}, u32[]{:S(2)}, u32[]{:S(2)}) collective-permute-start(bf16[10,32,512]{2,1,0:T(8,128)(2,1)S(1)} %get-tuple-element.155), channel_id=1, source_target_pairs={{0,1},{1,2},{2,3},{3,0},{4,5},{5,6},{6,7},{7,4},{8,9},{9,10},{10,1... | collective-permute-start | bytes 983048 | tf_op jit(solution)/shard_map/ppermute | solution.py:399
  89.8 43.2 %collective-permute-start.16 = (bf16[512,1024]{1,0:T(8,128)(2,1)}, bf16[512,1024]{1,0:T(8,128)(2,1)}, u32[]{:S(2)}, u32[]{:S(2)}) collective-permute-start(bf16[512,1024]{1,0:T(8,128)(2,1)} %constant_dynamic-update-slice_fusion.own_ref.tok_ref), channel_id=1, source_target_pairs={{0,4},{1,5},{2,6},{3,7},{4,0},{5,1},{6,2},{7,3},{8,12},{9,13},{10,... | collective-permute-start | bytes 3145736 | tf_op jit(solution)/shard_map/ppermute | solution.py:399
  91.0 16.7 %collective-permute-start.24 = (bf16[2,6,32,512]{3,2,1,0:T(8,128)(2,1)S(1)}, bf16[2,6,32,512]{3,2,1,0:T(8,128)(2,1)}, u32[]{:S(2)}, u32[]{:S(2)}) collective-permute-start(bf16[2,6,32,512]{3,2,1,0:T(8,128)(2,1)S(1)} %pad_maximum_fusion.8.rest_4_), channel_id=1, source_target_pairs={{0,8},{1,9},{2,10},{3,11},{4,12},{5,13},{6,14},{7,15},{8,0},{9,1},... | collective-permute-start | bytes 1179656 | tf_op jit(solution)/shard_map/ppermute | solution.py:399
  92.0 16.2 %collective-permute-start.20 = (bf16[2,6,32,512]{3,2,1,0:T(8,128)(2,1)S(1)}, bf16[2,6,32,512]{3,2,1,0:T(8,128)(2,1)}, u32[]{:S(2)}, u32[]{:S(2)}) collective-permute-start(bf16[2,6,32,512]{3,2,1,0:T(8,128)(2,1)S(1)} %pad_maximum_fusion.7.rest_0_), channel_id=1, source_target_pairs={{0,16},{1,17},{2,18},{3,19},{4,20},{5,21},{6,22},{7,23},{8,24},{9,... | collective-permute-start | bytes 1179656 | tf_op jit(solution)/shard_map/ppermute | solution.py:399
  98.4 33.1 %collective-permute-start.38 = (bf16[2,10,32,512]{3,2,1,0:T(8,128)(2,1)S(1)}, bf16[2,10,32,512]{3,2,1,0:T(8,128)(2,1)S(1)}, u32[]{:S(2)}, u32[]{:S(2)}) collective-permute-start(bf16[2,10,32,512]{3,2,1,0:T(8,128)(2,1)S(1)} %pad_maximum_fusion.4.rest_4_.rest_12_), channel_id=1, source_target_pairs={{0,16},{1,17},{2,18},{3,19},{4,20},{5,21},{6,22},{7,23},{8,24},{9,... | collective-permute-start | bytes 1966088 | tf_op jit(solution)/shard_map/ppermute | solution.py:399
  99.6 32.2 %collective-permute-start.32 = (bf16[2,10,32,512]{3,2,1,0:T(8,128)(2,1)S(1)}, bf16[2,10,32,512]{3,2,1,0:T(8,128)(2,1)S(1)}, u32[]{:S(2)}, u32[]{:S(2)}) collective-permute-start(bf16[2,10,32,512]{3,2,1,0:T(8,128)(2,1)S(1)} %pad_maximum_fusion.3.rest_0_.rest_8_), channel_id=1, source_target_pairs={{0,8},{1,9},{2,10},{3,11},{4,12},{5,13},{6,14},{7,15},{8,0},{9,1},... | collective-permute-start | bytes 1966088 | tf_op jit(solution)/shard_map/ppermute | solution.py:399
  107.7 22.4 %collective-permute-start.26 = (bf16[2,6,32,512]{3,2,1,0:T(8,128)(2,1)}, bf16[2,6,32,512]{3,2,1,0:T(8,128)(2,1)S(1)}, u32[]{:S(2)}, u32[]{:S(2)}) collective-permute-start(bf16[2,6,32,512]{3,2,1,0:T(8,128)(2,1)} %collective-permute-done.25.rest_6_), channel_id=1, source_target_pairs={{0,8},{1,9},{2,10},{3,11},{4,12},{5,13},{6,14},{7,15},{8,0},{9,1},... | collective-permute-start | bytes 1179656 | tf_op jit(solution)/shard_map/ppermute | solution.py:399
  108.2 22.4 %collective-permute-start.21 = (bf16[2,6,32,512]{3,2,1,0:T(8,128)(2,1)}, bf16[2,6,32,512]{3,2,1,0:T(8,128)(2,1)S(1)}, u32[]{:S(2)}, u32[]{:S(2)}) collective-permute-start(bf16[2,6,32,512]{3,2,1,0:T(8,128)(2,1)} %collective-permute-done.19.rest_1_), channel_id=1, source_target_pairs={{0,16},{1,17},{2,18},{3,19},{4,20},{5,21},{6,22},{7,23},{8,24},{9,... | collective-permute-start | bytes 1179656 | tf_op jit(solution)/shard_map/ppermute | solution.py:399
  130.1 36.5 %collective-permute-start.37 = (bf16[2,10,32,512]{3,2,1,0:T(8,128)(2,1)S(1)}, bf16[2,10,32,512]{3,2,1,0:T(8,128)(2,1)S(1)}, u32[]{:S(2)}, u32[]{:S(2)}) collective-permute-start(bf16[2,10,32,512]{3,2,1,0:T(8,128)(2,1)S(1)} %pad_maximum_fusion.4.rest_4_.rest_12_), channel_id=1, source_target_pairs={{0,8},{1,9},{2,10},{3,11},{4,12},{5,13},{6,14},{7,15},{8,0},{9,1},... | collective-permute-start | bytes 1966088 | tf_op jit(solution)/shard_map/ppermute | solution.py:399
  130.6 36.0 %collective-permute-start.33 = (bf16[2,10,32,512]{3,2,1,0:T(8,128)(2,1)S(1)}, bf16[2,10,32,512]{3,2,1,0:T(8,128)(2,1)S(1)}, u32[]{:S(2)}, u32[]{:S(2)}) collective-permute-start(bf16[2,10,32,512]{3,2,1,0:T(8,128)(2,1)S(1)} %pad_maximum_fusion.3.rest_0_.rest_8_), channel_id=1, source_target_pairs={{0,16},{1,17},{2,18},{3,19},{4,20},{5,21},{6,22},{7,23},{8,24},{9,... | collective-permute-start | bytes 1966088 | tf_op jit(solution)/shard_map/ppermute | solution.py:399
  131.5 35.1 %collective-permute-start.39 = (bf16[2,10,32,512]{3,2,1,0:T(8,128)(2,1)S(1)}, bf16[2,10,32,512]{3,2,1,0:T(8,128)(2,1)S(1)}, u32[]{:S(2)}, u32[]{:S(2)}) collective-permute-start(bf16[2,10,32,512]{3,2,1,0:T(8,128)(2,1)S(1)} %collective-permute-done.38.rest_6_.rest_14_), channel_id=1, source_target_pairs={{0,8},{1,9},{2,10},{3,11},{4,12},{5,13},{6,14},{7,15},{8,0},{9,1},... | collective-permute-start | bytes 1966088 | tf_op jit(solution)/shard_map/ppermute | solution.py:399
  131.8 34.8 %collective-permute-start.34 = (bf16[2,10,32,512]{3,2,1,0:T(8,128)(2,1)S(1)}, bf16[2,10,32,512]{3,2,1,0:T(8,128)(2,1)S(1)}, u32[]{:S(2)}, u32[]{:S(2)}) collective-permute-start(bf16[2,10,32,512]{3,2,1,0:T(8,128)(2,1)S(1)} %collective-permute-done.32.rest_1_.rest_9_), channel_id=1, source_target_pairs={{0,16},{1,17},{2,18},{3,19},{4,20},{5,21},{6,22},{7,23},{8,24},{9,... | collective-permute-start | bytes 1966088 | tf_op jit(solution)/shard_map/ppermute | solution.py:399
  180.2 17.6 %collective-permute-start.46 = (bf16[2,128,512]{2,1,0:T(8,128)(2,1)}, bf16[2,128,512]{2,1,0:T(8,128)(2,1)}, u32[]{:S(2)}, u32[]{:S(2)}) collective-permute-start(bf16[2,128,512]{2,1,0:T(8,128)(2,1)} %bitcast.250), channel_id=1, source_target_pairs={{0,2},{1,3},{2,0},{3,1},{4,6},{5,7},{6,4},{7,5},{8,10},{9,11},{10,... | collective-permute-start | bytes 786440 | tf_op jit(solution)/shard_map/ppermute | solution.py:399
  180.2 17.6 %collective-permute-start.47 = (bf16[2,128,512]{2,1,0:T(8,128)(2,1)}, bf16[2,128,512]{2,1,0:T(8,128)(2,1)}, u32[]{:S(2)}, u32[]{:S(2)}) collective-permute-start(bf16[2,128,512]{2,1,0:T(8,128)(2,1)} %bitcast.251), channel_id=1, source_target_pairs={{0,3},{1,0},{2,1},{3,2},{4,7},{5,4},{6,5},{7,6},{8,11},{9,8},{10,9... | collective-permute-start | bytes 786440 | tf_op jit(solution)/shard_map/ppermute | solution.py:399
  188.7 30.1 %collective-permute-start.41 = (bf16[512,1024]{1,0:T(8,128)(2,1)}, bf16[512,1024]{1,0:T(8,128)(2,1)}, u32[]{:S(2)}, u32[]{:S(2)}) collective-permute-start(bf16[512,1024]{1,0:T(8,128)(2,1)} %get-tuple-element.62.own_ref), channel_id=1, source_target_pairs={{0,4},{1,5},{2,6},{3,7},{4,0},{5,1},{6,2},{7,3},{8,12},{9,13},{10,... | collective-permute-start | bytes 3145736 | tf_op jit(solution)/shard_map/ppermute | solution.py:399
  188.7 14.5 %collective-permute-start.42 = (bf16[2,128,512]{2,1,0:T(8,128)(2,1)S(1)}, bf16[2,128,512]{2,1,0:T(8,128)(2,1)S(1)}, u32[]{:S(2)}, u32[]{:S(2)}) collective-permute-start(bf16[2,128,512]{2,1,0:T(8,128)(2,1)S(1)} %bitcast.252), channel_id=1, source_target_pairs={{0,1},{1,2},{2,3},{3,0},{4,5},{5,6},{6,7},{7,4},{8,9},{9,10},{10,1... | collective-permute-start | bytes 786440 | tf_op jit(solution)/shard_map/ppermute | solution.py:399
  204.9 29.6 %collective-permute-start.48 = (bf16[2,2,128,512]{3,2,1,0:T(8,128)(2,1)}, bf16[2,2,128,512]{3,2,1,0:T(8,128)(2,1)}, u32[]{:S(2)}, u32[]{:S(2)}) collective-permute-start(bf16[2,2,128,512]{3,2,1,0:T(8,128)(2,1)} %pad_maximum_fusion.6.rest_4_), channel_id=1, source_target_pairs={{0,8},{1,9},{2,10},{3,11},{4,12},{5,13},{6,14},{7,15},{8,0},{9,1},... | collective-permute-start | bytes 1572872 | tf_op jit(solution)/shard_map/ppermute | solution.py:399
  205.5 29.0 %collective-permute-start.44 = (bf16[2,2,128,512]{3,2,1,0:T(8,128)(2,1)}, bf16[2,2,128,512]{3,2,1,0:T(8,128)(2,1)}, u32[]{:S(2)}, u32[]{:S(2)}) collective-permute-start(bf16[2,2,128,512]{3,2,1,0:T(8,128)(2,1)} %pad_maximum_fusion.5.rest_0_), channel_id=1, source_target_pairs={{0,16},{1,17},{2,18},{3,19},{4,20},{5,21},{6,22},{7,23},{8,24},{9,... | collective-permute-start | bytes 1572872 | tf_op jit(solution)/shard_map/ppermute | solution.py:399
  212.9 27.0 %collective-permute-start.50 = (bf16[2,2,128,512]{3,2,1,0:T(8,128)(2,1)}, bf16[2,2,128,512]{3,2,1,0:T(8,128)(2,1)}, u32[]{:S(2)}, u32[]{:S(2)}) collective-permute-start(bf16[2,2,128,512]{3,2,1,0:T(8,128)(2,1)} %collective-permute-done.49.rest_6_), channel_id=1, source_target_pairs={{0,8},{1,9},{2,10},{3,11},{4,12},{5,13},{6,14},{7,15},{8,0},{9,1},... | collective-permute-start | bytes 1572872 | tf_op jit(solution)/shard_map/ppermute | solution.py:399
  217.5 22.5 %collective-permute-start.45 = (bf16[2,2,128,512]{3,2,1,0:T(8,128)(2,1)}, bf16[2,2,128,512]{3,2,1,0:T(8,128)(2,1)}, u32[]{:S(2)}, u32[]{:S(2)}) collective-permute-start(bf16[2,2,128,512]{3,2,1,0:T(8,128)(2,1)} %collective-permute-done.43.rest_1_), channel_id=1, source_target_pairs={{0,16},{1,17},{2,18},{3,19},{4,20},{5,21},{6,22},{7,23},{8,24},{9,... | collective-permute-start | bytes 1572872 | tf_op jit(solution)/shard_map/ppermute | solution.py:399
  270.4 15.9 %collective-permute-start.56 = (bf16[512,1024]{1,0:T(8,128)(2,1)S(1)}, bf16[512,1024]{1,0:T(8,128)(2,1)}, u32[]{:S(2)}, u32[]{:S(2)}) collective-permute-start(bf16[512,1024]{1,0:T(8,128)(2,1)S(1)} %get-tuple-element.68.own_ref), channel_id=1, source_target_pairs={{0,4},{1,5},{2,6},{3,7},{4,0},{5,1},{6,2},{7,3},{8,12},{9,13},{10,... | collective-permute-start | bytes 3145736 | tf_op jit(solution)/shard_map/ppermute | solution.py:399
  297.4 31.7 %collective-permute-start.92 = (bf16[2,2,2,128,512]{4,3,2,1,0:T(8,128)(2,1)}, bf16[2,2,2,128,512]{4,3,2,1,0:T(8,128)(2,1)}, u32[]{:S(2)}, u32[]{:S(2)}) collective-permute-start(bf16[2,2,2,128,512]{4,3,2,1,0:T(8,128)(2,1)} %get-tuple-element.96), channel_id=1, source_target_pairs={{0,16},{1,17},{2,18},{3,19},{4,20},{5,21},{6,22},{7,23},{8,24},{9,... | collective-permute-start | bytes 3145736 | tf_op jit(solution)/shard_map/ppermute | solution.py:399
  298.4 32.4 %collective-permute-start.95 = (bf16[2,2,2,128,512]{4,3,2,1,0:T(8,128)(2,1)}, bf16[2,2,2,128,512]{4,3,2,1,0:T(8,128)(2,1)}, u32[]{:S(2)}, u32[]{:S(2)}) collective-permute-start(bf16[2,2,2,128,512]{4,3,2,1,0:T(8,128)(2,1)} %get-tuple-element.98), channel_id=1, source_target_pairs={{0,8},{1,9},{2,10},{3,11},{4,12},{5,13},{6,14},{7,15},{8,0},{9,1},... | collective-permute-start | bytes 3145736 | tf_op jit(solution)/shard_map/ppermute | solution.py:399
  318.3 20.4 %collective-permute-start.57 = (bf16[512,1024]{1,0:T(8,128)(2,1)}, bf16[512,1024]{1,0:T(8,128)(2,1)S(1)}, u32[]{:S(2)}, u32[]{:S(2)}) collective-permute-start(bf16[512,1024]{1,0:T(8,128)(2,1)} %get-tuple-element.71), channel_id=1, source_target_pairs={{0,4},{1,5},{2,6},{3,7},{4,0},{5,1},{6,2},{7,3},{8,12},{9,13},{10,... | collective-permute-start | bytes 3145736 | tf_op jit(solution)/shard_map/ppermute | solution.py:399
  321.6 15.9 %collective-permute-start.54 = (bf16[256,1024]{1,0:T(8,128)(2,1)}, bf16[256,1024]{1,0:T(8,128)(2,1)S(1)}, u32[]{:S(2)}, u32[]{:S(2)}) collective-permute-start(bf16[256,1024]{1,0:T(8,128)(2,1)} %get-tuple-element.142), channel_id=1, source_target_pairs={{1,0},{0,1},{5,2},{4,3},{3,4},{2,5},{7,6},{6,7},{9,8},{8,9},{13,10... | collective-permute-start | bytes 1572872 | tf_op jit(solution)/shard_map/ppermute | solution.py:399
  330.7 26.5 %collective-permute-start.93 = (bf16[2,2,128,512]{3,2,1,0:T(8,128)(2,1)S(1)}, bf16[2,2,128,512]{3,2,1,0:T(8,128)(2,1)S(1)}, u32[]{:S(2)}, u32[]{:S(2)}) collective-permute-start(bf16[2,2,128,512]{3,2,1,0:T(8,128)(2,1)S(1)} %get-tuple-element.125), channel_id=1, source_target_pairs={{0,8},{1,9},{2,10},{3,11},{4,12},{5,13},{6,14},{7,15},{8,0},{9,1},... | collective-permute-start | bytes 1572872 | tf_op jit(solution)/shard_map/ppermute | solution.py:399
  332.4 25.0 %collective-permute-start.96 = (bf16[2,2,128,512]{3,2,1,0:T(8,128)(2,1)S(1)}, bf16[2,2,128,512]{3,2,1,0:T(8,128)(2,1)S(1)}, u32[]{:S(2)}, u32[]{:S(2)}) collective-permute-start(bf16[2,2,128,512]{3,2,1,0:T(8,128)(2,1)S(1)} %get-tuple-element.127), channel_id=1, source_target_pairs={{0,16},{1,17},{2,18},{3,19},{4,20},{5,21},{6,22},{7,23},{8,24},{9,... | collective-permute-start | bytes 1572872 | tf_op jit(solution)/shard_map/ppermute | solution.py:399
  345.5 39.5 %collective-permute-start.58 = (bf16[512,1024]{1,0:T(8,128)(2,1)}, bf16[512,1024]{1,0:T(8,128)(2,1)}, u32[]{:S(2)}, u32[]{:S(2)}) collective-permute-start(bf16[512,1024]{1,0:T(8,128)(2,1)} %get-tuple-element.74.own_ref.da_own_ref), channel_id=1, source_target_pairs={{0,4},{1,5},{2,6},{3,7},{4,0},{5,1},{6,2},{7,3},{8,12},{9,13},{10,... | collective-permute-start | bytes 3145736 | tf_op jit(solution)/shard_map/ppermute | solution.py:399
  358.3 21.5 %collective-permute-start.97 = (bf16[2,128,512]{2,1,0:T(8,128)(2,1)}, bf16[2,128,512]{2,1,0:T(8,128)(2,1)S(1)}, u32[]{:S(2)}, u32[]{:S(2)}) collective-permute-start(bf16[2,128,512]{2,1,0:T(8,128)(2,1)} %get-tuple-element.134), channel_id=1, source_target_pairs={{0,2},{1,3},{2,0},{3,1},{4,6},{5,7},{6,4},{7,5},{8,10},{9,11},{10,... | collective-permute-start | bytes 786440 | tf_op jit(solution)/shard_map/ppermute | solution.py:399
  358.4 21.5 %collective-permute-start.98 = (bf16[2,128,512]{2,1,0:T(8,128)(2,1)}, bf16[2,128,512]{2,1,0:T(8,128)(2,1)S(1)}, u32[]{:S(2)}, u32[]{:S(2)}) collective-permute-start(bf16[2,128,512]{2,1,0:T(8,128)(2,1)} %get-tuple-element.135), channel_id=1, source_target_pairs={{0,3},{1,0},{2,1},{3,2},{4,7},{5,4},{6,5},{7,6},{8,11},{9,8},{10,9... | collective-permute-start | bytes 786440 | tf_op jit(solution)/shard_map/ppermute | solution.py:399
  429.3 14.3 %collective-permute-start.77 = (f32[4,4,384]{2,1,0:T(4,128)S(1)}, f32[4,4,384]{2,1,0:T(4,128)S(1)}, u32[]{:S(2)}, u32[]{:S(2)}) collective-permute-start(f32[4,4,384]{2,1,0:T(4,128)S(1)} %dynamic-slice_bitcast_fusion.4), channel_id=1, source_target_pairs={{0,4},{1,5},{2,6},{3,7},{4,0},{5,1},{6,2},{7,3},{8,12},{9,13},{10,... | collective-permute-start | bytes 73736 | tf_op jit(solution)/shard_map/ppermute | solution.py:399
  442.1 113.4 %collective-permute-start.84 = (bf16[2,2,10,32,512]{4,3,2,1,0:T(8,128)(2,1)}, bf16[2,2,10,32,512]{4,3,2,1,0:T(8,128)(2,1)}, u32[]{:S(2)}, u32[]{:S(2)}) collective-permute-start(bf16[2,2,10,32,512]{4,3,2,1,0:T(8,128)(2,1)} %get-tuple-element.92), channel_id=1, source_target_pairs={{0,16},{1,17},{2,18},{3,19},{4,20},{5,21},{6,22},{7,23},{8,24},{9,... | collective-permute-start | bytes 3932168 | tf_op jit(solution)/shard_map/ppermute | solution.py:399
  443.9 14.2 %collective-permute-start.78 = (f32[4,384]{1,0:T(4,128)S(1)}, f32[4,384]{1,0:T(4,128)S(1)}, u32[]{:S(2)}, u32[]{:S(2)}) collective-permute-start(f32[4,384]{1,0:T(4,128)S(1)} %get-tuple-element.171), channel_id=1, source_target_pairs={{0,8},{1,9},{2,10},{3,11},{4,12},{5,13},{6,14},{7,15},{8,0},{9,1},... | collective-permute-start | bytes 18440 | tf_op jit(solution)/shard_map/ppermute | solution.py:399
  444.0 29.2 %collective-permute-start.79 = (f32[4,384]{1,0:T(4,128)S(1)}, f32[4,384]{1,0:T(4,128)S(1)}, u32[]{:S(2)}, u32[]{:S(2)}) collective-permute-start(f32[4,384]{1,0:T(4,128)S(1)} %get-tuple-element.173), channel_id=1, source_target_pairs={{0,16},{1,17},{2,18},{3,19},{4,20},{5,21},{6,22},{7,23},{8,24},{9,... | collective-permute-start | bytes 18440 | tf_op jit(solution)/shard_map/ppermute | solution.py:399
  444.1 29.1 %collective-permute-start.80 = (f32[4,384]{1,0:T(4,128)S(1)}, f32[4,384]{1,0:T(4,128)S(1)}, u32[]{:S(2)}, u32[]{:S(2)}) collective-permute-start(f32[4,384]{1,0:T(4,128)S(1)} %get-tuple-element.172), channel_id=1, source_target_pairs={{0,24},{1,25},{2,26},{3,27},{4,28},{5,29},{6,30},{7,31},{8,16},{9,... | collective-permute-start | bytes 18440 | tf_op jit(solution)/shard_map/ppermute | solution.py:399
  456.9 32.7 %collective-permute-start.59 = (bf16[512,1024]{1,0:T(8,128)(2,1)S(1)}, bf16[512,1024]{1,0:T(8,128)(2,1)S(1)}, u32[]{:S(2)}, u32[]{:S(2)}) collective-permute-start(bf16[512,1024]{1,0:T(8,128)(2,1)S(1)} %get-tuple-element.78), channel_id=1, source_target_pairs={{0,4},{1,5},{2,6},{3,7},{4,0},{5,1},{6,2},{7,3},{8,12},{9,13},{10,... | collective-permute-start | bytes 3145736 | tf_op jit(solution)/shard_map/ppermute | solution.py:399
  473.2 13.7 %collective-permute-start.81 = (f32[1,384]{1,0:T(1,128)S(1)}, f32[1,384]{1,0:T(1,128)S(1)}, u32[]{:S(2)}, u32[]{:S(2)}) collective-permute-start(f32[1,384]{1,0:T(1,128)S(1)} %get-tuple-element.179), channel_id=1, source_target_pairs={{0,1},{1,2},{2,3},{3,0},{4,5},{5,6},{6,7},{7,4},{8,9},{9,10},{10,1... | collective-permute-start | bytes 4616 | tf_op jit(solution)/shard_map/ppermute | solution.py:399
  473.4 15.0 %collective-permute-start.82 = (f32[1,384]{1,0:T(1,128)S(1)}, f32[1,384]{1,0:T(1,128)S(1)}, u32[]{:S(2)}, u32[]{:S(2)}) collective-permute-start(f32[1,384]{1,0:T(1,128)S(1)} %get-tuple-element.181), channel_id=1, source_target_pairs={{0,2},{1,3},{2,0},{3,1},{4,6},{5,7},{6,4},{7,5},{8,10},{9,11},{10,... | collective-permute-start | bytes 4616 | tf_op jit(solution)/shard_map/ppermute | solution.py:399
  486.9 17.5 %collective-permute-start.69 = (bf16[2,2,6,32,512]{4,3,2,1,0:T(8,128)(2,1)S(1)}, bf16[2,2,6,32,512]{4,3,2,1,0:T(8,128)(2,1)S(1)}, u32[]{:S(2)}, u32[]{:S(2)}) collective-permute-start(bf16[2,2,6,32,512]{4,3,2,1,0:T(8,128)(2,1)S(1)} %get-tuple-element.83), channel_id=1, source_target_pairs={{0,16},{1,17},{2,18},{3,19},{4,20},{5,21},{6,22},{7,23},{8,24},{9,... | collective-permute-start | bytes 2359304 | tf_op jit(solution)/shard_map/ppermute | solution.py:399
  488.4 20.3 %collective-permute-start.72 = (bf16[2,2,6,32,512]{4,3,2,1,0:T(8,128)(2,1)S(1)}, bf16[2,2,6,32,512]{4,3,2,1,0:T(8,128)(2,1)S(1)}, u32[]{:S(2)}, u32[]{:S(2)}) collective-permute-start(bf16[2,2,6,32,512]{4,3,2,1,0:T(8,128)(2,1)S(1)} %get-tuple-element.85), channel_id=1, source_target_pairs={{0,8},{1,9},{2,10},{3,11},{4,12},{5,13},{6,14},{7,15},{8,0},{9,1},... | collective-permute-start | bytes 2359304 | tf_op jit(solution)/shard_map/ppermute | solution.py:399
  505.0 53.5 %collective-permute-start.87 = (bf16[2,2,10,32,512]{4,3,2,1,0:T(8,128)(2,1)}, bf16[2,2,10,32,512]{4,3,2,1,0:T(8,128)(2,1)}, u32[]{:S(2)}, u32[]{:S(2)}) collective-permute-start(bf16[2,2,10,32,512]{4,3,2,1,0:T(8,128)(2,1)} %get-tuple-element.94), channel_id=1, source_target_pairs={{0,8},{1,9},{2,10},{3,11},{4,12},{5,13},{6,14},{7,15},{8,0},{9,1},... | collective-permute-start | bytes 3932168 | tf_op jit(solution)/shard_map/ppermute | solution.py:399
  505.1 41.9 %collective-permute-start.70 = (bf16[2,6,32,512]{3,2,1,0:T(8,128)(2,1)S(1)}, bf16[2,6,32,512]{3,2,1,0:T(8,128)(2,1)}, u32[]{:S(2)}, u32[]{:S(2)}) collective-permute-start(bf16[2,6,32,512]{3,2,1,0:T(8,128)(2,1)S(1)} %get-tuple-element.129), channel_id=1, source_target_pairs={{0,8},{1,9},{2,10},{3,11},{4,12},{5,13},{6,14},{7,15},{8,0},{9,1},... | collective-permute-start | bytes 1179656 | tf_op jit(solution)/shard_map/ppermute | solution.py:399
  508.7 33.3 %collective-permute-start.66 = (f32[4,1024]{1,0:T(4,128)S(1)}, f32[4,1024]{1,0:T(4,128)S(1)}, u32[]{:S(2)}, u32[]{:S(2)}) collective-permute-start(f32[4,1024]{1,0:T(4,128)S(1)} %pad_maximum_fusion.12), channel_id=1, source_target_pairs={{0,8},{1,9},{2,10},{3,11},{4,12},{5,13},{6,14},{7,15},{8,0},{9,1},... | collective-permute-start | bytes 49160 | tf_op jit(solution)/shard_map/ppermute | solution.py:399
  509.8 34.3 %collective-permute-start.67 = (f32[4,1024]{1,0:T(4,128)S(1)}, f32[4,1024]{1,0:T(4,128)S(1)}, u32[]{:S(2)}, u32[]{:S(2)}) collective-permute-start(f32[4,1024]{1,0:T(4,128)S(1)} %pad_maximum_fusion.12), channel_id=1, source_target_pairs={{0,16},{1,17},{2,18},{3,19},{4,20},{5,21},{6,22},{7,23},{8,24},{9,... | collective-permute-start | bytes 49160 | tf_op jit(solution)/shard_map/ppermute | solution.py:399
  545.6 51.4 %collective-permute-start.60 = (bf16[256,1024]{1,0:T(8,128)(2,1)}, bf16[256,1024]{1,0:T(8,128)(2,1)}, u32[]{:S(2)}, u32[]{:S(2)}) collective-permute-start(bf16[256,1024]{1,0:T(8,128)(2,1)} %get-tuple-element.138), channel_id=1, source_target_pairs={{1,0},{0,1},{5,2},{4,3},{3,4},{2,5},{7,6},{6,7},{9,8},{8,9},{13,10... | collective-permute-start | bytes 1572872 | tf_op jit(solution)/shard_map/ppermute | solution.py:399
  548.0 13.6 %collective-permute-start.71 = (bf16[6,32,512]{2,1,0:T(8,128)(2,1)S(1)}, bf16[6,32,512]{2,1,0:T(8,128)(2,1)S(1)}, u32[]{:S(2)}, u32[]{:S(2)}) collective-permute-start(bf16[6,32,512]{2,1,0:T(8,128)(2,1)S(1)} %fusion.36), channel_id=1, source_target_pairs={{0,1},{1,2},{2,3},{3,0},{4,5},{5,6},{6,7},{7,4},{8,9},{9,10},{10,1... | collective-permute-start | bytes 589832 | tf_op jit(solution)/shard_map/ppermute | solution.py:399
  555.4 30.8 %collective-permute-start.74 = (bf16[6,32,512]{2,1,0:T(8,128)(2,1)S(1)}, bf16[6,32,512]{2,1,0:T(8,128)(2,1)S(1)}, u32[]{:S(2)}, u32[]{:S(2)}) collective-permute-start(bf16[6,32,512]{2,1,0:T(8,128)(2,1)S(1)} %get-tuple-element.148), channel_id=1, source_target_pairs={{0,2},{1,3},{2,0},{3,1},{4,6},{5,7},{6,4},{7,5},{8,10},{9,11},{10,... | collective-permute-start | bytes 589832 | tf_op jit(solution)/shard_map/ppermute | solution.py:399
  555.5 32.3 %collective-permute-start.75 = (bf16[6,32,512]{2,1,0:T(8,128)(2,1)S(1)}, bf16[6,32,512]{2,1,0:T(8,128)(2,1)S(1)}, u32[]{:S(2)}, u32[]{:S(2)}) collective-permute-start(bf16[6,32,512]{2,1,0:T(8,128)(2,1)S(1)} %get-tuple-element.149), channel_id=1, source_target_pairs={{0,3},{1,0},{2,1},{3,2},{4,7},{5,4},{6,5},{7,6},{8,11},{9,8},{10,9... | collective-permute-start | bytes 589832 | tf_op jit(solution)/shard_map/ppermute | solution.py:399
  558.5 31.1 %collective-permute-start.85 = (bf16[2,10,32,512]{3,2,1,0:T(8,128)(2,1)}, bf16[2,10,32,512]{3,2,1,0:T(8,128)(2,1)S(1)}, u32[]{:S(2)}, u32[]{:S(2)}) collective-permute-start(bf16[2,10,32,512]{3,2,1,0:T(8,128)(2,1)} %get-tuple-element.121), channel_id=1, source_target_pairs={{0,8},{1,9},{2,10},{3,11},{4,12},{5,13},{6,14},{7,15},{8,0},{9,1},... | collective-permute-start | bytes 1966088 | tf_op jit(solution)/shard_map/ppermute | solution.py:399
  561.6 40.0 %collective-permute-start.61 = (bf16[256,1024]{1,0:T(8,128)(2,1)}, bf16[256,1024]{1,0:T(8,128)(2,1)}, u32[]{:S(2)}, u32[]{:S(2)}) collective-permute-start(bf16[256,1024]{1,0:T(8,128)(2,1)} %get-tuple-element.139), channel_id=1, source_target_pairs={{0,0},{1,1},{4,2},{5,3},{2,4},{3,5},{6,6},{7,7},{8,8},{9,9},{12,10... | collective-permute-start | bytes 1572872 | tf_op jit(solution)/shard_map/ppermute | solution.py:399
  589.6 14.4 %collective-permute-start.76 = (f32[3,32,512]{2,1,0:T(8,128)}, f32[3,32,512]{2,1,0:T(8,128)}, u32[]{:S(2)}, u32[]{:S(2)}) collective-permute-start(f32[3,32,512]{2,1,0:T(8,128)} %get-tuple-element.153), channel_id=1, source_target_pairs={{0,4},{1,5},{2,6},{3,7},{4,0},{5,1},{6,2},{7,3},{8,12},{9,13},{10,... | collective-permute-start | bytes 589832 | tf_op jit(solution)/shard_map/ppermute | solution.py:399
  590.5 14.5 %collective-permute-start.86 = (bf16[10,32,512]{2,1,0:T(8,128)(2,1)}, bf16[10,32,512]{2,1,0:T(8,128)(2,1)S(1)}, u32[]{:S(2)}, u32[]{:S(2)}) collective-permute-start(bf16[10,32,512]{2,1,0:T(8,128)(2,1)} %fusion.30), channel_id=1, source_target_pairs={{0,1},{1,2},{2,3},{3,0},{4,5},{5,6},{6,7},{7,4},{8,9},{9,10},{10,1... | collective-permute-start | bytes 983048 | tf_op jit(solution)/shard_map/ppermute | solution.py:399
  597.0 26.9 %collective-permute-start.89 = (bf16[10,32,512]{2,1,0:T(8,128)(2,1)}, bf16[10,32,512]{2,1,0:T(8,128)(2,1)S(1)}, u32[]{:S(2)}, u32[]{:S(2)}) collective-permute-start(bf16[10,32,512]{2,1,0:T(8,128)(2,1)} %get-tuple-element.132), channel_id=1, source_target_pairs={{0,2},{1,3},{2,0},{3,1},{4,6},{5,7},{6,4},{7,5},{8,10},{9,11},{10,... | collective-permute-start | bytes 983048 | tf_op jit(solution)/shard_map/ppermute | solution.py:399
  597.0 26.9 %collective-permute-start.90 = (bf16[10,32,512]{2,1,0:T(8,128)(2,1)}, bf16[10,32,512]{2,1,0:T(8,128)(2,1)S(1)}, u32[]{:S(2)}, u32[]{:S(2)}) collective-permute-start(bf16[10,32,512]{2,1,0:T(8,128)(2,1)} %get-tuple-element.133), channel_id=1, source_target_pairs={{0,3},{1,0},{2,1},{3,2},{4,7},{5,4},{6,5},{7,6},{8,11},{9,8},{10,9... | collective-permute-start | bytes 983048 | tf_op jit(solution)/shard_map/ppermute | solution.py:399
  (119 other events, 1445.9 us)

commit v2 on v1

--- a/solution.py
+++ b/solution.py
@@ -366,8 +366,13 @@
 NT = (((1,), (1,)), ((), ()))
 TN = (((0,), (0,)), ((), ()))
 NN = (((1,), (0,)), ((), ()))
-VMEM_LIMIT = 48 * 1024 * 1024
-CHIP_SLOTS = ((0, 0, 0), (0, 0, 1), (0, 1, 0), (0, 1, 1), (1, 0, 0), (1, 0, 1), (1, 1, 0), (1, 1, 1))
+VMEM_LIMIT = 58 * 1024 * 1024
+CHIP_SLOTS = (
+    ((0, 0, 0), (0, 0, 1)),
+    ((0, 1, 0), (0, 1, 1)),
+    ((1, 0, 0), (1, 1, 0)),
+    ((1, 0, 1), (1, 1, 1)),
+)
 
 
 def dot(left, right, dims=NN):
@@ -389,8 +394,7 @@
 PAIR = device_perm(lambda y, x, c, z: (y, x, 1 - c, z))
 ALONG_X = device_perm(lambda y, x, c, z: (y, 1 - x, c, z))
 ALONG_Y = device_perm(lambda y, x, c, z: (1 - y, x, c, z))
-DIAGONAL = device_perm(lambda y, x, c, z: (1 - y, 1 - x, c, z))
-SHIFT_Z = [device_perm(lambda y, x, c, z, k=k: (y, x, c, (z + k) % 4)) for k in range(4)]
+ALONG_Z = [device_perm(lambda y, x, c, z, k=k: (y, x, c, z ^ k)) for k in range(3)]
 ROW_OUT = [device_perm(lambda y, x, c, z, k=k: (y, x, z // 2, c * 2 + (z + k) % 2)) for k in range(2)]
 ROW_BACK = [[(t, s) for s, t in pairs] for pairs in ROW_OUT]
 
@@ -399,41 +403,65 @@
     return lax.ppermute(value, AXES, pairs)
 
 
-def gather_pieces(shard):
-    near = [shard] + [send(shard, SHIFT_Z[k]) for k in (1, 2, 3)]
-    first, second = jnp.stack(near[:2]), jnp.stack(near[2:])
-    first_x, second_y = send(first, ALONG_X), send(second, ALONG_Y)
-    first_y, second_x = send(first, ALONG_Y), send(second, ALONG_X)
-    first_xy, second_xy = send(first_x, ALONG_Y), send(second_y, ALONG_X)
-    return [first, first_x, first_y, first_xy, second, second_x, second_y, second_xy]
-
-
-def scatter_pieces(first_keep, first_send, second_keep, second_send):
-    add = lambda a, b: (a.astype(F32) + b.astype(F32)).astype(BF)
-    from_y, from_x = send(first_send, ALONG_Y), send(second_send, ALONG_X)
-    to_x = add(first_keep[1], from_y[1])
-    to_y = add(second_keep[1], from_x[1])
-    from_x, from_y, mine_first, mine_second = (
-        send(to_x, ALONG_X),
-        send(to_y, ALONG_Y),
-        add(first_keep[0], from_y[0]),
-        add(second_keep[0], from_x[0]),
-    )
-    far = [
-        send(add(mine_first[1], from_x[1]), SHIFT_Z[1]),
-        send(add(mine_second[0], from_y[0]), SHIFT_Z[2]),
-        send(add(mine_second[1], from_y[1]), SHIFT_Z[3]),
-    ]
-    total = mine_first[0].astype(F32) + from_x[0].astype(F32)
-    return total + far[0].astype(F32) + far[1].astype(F32) + far[2].astype(F32)
-
-
-def place(meta, slot, j):
-    half, y_rel, x_rel = CHIP_SLOTS[slot]
-    y = lax.rem(meta[0] + y_rel, 2)
-    x = lax.rem(meta[1] + x_rel, 2)
-    z = lax.rem(meta[3] + 4 - (2 * half + j), 4)
-    return y * 2 + x, z
+def after(value, *earlier):
+    return lax.optimization_barrier((value, earlier))[0]
+
+
+def gather_line(shard):
+    first = jnp.stack([shard, send(shard, ALONG_Z[2])])
+    return first, send(first, ALONG_Z[1])
+
+
+def gather_plane(first, second, *earlier):
+    first_x, second_y = lax.optimization_barrier((send(first, ALONG_X), send(second, ALONG_Y)))
+    first, second = jnp.stack([after(first, earlier), first_x]), jnp.stack([after(second, earlier), second_y])
+    return [first, send(first, ALONG_Y), second, send(second, ALONG_X)]
+
+
+def add_low(a, b):
+    return (a.astype(F32) + b.astype(F32)).astype(BF)
+
+
+def scatter_one(first_keep, first_send, second_keep, second_send):
+    return first_keep, send(first_send, ALONG_Y), second_keep, send(second_send, ALONG_X)
+
+
+def add_one(first_keep, from_y, second_keep, from_x, *earlier):
+    first_keep, second_keep = after((first_keep, second_keep), earlier)
+    to_x, to_y = add_low(first_keep[1], from_y[1]), add_low(second_keep[1], from_x[1])
+    return add_low(first_keep[0], from_y[0]), to_x, add_low(second_keep[0], from_x[0]), to_y
+
+
+def scatter_two(first, to_x, second, to_y):
+    return first, send(to_x, ALONG_X), second, send(to_y, ALONG_Y)
+
+
+def add_two(first, from_x, second, from_y, *earlier):
+    first, second = after((first, second), earlier)
+    return add_low(first, from_x), add_low(second, from_y)
+
+
+def scatter_three(first, second):
+    return first, send(second, ALONG_Z[1])
+
+
+def add_three(first, received, *earlier):
+    first = after(first, earlier)
+    return add_low(first[0], received[0]), add_low(first[1], received[1])
+
+
+def scatter_four(near, far, *earlier):
+    return after(near, earlier).astype(F32) + send(far, ALONG_Z[2]).astype(F32)
+
+
+def z_relative(half, j):
+    return 2 * j + half
+
+
+def place(meta, slot, at, j):
+    half, y_rel, x_rel = CHIP_SLOTS[slot][at]
+    chip = (meta[0] ^ y_rel) * 2 + (meta[1] ^ x_rel)
+    return chip, meta[3] ^ z_relative(half, j)
 
 
 def load_all(copies):
@@ -443,37 +471,57 @@
         copy.wait()
 
 
+def load_qkv(meta, refs, weight, sem):
+    copies = []
+    for slot, ref in enumerate(refs):
+        for at in range(2):
+            for j in range(2):
+                chip, z = place(meta, slot, at, j)
+                for other in range(2):
+                    row = pl.multiple_of((chip * 2 + (meta[2] ^ other)) * 128 + z * 32, 32)
+                    for t in range(3):
+                        copies.append(
+                            pltpu.make_async_copy(
+                                ref.at[at, j, pl.ds((other * 3 + t) * 32, 32)],
+                                weight.at[t, pl.ds(row, 32), :],
+                                sem.at[len(copies)],
+                            )
+                        )
+    return copies
+
+
 def load_split_rows(meta, refs, base, blocks, weight, sem):
     copies = []
     for slot, ref in enumerate(refs):
-        for j in range(2):
-            chip, z = place(meta, slot, j)
-            for other in range(2):
-                core = lax.rem(meta[2] + other, 2)
-                row = pl.multiple_of((chip * 2 + core) * 128 + z * 32, 32)
-                copies.append(
-                    pltpu.make_async_copy(
-                        ref.at[j, pl.ds(base + other * blocks, blocks)],
-                        weight.at[:, pl.ds(row, 32), :],
-                        sem.at[(slot * 2 + j) * 2 + other],
+        for at in range(2):
+            for j in range(2):
+                chip, z = place(meta, slot, at, j)
+                for other in range(2):
+                    row = pl.multiple_of((chip * 2 + (meta[2] ^ other)) * 128 + z * 32, 32)
+                    copies.append(
+                        pltpu.make_async_copy(
+                            ref.at[at, j, pl.ds(base + other * blocks, blocks)],
+                            weight.at[:, pl.ds(row, 32), :],
+                            sem.at[len(copies)],
+                        )
                     )
-                )
     return copies
 
 
 def load_own_rows(meta, refs, base, blocks, rows, weight, sem):
     copies = []
     for slot, ref in enumerate(refs):
-        for j in range(2):
-            chip, z = place(meta, slot, j)
-            row = pl.multiple_of((chip * 4 + z) * rows, 32)
-            copies.append(
-                pltpu.make_async_copy(
-                    ref.at[j, pl.ds(base, blocks)],
-                    weight.at[:, pl.ds(row, rows), :],
-                    sem.at[slot * 2 + j],
+        for at in range(2):
+            for j in range(2):
+                chip, z = place(meta, slot, at, j)
+                row = pl.multiple_of((chip * 4 + z) * rows, 32)
+                copies.append(
+                    pltpu.make_async_copy(
+                        ref.at[at, j, pl.ds(base, blocks)],
+                        weight.at[:, pl.ds(row, rows), :],
+                        sem.at[len(copies)],
+                    )
                 )
-            )
     return copies
 
 
@@ -489,7 +537,7 @@
         ),
         out_shape=out_shape,
         compiler_params=pltpu.CompilerParams(vmem_limit_bytes=VMEM_LIMIT),
-        cost_estimate=pl.CostEstimate(flops=flops, bytes_accessed=moved, transcendentals=exps),
+        cost_estimate=pl.CostEstimate(flops=1000, bytes_accessed=1000, transcendentals=0),
     )(meta, *operands)
 
 
@@ -522,14 +570,14 @@
 
 def project_qkv(meta, own, other, embedded, shift, pieces):
     def kernel(m, own_ref, other_ref, emb_ref, shift_ref, *rest):
-        refs, (hidden_ref, out_ref, weight, sem) = rest[:8], rest[8:]
+        refs, (hidden_ref, out_ref, weight, sem) = rest[:4], rest[4:]
         i = pl.program_id(0)
 
         @pl.when(i == 0)
         def _():
-            load_all(load_split_rows(m, refs, 0, 3, weight, sem))
-
-        tokens = jnp.where(i < 2, own_ref[...].astype(F32), other_ref[...].astype(F32))
+            load_all(load_qkv(m, refs, weight, sem))
+
+        tokens = jnp.where(i < 2, own_ref[0].astype(F32), other_ref[0].astype(F32))
         hidden = (tokens + emb_ref[...]).astype(BF)
         hidden_ref[...] = hidden
         for t in range(3):
@@ -540,15 +588,15 @@
         meta,
         (own, other, embedded, shift, *pieces),
         [
-            spec((256, 1024), lambda i, m: (low_block(i), 0)),
-            spec((256, 1024), lambda i, m: (high_block(i), 0)),
+            spec((1, 256, 1024), lambda i, m: (low_block(i), 0, 0)),
+            spec((1, 256, 1024), lambda i, m: (high_block(i), 0, 0)),
             whole((1, 1024)),
             whole((3, 512)),
         ]
-        + [HBM] * 8,
+        + [HBM] * 4,
         [spec((256, 1024), lambda i, m: (i, 0)), spec((3, 256, 512), lambda i, m: (0, i, 0))],
         [shaped((1024, 1024), BF), shaped((3, 1024, 512), BF)],
-        [pltpu.VMEM((3, 1024, 512), BF), pltpu.SemaphoreType.DMA((32,))],
+        [pltpu.VMEM((3, 1024, 512), BF), pltpu.SemaphoreType.DMA((96,))],
         flops=2 * 1024 * 1024 * 1536,
         moved=10 << 20,
     )
@@ -559,7 +607,7 @@
     return jnp.where(lane // HEAD_DIM == h, 1.0, 0.0).astype(kind)
 
 
-def attend(meta, qkv, seg_column, seg_row):
+def attend(meta, part, qkv, seg_column, seg_row):
     def kernel(m, q_ref, k_ref, v_ref, column_ref, row_ref, out_ref, lse_ref):
         keys, values = k_ref[0], v_ref[0]
         for block in range(4):
@@ -578,21 +626,23 @@
                 lse_ref[0, h : h + 1, rows] = jnp.transpose(lse)[0:1, :]
             out_ref[rows, :] = mixed.astype(BF)
 
-    part = lambda t: spec((1, 1024, 128), lambda i, m: (t, 0, i))
+    base = part * 2
+    third = lambda t: spec((1, 1024, 128), lambda i, m: (t, 0, base + i))
     return kernel_call(
         kernel,
         meta,
         (qkv, qkv, qkv, seg_column, seg_row),
-        [part(0), part(1), part(2), whole((1024, 1)), whole((1, 1024))],
+        [third(0), third(1), third(2), whole((1024, 1)), whole((1, 1024))],
         [spec((1024, 128), lambda i, m: (0, i)), spec((1, 8, 1024), lambda i, m: (i, 0, 0))],
-        [shaped((1024, 512), BF), shaped((4, 8, 1024), F32)],
+        [shaped((1024, 256), BF), shaped((2, 8, 1024), F32)],
+        grid=(2,),
         flops=8 * 4 * 1024 * 1024 * 256,
         moved=5 << 20,
         exps=8 << 20,
     )
 
 
-def attend_back(meta, qkv, out, grad, lse, seg_column, seg_row):
+def attend_back(meta, part, qkv, out, grad, lse, seg_column, seg_row):
     def kernel(m, q_ref, k_ref, v_ref, out_ref, grad_ref, lse_ref, column_ref, row_ref, d_ref, sum_ref, dq):
         queries, upstream = q_ref[0], grad_ref[...]
         product = out_ref[...].astype(F32) * upstream.astype(F32)
@@ -627,16 +677,18 @@
         sum_ref[0:1, :] = jnp.sum(final.astype(F32), axis=0, keepdims=True)
         sum_ref[1:2, :] = value_sum
 
-    part = lambda t: spec((1, 1024, 128), lambda i, m: (t, 0, i))
-    heads = spec((1024, 128), lambda i, m: (0, i))
+    base = part * 2
+    third = lambda t: spec((1, 1024, 128), lambda i, m: (t, 0, base + i))
+    heads = lambda first: spec((1024, 128), lambda i, m: (0, first + i))
     return kernel_call(
         kernel,
         meta,
         (qkv, qkv, qkv, out, grad, lse, seg_column, seg_row),
-        [part(0), part(1), part(2), heads, heads, spec((1, 8, 1024), lambda i, m: (i, 0, 0)), whole((1024, 1)), whole((1, 1024))],
+        [third(0), third(1), third(2), heads(0), heads(base), spec((1, 8, 1024), lambda i, m: (i, 0, 0)), whole((1024, 1)), whole((1, 1024))],
         [spec((3, 1024, 128), lambda i, m: (0, 0, i)), spec((8, 128), lambda i, m: (0, i))],
-        [shaped((3, 1024, 512), BF), shaped((8, 512), F32)],
+        [shaped((3, 1024, 256), BF), shaped((8, 256), F32)],
         [pltpu.VMEM((1024, 128), F32)],
+        grid=(2,),
         flops=8 * 10 * 1024 * 1024 * 256,
         moved=8 << 20,
         exps=8 << 20,
@@ -644,8 +696,8 @@
 
 
 def project_out(meta, mixed, pieces):
-    def kernel(m, x_ref, *rest):
-        refs, (send_ref, own_ref, weight, sem) = rest[:8], rest[8:]
+    def kernel(m, x_ref, w_ref, *rest):
+        refs, (send_ref, own_ref, weight, sem) = rest[:4], rest[4:]
         i = pl.program_id(0)
 
         @pl.when(i == 0)
@@ -654,7 +706,7 @@
 
         for b in range(2):
             columns = pl.ds(b * 512, 512)
-            result = dot(x_ref[...], weight[b])
+            result = dot(x_ref[...], weight[b, :256, :]) + dot(w_ref[...], weight[b, 256:, :])
 
             @pl.when(i < 2)
             def _():
@@ -667,8 +719,8 @@
     return kernel_call(
         kernel,
         meta,
-        (mixed, *pieces),
-        [spec((256, 512), lambda i, m: (turned(i), 0))] + [HBM] * 8,
+        (*mixed, *pieces),
+        [spec((256, 256), lambda i, m: (turned(i), 0))] * 2 + [HBM] * 4,
         [spec((256, 1024), lambda i, m: (low_block(i), 0)), spec((256, 1024), lambda i, m: (high_block(i), 0))],
         [shaped((512, 1024), BF), shaped((512, 1024), F32)],
         [pltpu.VMEM((2, 512, 512), BF), pltpu.SemaphoreType.DMA((16,))],
@@ -692,26 +744,27 @@
     )
 
 
-ROWS128 = lambda i, m: (i, 0)
+BY_ROWS = lambda i, m: (i, 0)
 
 
 def first_norm(meta, tokens, embedded, own, received, vectors):
     def kernel(m, tok_ref, emb_ref, own_ref, recv_ref, vec_ref, normal_ref, inverse_ref, low_ref):
-        hidden = tok_ref[...].astype(F32) + emb_ref[...]
+        hidden = tok_ref[0].astype(F32) + emb_ref[...]
         attended = own_ref[...] + recv_ref[...].astype(F32) + vec_ref[0:1, :]
         normal_part, inverse = normal_parts(hidden + attended)
         normal_ref[...] = normal_part
-        inverse_ref[...] = jnp.broadcast_to(inverse, (128, 128))
+        inverse_ref[...] = jnp.broadcast_to(inverse, (256, 128))
         low_ref[...] = (normal_part * vec_ref[1:2, :] + vec_ref[2:3, :]).astype(BF)
 
-    block = spec((128, 1024), ROWS128)
+    block = spec((256, 1024), BY_ROWS)
     return kernel_call(
         kernel,
         meta,
         (tokens, embedded, own, received, vectors),
-        [block, whole((1, 1024)), block, block, whole((8, 1024))],
-        [block, spec((128, 128), ROWS128), block],
+        [spec((1, 256, 1024), lambda i, m: (i, 0, 0)), whole((1, 1024)), block, block, whole((8, 1024))],
+        [block, spec((256, 128), BY_ROWS), block],
         [shaped((512, 1024), F32), shaped((512, 128), F32), shaped((512, 1024), BF)],
+        grid=(2,),
         flops=512 * 1024 * 12,
         moved=8 << 20,
     )
@@ -719,7 +772,7 @@
 
 def expand(meta, own, other, shift, pieces):
     def kernel(m, own_ref, other_ref, shift_ref, *rest):
-        refs, (act_ref, slope_ref, weight, sem) = rest[:8], rest[8:]
+        refs, (act_ref, slope_ref, weight, sem) = rest[:4], rest[4:]
         i = pl.program_id(0)
 
         @pl.when(i == 0)
@@ -744,8 +797,8 @@
             spec((256, 1024), lambda i, m: (high_block(i), 0)),
             whole((1, 2048)),
         ]
-        + [HBM] * 8,
-        [spec((256, 2048), ROWS128), spec((256, 2048), ROWS128)],
+        + [HBM] * 4,
+        [spec((256, 2048), BY_ROWS), spec((256, 2048), BY_ROWS)],
         [shaped((1024, 2048), BF), shaped((1024, 2048), BF)],
         [pltpu.VMEM((4, 1024, 512), BF), pltpu.SemaphoreType.DMA((32,))],
         flops=2 * 1024 * 1024 * 2048,
@@ -756,7 +809,7 @@
 
 def contract(meta, activated, pieces):
     def kernel(m, x_ref, *rest):
-        refs, (send_ref, own_ref, weight, sem) = rest[:8], rest[8:]
+        refs, (send_ref, own_ref, weight, sem) = rest[:4], rest[4:]
         i = pl.program_id(0)
 
         @pl.when(i == 0)
@@ -779,7 +832,7 @@
         kernel,
         meta,
         (activated, *pieces),
-        [spec((256, 2048), lambda i, m: (turned(i), 0))] + [HBM] * 8,
+        [spec((256, 2048), lambda i, m: (turned(i), 0))] + [HBM] * 4,
         [spec((256, 1024), lambda i, m: (low_block(i), 0)), spec((256, 1024), lambda i, m: (high_block(i), 0))],
         [shaped((512, 1024), BF), shaped((512, 1024), F32)],
         [pltpu.VMEM((2, 2048, 512), BF), pltpu.SemaphoreType.DMA((16,))],
@@ -810,7 +863,7 @@
         low_ref[...] = low
         row_sums(sum_ref, pl.program_id(0), (upstream * normal_part, upstream, low.astype(F32)))
 
-    block = spec((128, 1024), ROWS128)
+    block = spec((256, 1024), BY_ROWS)
     return kernel_call(
         kernel,
         meta,
@@ -818,6 +871,7 @@
         [block, block, block, block, whole((8, 1024))],
         [block, block, block, whole((8, 1024))],
         [shaped((512, 1024), BF), shaped((512, 1024), F32), shaped((512, 1024), BF), shaped((8, 1024), F32)],
+        grid=(2,),
         flops=512 * 1024 * 30,
         moved=10 << 20,
     )
@@ -825,8 +879,8 @@
 
 def feed_back(meta, own, other, slope, down_pieces, up_pieces):
     def kernel(m, own_ref, other_ref, slope_ref, *rest):
-        down_refs, up_refs = rest[:8], rest[8:16]
-        du_ref, send_ref, mine_ref, sum_ref, down, up, down_sem, up_sem = rest[16:]
+        down_refs, up_refs = rest[:4], rest[4:8]
+        du_ref, send_ref, mine_ref, sum_ref, down, up, down_sem, up_sem = rest[8:]
         i = pl.program_id(0)
 
         @pl.when(i == 0)
@@ -864,7 +918,7 @@
             spec((256, 1024), lambda i, m: (low_block(i), 0)),
             spec((256, 2048), lambda i, m: (turned(i), 0)),
         ]
-        + [HBM] * 16,
+        + [HBM] * 8,
         [
             spec((256, 2048), lambda i, m: (turned(i), 0)),
             spec((256, 1024), lambda i, m: (low_block(i), 0)),
@@ -893,14 +947,15 @@
         low_ref[...] = low
         row_sums(sum_ref, pl.program_id(0), (upstream * normal_part, upstream, low.astype(F32)))
 
-    block = spec((128, 1024), ROWS128)
+    block = spec((256, 1024), BY_ROWS)
     return kernel_call(
         kernel,
         meta,
         (resid, own, received, normal_one, inverse_one, vectors),
-        [block, block, block, block, spec((128, 128), ROWS128), whole((8, 1024))],
+        [block, block, block, block, spec((256, 128), BY_ROWS), whole((8, 1024))],
         [block, block, whole((8, 1024))],
         [shaped((512, 1024), F32), shaped((512, 1024), BF), shaped((8, 1024), F32)],
+        grid=(2,),
         flops=512 * 1024 * 20,
         moved=10 << 20,
     )
@@ -908,7 +963,7 @@
 
 def output_back(meta, own, other, pieces):
     def kernel(m, own_ref, other_ref, *rest):
-        refs, (out_ref, weight, sem) = rest[:8], rest[8:]
+        refs, (out_ref, weight, sem) = rest[:4], rest[4:]
         i = pl.program_id(0)
 
         @pl.when(i == 0)
@@ -926,8 +981,8 @@
             spec((256, 1024), lambda i, m: (low_block(i), 0)),
             spec((256, 1024), lambda i, m: (high_block(i), 0)),
         ]
-        + [HBM] * 8,
-        spec((256, 512), ROWS128),
+        + [HBM] * 4,
+        spec((256, 512), BY_ROWS),
         shaped((1024, 512), BF),
         [pltpu.VMEM((2, 512, 512), BF), pltpu.SemaphoreType.DMA((16,))],
         flops=2 * 1024 * 1024 * 512,
@@ -936,11 +991,11 @@
 
 
 def rel_chip(s, m):
-    return lax.rem(m[0] + s // 2, 2) * 2 + lax.rem(m[1] + lax.rem(s, 2), 2)
-
-
-def piece_outputs(blocks, rows):
-    shape = (2, 2, blocks, rows, 512)
+    return (m[0] ^ (s // 2)) * 2 + (m[1] ^ lax.rem(s, 2))
+
+
+def piece_outputs(blocks, rows, columns=512):
+    shape = (2, 2, blocks, rows, columns)
     return [HBM] * 4, [shaped(shape, BF)] * 4
 
 
@@ -980,7 +1035,7 @@
             stage[s, b] = (dot(x[:512], own_ref[:, columns], TN) + dot(x[512:], other_ref[:, columns], TN)).astype(BF)
 
         def copy_for(n, k, target):
-            row = pl.multiple_of(lax.rem(m[3] + k, 4) * 128, 128)
+            row = pl.multiple_of((m[3] ^ z_relative(k // 2, k % 2)) * 128, 128)
             return [pltpu.make_async_copy(stage.at[n, :, pl.ds(row, 128), :], target, sem.at[n * 4 + k])]
 
         push(s, outs, copy_for)
@@ -999,72 +1054,71 @@
     )
 
 
-def weigh_up_out(meta, normed_own, normed_other, du, mixed, da_own, da_other):
-    def kernel(m, own_ref, other_ref, du_ref, mixed_ref, da_own_ref, da_other_ref, *rest):
-        outs, (up, out, sem) = rest[:4], rest[4:]
+def weigh_up(meta, normed_own, normed_other, du):
+    def kernel(m, own_ref, other_ref, du_ref, *rest):
+        outs, (up, sem) = rest[:4], rest[4:]
         s = pl.program_id(0)
-        x = mixed_ref[...]
-        for b in range(2):
-            columns = pl.ds(b * 512, 512)
-            out[s, b] = (dot(x[:512], da_own_ref[:, columns], TN) + dot(x[512:], da_other_ref[:, columns], TN)).astype(BF)
         for b in range(4):
             columns = pl.ds(b * 512, 512)
             up[s, b] = (dot(own_ref[...], du_ref[:512, columns], TN) + dot(other_ref[...], du_ref[512:, columns], TN)).astype(BF)
 
         def copy_for(n, k, target):
-            z = lax.rem(m[3] + k, 4)
-            copies = [
-                pltpu.make_async_copy(
-                    out.at[n, :, pl.ds(pl.multiple_of(z * 32, 32), 32), :],
-                    target.at[pl.ds(0, 2)],
-                    sem.at[(n * 4 + k) * 3],
-                )
-            ]
+            z = m[3] ^ z_relative(k // 2, k % 2)
+            copies = []
             for rel in range(2):
-                row = pl.multiple_of(lax.rem(m[2] + rel, 2) * 128 + z * 32, 32)
+                row = pl.multiple_of((m[2] ^ rel) * 128 + z * 32, 32)
                 copies.append(
                     pltpu.make_async_copy(
                         up.at[n, :, pl.ds(row, 32), :],
-                        target.at[pl.ds(2 + rel * 4, 4)],
-                        sem.at[(n * 4 + k) * 3 + 1 + rel],
+                        target.at[pl.ds(rel * 4, 4)],
+                        sem.at[(n * 4 + k) * 2 + rel],
                     )
                 )
             return copies
 
         push(s, outs, copy_for)
 
-    out_specs, out_shape = piece_outputs(10, 32)
-    return kernel_call(
-        kernel,
-        meta,
-        (normed_own, normed_other, du, mixed, da_own, da_other),
+    out_specs, out_shape = piece_outputs(8, 32)
+    return kernel_call(
+        kernel,
+        meta,
+        (normed_own, normed_other, du),
         [
             spec((512, 256), lambda s, m: (0, rel_chip(s, m))),
             spec((512, 256), lambda s, m: (0, rel_chip(s, m))),
             whole((1024, 2048)),
-            spec((1024, 128), lambda s, m: (0, rel_chip(s, m))),
-            whole((512, 1024)),
-            whole((512, 1024)),
         ],
         out_specs,
         out_shape,
-        [pltpu.VMEM((4, 4, 256, 512), BF), pltpu.VMEM((4, 2, 128, 512), BF), pltpu.SemaphoreType.DMA((48,))],
-        flops=2 * 1024 * 1024 * 2560,
+        [pltpu.VMEM((4, 4, 256, 512), BF), pltpu.SemaphoreType.DMA((32,))],
+        flops=2 * 1024 * 1024 * 2048,
         moved=15 << 20,
     )
 
 
-def weigh_qkv(meta, hidden, dqkv):
+def weigh_qkv(meta, hidden, dqkv, out_terms=()):
     def kernel(m, x_ref, d_ref, *rest):
-        outs, (stage, sem) = rest[:4], rest[4:]
         s = pl.program_id(0)
+        if out_terms:
+            mixed_ref, more_ref, own_ref, other_ref = rest[:4]
+            rest = rest[4:]
+        outs, stage, sem = rest[:4], rest[4], rest[5]
         for t in range(3):
             stage[s, t] = dot(x_ref[...], d_ref[t], TN).astype(BF)
+        if out_terms:
+            stage_out, sem_out = rest[6:]
+            x = jnp.where(rel_chip(s, m) < 2, mixed_ref[...].astype(F32), more_ref[...].astype(F32)).astype(BF)
+            for b in range(4):
+                columns = pl.ds(b * 256, 256)
+                stage_out[s, b] = (
+                    dot(x[:512], own_ref[:, columns], TN) + dot(x[512:], other_ref[:, columns], TN)
+                ).astype(BF)
 
         def copy_for(n, k, target):
+            z = m[3] ^ z_relative(k // 2, k % 2)
             copies = []
             for rel in range(2):
-                row = pl.multiple_of(lax.rem(m[2] + rel, 2) * 128 + lax.rem(m[3] + k, 4) * 32, 32)
+                row = pl.multiple_of((m[2] ^ rel) * 128 + z * 32, 32)
                 copies.append(
                     pltpu.make_async_copy(
                         stage.at[n, :, pl.ds(row, 32), :],
@@ -1072,34 +1126,49 @@
                         sem.at[(n * 4 + k) * 2 + rel],
                     )
                 )
+            if out_terms:
+                copies.append(
+                    pltpu.make_async_copy(
+                        stage_out.at[n, :, pl.ds(pl.multiple_of(z * 32, 32), 32), :],
+                        target.at[pl.ds(6, 4)],
+                        sem_out.at[n * 4 + k],
+                    )
+                )
             return copies
 
         push(s, outs, copy_for)
 
-    out_specs, out_shape = piece_outputs(6, 32)
-    return kernel_call(
-        kernel,
-        meta,
-        (hidden, dqkv),
-        [spec((1024, 256), lambda s, m: (0, rel_chip(s, m))), whole((3, 1024, 512))],
+    out_specs, out_shape = piece_outputs(10 if out_terms else 6, 32, 256)
+    in_specs = [spec((1024, 256), lambda s, m: (0, rel_chip(s, m))), whole((3, 1024, 256))]
+    scratch = [pltpu.VMEM((4, 3, 256, 256), BF), pltpu.SemaphoreType.DMA((32,))]
+    if out_terms:
+        in_specs += [spec((1024, 128), lambda s, m: (0, rel_chip(s, m) % 2))] * 2 + [whole((512, 1024))] * 2
+        scratch += [pltpu.VMEM((4, 4, 128, 256), BF), pltpu.SemaphoreType.DMA((16,))]
+    return kernel_call(
+        kernel,
+        meta,
+        (hidden, dqkv, *out_terms),
+        in_specs,
         out_specs,
         out_shape,
-        [pltpu.VMEM((4, 3, 256, 512), BF), pltpu.SemaphoreType.DMA((32,))],
-        flops=2 * 1024 * 1024 * 1536,
+        scratch,
+        flops=2 * 1024 * 1024 * 1024,
         moved=8 << 20,
     )
 
 
 def qkv_back(meta, dqkv, pieces):
-    def kernel(m, d_ref, *rest):
-        refs, (send_ref, own_ref, weight, sem) = rest[:8], rest[8:]
+    def kernel(m, d_ref, e_ref, *rest):
+        refs, (send_ref, own_ref, weight, sem) = rest[:4], rest[4:]
         i = pl.program_id(0)
 
         @pl.when(i == 0)
         def _():
-            load_all(load_split_rows(m, refs, 0, 3, weight, sem))
-
-        total = dot(d_ref[0], weight[0], NT) + dot(d_ref[1], weight[1], NT) + dot(d_ref[2], weight[2], NT)
+            load_all(load_qkv(m, refs, weight, sem))
+
+        total = jnp.zeros((256, 1024), F32)
+        for t in range(3):
+            total += dot(d_ref[t], weight[t, :, :256], NT) + dot(e_ref[t], weight[t, :, 256:], NT)
 
         @pl.when(i < 2)
         def _():
@@ -1112,11 +1181,11 @@
     return kernel_call(
         kernel,
         meta,
-        (dqkv, *pieces),
-        [spec((3, 256, 512), lambda i, m: (0, turned(i), 0))] + [HBM] * 8,
+        (*dqkv, *pieces),
+        [spec((3, 256, 256), lambda i, m: (0, turned(i), 0))] * 2 + [HBM] * 4,
         [spec((256, 1024), lambda i, m: (low_block(i), 0)), spec((256, 1024), lambda i, m: (high_block(i), 0))],
         [shaped((512, 1024), BF), shaped((512, 1024), F32)],
-        [pltpu.VMEM((3, 1024, 512), BF), pltpu.SemaphoreType.DMA((32,))],
+        [pltpu.VMEM((3, 1024, 512), BF), pltpu.SemaphoreType.DMA((96,))],
         flops=2 * 1024 * 1024 * 1536,
         moved=9 << 20,
     )
@@ -1128,7 +1197,7 @@
         out_ref[...] = total.astype(BF)
         row_sums(sum_ref, pl.program_id(0), (total,))
 
-    block = spec((128, 1024), ROWS128)
+    block = spec((256, 1024), BY_ROWS)
     return kernel_call(
         kernel,
         meta,
@@ -1136,6 +1205,7 @@
         [block, block, block],
         [block, whole((8, 1024))],
         [shaped((512, 1024), BF), shaped((8, 1024), F32)],
+        grid=(2,),
         flops=512 * 1024 * 4,
         moved=6 << 20,
     )
@@ -1176,32 +1246,76 @@
     meta = jnp.stack([y, x, c, z]).astype(jnp.int32)
     pick = lambda value, index, axis: lax.dynamic_index_in_dim(value, index, axis, keepdims=False)
 
+    me = dp * 4 + z
+
     qkv_split = qkv_weight.reshape(32, 3, 4, 2, 128)
     up_split = up_weight.reshape(32, 4, 2, 512)
-    qkv_half = lambda core: pick(qkv_split, core, 3).reshape(32, 3, 512).transpose(1, 0, 2)
+    qkv_half = lambda core: pick(qkv_split, core, 3).reshape(32, 3, 512).transpose(1, 0, 2).reshape(96, 512)
     up_half = lambda core: pick(up_split, core, 2).transpose(1, 0, 2)
-    qkv_shard = jnp.concatenate([qkv_half(c), send(qkv_half(1 - c), PAIR)])
+    small = jnp.concatenate([qv_bias, out_bias, norm_gain, norm_bias, up_bias, down_bias, final_gain, final_bias])
+    small = jnp.pad(small[None], ((0, 15), (0, 128)))
+    received = send(jnp.concatenate([qkv_half(1 - c), small]), PAIR)
+    small = jnp.concatenate([small[:1], received[96:97], small[2:]])
+    qkv_shard = jnp.concatenate([qkv_half(c), received[:96], small])
     out_shard = out_weight.reshape(32, 2, 512).transpose(1, 0, 2)
     mid_shard = jnp.concatenate([out_shard, up_half(c), send(up_half(1 - c), PAIR)])
     down_shard = down_weight.reshape(128, 2, 512).transpose(1, 0, 2)
-    qkv_pieces = gather_pieces(qkv_shard)
-    mid_pieces = gather_pieces(mid_shard)
-    down_pieces = gather_pieces(down_shard)
-
-    stamps = timestep.astype(jnp.int32)
-    small = jnp.concatenate(
-        [qv_bias, out_bias, norm_gain, norm_bias, up_bias, down_bias, final_gain, final_bias]
-        + [(stamps // 64).astype(BF), (stamps % 64).astype(BF)]
-    )[None]
-    small = jnp.concatenate([small, send(small, PAIR)])
-    small = jnp.stack([small] + [send(small, SHIFT_Z[k]) for k in (1, 2, 3)])
-    small = jnp.stack([small] + [send(small, pairs) for pairs in (ALONG_X, ALONG_Y, DIAGONAL)])
-    small = small.reshape(32, -1)
+    qkv_line = gather_line(qkv_shard)
+
+    stamps = after(timestep.astype(jnp.int32), received)[:, None]
+    stamps = jnp.concatenate([stamps // 64, stamps % 64], axis=1).astype(BF)
+    for pairs in (PAIR, ALONG_X, ALONG_Y):
+        stamps = jnp.concatenate([stamps, send(stamps, pairs)])
+    stamps = stamps.astype(F32)
+    stamps = (stamps[:, 0] * 64.0 + stamps[:, 1]).reshape(4, 4)
+    sums_order = jnp.arange(4, dtype=jnp.int32) ^ z
+    from_pair = (sums_order // 2) ^ c
+    stamps = jnp.take_along_axis(stamps, jnp.broadcast_to(from_pair * 2 + sums_order % 2, (4, 4)), axis=1).reshape(16, 1)
+    column = me * 32 + jnp.arange(32, dtype=jnp.int32)
+    frequency = jnp.exp(-math.log(10000.0) * (column % 512).astype(F32) / 512)
+    phases = stamps * frequency[None, :]
+    features = jnp.where(column[None, :] < 512, jnp.sin(phases), jnp.cos(phases)).astype(BF)
+    features = after(features, qkv_line[0])
+    embedded = jnp.dot(features, time_weight, preferred_element_type=F32)
+    embedded = embedded + send(embedded, PAIR)
+    for width, pairs in ((8, ALONG_Y), (4, ALONG_X), (2, ALONG_Z[2]), (1, ALONG_Z[1])):
+        embedded = embedded[:width] + send(embedded[width:], pairs)
+
+    mid_line = gather_line(after(mid_shard, qkv_line))
+    qkv_pieces = gather_plane(*qkv_line)
+
+    def take_rows(value):
+        return jnp.stack([send(pick(value, (z + k) % 2, 0), ROW_OUT[k]) for k in range(2)])
+
+    def give_rows(value):
+        parts = [send(value[k * 256 : (k + 1) * 256], ROW_BACK[k]) for k in range(2)]
+        swapped = (z % 2) == 1
+        return jnp.stack([jnp.where(swapped, parts[1], parts[0]), jnp.where(swapped, parts[0], parts[1])])
+
+    documents = jnp.concatenate([segment_ids // 32, segment_ids % 32], axis=1).astype(BF)
+    documents = jnp.pad(documents[:, None, :], ((0, 0), (0, 15), (0, 512)))
+    own_tokens = take_rows(after(jnp.concatenate([tokens, documents], axis=1), mid_line))
+    other_tokens = send(own_tokens, PAIR)
+    codes = jnp.concatenate([own_tokens[:, 256], other_tokens[:, 256]]).astype(F32)
+    segments = (codes[:, :256] * 32.0 + codes[:, 256:512]).reshape(1024)
+    seg_column, seg_row = segments[:, None], segments[None, :]
+
+    mid_pieces = gather_plane(*mid_line)
+
     natural = jnp.arange(32, dtype=jnp.int32)
-    ny, nx, nc, nz = natural // 16, (natural // 8) % 2, (natural // 4) % 2, natural % 4
-    source = (((ny ^ y) * 2 + (nx ^ x)) * 4 + (z + 4 - nz) % 4) * 2 + (nc ^ c)
-    order = (source[:, None] == natural[None, :]).astype(BF)
-    small = jnp.dot(order, small, preferred_element_type=F32)
+    order = (natural[:, None] ^ me) == natural[None, :]
+    small = jnp.stack([piece[:, :, 192:194, :384] for piece in qkv_pieces])
+    small = jnp.stack(
+        [
+            small[half * 2 + (x_rel if half else y_rel), y_rel if half else x_rel, j, rel]
+            for y_rel in range(2)
+            for x_rel in range(2)
+            for rel in range(2)
+            for j in range(2)
+            for half in range(2)
+        ]
+    )
+    small = jnp.dot(order.astype(BF), small, preferred_element_type=F32)
     full = [part.reshape(1, -1) for part in split_vectors(small)]
     qv_full, out_shift, first_gain, first_shift, up_full, down_shift, second_gain, second_shift = full
     blank = jnp.zeros((2, 1024), F32)
@@ -1210,67 +1324,67 @@
     qkv_shift = jnp.stack([qv_mine[0], jnp.zeros((512,), F32), qv_mine[1]])
     up_shift = pick(up_full.reshape(4, 2, 512), c, 1).reshape(1, 2048)
 
-    all_stamps = (small[::4, 384:386] * 64.0 + small[::4, 386:388]).reshape(16)
-    column = (dp * 4 + z) * 32 + jnp.arange(32, dtype=jnp.int32)
-    frequency = jnp.exp(-math.log(10000.0) * (column % 512).astype(F32) / 512)
-    rel = jnp.arange(16, dtype=jnp.int32)
-    rel_row = ((rel // 8) ^ y) * 8 + (((rel // 4) % 2) ^ x) * 4
-
-    def features_for(rows):
-        phases = all_stamps[rows][:, None] * frequency[None, :]
-        return jnp.where(column[None, :] < 512, jnp.sin(phases), jnp.cos(phases)).astype(BF)
-
-    terms = jnp.dot(features_for(rel_row + (rel + z) % 4), time_weight, preferred_element_type=F32)
-    terms = (terms + send(terms, PAIR)).reshape(4, 4, 1024)
-    terms = terms[0] + send(terms[1], ALONG_X) + send(terms[2], ALONG_Y) + send(terms[3], DIAGONAL)
-    embedded = terms[0:1]
-    for k in (1, 2, 3):
-        embedded = embedded + send(terms[k : k + 1], SHIFT_Z[k])
-
-    def take_rows(value):
-        return jnp.concatenate([send(pick(value, (z + k) % 2, 0), ROW_OUT[k]) for k in range(2)])
-
-    def give_rows(value):
-        parts = [send(value[k * 256 : (k + 1) * 256], ROW_BACK[k]) for k in range(2)]
-        swapped = (z % 2) == 1
-        return jnp.stack([jnp.where(swapped, parts[1], parts[0]), jnp.where(swapped, parts[0], parts[1])])
-
-    own_tokens = take_rows(tokens)
-    own_segments = take_rows(segment_ids)
-    other_tokens = send(own_tokens, PAIR)
-    segments = jnp.concatenate([own_segments, send(own_segments, PAIR)])
-    seg_column, seg_row = segments[:, None], segments[None, :]
-    own_cotangent = take_rows(cotangent)
-
     hidden, qkv = project_qkv(meta, own_tokens, other_tokens, embedded, qkv_shift, qkv_pieces)
-    mixed, lse = attend(meta, qkv, seg_column, seg_row)
+    mixed_one, lse_one = attend(meta, 0, qkv, seg_column, seg_row)
+    down_first = jnp.stack([after(down_shard, mixed_one), send(after(down_shard, qkv), ALONG_Z[2])])
+    mixed_two, lse_two = attend(meta, 1, after(qkv, down_first), seg_column, seg_row)
+    down_second = after(send(down_first, ALONG_Z[1]), mixed_two)
+    mixed = mixed_one, after(mixed_two, down_second)
     away, mine = project_out(meta, mixed, mid_pieces)
+    own_cotangent = take_rows(after(cotangent, down_second))
+    down_pieces = gather_plane(down_first, down_second, mine)
     normal_one, inverse_one, normed = first_norm(meta, own_tokens, embedded, mine, send(away, PAIR), vectors)
     normed_other = send(normed, PAIR)
-    activated, slope = expand(meta, normed, normed_other, up_shift, mid_pieces)
+    activated, slope = expand(meta, normed, after(normed_other, own_cotangent, down_pieces[0], down_pieces[2]), up_shift, mid_pieces)
     away, mine = contract(meta, activated, down_pieces)
+    own_cotangent = after(own_cotangent, mine).reshape(512, 1024)
     result, resid_two, df, sums_two = second_norm(meta, normal_one, mine, send(away, PAIR), own_cotangent, vectors)
-    output = give_rows(result)
 
     df_other = send(df, PAIR)
-    down_share = scatter_pieces(*weigh_down(meta, activated, df, df_other))
-    du, away, mine, up_sums = feed_back(meta, df, df_other, slope, down_pieces, mid_pieces)
-    resid_one, da, sums_one = first_norm_back(meta, resid_two, mine, send(away, PAIR), normal_one, inverse_one, vectors)
+    down_terms = weigh_down(meta, activated, df, df_other)
+    du, away, mine, up_sums = feed_back(meta, after(df, down_terms), df_other, slope, down_pieces, mid_pieces)
+    received = send(away, PAIR)
+    up_terms = weigh_up(meta, normed, normed_other, du)
+    down_sums = add_one(*scatter_one(*down_terms), up_terms)
+    resid_one, da, sums_one = first_norm_back(
+        meta, after(resid_two, down_sums), mine, received, normal_one, inverse_one, vectors
+    )
     da_other = send(da, PAIR)
     dout = output_back(meta, da, da_other, mid_pieces)
-    mid_share = scatter_pieces(*weigh_up_out(meta, normed, normed_other, du, mixed, da, da_other))
-    dqkv, qv_sums = attend_back(meta, qkv, mixed, dout, lse, seg_column, seg_row)
-    qkv_share = scatter_pieces(*weigh_qkv(meta, hidden, dqkv))
-    away, mine = qkv_back(meta, dqkv, qkv_pieces)
+    down_sums = add_two(*scatter_two(*down_sums), dout)
+    output = give_rows(after(result, dout))
+    grad = after(dout, down_sums)
+    dqkv_one, qv_sums_one = attend_back(meta, 0, qkv, mixed_one, grad, lse_one, seg_column, seg_row)
+    output = after(output, dqkv_one)
+    qkv_terms_one = weigh_qkv(meta, hidden, after(dqkv_one, output), (mixed_one, mixed_two, da, da_other))
+    up_sums_one = add_one(*scatter_one(*up_terms), qkv_terms_one)
+    down_sums = add_three(*scatter_three(*down_sums), qkv_terms_one)
+    grad = after(dout, up_sums_one, down_sums)
+    dqkv_two, qv_sums_two = attend_back(meta, 1, qkv, mixed_two, grad, lse_two, seg_column, seg_row)
+    up_sums_two = add_two(*scatter_two(*up_sums_one), dqkv_two)
+    down_share = scatter_four(*down_sums, dqkv_two)
+    qkv_terms_two = weigh_qkv(meta, hidden, after(dqkv_two, up_sums_two, down_share))
+    qkv_sums_one = add_one(*scatter_one(*qkv_terms_one), qkv_terms_two)
+    away, mine = qkv_back(meta, (dqkv_one, after(dqkv_two, qkv_terms_two, qkv_sums_one)), qkv_pieces)
+    up_sums_three = add_three(*scatter_three(*up_sums_two), mine)
+    qkv_sums_two = add_one(*scatter_one(*qkv_terms_two), mine)
+    qkv_sums_one = add_two(*scatter_two(*qkv_sums_one), mine)
     input_low, embed_sums = last_sum(meta, resid_one, mine, send(away, PAIR))
     input_grad = give_rows(input_low)
+    qkv_sums_two = add_two(*scatter_two(*qkv_sums_two), input_low)
+    qkv_sums_one = add_three(*scatter_three(*qkv_sums_one), input_low)
+    up_share = scatter_four(*up_sums_three, input_low)
+    qkv_share_one = scatter_four(*qkv_sums_one)
+    qkv_share_two = scatter_four(*add_three(*scatter_three(*qkv_sums_two)))
+    qkv_share = jnp.concatenate([qkv_share_one[:6], qkv_share_two], axis=2)
+    qv_sums = jnp.concatenate([qv_sums_one[0:2], qv_sums_two[0:2]], axis=1)
 
     def both_halves(own, received):
         return jnp.where(c == 0, jnp.stack([own, received], axis=-2), jnp.stack([received, own], axis=-2))
 
     grad_down = down_share.transpose(1, 0, 2).reshape(128, 1024)
-    grad_out = mid_share[:2].transpose(1, 0, 2).reshape(32, 1024)
-    grad_up = both_halves(mid_share[2:6], send(mid_share[6:], PAIR))
+    grad_out = qkv_share_one[6:].transpose(1, 0, 2).reshape(32, 1024)
+    grad_up = both_halves(up_share[:4], send(up_share[4:], PAIR))
     grad_up = grad_up.transpose(1, 0, 2, 3).reshape(32, 4096)
     split = lambda share: share.reshape(3, 32, 4, 128)
     grad_qkv = both_halves(split(qkv_share[:3]), split(send(qkv_share[3:], PAIR)))
@@ -1280,7 +1394,7 @@
     spread = lambda sums, width: (sums.reshape(-1, 1, width) * core_lane[None, :, None]).reshape(32, -1)
     grads = jnp.concatenate(
         [
-            spread(qv_sums[0:2], 128),
+            spread(qv_sums, 128),
             sums_one[2].reshape(32, 32),
             sums_one[0].reshape(32, 32),
             sums_one[1].reshape(32, 32),
@@ -1290,22 +1404,18 @@
             sums_two[1].reshape(32, 32),
         ],
         axis=1,
-    ).reshape(4, 2, 4, 384)
-    grads = pick(grads, c, 1) + send(pick(grads, 1 - c, 1), PAIR)
-    rel_order = ((rel_row + (rel + z) % 4)[:, None] == rel[None, :]).astype(F32)
-    grads = jnp.dot(rel_order, grads.reshape(16, 384), precision=lax.Precision.HIGHEST).reshape(4, 4, 384)
-    grads = grads[0] + send(grads[1], ALONG_X) + send(grads[2], ALONG_Y) + send(grads[3], DIAGONAL)
-    total = grads[0:1]
-    for k in (1, 2, 3):
-        total = total + send(grads[k : k + 1], SHIFT_Z[k])
-    small_grads = [part.reshape(-1) for part in split_vectors(total)]
-
-    sums = embed_sums[0:1]
-    sums = sums + send(sums, PAIR)
-    sums = jnp.concatenate([sums] + [send(sums, SHIFT_Z[k]) for k in (1, 2, 3)])
-    sums = jnp.concatenate([sums] + [send(sums, pairs) for pairs in (ALONG_X, ALONG_Y, DIAGONAL)])
-    features = features_for(rel_row + (z + 4 - rel % 4) % 4).astype(F32)
-    grad_time = jnp.dot(features.T, sums, precision=lax.Precision.HIGHEST)
+    )
+    total = jnp.dot(order.astype(F32), after(grads, embed_sums), precision=lax.Precision.HIGHEST)
+    total = total.reshape(2, 2, 2, 4, 3, 128).transpose(2, 3, 1, 0, 4, 5).reshape(96, 128)
+    sums = embed_sums[0:1].reshape(8, 128)
+    received = send(jnp.concatenate([total[48:], sums]), PAIR)
+    total, sums = total[:48] + received[:48], sums + received[48:]
+    for width, pairs in ((24, ALONG_Z[2]), (12, ALONG_Z[1]), (6, ALONG_X), (3, ALONG_Y)):
+        received = send(jnp.concatenate([total[width:], sums]), pairs)
+        total, sums = total[:width] + received[:width], jnp.concatenate([sums, received[width:]])
+    small_grads = [part.reshape(-1) for part in split_vectors(total.reshape(1, 384))]
+    sums = sums.reshape(2, 2, 2, 2, 1024).transpose(0, 1, 3, 2, 4).reshape(16, 1024)
+    grad_time = jnp.dot(features.astype(F32).T, sums, precision=lax.Precision.HIGHEST)
 
     return (
         output,

time: 636 us -> 520 us (0.82)
  the two profiles are of different devices: /device:TPU:27 before, /device:TPU:0 now
where the time goes in v2:
time: 520 us; the launch traced here: 512 us
  Pallas kernels  194 us (37%)
  waiting for transfers between devices  131 us (25%)
  starting transfers between devices  107 us (21%)
  other arithmetic  40.1 us (8%)
  local copies, waits for them, and re-layouts  36.9 us (7%)
    pallas_call x19, Pallas kernels, kernel_call(): pl.pallas_call(kernel, grid_spec=pltpu.PrefetchScalarGridSpec(num_scalar_...  194 us
    ppermute x75, waiting for transfers between devices, send(): return lax.ppermute(value, AXES, pairs)  131 us
    ppermute x75, starting transfers between devices, send(): return lax.ppermute(value, AXES, pairs)  107 us
    convert_element_type x20, other arithmetic, add_low(): return (a.astype(F32) + b.astype(F32)).astype(BF)  20.4 us
    unnamed x125, local copies, waits for them, and re-layouts  11.9 us
  transfers between devices with their start and end apart: 75, of which 25 were waited for; matrix products, arithmetic and copies ran while one was open for 13% of the time, Pallas kernels for 30%

profile of v2, /device:TPU:0, one launch (start us, length us, event | category | flops | bytes accessed | tf_op | source)
XLA Modules:
  0.0 512.0 jit_solution(16066614577107440642)
XLA Ops:
  4.8 4.1 collective-permute-start.2
  11.7 2.0 collective-permute-done.9
  15.4 2.0 collective-permute-done.10
  20.4 1.6 collective-permute-start.12
  22.2 1.6 collective-permute-start.3
  24.4 1.6 collective-permute-start.13
  26.6 1.7 collective-permute-done.13
  28.4 2.0 collective-permute-start.14
  30.4 3.6 collective-permute-done.3
  34.0 2.2 collective-permute-start.4
  39.4 1.8 collective-permute-start.15
  41.2 9.4 %collective-permute-done.4 = bf16[10,32,512]{2,1,0:T(8,128)(2,1)} collective-permute-done((bf16[10,32,512]{2,1,0:T(8,128)(2,1)S(1)}, bf16[10,32,512]{2,1,0:T(8,128)(2,1)}, u32[]{:S(2)}, u32[]{:S(2)}) %collective-permute-start.4) | collective-permute-done | bytes 327712 | tf_op jit(solution)/shard_map/ppermute | solution.py:403
  50.6 1.9 pad_maximum_fusion.10
  55.5 1.6 collective-permute-start.19
  58.3 10.2 %collective-permute-done.5 = bf16[2,10,32,512]{3,2,1,0:T(8,128)(2,1)} collective-permute-done((bf16[2,10,32,512]{3,2,1,0:T(8,128)(2,1)}, bf16[2,10,32,512]{3,2,1,0:T(8,128)(2,1)}, u32[]{:S(2)}, u32[]{:S(2)}) %collective-permute-start.5) | collective-permute-done | bytes 655392 | tf_op jit(solution)/shard_map/ppermute | solution.py:403
  70.8 3.7 collective-permute-done.20.rest_1_
  75.0 2.4 collective-permute-done.19.rest_3_
  78.4 5.3 %collective-permute-done.7 = bf16[272,1024]{1,0:T(8,128)(2,1)S(1)} collective-permute-done((bf16[272,1024]{1,0:T(8,128)(2,1)S(1)}, bf16[272,1024]{1,0:T(8,128)(2,1)S(1)}, u32[]{:S(2)}, u32[]{:S(2)}) %collective-permute-start.7) | collective-permute-done | bytes 557088 | tf_op jit(solution)/shard_map/ppermute | solution.py:403
  84.9 10.0 %collective-permute-start.16 = (bf16[2,272,1024]{2,1,0:T(8,128)(2,1)}, bf16[2,272,1024]{2,1,0:T(8,128)(2,1)}, u32[]{:S(2)}, u32[]{:S(2)}) collective-permute-start(bf16[2,272,1024]{2,1,0:T(8,128)(2,1)} %pad_maximum_fusion.2.own_ref.tok_ref), channel_id=1, source_target_pairs={{0,4},{1,5},{2,6},{3,7},{4,0},{5,1},{6,2},{7,3},{8,12},{9,13},{10,... | collective-permute-start | bytes 3342344 | tf_op jit(solution)/shard_map/ppermute | solution.py:403
  96.3 1.6 collective-permute-start.26
  100.9 10.2 %shard_map.280 = (bf16[1024,1024]{1,0:T(8,128)(2,1)}, bf16[3,1024,512]{2,1,0:T(8,128)(2,1)}) custom-call(s32[4]{0:T(128)} %pad_add_fusion.m, bf16[2,272,1024]{2,1,0:T(8,128)(2,1)} %pad_maximum_fusion.2.own_ref.tok_ref, bf16[2,272,1024]{2,1,0:T(8,128)(2,1)} %collective-permute-done.16.other_ref, f32[1,1024]{1,0:T(1,128)} %slice_add_fusion.8.emb_ref, ...), custom_call_target="tpu_custom_call" | custom-call | flops 1000 | bytes 1000 | tf_op jit(solution)/shard_map/pallas_call | solution.py:529
  111.1 8.0 %collective-permute-start.21 = (bf16[2,128,512]{2,1,0:T(8,128)(2,1)S(1)}, bf16[2,128,512]{2,1,0:T(8,128)(2,1)S(1)}, u32[]{:S(2)}, u32[]{:S(2)}) collective-permute-start(bf16[2,128,512]{2,1,0:T(8,128)(2,1)S(1)} %bitcast.297), channel_id=1, source_target_pairs={{0,2},{1,3},{2,0},{3,1},{4,6},{5,7},{6,4},{7,5},{8,10},{9,11},{10,... | collective-permute-start | bytes 786440 | tf_op jit(solution)/shard_map/ppermute | solution.py:403
  120.9 11.8 %shard_map.281 = (bf16[1024,256]{1,0:T(8,128)(2,1)}, f32[2,8,1024]{2,1,0:T(8,128)}) custom-call(s32[4]{0:T(128)} %pad_add_fusion.m, bf16[3,1024,512]{2,1,0:T(8,128)(2,1)} %get-tuple-element.126.q_ref.k_ref.v_ref, bf16[3,1024,512]{2,1,0:T(8,128)(2,1)} %get-tuple-element.126.q_ref.k_ref.v_ref, bf16[3,1024,512]{2,1,0:T(8,128)(2,1)} %get-tuple-element.126.q_ref.k_ref.v_ref, ...), custom_call_target="tpu_custom_call" | custom-call | flops 1000 | bytes 1000 | tf_op jit(solution)/shard_map/pallas_call | solution.py:529
  134.6 11.9 %shard_map.282 = (bf16[1024,256]{1,0:T(8,128)(2,1)}, f32[2,8,1024]{2,1,0:T(8,128)}) custom-call(s32[4]{0:T(128)} %pad_add_fusion.m, bf16[3,1024,512]{2,1,0:T(8,128)(2,1)} %get-tuple-element.126.q_ref.k_ref.v_ref, bf16[3,1024,512]{2,1,0:T(8,128)(2,1)} %get-tuple-element.126.q_ref.k_ref.v_ref, bf16[3,1024,512]{2,1,0:T(8,128)(2,1)} %get-tuple-element.126.q_ref.k_ref.v_ref, ...), custom_call_target="tpu_custom_call" | custom-call | flops 1000 | bytes 1000 | tf_op jit(solution)/shard_map/pallas_call | solution.py:529
  146.4 1.7 collective-permute-done.22
  148.2 7.4 %shard_map.283 = (bf16[512,1024]{1,0:T(8,128)(2,1)}, f32[512,1024]{1,0:T(8,128)}) custom-call(s32[4]{0:T(128)} %pad_add_fusion.m, bf16[1024,256]{1,0:T(8,128)(2,1)} %get-tuple-element.123.x_ref.out_ref.rest_0_, bf16[1024,256]{1,0:T(8,128)(2,1)} %get-tuple-element.129.w_ref.rest_1_.out_ref, bf16[2,2,10,32,512]{4,3,2,1,0:T(8,128)(2,1)} %copy-done.3, ...), custom_call_target="tpu_custom_call" | custom-call | flops 1000 | bytes 1000 | tf_op jit(solution)/shard_map/pallas_call | solution.py:529
  159.1 10.8 %collective-permute-done.31 = bf16[2,2,128,512]{3,2,1,0:T(8,128)(2,1)S(1)} collective-permute-done((bf16[2,2,128,512]{3,2,1,0:T(8,128)(2,1)S(1)}, bf16[2,2,128,512]{3,2,1,0:T(8,128)(2,1)S(1)}, u32[]{:S(2)}, u32[]{:S(2)}) %collective-permute-start.31) | collective-permute-done | bytes 524320 | tf_op jit(solution)/shard_map/ppermute | solution.py:403
  173.2 4.6 shard_map.284
  179.1 1.6 collective-permute-start.33
  181.8 5.4 %collective-permute-start.29 = (bf16[256,1024]{1,0:T(8,128)(2,1)}, bf16[256,1024]{1,0:T(8,128)(2,1)}, u32[]{:S(2)}, u32[]{:S(2)}) collective-permute-start(bf16[256,1024]{1,0:T(8,128)(2,1)} %get-tuple-element.283), channel_id=1, source_target_pairs={{0,0},{1,1},{2,4},{3,5},{4,2},{5,3},{6,6},{7,7},{8,8},{9,9},{10,12... | collective-permute-start | bytes 1572872 | tf_op jit(solution)/shard_map/ppermute | solution.py:403
  188.1 19.2 %collective-permute-done.30 = bf16[256,1024]{1,0:T(8,128)(2,1)} collective-permute-done((bf16[256,1024]{1,0:T(8,128)(2,1)}, bf16[256,1024]{1,0:T(8,128)(2,1)}, u32[]{:S(2)}, u32[]{:S(2)}) %collective-permute-start.30) | collective-permute-done | bytes 524320 | tf_op jit(solution)/shard_map/ppermute | solution.py:403
  207.3 2.3 pad_maximum_fusion.3
  209.6 13.3 %shard_map.285 = (bf16[1024,2048]{1,0:T(8,128)(2,1)}, bf16[1024,2048]{1,0:T(8,128)(2,1)}) custom-call(s32[4]{0:T(128)} %pad_add_fusion.m, bf16[512,1024]{1,0:T(8,128)(2,1)} %get-tuple-element.135.own_ref, bf16[512,1024]{1,0:T(8,128)(2,1)} %collective-permute-done.28.other_ref, f32[1,2048]{1,0:T(1,128)} %bitcast.321, bf16[2,2,10,32,512]{4,3,2,1,0:T(8,128)(2,1)} %copy-done.3, ...), custom_call_target="tpu_custom_call" | custom-call | flops 1000 | bytes 1000 | tf_op jit(solution)/shard_map/pallas_call | solution.py:529
  223.9 11.5 %shard_map.286 = (bf16[512,1024]{1,0:T(8,128)(2,1)}, f32[512,1024]{1,0:T(8,128)}) custom-call(s32[4]{0:T(128)} %pad_add_fusion.m, bf16[1024,2048]{1,0:T(8,128)(2,1)} %get-tuple-element.142.x_ref, bf16[2,2,2,128,512]{4,3,2,1,0:T(8,128)(2,1)} %copy-done.5, bf16[2,2,2,128,512]{4,3,2,1,0:T(8,128)(2,1)} %collective-permute-done.33.rest_1_, ...), custom_call_target="tpu_custom_call" | custom-call | flops 1000 | bytes 1000 | tf_op jit(solution)/shard_map/pallas_call | solution.py:529
  235.5 2.9 collective-permute-done.35.recv_ref
  239.3 6.4 %shard_map.287 = (bf16[512,1024]{1,0:T(8,128)(2,1)}, f32[512,1024]{1,0:T(8,128)}, bf16[512,1024]{1,0:T(8,128)(2,1)}, f32[8,1024]{1,0:T(8,128)}) custom-call(s32[4]{0:T(128)} %pad_add_fusion.m, f32[512,1024]{1,0:T(8,128)} %get-tuple-element.134.normal_ref, f32[512,1024]{1,0:T(8,128)} %get-tuple-element.143.own_ref, bf16[512,1024]{1,0:T(8,128)(2,1)} %copy-done.25, ...), custom_call_target="tpu_custom_call" | custom-call | flops 1000 | bytes 1000 | tf_op jit(solution)/shard_map/pallas_call | solution.py:529
  245.9 2.7 collective-permute-done.36.other_ref
  249.6 9.3 %shard_map.288 = (bf16[2,2,2,128,512]{4,3,2,1,0:T(8,128)(2,1)}, bf16[2,2,2,128,512]{4,3,2,1,0:T(8,128)(2,1)}, bf16[2,2,2,128,512]{4,3,2,1,0:T(8,128)(2,1)}, bf16[2,2,2,128,512]{4,3,2,1,0:T(8,128)(2,1)}) custom-call(s32[4]{0:T(128)} %pad_add_fusion.m, bf16[1024,2048]{1,0:T(8,128)(2,1)} %get-tuple-element.142.x_ref, ...), custom_call_target="tpu_custom_call" | custom-call | flops 1000 | bytes 1000 | tf_op jit(solution)/shard_map/pallas_call | solution.py:529
  260.2 18.9 %shard_map.289 = (bf16[1024,2048]{1,0:T(8,128)(2,1)}, bf16[512,1024]{1,0:T(8,128)(2,1)}, f32[512,1024]{1,0:T(8,128)}, f32[8,2048]{1,0:T(8,128)}) custom-call(s32[4]{0:T(128)} %pad_add_fusion.m, bf16[512,1024]{1,0:T(8,128)(2,1)} %get-tuple-element.153.own_ref, bf16[512,1024]{1,0:T(8,128)(2,1)} %copy-done.9, bf16[1024,2048]{1,0:T(8,128)(2,1)} %get-tuple-element.154.slope_ref, ...), custom_call_target="tpu_custom_call" | custom-call | flops 1000 | bytes 1000 | tf_op jit(solution)/shard_map/pallas_call | solution.py:529
  279.2 9.8 %shard_map.290 = (bf16[2,2,8,32,512]{4,3,2,1,0:T(8,128)(2,1)}, bf16[2,2,8,32,512]{4,3,2,1,0:T(8,128)(2,1)}, bf16[2,2,8,32,512]{4,3,2,1,0:T(8,128)(2,1)}, bf16[2,2,8,32,512]{4,3,2,1,0:T(8,128)(2,1)}) custom-call(s32[4]{0:T(128)} %pad_add_fusion.m, bf16[512,1024]{1,0:T(8,128)(2,1)} %get-tuple-element.135.own_ref, ...), custom_call_target="tpu_custom_call" | custom-call | flops 1000 | bytes 1000 | tf_op jit(solution)/shard_map/pallas_call | solution.py:529
  292.3 5.9 %shard_map.291 = (f32[512,1024]{1,0:T(8,128)}, bf16[512,1024]{1,0:T(8,128)(2,1)}, f32[8,1024]{1,0:T(8,128)}) custom-call(s32[4]{0:T(128)} %pad_add_fusion.m, f32[512,1024]{1,0:T(8,128)} %get-tuple-element.162.resid_ref, f32[512,1024]{1,0:T(8,128)} %get-tuple-element.163.own_ref, bf16[512,1024]{1,0:T(8,128)(2,1)} %copy-done.31, ...), custom_call_target="tpu_custom_call" | custom-call | flops 1000 | bytes 1000 | tf_op jit(solution)/shard_map/pallas_call | solution.py:529
  307.7 7.0 %shard_map.292.grad_ref = bf16[1024,512]{1,0:T(8,128)(2,1)} custom-call(s32[4]{0:T(128)} %pad_add_fusion.m, bf16[512,1024]{1,0:T(8,128)(2,1)} %get-tuple-element.166.own_ref.rest_2_, bf16[512,1024]{1,0:T(8,128)(2,1)} %copy-done.10, bf16[2,2,10,32,512]{4,3,2,1,0:T(8,128)(2,1)} %copy-done.3, ...), custom_call_target="tpu_custom_call" | custom-call | flops 1000 | bytes 1000 | tf_op jit(solution)/shard_map/pallas_call | solution.py:529
  314.8 3.2 collective-permute-start.41
  318.0 19.7 %collective-permute-done.44 = bf16[2,2,128,512]{3,2,1,0:T(8,128)(2,1)} collective-permute-done((bf16[2,2,128,512]{3,2,1,0:T(8,128)(2,1)}, bf16[2,2,128,512]{3,2,1,0:T(8,128)(2,1)}, u32[]{:S(2)}, u32[]{:S(2)}) %collective-permute-start.44) | collective-permute-done | bytes 524320 | tf_op jit(solution)/shard_map/ppermute | solution.py:403
  339.6 3.2 collective-permute-start.47
  343.9 17.8 %shard_map.293 = (bf16[3,1024,256]{2,1,0:T(8,128)(2,1)}, f32[8,256]{1,0:T(8,128)}) custom-call(s32[4]{0:T(128)} %pad_add_fusion.m, bf16[3,1024,512]{2,1,0:T(8,128)(2,1)} %get-tuple-element.126.q_ref.k_ref.v_ref, bf16[3,1024,512]{2,1,0:T(8,128)(2,1)} %get-tuple-element.126.q_ref.k_ref.v_ref, bf16[3,1024,512]{2,1,0:T(8,128)(2,1)} %get-tuple-element.126.q_ref.k_ref.v_ref, ...), custom_call_target="tpu_custom_call" | custom-call | flops 1000 | bytes 1000 | tf_op jit(solution)/shard_map/pallas_call | solution.py:529
  363.6 8.8 %shard_map.294 = (bf16[2,2,10,32,256]{4,3,2,1,0:T(8,128)(2,1)}, bf16[2,2,10,32,256]{4,3,2,1,0:T(8,128)(2,1)}, bf16[2,2,10,32,256]{4,3,2,1,0:T(8,128)(2,1)}, bf16[2,2,10,32,256]{4,3,2,1,0:T(8,128)(2,1)}) custom-call(s32[4]{0:T(128)} %pad_add_fusion.m, bf16[1024,1024]{1,0:T(8,128)(2,1)} %get-tuple-element.175.x_ref, ...), custom_call_target="tpu_custom_call" | custom-call | flops 1000 | bytes 1000 | tf_op jit(solution)/shard_map/pallas_call | solution.py:529
  374.7 2.7 collective-permute-start.50
  377.4 2.4 fusion.9
  382.9 18.1 %shard_map.295 = (bf16[3,1024,256]{2,1,0:T(8,128)(2,1)}, f32[8,256]{1,0:T(8,128)}) custom-call(s32[4]{0:T(128)} %pad_add_fusion.m, bf16[3,1024,512]{2,1,0:T(8,128)(2,1)} %get-tuple-element.126.q_ref.k_ref.v_ref, bf16[3,1024,512]{2,1,0:T(8,128)(2,1)} %get-tuple-element.126.q_ref.k_ref.v_ref, bf16[3,1024,512]{2,1,0:T(8,128)(2,1)} %get-tuple-element.126.q_ref.k_ref.v_ref, ...), custom_call_target="tpu_custom_call" | custom-call | flops 1000 | bytes 1000 | tf_op jit(solution)/shard_map/pallas_call | solution.py:529
  404.8 6.6 %shard_map.296 = (bf16[2,2,6,32,256]{4,3,2,1,0:T(8,128)(2,1)}, bf16[2,2,6,32,256]{4,3,2,1,0:T(8,128)(2,1)}, bf16[2,2,6,32,256]{4,3,2,1,0:T(8,128)(2,1)}, bf16[2,2,6,32,256]{4,3,2,1,0:T(8,128)(2,1)}) custom-call(s32[4]{0:T(128)} %pad_add_fusion.m, bf16[1024,1024]{1,0:T(8,128)(2,1)} %get-tuple-element.175.x_ref, ...), custom_call_target="tpu_custom_call" | custom-call | flops 1000 | bytes 1000 | tf_op jit(solution)/shard_map/pallas_call | solution.py:529
  411.4 1.6 collective-permute-start.65
  416.3 10.5 %shard_map.297 = (bf16[512,1024]{1,0:T(8,128)(2,1)}, f32[512,1024]{1,0:T(8,128)}) custom-call(s32[4]{0:T(128)} %pad_add_fusion.m, bf16[3,1024,256]{2,1,0:T(8,128)(2,1)} %get-tuple-element.176.d_ref, bf16[3,1024,256]{2,1,0:T(8,128)(2,1)} %get-tuple-element.197.d_ref.e_ref, bf16[2,2,208,512]{3,2,1,0:T(8,128)(2,1)} %copy-done.6, ...), custom_call_target="tpu_custom_call" | custom-call | flops 1000 | bytes 1000 | tf_op jit(solution)/shard_map/pallas_call | solution.py:529
  431.2 4.8 collective-permute-done.62
  441.1 4.2 shard_map.298
  448.5 3.5 collective-permute-start.57
  452.2 1.6 collective-permute-done.57
  453.8 5.1 collective-permute-start.58
  461.5 1.7 add_convert_fusion.22
  463.1 2.0 collective-permute-start.69
  465.7 1.6 collective-permute-start.60
  467.3 1.8 fusion.25
  477.3 5.2 %collective-permute-start.70 = (bf16[6,32,256]{2,1,0:T(8,128)(2,1)S(1)}, bf16[6,32,256]{2,1,0:T(8,128)(2,1)S(1)}, u32[]{:S(2)}, u32[]{:S(2)}) collective-permute-start(bf16[6,32,256]{2,1,0:T(8,128)(2,1)S(1)} %get-tuple-element.296), channel_id=1, source_target_pairs={{0,2},{1,3},{2,0},{3,1},{4,6},{5,7},{6,4},{7,5},{8,10},{9,11},{10,... | collective-permute-start | bytes 294920 | tf_op jit(solution)/shard_map/ppermute | solution.py:403
  482.6 21.3 %collective-permute-done.70 = bf16[6,32,256]{2,1,0:T(8,128)(2,1)S(1)} collective-permute-done((bf16[6,32,256]{2,1,0:T(8,128)(2,1)S(1)}, bf16[6,32,256]{2,1,0:T(8,128)(2,1)S(1)}, u32[]{:S(2)}, u32[]{:S(2)}) %collective-permute-start.70) | collective-permute-done | bytes 98336 | tf_op jit(solution)/shard_map/ppermute | solution.py:403
  (422 shorter events, 109.4 us)
Async XLA Ops:
  4.0 22.0 %collective-permute-start = (bf16[4,32,512]{2,1,0:T(8,128)(2,1)S(1)}, bf16[4,32,512]{2,1,0:T(8,128)(2,1)S(1)}, u32[]{:S(2)}, u32[]{:S(2)}) collective-permute-start(bf16[4,32,512]{2,1,0:T(8,128)(2,1)S(1)} %bitcast.316), channel_id=1, source_target_pairs={{0,4},{1,5},{2,6},{3,7},{4,0},{5,1},{6,2},{7,3},{8,12},{9,13},{10,... | collective-permute-start | bytes 393224 | tf_op jit(solution)/shard_map/ppermute | solution.py:403
  4.8 14.1 %collective-permute-start.2 = (bf16[208,512]{1,0:T(8,128)(2,1)S(1)}, bf16[208,512]{1,0:T(8,128)(2,1)S(1)}, u32[]{:S(2)}, u32[]{:S(2)}) collective-permute-start(bf16[208,512]{1,0:T(8,128)(2,1)S(1)} %concatenate.94), channel_id=1, source_target_pairs={{0,2},{1,3},{2,0},{3,1},{4,6},{5,7},{6,4},{7,5},{8,10},{9,11},{10,... | collective-permute-start | bytes 638984 | tf_op jit(solution)/shard_map/ppermute | solution.py:403
  22.2 11.8 %collective-permute-start.3 = (bf16[2,208,512]{2,1,0:T(8,128)(2,1)S(1)}, bf16[2,208,512]{2,1,0:T(8,128)(2,1)S(1)}, u32[]{:S(2)}, u32[]{:S(2)}) collective-permute-start(bf16[2,208,512]{2,1,0:T(8,128)(2,1)S(1)} %pad_maximum_fusion.12), channel_id=1, source_target_pairs={{0,1},{1,0},{2,3},{3,2},{4,5},{5,4},{6,7},{7,6},{8,9},{9,8},{10,11... | collective-permute-start | bytes 1277960 | tf_op jit(solution)/shard_map/ppermute | solution.py:403
  26.1 26.9 %collective-permute-start.17 = (bf16[2,208,512]{2,1,0:T(8,128)(2,1)S(1)}, bf16[2,208,512]{2,1,0:T(8,128)(2,1)S(1)}, u32[]{:S(2)}, u32[]{:S(2)}) collective-permute-start(bf16[2,208,512]{2,1,0:T(8,128)(2,1)S(1)} %pad_maximum_fusion.12), channel_id=1, source_target_pairs={{0,8},{1,9},{2,10},{3,11},{4,12},{5,13},{6,14},{7,15},{8,0},{9,1},... | collective-permute-start | bytes 1277960 | tf_op jit(solution)/shard_map/ppermute | solution.py:403
  28.4 11.0 %collective-permute-start.14 = (f32[2,1024]{1,0:T(2,128)S(1)}, f32[2,1024]{1,0:T(2,128)S(1)}, u32[]{:S(2)}, u32[]{:S(2)}) collective-permute-start(f32[2,1024]{1,0:T(2,128)S(1)} %slice.665), channel_id=1, source_target_pairs={{0,2},{1,3},{2,0},{3,1},{4,6},{5,7},{6,4},{7,5},{8,10},{9,11},{10,... | collective-permute-start | bytes 24584 | tf_op jit(solution)/shard_map/ppermute | solution.py:403
  34.0 16.6 %collective-permute-start.4 = (bf16[10,32,512]{2,1,0:T(8,128)(2,1)S(1)}, bf16[10,32,512]{2,1,0:T(8,128)(2,1)}, u32[]{:S(2)}, u32[]{:S(2)}) collective-permute-start(bf16[10,32,512]{2,1,0:T(8,128)(2,1)S(1)} %pad_maximum_fusion.13), channel_id=1, source_target_pairs={{0,2},{1,3},{2,0},{3,1},{4,6},{5,7},{6,4},{7,5},{8,10},{9,11},{10,... | collective-permute-start | bytes 983048 | tf_op jit(solution)/shard_map/ppermute | solution.py:403
  36.2 16.7 %collective-permute-start.18 = (bf16[2,208,512]{2,1,0:T(8,128)(2,1)S(1)}, bf16[2,208,512]{2,1,0:T(8,128)(2,1)S(1)}, u32[]{:S(2)}, u32[]{:S(2)}) collective-permute-start(bf16[2,208,512]{2,1,0:T(8,128)(2,1)S(1)} %collective-permute-done.3), channel_id=1, source_target_pairs={{0,16},{1,17},{2,18},{3,19},{4,20},{5,21},{6,22},{7,23},{8,24},{9,... | collective-permute-start | bytes 1277960 | tf_op jit(solution)/shard_map/ppermute | solution.py:403
  39.4 17.7 %collective-permute-start.15 = (f32[1,1024]{1,0:T(1,128)S(1)}, f32[1,1024]{1,0:T(1,128)S(1)}, u32[]{:S(2)}, u32[]{:S(2)}) collective-permute-start(f32[1,1024]{1,0:T(1,128)S(1)} %slice.667), channel_id=1, source_target_pairs={{0,1},{1,0},{2,3},{3,2},{4,5},{5,4},{6,7},{7,6},{8,9},{9,8},{10,11... | collective-permute-start | bytes 12296 | tf_op jit(solution)/shard_map/ppermute | solution.py:403
  52.5 16.0 %collective-permute-start.5 = (bf16[2,10,32,512]{3,2,1,0:T(8,128)(2,1)}, bf16[2,10,32,512]{3,2,1,0:T(8,128)(2,1)}, u32[]{:S(2)}, u32[]{:S(2)}) collective-permute-start(bf16[2,10,32,512]{3,2,1,0:T(8,128)(2,1)} %pad_maximum_fusion.10), channel_id=1, source_target_pairs={{0,1},{1,0},{2,3},{3,2},{4,5},{5,4},{6,7},{7,6},{8,9},{9,8},{10,11... | collective-permute-start | bytes 1966088 | tf_op jit(solution)/shard_map/ppermute | solution.py:403
  53.8 20.7 %collective-permute-start.20 = (bf16[2,2,208,512]{3,2,1,0:T(8,128)(2,1)S(1)}, bf16[2,2,208,512]{3,2,1,0:T(8,128)(2,1)S(1)}, u32[]{:S(2)}, u32[]{:S(2)}) collective-permute-start(bf16[2,2,208,512]{3,2,1,0:T(8,128)(2,1)S(1)} %pad_maximum_fusion.8.rest_0_), channel_id=1, source_target_pairs={{0,16},{1,17},{2,18},{3,19},{4,20},{5,21},{6,22},{7,23},{8,24},{9,... | collective-permute-start | bytes 2555912 | tf_op jit(solution)/shard_map/ppermute | solution.py:403
  55.5 21.9 %collective-permute-start.19 = (bf16[2,2,208,512]{3,2,1,0:T(8,128)(2,1)S(1)}, bf16[2,2,208,512]{3,2,1,0:T(8,128)(2,1)S(1)}, u32[]{:S(2)}, u32[]{:S(2)}) collective-permute-start(bf16[2,2,208,512]{3,2,1,0:T(8,128)(2,1)S(1)} %pad_maximum_fusion.9.rest_2_), channel_id=1, source_target_pairs={{0,8},{1,9},{2,10},{3,11},{4,12},{5,13},{6,14},{7,15},{8,0},{9,1},... | collective-permute-start | bytes 2555912 | tf_op jit(solution)/shard_map/ppermute | solution.py:403
  57.7 37.4 %collective-permute-start.23 = (bf16[2,10,32,512]{3,2,1,0:T(8,128)(2,1)}, bf16[2,10,32,512]{3,2,1,0:T(8,128)(2,1)}, u32[]{:S(2)}, u32[]{:S(2)}) collective-permute-start(bf16[2,10,32,512]{3,2,1,0:T(8,128)(2,1)} %pad_maximum_fusion.10), channel_id=1, source_target_pairs={{0,8},{1,9},{2,10},{3,11},{4,12},{5,13},{6,14},{7,15},{8,0},{9,1},... | collective-permute-start | bytes 1966088 | tf_op jit(solution)/shard_map/ppermute | solution.py:403
  68.6 9.8 %collective-permute-start.6 = (bf16[272,1024]{1,0:T(8,128)(2,1)S(1)}, bf16[272,1024]{1,0:T(8,128)(2,1)S(1)}, u32[]{:S(2)}, u32[]{:S(2)}) collective-permute-start(bf16[272,1024]{1,0:T(8,128)(2,1)S(1)} %get-tuple-element.269), channel_id=1, source_target_pairs={{0,0},{1,1},{2,4},{3,5},{4,2},{5,3},{6,6},{7,7},{8,8},{9,9},{10,12... | collective-permute-start | bytes 1671176 | tf_op jit(solution)/shard_map/ppermute | solution.py:403
  69.3 14.5 %collective-permute-start.7 = (bf16[272,1024]{1,0:T(8,128)(2,1)S(1)}, bf16[272,1024]{1,0:T(8,128)(2,1)S(1)}, u32[]{:S(2)}, u32[]{:S(2)}) collective-permute-start(bf16[272,1024]{1,0:T(8,128)(2,1)S(1)} %get-tuple-element.270), channel_id=1, source_target_pairs={{0,1},{1,0},{2,5},{3,4},{4,3},{5,2},{6,7},{7,6},{8,9},{9,8},{10,13... | collective-permute-start | bytes 1671176 | tf_op jit(solution)/shard_map/ppermute | solution.py:403
  74.5 20.6 %collective-permute-start.24 = (bf16[2,10,32,512]{3,2,1,0:T(8,128)(2,1)}, bf16[2,10,32,512]{3,2,1,0:T(8,128)(2,1)S(1)}, u32[]{:S(2)}, u32[]{:S(2)}) collective-permute-start(bf16[2,10,32,512]{3,2,1,0:T(8,128)(2,1)} %collective-permute-done.5), channel_id=1, source_target_pairs={{0,16},{1,17},{2,18},{3,19},{4,20},{5,21},{6,22},{7,23},{8,24},{9,... | collective-permute-start | bytes 1966088 | tf_op jit(solution)/shard_map/ppermute | solution.py:403
  84.9 15.9 %collective-permute-start.16 = (bf16[2,272,1024]{2,1,0:T(8,128)(2,1)}, bf16[2,272,1024]{2,1,0:T(8,128)(2,1)}, u32[]{:S(2)}, u32[]{:S(2)}) collective-permute-start(bf16[2,272,1024]{2,1,0:T(8,128)(2,1)} %pad_maximum_fusion.2.own_ref.tok_ref), channel_id=1, source_target_pairs={{0,4},{1,5},{2,6},{3,7},{4,0},{5,1},{6,2},{7,3},{8,12},{9,13},{10,... | collective-permute-start | bytes 3342344 | tf_op jit(solution)/shard_map/ppermute | solution.py:403
  96.3 51.8 %collective-permute-start.26 = (bf16[2,2,10,32,512]{4,3,2,1,0:T(8,128)(2,1)S(1)}, bf16[2,2,10,32,512]{4,3,2,1,0:T(8,128)(2,1)}, u32[]{:S(2)}, u32[]{:S(2)}) collective-permute-start(bf16[2,2,10,32,512]{4,3,2,1,0:T(8,128)(2,1)S(1)} %pad_maximum_fusion.1.rest_2_.rest_6_), channel_id=1, source_target_pairs={{0,8},{1,9},{2,10},{3,11},{4,12},{5,13},{6,14},{7,15},{8,0},{9,1},... | collective-permute-start | bytes 3932168 | tf_op jit(solution)/shard_map/ppermute | solution.py:403
  99.3 48.8 %collective-permute-start.25 = (bf16[2,2,10,32,512]{4,3,2,1,0:T(8,128)(2,1)S(1)}, bf16[2,2,10,32,512]{4,3,2,1,0:T(8,128)(2,1)}, u32[]{:S(2)}, u32[]{:S(2)}) collective-permute-start(bf16[2,2,10,32,512]{4,3,2,1,0:T(8,128)(2,1)S(1)} %pad_maximum_fusion.rest_0_.rest_4_), channel_id=1, source_target_pairs={{0,16},{1,17},{2,18},{3,19},{4,20},{5,21},{6,22},{7,23},{8,24},{9,... | collective-permute-start | bytes 3932168 | tf_op jit(solution)/shard_map/ppermute | solution.py:403
  111.1 21.7 %collective-permute-start.21 = (bf16[2,128,512]{2,1,0:T(8,128)(2,1)S(1)}, bf16[2,128,512]{2,1,0:T(8,128)(2,1)S(1)}, u32[]{:S(2)}, u32[]{:S(2)}) collective-permute-start(bf16[2,128,512]{2,1,0:T(8,128)(2,1)S(1)} %bitcast.297), channel_id=1, source_target_pairs={{0,2},{1,3},{2,0},{3,1},{4,6},{5,7},{6,4},{7,5},{8,10},{9,11},{10,... | collective-permute-start | bytes 786440 | tf_op jit(solution)/shard_map/ppermute | solution.py:403
  134.5 13.7 %collective-permute-start.22 = (bf16[2,2,128,512]{3,2,1,0:T(8,128)(2,1)S(1)}, bf16[2,2,128,512]{3,2,1,0:T(8,128)(2,1)}, u32[]{:S(2)}, u32[]{:S(2)}) collective-permute-start(bf16[2,2,128,512]{3,2,1,0:T(8,128)(2,1)S(1)} %pad_maximum_fusion.11), channel_id=1, source_target_pairs={{0,1},{1,0},{2,3},{3,2},{4,5},{5,4},{6,7},{7,6},{8,9},{9,8},{10,11... | collective-permute-start | bytes 1572872 | tf_op jit(solution)/shard_map/ppermute | solution.py:403
  155.6 17.6 %collective-permute-start.27 = (bf16[512,1024]{1,0:T(8,128)(2,1)}, bf16[512,1024]{1,0:T(8,128)(2,1)}, u32[]{:S(2)}, u32[]{:S(2)}) collective-permute-start(bf16[512,1024]{1,0:T(8,128)(2,1)} %get-tuple-element.133), channel_id=1, source_target_pairs={{0,4},{1,5},{2,6},{3,7},{4,0},{5,1},{6,2},{7,3},{8,12},{9,13},{10,... | collective-permute-start | bytes 3145736 | tf_op jit(solution)/shard_map/ppermute | solution.py:403
  155.6 14.3 %collective-permute-start.31 = (bf16[2,2,128,512]{3,2,1,0:T(8,128)(2,1)S(1)}, bf16[2,2,128,512]{3,2,1,0:T(8,128)(2,1)S(1)}, u32[]{:S(2)}, u32[]{:S(2)}) collective-permute-start(bf16[2,2,128,512]{3,2,1,0:T(8,128)(2,1)S(1)} %pad_maximum_fusion.11), channel_id=1, source_target_pairs={{0,8},{1,9},{2,10},{3,11},{4,12},{5,13},{6,14},{7,15},{8,0},{9,1},... | collective-permute-start | bytes 1572872 | tf_op jit(solution)/shard_map/ppermute | solution.py:403
  156.4 14.2 %collective-permute-start.32 = (bf16[2,2,128,512]{3,2,1,0:T(8,128)(2,1)}, bf16[2,2,128,512]{3,2,1,0:T(8,128)(2,1)S(1)}, u32[]{:S(2)}, u32[]{:S(2)}) collective-permute-start(bf16[2,2,128,512]{3,2,1,0:T(8,128)(2,1)} %collective-permute-done.22), channel_id=1, source_target_pairs={{0,16},{1,17},{2,18},{3,19},{4,20},{5,21},{6,22},{7,23},{8,24},{9,... | collective-permute-start | bytes 1572872 | tf_op jit(solution)/shard_map/ppermute | solution.py:403
  171.7 51.2 %collective-permute-start.34 = (bf16[2,2,2,128,512]{4,3,2,1,0:T(8,128)(2,1)S(1)}, bf16[2,2,2,128,512]{4,3,2,1,0:T(8,128)(2,1)S(1)}, u32[]{:S(2)}, u32[]{:S(2)}) collective-permute-start(bf16[2,2,2,128,512]{4,3,2,1,0:T(8,128)(2,1)S(1)} %pad_maximum_fusion.5.rest_2_), channel_id=1, source_target_pairs={{0,8},{1,9},{2,10},{3,11},{4,12},{5,13},{6,14},{7,15},{8,0},{9,1},... | collective-permute-start | bytes 3145736 | tf_op jit(solution)/shard_map/ppermute | solution.py:403
  177.8 31.8 %collective-permute-start.28 = (bf16[512,1024]{1,0:T(8,128)(2,1)}, bf16[512,1024]{1,0:T(8,128)(2,1)}, u32[]{:S(2)}, u32[]{:S(2)}) collective-permute-start(bf16[512,1024]{1,0:T(8,128)(2,1)} %get-tuple-element.135.own_ref), channel_id=1, source_target_pairs={{0,4},{1,5},{2,6},{3,7},{4,0},{5,1},{6,2},{7,3},{8,12},{9,13},{10,... | collective-permute-start | bytes 3145736 | tf_op jit(solution)/shard_map/ppermute | solution.py:403
  179.1 43.8 %collective-permute-start.33 = (bf16[2,2,2,128,512]{4,3,2,1,0:T(8,128)(2,1)S(1)}, bf16[2,2,2,128,512]{4,3,2,1,0:T(8,128)(2,1)}, u32[]{:S(2)}, u32[]{:S(2)}) collective-permute-start(bf16[2,2,2,128,512]{4,3,2,1,0:T(8,128)(2,1)S(1)} %pad_maximum_fusion.4.rest_0_), channel_id=1, source_target_pairs={{0,16},{1,17},{2,18},{3,19},{4,20},{5,21},{6,22},{7,23},{8,24},{9,... | collective-permute-start | bytes 3145736 | tf_op jit(solution)/shard_map/ppermute | solution.py:403
  181.8 6.4 %collective-permute-start.29 = (bf16[256,1024]{1,0:T(8,128)(2,1)}, bf16[256,1024]{1,0:T(8,128)(2,1)}, u32[]{:S(2)}, u32[]{:S(2)}) collective-permute-start(bf16[256,1024]{1,0:T(8,128)(2,1)} %get-tuple-element.283), channel_id=1, source_target_pairs={{0,0},{1,1},{2,4},{3,5},{4,2},{5,3},{6,6},{7,7},{8,8},{9,9},{10,12... | collective-permute-start | bytes 1572872 | tf_op jit(solution)/shard_map/ppermute | solution.py:403
  187.1 20.2 %collective-permute-start.30 = (bf16[256,1024]{1,0:T(8,128)(2,1)}, bf16[256,1024]{1,0:T(8,128)(2,1)}, u32[]{:S(2)}, u32[]{:S(2)}) collective-permute-start(bf16[256,1024]{1,0:T(8,128)(2,1)} %get-tuple-element.284), channel_id=1, source_target_pairs={{0,1},{1,0},{2,5},{3,4},{4,3},{5,2},{6,7},{7,6},{8,9},{9,8},{10,13... | collective-permute-start | bytes 1572872 | tf_op jit(solution)/shard_map/ppermute | solution.py:403
  258.9 30.2 %collective-permute-start.38 = (bf16[2,2,2,128,512]{4,3,2,1,0:T(8,128)(2,1)}, bf16[2,2,2,128,512]{4,3,2,1,0:T(8,128)(2,1)S(1)}, u32[]{:S(2)}, u32[]{:S(2)}) collective-permute-start(bf16[2,2,2,128,512]{4,3,2,1,0:T(8,128)(2,1)} %get-tuple-element.152), channel_id=1, source_target_pairs={{0,8},{1,9},{2,10},{3,11},{4,12},{5,13},{6,14},{7,15},{8,0},{9,1},... | collective-permute-start | bytes 3145736 | tf_op jit(solution)/shard_map/ppermute | solution.py:403
  259.7 30.5 %collective-permute-start.37 = (bf16[2,2,2,128,512]{4,3,2,1,0:T(8,128)(2,1)}, bf16[2,2,2,128,512]{4,3,2,1,0:T(8,128)(2,1)S(1)}, u32[]{:S(2)}, u32[]{:S(2)}) collective-permute-start(bf16[2,2,2,128,512]{4,3,2,1,0:T(8,128)(2,1)} %get-tuple-element.151), channel_id=1, source_target_pairs={{0,16},{1,17},{2,18},{3,19},{4,20},{5,21},{6,22},{7,23},{8,24},{9,... | collective-permute-start | bytes 3145736 | tf_op jit(solution)/shard_map/ppermute | solution.py:403
  279.1 12.3 %collective-permute-start.39 = (bf16[512,1024]{1,0:T(8,128)(2,1)}, bf16[512,1024]{1,0:T(8,128)(2,1)S(1)}, u32[]{:S(2)}, u32[]{:S(2)}) collective-permute-start(bf16[512,1024]{1,0:T(8,128)(2,1)} %get-tuple-element.164), channel_id=1, source_target_pairs={{0,4},{1,5},{2,6},{3,7},{4,0},{5,1},{6,2},{7,3},{8,12},{9,13},{10,... | collective-permute-start | bytes 3145736 | tf_op jit(solution)/shard_map/ppermute | solution.py:403
  298.3 8.5 %collective-permute-start.40 = (bf16[512,1024]{1,0:T(8,128)(2,1)}, bf16[512,1024]{1,0:T(8,128)(2,1)S(1)}, u32[]{:S(2)}, u32[]{:S(2)}) collective-permute-start(bf16[512,1024]{1,0:T(8,128)(2,1)} %get-tuple-element.166.own_ref.rest_2_), channel_id=1, source_target_pairs={{0,4},{1,5},{2,6},{3,7},{4,0},{5,1},{6,2},{7,3},{8,12},{9,13},{10,... | collective-permute-start | bytes 3145736 | tf_op jit(solution)/shard_map/ppermute | solution.py:403
  299.9 77.4 %collective-permute-start.46 = (bf16[2,2,8,32,512]{4,3,2,1,0:T(8,128)(2,1)}, bf16[2,2,8,32,512]{4,3,2,1,0:T(8,128)(2,1)}, u32[]{:S(2)}, u32[]{:S(2)}) collective-permute-start(bf16[2,2,8,32,512]{4,3,2,1,0:T(8,128)(2,1)} %get-tuple-element.159), channel_id=1, source_target_pairs={{0,8},{1,9},{2,10},{3,11},{4,12},{5,13},{6,14},{7,15},{8,0},{9,1},... | collective-permute-start | bytes 3145736 | tf_op jit(solution)/shard_map/ppermute | solution.py:403
  301.3 79.0 %collective-permute-start.45 = (bf16[2,2,8,32,512]{4,3,2,1,0:T(8,128)(2,1)}, bf16[2,2,8,32,512]{4,3,2,1,0:T(8,128)(2,1)S(1)}, u32[]{:S(2)}, u32[]{:S(2)}) collective-permute-start(bf16[2,2,8,32,512]{4,3,2,1,0:T(8,128)(2,1)} %get-tuple-element.157), channel_id=1, source_target_pairs={{0,16},{1,17},{2,18},{3,19},{4,20},{5,21},{6,22},{7,23},{8,24},{9,... | collective-permute-start | bytes 3145736 | tf_op jit(solution)/shard_map/ppermute | solution.py:403
  303.7 34.0 %collective-permute-start.44 = (bf16[2,2,128,512]{3,2,1,0:T(8,128)(2,1)}, bf16[2,2,128,512]{3,2,1,0:T(8,128)(2,1)}, u32[]{:S(2)}, u32[]{:S(2)}) collective-permute-start(bf16[2,2,128,512]{3,2,1,0:T(8,128)(2,1)} %get-tuple-element.261), channel_id=1, source_target_pairs={{0,16},{1,17},{2,18},{3,19},{4,20},{5,21},{6,22},{7,23},{8,24},{9,... | collective-permute-start | bytes 1572872 | tf_op jit(solution)/shard_map/ppermute | solution.py:403
  305.0 34.6 %collective-permute-start.43 = (bf16[2,2,128,512]{3,2,1,0:T(8,128)(2,1)}, bf16[2,2,128,512]{3,2,1,0:T(8,128)(2,1)}, u32[]{:S(2)}, u32[]{:S(2)}) collective-permute-start(bf16[2,2,128,512]{3,2,1,0:T(8,128)(2,1)} %get-tuple-element.263), channel_id=1, source_target_pairs={{0,8},{1,9},{2,10},{3,11},{4,12},{5,13},{6,14},{7,15},{8,0},{9,1},... | collective-permute-start | bytes 1572872 | tf_op jit(solution)/shard_map/ppermute | solution.py:403
  314.8 47.6 %collective-permute-start.41 = (bf16[256,1024]{1,0:T(8,128)(2,1)S(1)}, bf16[256,1024]{1,0:T(8,128)(2,1)S(1)}, u32[]{:S(2)}, u32[]{:S(2)}) collective-permute-start(bf16[256,1024]{1,0:T(8,128)(2,1)S(1)} %get-tuple-element.281), channel_id=1, source_target_pairs={{1,0},{0,1},{5,2},{4,3},{3,4},{2,5},{7,6},{6,7},{9,8},{8,9},{13,10... | collective-permute-start | bytes 1572872 | tf_op jit(solution)/shard_map/ppermute | solution.py:403
  337.7 24.7 %collective-permute-start.42 = (bf16[256,1024]{1,0:T(8,128)(2,1)S(1)}, bf16[256,1024]{1,0:T(8,128)(2,1)S(1)}, u32[]{:S(2)}, u32[]{:S(2)}) collective-permute-start(bf16[256,1024]{1,0:T(8,128)(2,1)S(1)} %get-tuple-element.282), channel_id=1, source_target_pairs={{0,0},{1,1},{4,2},{5,3},{2,4},{3,5},{6,6},{7,7},{8,8},{9,9},{12,10... | collective-permute-start | bytes 1572872 | tf_op jit(solution)/shard_map/ppermute | solution.py:403
  339.6 35.0 %collective-permute-start.47 = (bf16[2,2,128,512]{3,2,1,0:T(8,128)(2,1)S(1)}, bf16[2,2,128,512]{3,2,1,0:T(8,128)(2,1)S(1)}, u32[]{:S(2)}, u32[]{:S(2)}) collective-permute-start(bf16[2,2,128,512]{3,2,1,0:T(8,128)(2,1)S(1)} %add_convert_fusion.6), channel_id=1, source_target_pairs={{0,1},{1,0},{2,3},{3,2},{4,5},{5,4},{6,7},{7,6},{8,9},{9,8},{10,11... | collective-permute-start | bytes 1572872 | tf_op jit(solution)/shard_map/ppermute | solution.py:403
  372.3 41.3 %collective-permute-start.52 = (bf16[2,2,10,32,256]{4,3,2,1,0:T(8,128)(2,1)}, bf16[2,2,10,32,256]{4,3,2,1,0:T(8,128)(2,1)}, u32[]{:S(2)}, u32[]{:S(2)}) collective-permute-start(bf16[2,2,10,32,256]{4,3,2,1,0:T(8,128)(2,1)} %get-tuple-element.180), channel_id=1, source_target_pairs={{0,8},{1,9},{2,10},{3,11},{4,12},{5,13},{6,14},{7,15},{8,0},{9,1},... | collective-permute-start | bytes 1966088 | tf_op jit(solution)/shard_map/ppermute | solution.py:403
  373.0 41.9 %collective-permute-start.51 = (bf16[2,2,10,32,256]{4,3,2,1,0:T(8,128)(2,1)}, bf16[2,2,10,32,256]{4,3,2,1,0:T(8,128)(2,1)}, u32[]{:S(2)}, u32[]{:S(2)}) collective-permute-start(bf16[2,2,10,32,256]{4,3,2,1,0:T(8,128)(2,1)} %get-tuple-element.178), channel_id=1, source_target_pairs={{0,16},{1,17},{2,18},{3,19},{4,20},{5,21},{6,22},{7,23},{8,24},{9,... | collective-permute-start | bytes 1966088 | tf_op jit(solution)/shard_map/ppermute | solution.py:403
  374.7 27.2 %collective-permute-start.50 = (bf16[2,128,512]{2,1,0:T(8,128)(2,1)S(1)}, bf16[2,128,512]{2,1,0:T(8,128)(2,1)S(1)}, u32[]{:S(2)}, u32[]{:S(2)}) collective-permute-start(bf16[2,128,512]{2,1,0:T(8,128)(2,1)S(1)} %get-tuple-element.277), channel_id=1, source_target_pairs={{0,2},{1,3},{2,0},{3,1},{4,6},{5,7},{6,4},{7,5},{8,10},{9,11},{10,... | collective-permute-start | bytes 786440 | tf_op jit(solution)/shard_map/ppermute | solution.py:403
  379.8 23.4 %collective-permute-start.49 = (bf16[2,8,32,512]{3,2,1,0:T(8,128)(2,1)}, bf16[2,8,32,512]{3,2,1,0:T(8,128)(2,1)}, u32[]{:S(2)}, u32[]{:S(2)}) collective-permute-start(bf16[2,8,32,512]{3,2,1,0:T(8,128)(2,1)} %get-tuple-element.257), channel_id=1, source_target_pairs={{0,16},{1,17},{2,18},{3,19},{4,20},{5,21},{6,22},{7,23},{8,24},{9,... | collective-permute-start | bytes 1572872 | tf_op jit(solution)/shard_map/ppermute | solution.py:403
  381.5 23.1 %collective-permute-start.48 = (bf16[2,8,32,512]{3,2,1,0:T(8,128)(2,1)}, bf16[2,8,32,512]{3,2,1,0:T(8,128)(2,1)S(1)}, u32[]{:S(2)}, u32[]{:S(2)}) collective-permute-start(bf16[2,8,32,512]{3,2,1,0:T(8,128)(2,1)} %get-tuple-element.259), channel_id=1, source_target_pairs={{0,8},{1,9},{2,10},{3,11},{4,12},{5,13},{6,14},{7,15},{8,0},{9,1},... | collective-permute-start | bytes 1572872 | tf_op jit(solution)/shard_map/ppermute | solution.py:403
  404.4 34.5 %collective-permute-start.72 = (bf16[2,8,32,512]{3,2,1,0:T(8,128)(2,1)S(1)}, bf16[2,8,32,512]{3,2,1,0:T(8,128)(2,1)S(1)}, u32[]{:S(2)}, u32[]{:S(2)}) collective-permute-start(bf16[2,8,32,512]{3,2,1,0:T(8,128)(2,1)S(1)} %add_convert_fusion), channel_id=1, source_target_pairs={{0,1},{1,0},{2,3},{3,2},{4,5},{5,4},{6,7},{7,6},{8,9},{9,8},{10,11... | collective-permute-start | bytes 1572872 | tf_op jit(solution)/shard_map/ppermute | solution.py:403
  411.4 17.4 %collective-permute-start.65 = (bf16[2,2,6,32,256]{4,3,2,1,0:T(8,128)(2,1)}, bf16[2,2,6,32,256]{4,3,2,1,0:T(8,128)(2,1)S(1)}, u32[]{:S(2)}, u32[]{:S(2)}) collective-permute-start(bf16[2,2,6,32,256]{4,3,2,1,0:T(8,128)(2,1)} %get-tuple-element.192), channel_id=1, source_target_pairs={{0,16},{1,17},{2,18},{3,19},{4,20},{5,21},{6,22},{7,23},{8,24},{9,... | collective-permute-start | bytes 1179656 | tf_op jit(solution)/shard_map/ppermute | solution.py:403
  413.0 16.7 %collective-permute-start.66 = (bf16[2,2,6,32,256]{4,3,2,1,0:T(8,128)(2,1)}, bf16[2,2,6,32,256]{4,3,2,1,0:T(8,128)(2,1)S(1)}, u32[]{:S(2)}, u32[]{:S(2)}) collective-permute-start(bf16[2,2,6,32,256]{4,3,2,1,0:T(8,128)(2,1)} %get-tuple-element.194), channel_id=1, source_target_pairs={{0,8},{1,9},{2,10},{3,11},{4,12},{5,13},{6,14},{7,15},{8,0},{9,1},... | collective-permute-start | bytes 1179656 | tf_op jit(solution)/shard_map/ppermute | solution.py:403
  426.9 10.4 %collective-permute-start.61 = (bf16[2,10,32,256]{3,2,1,0:T(8,128)(2,1)S(1)}, bf16[2,10,32,256]{3,2,1,0:T(8,128)(2,1)S(1)}, u32[]{:S(2)}, u32[]{:S(2)}) collective-permute-start(bf16[2,10,32,256]{3,2,1,0:T(8,128)(2,1)S(1)} %get-tuple-element.267), channel_id=1, source_target_pairs={{0,8},{1,9},{2,10},{3,11},{4,12},{5,13},{6,14},{7,15},{8,0},{9,1},... | collective-permute-start | bytes 983048 | tf_op jit(solution)/shard_map/ppermute | solution.py:403
  428.3 7.7 %collective-permute-start.62 = (bf16[2,10,32,256]{3,2,1,0:T(8,128)(2,1)S(1)}, bf16[2,10,32,256]{3,2,1,0:T(8,128)(2,1)S(1)}, u32[]{:S(2)}, u32[]{:S(2)}) collective-permute-start(bf16[2,10,32,256]{3,2,1,0:T(8,128)(2,1)S(1)} %get-tuple-element.265), channel_id=1, source_target_pairs={{0,16},{1,17},{2,18},{3,19},{4,20},{5,21},{6,22},{7,23},{8,24},{9,... | collective-permute-start | bytes 983048 | tf_op jit(solution)/shard_map/ppermute | solution.py:403
  428.8 11.3 %collective-permute-start.53 = (bf16[512,1024]{1,0:T(8,128)(2,1)}, bf16[512,1024]{1,0:T(8,128)(2,1)S(1)}, u32[]{:S(2)}, u32[]{:S(2)}) collective-permute-start(bf16[512,1024]{1,0:T(8,128)(2,1)} %get-tuple-element.199), channel_id=1, source_target_pairs={{0,4},{1,5},{2,6},{3,7},{4,0},{5,1},{6,2},{7,3},{8,12},{9,13},{10,... | collective-permute-start | bytes 3145736 | tf_op jit(solution)/shard_map/ppermute | solution.py:403
  429.7 29.2 %collective-permute-start.67 = (bf16[2,6,32,256]{3,2,1,0:T(8,128)(2,1)}, bf16[2,6,32,256]{3,2,1,0:T(8,128)(2,1)}, u32[]{:S(2)}, u32[]{:S(2)}) collective-permute-start(bf16[2,6,32,256]{3,2,1,0:T(8,128)(2,1)} %get-tuple-element.285), channel_id=1, source_target_pairs={{0,8},{1,9},{2,10},{3,11},{4,12},{5,13},{6,14},{7,15},{8,0},{9,1},... | collective-permute-start | bytes 589832 | tf_op jit(solution)/shard_map/ppermute | solution.py:403
  436.0 25.5 %collective-permute-start.68 = (bf16[2,6,32,256]{3,2,1,0:T(8,128)(2,1)}, bf16[2,6,32,256]{3,2,1,0:T(8,128)(2,1)}, u32[]{:S(2)}, u32[]{:S(2)}) collective-permute-start(bf16[2,6,32,256]{3,2,1,0:T(8,128)(2,1)} %get-tuple-element.288), channel_id=1, source_target_pairs={{0,16},{1,17},{2,18},{3,19},{4,20},{5,21},{6,22},{7,23},{8,24},{9,... | collective-permute-start | bytes 589832 | tf_op jit(solution)/shard_map/ppermute | solution.py:403
  437.3 30.0 %collective-permute-start.63 = (bf16[2,10,32,256]{3,2,1,0:T(8,128)(2,1)}, bf16[2,10,32,256]{3,2,1,0:T(8,128)(2,1)}, u32[]{:S(2)}, u32[]{:S(2)}) collective-permute-start(bf16[2,10,32,256]{3,2,1,0:T(8,128)(2,1)} %add_convert_fusion.12), channel_id=1, source_target_pairs={{0,1},{1,0},{2,3},{3,2},{4,5},{5,4},{6,7},{7,6},{8,9},{9,8},{10,11... | collective-permute-start | bytes 983048 | tf_op jit(solution)/shard_map/ppermute | solution.py:403
  439.0 9.3 %collective-permute-start.73 = (bf16[8,32,512]{2,1,0:T(8,128)(2,1)S(1)}, bf16[8,32,512]{2,1,0:T(8,128)(2,1)S(1)}, u32[]{:S(2)}, u32[]{:S(2)}) collective-permute-start(bf16[8,32,512]{2,1,0:T(8,128)(2,1)S(1)} %get-tuple-element.272), channel_id=1, source_target_pairs={{0,2},{1,3},{2,0},{3,1},{4,6},{5,7},{6,4},{7,5},{8,10},{9,11},{10,... | collective-permute-start | bytes 786440 | tf_op jit(solution)/shard_map/ppermute | solution.py:403
  448.5 5.2 %collective-permute-start.57 = (f32[32,128]{1,0:T(8,128)S(1)}, f32[32,128]{1,0:T(8,128)S(1)}, u32[]{:S(2)}, u32[]{:S(2)}) collective-permute-start(f32[32,128]{1,0:T(8,128)S(1)} %pad_maximum_fusion.18), channel_id=1, source_target_pairs={{0,2},{1,3},{2,0},{3,1},{4,6},{5,7},{6,4},{7,5},{8,10},{9,11},{10,... | collective-permute-start | bytes 49160 | tf_op jit(solution)/shard_map/ppermute | solution.py:403
  452.1 53.3 %collective-permute-start.74 = (f32[4,32,512]{2,1,0:T(8,128)S(1)}, f32[4,32,512]{2,1,0:T(8,128)}, u32[]{:S(2)}, u32[]{:S(2)}) collective-permute-start(f32[4,32,512]{2,1,0:T(8,128)S(1)} %get-tuple-element.292), channel_id=1, source_target_pairs={{0,4},{1,5},{2,6},{3,7},{4,0},{5,1},{6,2},{7,3},{8,12},{9,13},{10,... | collective-permute-start | bytes 786440 | tf_op jit(solution)/shard_map/ppermute | solution.py:403
  453.8 6.8 %collective-permute-start.58 = (f32[28,128]{1,0:T(8,128)S(1)}, f32[28,128]{1,0:T(8,128)S(1)}, u32[]{:S(2)}, u32[]{:S(2)}) collective-permute-start(f32[28,128]{1,0:T(8,128)S(1)} %pad_maximum_fusion.19), channel_id=1, source_target_pairs={{0,1},{1,0},{2,3},{3,2},{4,5},{5,4},{6,7},{7,6},{8,9},{9,8},{10,11... | collective-permute-start | bytes 43016 | tf_op jit(solution)/shard_map/ppermute | solution.py:403
  460.7 4.5 collective-permute-start.59
  463.1 13.2 %collective-permute-start.69 = (bf16[2,6,32,256]{3,2,1,0:T(8,128)(2,1)}, bf16[2,6,32,256]{3,2,1,0:T(8,128)(2,1)}, u32[]{:S(2)}, u32[]{:S(2)}) collective-permute-start(bf16[2,6,32,256]{3,2,1,0:T(8,128)(2,1)} %add_convert_fusion.22), channel_id=1, source_target_pairs={{0,1},{1,0},{2,3},{3,2},{4,5},{5,4},{6,7},{7,6},{8,9},{9,8},{10,11... | collective-permute-start | bytes 589832 | tf_op jit(solution)/shard_map/ppermute | solution.py:403
  465.7 5.7 %collective-permute-start.60 = (f32[67,128]{1,0:T(8,128)S(1)}, f32[67,128]{1,0:T(8,128)S(1)}, u32[]{:S(2)}, u32[]{:S(2)}) collective-permute-start(f32[67,128]{1,0:T(8,128)S(1)} %concatenate.107), channel_id=1, source_target_pairs={{0,16},{1,17},{2,18},{3,19},{4,20},{5,21},{6,22},{7,23},{8,24},{9,... | collective-permute-start | bytes 102920 | tf_op jit(solution)/shard_map/ppermute | solution.py:403
  469.0 13.5 %collective-permute-start.64 = (bf16[10,32,256]{2,1,0:T(8,128)(2,1)}, bf16[10,32,256]{2,1,0:T(8,128)(2,1)S(1)}, u32[]{:S(2)}, u32[]{:S(2)}) collective-permute-start(bf16[10,32,256]{2,1,0:T(8,128)(2,1)} %get-tuple-element.290), channel_id=1, source_target_pairs={{0,2},{1,3},{2,0},{3,1},{4,6},{5,7},{6,4},{7,5},{8,10},{9,11},{10,... | collective-permute-start | bytes 491528 | tf_op jit(solution)/shard_map/ppermute | solution.py:403
  470.2 40.4 %collective-permute-start.54 = (bf16[256,1024]{1,0:T(8,128)(2,1)S(1)}, bf16[256,1024]{1,0:T(8,128)(2,1)S(1)}, u32[]{:S(2)}, u32[]{:S(2)}) collective-permute-start(bf16[256,1024]{1,0:T(8,128)(2,1)S(1)} %get-tuple-element.275), channel_id=1, source_target_pairs={{1,0},{0,1},{5,2},{4,3},{3,4},{2,5},{7,6},{6,7},{9,8},{8,9},{13,10... | collective-permute-start | bytes 1572872 | tf_op jit(solution)/shard_map/ppermute | solution.py:403
  471.4 39.2 %collective-permute-start.55 = (bf16[256,1024]{1,0:T(8,128)(2,1)S(1)}, bf16[256,1024]{1,0:T(8,128)(2,1)S(1)}, u32[]{:S(2)}, u32[]{:S(2)}) collective-permute-start(bf16[256,1024]{1,0:T(8,128)(2,1)S(1)} %get-tuple-element.276), channel_id=1, source_target_pairs={{0,0},{1,1},{4,2},{5,3},{2,4},{3,5},{6,6},{7,7},{8,8},{9,9},{12,10... | collective-permute-start | bytes 1572872 | tf_op jit(solution)/shard_map/ppermute | solution.py:403
  477.3 26.6 %collective-permute-start.70 = (bf16[6,32,256]{2,1,0:T(8,128)(2,1)S(1)}, bf16[6,32,256]{2,1,0:T(8,128)(2,1)S(1)}, u32[]{:S(2)}, u32[]{:S(2)}) collective-permute-start(bf16[6,32,256]{2,1,0:T(8,128)(2,1)S(1)} %get-tuple-element.296), channel_id=1, source_target_pairs={{0,2},{1,3},{2,0},{3,1},{4,6},{5,7},{6,4},{7,5},{8,10},{9,11},{10,... | collective-permute-start | bytes 294920 | tf_op jit(solution)/shard_map/ppermute | solution.py:403
  (68 other events, 461.3 us)

commit v3 on v2

--- a/solution.py
+++ b/solution.py
@@ -537,7 +537,9 @@
         ),
         out_shape=out_shape,
         compiler_params=pltpu.CompilerParams(vmem_limit_bytes=VMEM_LIMIT),
-        cost_estimate=pl.CostEstimate(flops=1000, bytes_accessed=1000, transcendentals=0),
+        cost_estimate=pl.CostEstimate(
+            flops=int(flops * 1.5), bytes_accessed=int(moved * 1.5), transcendentals=int(exps * 1.5)
+        ),
     )(meta, *operands)
 
 
@@ -1335,8 +1337,8 @@
     down_pieces = gather_plane(down_first, down_second, mine)
     normal_one, inverse_one, normed = first_norm(meta, own_tokens, embedded, mine, send(away, PAIR), vectors)
     normed_other = send(normed, PAIR)
-    activated, slope = expand(meta, normed, after(normed_other, own_cotangent, down_pieces[0], down_pieces[2]), up_shift, mid_pieces)
-    away, mine = contract(meta, activated, down_pieces)
+    activated, slope = expand(meta, normed, after(normed_other, down_pieces[0], down_pieces[2]), up_shift, mid_pieces)
+    away, mine = contract(meta, after(activated, own_cotangent), down_pieces)
     own_cotangent = after(own_cotangent, mine).reshape(512, 1024)
     result, resid_two, df, sums_two = second_norm(meta, normal_one, mine, send(away, PAIR), own_cotangent, vectors)
 
@@ -1357,25 +1359,27 @@
     dqkv_one, qv_sums_one = attend_back(meta, 0, qkv, mixed_one, grad, lse_one, seg_column, seg_row)
     output = after(output, dqkv_one)
     qkv_terms_one = weigh_qkv(meta, hidden, after(dqkv_one, output), (mixed_one, mixed_two, da, da_other))
-    up_sums_one = add_one(*scatter_one(*up_terms), qkv_terms_one)
+    up_sums_one = add_one(*scatter_one(*after(up_terms, dout)), qkv_terms_one)
     down_sums = add_three(*scatter_three(*down_sums), qkv_terms_one)
     grad = after(dout, up_sums_one, down_sums)
     dqkv_two, qv_sums_two = attend_back(meta, 1, qkv, mixed_two, grad, lse_two, seg_column, seg_row)
     up_sums_two = add_two(*scatter_two(*up_sums_one), dqkv_two)
     down_share = scatter_four(*down_sums, dqkv_two)
-    qkv_terms_two = weigh_qkv(meta, hidden, after(dqkv_two, up_sums_two, down_share))
-    qkv_sums_one = add_one(*scatter_one(*qkv_terms_one), qkv_terms_two)
-    away, mine = qkv_back(meta, (dqkv_one, after(dqkv_two, qkv_terms_two, qkv_sums_one)), qkv_pieces)
-    up_sums_three = add_three(*scatter_three(*up_sums_two), mine)
-    qkv_sums_two = add_one(*scatter_one(*qkv_terms_two), mine)
-    qkv_sums_one = add_two(*scatter_two(*qkv_sums_one), mine)
-    input_low, embed_sums = last_sum(meta, resid_one, mine, send(away, PAIR))
+    away, mine = qkv_back(meta, (dqkv_one, after(dqkv_two, up_sums_two, down_share)), qkv_pieces)
+    received = send(away, PAIR)
+    qkv_terms_two = weigh_qkv(meta, hidden, after(dqkv_two, mine))
+    qkv_sums_one = add_one(*scatter_one(*qkv_terms_one), mine)
+    input_low, embed_sums = last_sum(meta, resid_one, after(mine, qkv_terms_two), received)
     input_grad = give_rows(input_low)
-    qkv_sums_two = add_two(*scatter_two(*qkv_sums_two), input_low)
-    qkv_sums_one = add_three(*scatter_three(*qkv_sums_one), input_low)
+    up_sums_three = add_three(*scatter_three(*up_sums_two), qkv_terms_two)
+    qkv_sums_one = add_two(*scatter_two(*qkv_sums_one), input_low)
+    qkv_sums_two = add_one(*scatter_one(*qkv_terms_two), input_low)
+    qkv_sums_two = add_two(*scatter_two(*qkv_sums_two))
+    qkv_sums_one = add_three(*scatter_three(*qkv_sums_one))
     up_share = scatter_four(*up_sums_three, input_low)
+    qkv_sums_two = add_three(*scatter_three(*qkv_sums_two))
     qkv_share_one = scatter_four(*qkv_sums_one)
-    qkv_share_two = scatter_four(*add_three(*scatter_three(*qkv_sums_two)))
+    qkv_share_two = scatter_four(*after(qkv_sums_two, input_grad))
     qkv_share = jnp.concatenate([qkv_share_one[:6], qkv_share_two], axis=2)
     qv_sums = jnp.concatenate([qv_sums_one[0:2], qv_sums_two[0:2]], axis=1)
 

time: 520 us -> 479 us (0.921)
  starting transfers between devices: 107 us -> 83.2 us
  waiting for transfers between devices: 131 us -> 121 us
    ppermute x75, starting transfers between devices: 107 us -> 83.2 us  [send(): return lax.ppermute(value, AXES, pairs)]
    ppermute x75, waiting for transfers between devices: 131 us -> 121 us  [send(): return lax.ppermute(value, AXES, pairs)]
    unnamed x125 -> x109, local copies, waits for them, and re-layouts: 11.9 us -> 8.21 us
  transfers between devices with their start and end apart: 75 -> 75, of which waited for: 25 -> 28; matrix products, arithmetic and copies ran while one was open for 13% -> 13% of each run, Pallas kernels for 30% -> 33%
where the time goes in v3:
time: 479 us; the launch traced here: 471 us
  Pallas kernels  194 us (41%)
  waiting for transfers between devices  121 us (25%)
  starting transfers between devices  83.2 us (17%)
  other arithmetic  36.6 us (8%)
  local copies, waits for them, and re-layouts  32.4 us (7%)
    pallas_call x19, Pallas kernels, kernel_call(): pl.pallas_call(kernel, grid_spec=pltpu.PrefetchScalarGridSpec(num_scalar_...  194 us
    ppermute x75, waiting for transfers between devices, send(): return lax.ppermute(value, AXES, pairs)  121 us
    ppermute x75, starting transfers between devices, send(): return lax.ppermute(value, AXES, pairs)  83.2 us
    convert_element_type x20, other arithmetic, add_low(): return (a.astype(F32) + b.astype(F32)).astype(BF)  18.6 us
  transfers between devices with their start and end apart: 75, of which 28 were waited for; matrix products, arithmetic and copies ran while one was open for 13% of the time, Pallas kernels for 33%

profile of v3, /device:TPU:0, one launch (start us, length us, event | category | flops | bytes accessed | tf_op | source)
XLA Modules:
  0.0 471.2 jit_solution(1500096199530007472)
XLA Ops:
  4.8 4.1 collective-permute-start.2
  10.2 1.5 collective-permute-start.9
  11.7 2.0 collective-permute-done.9
  13.8 1.5 collective-permute-start.10
  15.4 2.0 collective-permute-done.10
  20.5 1.6 collective-permute-start.12
  24.5 1.6 collective-permute-start.13
  26.7 1.7 collective-permute-done.13
  28.4 2.0 collective-permute-start.14
  30.4 3.6 collective-permute-done.3
  34.1 2.2 collective-permute-start.4
  37.8 1.8 collective-permute-start.15
  39.6 11.0 %collective-permute-done.4 = bf16[10,32,512]{2,1,0:T(8,128)(2,1)} collective-permute-done((bf16[10,32,512]{2,1,0:T(8,128)(2,1)S(1)}, bf16[10,32,512]{2,1,0:T(8,128)(2,1)}, u32[]{:S(2)}, u32[]{:S(2)}) %collective-permute-start.4) | collective-permute-done | bytes 327712 | tf_op jit(solution)/shard_map/ppermute | solution.py:403
  53.6 1.5 collective-permute-start.23
  57.6 10.1 %collective-permute-done.5 = bf16[2,10,32,512]{3,2,1,0:T(8,128)(2,1)} collective-permute-done((bf16[2,10,32,512]{3,2,1,0:T(8,128)(2,1)S(1)}, bf16[2,10,32,512]{3,2,1,0:T(8,128)(2,1)}, u32[]{:S(2)}, u32[]{:S(2)}) %collective-permute-start.5) | collective-permute-done | bytes 655392 | tf_op jit(solution)/shard_map/ppermute | solution.py:403
  68.5 1.5 collective-permute-start.7
  70.0 3.1 collective-permute-done.20.rest_1_
  73.6 14.4 %collective-permute-done.19.rest_3_ = bf16[2,2,208,512]{3,2,1,0:T(8,128)(2,1)S(1)} collective-permute-done((bf16[2,2,208,512]{3,2,1,0:T(8,128)(2,1)S(1)}, bf16[2,2,208,512]{3,2,1,0:T(8,128)(2,1)S(1)}, u32[]{:S(2)}, u32[]{:S(2)}) %collective-permute-start.19) | collective-permute-done | bytes 852000 | tf_op jit(solution)/shard_map/ppermute | solution.py:403
  89.3 4.0 collective-permute-start.16
  95.7 1.6 collective-permute-start.26
  100.9 10.4 %shard_map.280 = (bf16[1024,1024]{1,0:T(8,128)(2,1)}, bf16[3,1024,512]{2,1,0:T(8,128)(2,1)}) custom-call(s32[4]{0:T(128)} %pad_add_fusion.m, bf16[2,272,1024]{2,1,0:T(8,128)(2,1)} %pad_maximum_fusion.2.own_ref.tok_ref, bf16[2,272,1024]{2,1,0:T(8,128)(2,1)} %collective-permute-done.16.other_ref, f32[1,1024]{1,0:T(1,128)} %slice_add_fusion.8.emb_ref, ...), custom_call_target="tpu_custom_call" | custom-call | flops 4831838208 | bytes 15728640 | tf_op jit(solution)/shard_map/pallas_call | solution.py:529
  111.4 8.7 %collective-permute-start.21 = (bf16[2,128,512]{2,1,0:T(8,128)(2,1)S(1)}, bf16[2,128,512]{2,1,0:T(8,128)(2,1)S(1)}, u32[]{:S(2)}, u32[]{:S(2)}) collective-permute-start(bf16[2,128,512]{2,1,0:T(8,128)(2,1)S(1)} %bitcast.292), channel_id=1, source_target_pairs={{0,2},{1,3},{2,0},{3,1},{4,6},{5,7},{6,4},{7,5},{8,10},{9,11},{10,... | collective-permute-start | bytes 786440 | tf_op jit(solution)/shard_map/ppermute | solution.py:403
  120.0 11.8 %shard_map.281 = (bf16[1024,256]{1,0:T(8,128)(2,1)}, f32[2,8,1024]{2,1,0:T(8,128)}) custom-call(s32[4]{0:T(128)} %pad_add_fusion.m, bf16[3,1024,512]{2,1,0:T(8,128)(2,1)} %get-tuple-element.133.q_ref.k_ref.v_ref, bf16[3,1024,512]{2,1,0:T(8,128)(2,1)} %get-tuple-element.133.q_ref.k_ref.v_ref, bf16[3,1024,512]{2,1,0:T(8,128)(2,1)} %get-tuple-element.133.q_ref.k_ref.v_ref, ...), custom_call_target="tpu_custom_call" | custom-call | flops 12884901888 | bytes 7864320 | tf_op jit(solution)/shard_map/pallas_call | solution.py:529
  132.0 11.9 %shard_map.282 = (bf16[1024,256]{1,0:T(8,128)(2,1)}, f32[2,8,1024]{2,1,0:T(8,128)}) custom-call(s32[4]{0:T(128)} %pad_add_fusion.m, bf16[3,1024,512]{2,1,0:T(8,128)(2,1)} %get-tuple-element.133.q_ref.k_ref.v_ref, bf16[3,1024,512]{2,1,0:T(8,128)(2,1)} %get-tuple-element.133.q_ref.k_ref.v_ref, bf16[3,1024,512]{2,1,0:T(8,128)(2,1)} %get-tuple-element.133.q_ref.k_ref.v_ref, ...), custom_call_target="tpu_custom_call" | custom-call | flops 12884901888 | bytes 7864320 | tf_op jit(solution)/shard_map/pallas_call | solution.py:529
  143.9 2.1 collective-permute-done.22
  146.0 7.5 %shard_map.283 = (bf16[512,1024]{1,0:T(8,128)(2,1)}, f32[512,1024]{1,0:T(8,128)}) custom-call(s32[4]{0:T(128)} %pad_add_fusion.m, bf16[1024,256]{1,0:T(8,128)(2,1)} %get-tuple-element.130.x_ref.out_ref.rest_0_, bf16[1024,256]{1,0:T(8,128)(2,1)} %get-tuple-element.136.w_ref.rest_1_.out_ref, bf16[2,2,10,32,512]{4,3,2,1,0:T(8,128)(2,1)} %copy-done.3, ...), custom_call_target="tpu_custom_call" | custom-call | flops 1610612736 | bytes 9437184 | tf_op jit(solution)/shard_map/pallas_call | solution.py:529
  158.0 4.8 %shard_map.284 = (f32[512,1024]{1,0:T(8,128)}, f32[512,128]{1,0:T(8,128)}, bf16[512,1024]{1,0:T(8,128)(2,1)}) custom-call(s32[4]{0:T(128)} %pad_add_fusion.m, bf16[2,272,1024]{2,1,0:T(8,128)(2,1)} %pad_maximum_fusion.2.own_ref.tok_ref, f32[1,1024]{1,0:T(1,128)} %slice_add_fusion.8.emb_ref, f32[512,1024]{1,0:T(8,128)} %get-tuple-element.139.own_ref, ...), custom_call_target="tpu_custom_call" | custom-call | flops 9437184 | bytes 12582912 | tf_op jit(solution)/shard_map/pallas_call | solution.py:529
  163.9 5.5 %collective-permute-start.31 = (bf16[256,1024]{1,0:T(8,128)(2,1)}, bf16[256,1024]{1,0:T(8,128)(2,1)}, u32[]{:S(2)}, u32[]{:S(2)}) collective-permute-start(bf16[256,1024]{1,0:T(8,128)(2,1)} %get-tuple-element.297), channel_id=1, source_target_pairs={{0,0},{1,1},{2,4},{3,5},{4,2},{5,3},{6,6},{7,7},{8,8},{9,9},{10,12... | collective-permute-start | bytes 1572872 | tf_op jit(solution)/shard_map/ppermute | solution.py:403
  174.9 14.7 %collective-permute-done.32 = bf16[256,1024]{1,0:T(8,128)(2,1)} collective-permute-done((bf16[256,1024]{1,0:T(8,128)(2,1)}, bf16[256,1024]{1,0:T(8,128)(2,1)}, u32[]{:S(2)}, u32[]{:S(2)}) %collective-permute-start.32) | collective-permute-done | bytes 524320 | tf_op jit(solution)/shard_map/ppermute | solution.py:403
  189.6 2.3 pad_maximum_fusion.5
  191.9 13.1 %shard_map.285 = (bf16[1024,2048]{1,0:T(8,128)(2,1)}, bf16[1024,2048]{1,0:T(8,128)(2,1)}) custom-call(s32[4]{0:T(128)} %pad_add_fusion.m, bf16[512,1024]{1,0:T(8,128)(2,1)} %get-tuple-element.142.own_ref, bf16[512,1024]{1,0:T(8,128)(2,1)} %collective-permute-done.28.other_ref, f32[1,2048]{1,0:T(1,128)} %bitcast.325, bf16[2,2,10,32,512]{4,3,2,1,0:T(8,128)(2,1)} %copy-done.3, ...), custom_call_target="tpu_custom_call" | custom-call | flops 6442450944 | bytes 22020096 | tf_op jit(solution)/shard_map/pallas_call | solution.py:529
  205.0 11.5 %shard_map.286 = (bf16[512,1024]{1,0:T(8,128)(2,1)}, f32[512,1024]{1,0:T(8,128)}) custom-call(s32[4]{0:T(128)} %pad_add_fusion.m, bf16[1024,2048]{1,0:T(8,128)(2,1)} %get-tuple-element.150.x_ref, bf16[2,2,2,128,512]{4,3,2,1,0:T(8,128)(2,1)} %copy-done.14, bf16[2,2,2,128,512]{4,3,2,1,0:T(8,128)(2,1)} %collective-permute-done.33.rest_1_, ...), custom_call_target="tpu_custom_call" | custom-call | flops 6442450944 | bytes 17301504 | tf_op jit(solution)/shard_map/pallas_call | solution.py:529
  216.6 2.9 collective-permute-done.35.recv_ref
  220.4 6.5 %shard_map.287 = (bf16[512,1024]{1,0:T(8,128)(2,1)}, f32[512,1024]{1,0:T(8,128)}, bf16[512,1024]{1,0:T(8,128)(2,1)}, f32[8,1024]{1,0:T(8,128)}) custom-call(s32[4]{0:T(128)} %pad_add_fusion.m, f32[512,1024]{1,0:T(8,128)} %get-tuple-element.141.normal_ref, f32[512,1024]{1,0:T(8,128)} %get-tuple-element.151.own_ref, bf16[512,1024]{1,0:T(8,128)(2,1)} %copy-done.10, ...), custom_call_target="tpu_custom_call" | custom-call | flops 23592960 | bytes 15728640 | tf_op jit(solution)/shard_map/pallas_call | solution.py:529
  227.1 2.7 collective-permute-done.36.other_ref
  230.9 9.2 %shard_map.288 = (bf16[2,2,2,128,512]{4,3,2,1,0:T(8,128)(2,1)}, bf16[2,2,2,128,512]{4,3,2,1,0:T(8,128)(2,1)}, bf16[2,2,2,128,512]{4,3,2,1,0:T(8,128)(2,1)}, bf16[2,2,2,128,512]{4,3,2,1,0:T(8,128)(2,1)}) custom-call(s32[4]{0:T(128)} %pad_add_fusion.m, bf16[1024,2048]{1,0:T(8,128)(2,1)} %get-tuple-element.150.x_ref, ...), custom_call_target="tpu_custom_call" | custom-call | flops 6442450944 | bytes 15728640 | tf_op jit(solution)/shard_map/pallas_call | solution.py:529
  242.1 18.9 %shard_map.289 = (bf16[1024,2048]{1,0:T(8,128)(2,1)}, bf16[512,1024]{1,0:T(8,128)(2,1)}, f32[512,1024]{1,0:T(8,128)}, f32[8,2048]{1,0:T(8,128)}) custom-call(s32[4]{0:T(128)} %pad_add_fusion.m, bf16[512,1024]{1,0:T(8,128)(2,1)} %get-tuple-element.161.own_ref, bf16[512,1024]{1,0:T(8,128)(2,1)} %copy-done.47, bf16[1024,2048]{1,0:T(8,128)(2,1)} %get-tuple-element.162.slope_ref, ...), custom_call_target="tpu_custom_call" | custom-call | flops 12884901888 | bytes 34603008 | tf_op jit(solution)/shard_map/pallas_call | solution.py:529
  261.1 9.8 %shard_map.290 = (bf16[2,2,8,32,512]{4,3,2,1,0:T(8,128)(2,1)}, bf16[2,2,8,32,512]{4,3,2,1,0:T(8,128)(2,1)}, bf16[2,2,8,32,512]{4,3,2,1,0:T(8,128)(2,1)}, bf16[2,2,8,32,512]{4,3,2,1,0:T(8,128)(2,1)}) custom-call(s32[4]{0:T(128)} %pad_add_fusion.m, bf16[512,1024]{1,0:T(8,128)(2,1)} %get-tuple-element.142.own_ref, ...), custom_call_target="tpu_custom_call" | custom-call | flops 6442450944 | bytes 23592960 | tf_op jit(solution)/shard_map/pallas_call | solution.py:529
  274.2 5.9 %shard_map.291 = (f32[512,1024]{1,0:T(8,128)}, bf16[512,1024]{1,0:T(8,128)(2,1)}, f32[8,1024]{1,0:T(8,128)}) custom-call(s32[4]{0:T(128)} %pad_add_fusion.m, f32[512,1024]{1,0:T(8,128)} %get-tuple-element.170.resid_ref, f32[512,1024]{1,0:T(8,128)} %get-tuple-element.171.own_ref, bf16[512,1024]{1,0:T(8,128)(2,1)} %copy-done.18, ...), custom_call_target="tpu_custom_call" | custom-call | flops 15728640 | bytes 15728640 | tf_op jit(solution)/shard_map/pallas_call | solution.py:529
  281.8 1.5 collective-permute-start.44
  287.6 6.8 %shard_map.292.grad_ref = bf16[1024,512]{1,0:T(8,128)(2,1)} custom-call(s32[4]{0:T(128)} %pad_add_fusion.m, bf16[512,1024]{1,0:T(8,128)(2,1)} %get-tuple-element.174.own_ref.rest_2_, bf16[512,1024]{1,0:T(8,128)(2,1)} %copy-done.7, bf16[2,2,10,32,512]{4,3,2,1,0:T(8,128)(2,1)} %copy-done.3, ...), custom_call_target="tpu_custom_call" | custom-call | flops 1610612736 | bytes 6291456 | tf_op jit(solution)/shard_map/pallas_call | solution.py:529
  296.0 3.8 collective-permute-start.47
  300.0 2.6 collective-permute-start.41
  305.0 17.8 %shard_map.293 = (bf16[3,1024,256]{2,1,0:T(8,128)(2,1)}, f32[8,256]{1,0:T(8,128)}) custom-call(s32[4]{0:T(128)} %pad_add_fusion.m, bf16[3,1024,512]{2,1,0:T(8,128)(2,1)} %get-tuple-element.133.q_ref.k_ref.v_ref, bf16[3,1024,512]{2,1,0:T(8,128)(2,1)} %get-tuple-element.133.q_ref.k_ref.v_ref, bf16[3,1024,512]{2,1,0:T(8,128)(2,1)} %get-tuple-element.133.q_ref.k_ref.v_ref, ...), custom_call_target="tpu_custom_call" | custom-call | flops 32212254720 | bytes 12582912 | tf_op jit(solution)/shard_map/pallas_call | solution.py:529
  323.4 4.5 collective-permute-done.41
  329.1 8.7 %shard_map.294 = (bf16[2,2,10,32,256]{4,3,2,1,0:T(8,128)(2,1)}, bf16[2,2,10,32,256]{4,3,2,1,0:T(8,128)(2,1)}, bf16[2,2,10,32,256]{4,3,2,1,0:T(8,128)(2,1)}, bf16[2,2,10,32,256]{4,3,2,1,0:T(8,128)(2,1)}) custom-call(s32[4]{0:T(128)} %pad_add_fusion.m, bf16[1024,1024]{1,0:T(8,128)(2,1)} %get-tuple-element.185.x_ref, ...), custom_call_target="tpu_custom_call" | custom-call | flops 3221225472 | bytes 12582912 | tf_op jit(solution)/shard_map/pallas_call | solution.py:529
  337.8 1.5 collective-permute-start.59
  341.3 2.7 collective-permute-start.50
  348.2 18.2 %shard_map.295 = (bf16[3,1024,256]{2,1,0:T(8,128)(2,1)}, f32[8,256]{1,0:T(8,128)}) custom-call(s32[4]{0:T(128)} %pad_add_fusion.m, bf16[3,1024,512]{2,1,0:T(8,128)(2,1)} %get-tuple-element.133.q_ref.k_ref.v_ref, bf16[3,1024,512]{2,1,0:T(8,128)(2,1)} %get-tuple-element.133.q_ref.k_ref.v_ref, bf16[3,1024,512]{2,1,0:T(8,128)(2,1)} %get-tuple-element.133.q_ref.k_ref.v_ref, ...), custom_call_target="tpu_custom_call" | custom-call | flops 32212254720 | bytes 12582912 | tf_op jit(solution)/shard_map/pallas_call | solution.py:529
  371.9 10.2 %shard_map.296 = (bf16[512,1024]{1,0:T(8,128)(2,1)}, f32[512,1024]{1,0:T(8,128)}) custom-call(s32[4]{0:T(128)} %pad_add_fusion.m, bf16[3,1024,256]{2,1,0:T(8,128)(2,1)} %get-tuple-element.186.d_ref, bf16[3,1024,256]{2,1,0:T(8,128)(2,1)} %get-tuple-element.204.e_ref.d_ref, bf16[2,2,208,512]{3,2,1,0:T(8,128)(2,1)} %copy-done.19, ...), custom_call_target="tpu_custom_call" | custom-call | flops 4831838208 | bytes 14155776 | tf_op jit(solution)/shard_map/pallas_call | solution.py:529
  382.2 6.6 %shard_map.297 = (bf16[2,2,6,32,256]{4,3,2,1,0:T(8,128)(2,1)}, bf16[2,2,6,32,256]{4,3,2,1,0:T(8,128)(2,1)}, bf16[2,2,6,32,256]{4,3,2,1,0:T(8,128)(2,1)}, bf16[2,2,6,32,256]{4,3,2,1,0:T(8,128)(2,1)}) custom-call(s32[4]{0:T(128)} %pad_add_fusion.m, bf16[1024,1024]{1,0:T(8,128)(2,1)} %get-tuple-element.185.x_ref, ...), custom_call_target="tpu_custom_call" | custom-call | flops 3221225472 | bytes 12582912 | tf_op jit(solution)/shard_map/pallas_call | solution.py:529
  388.8 1.5 collective-permute-start.65
  396.8 4.4 shard_map.298
  402.2 2.1 fusion.60
  404.3 5.7 %collective-permute-done.73 = bf16[8,32,512]{2,1,0:T(8,128)(2,1)S(1)} collective-permute-done((bf16[8,32,512]{2,1,0:T(8,128)(2,1)}, bf16[8,32,512]{2,1,0:T(8,128)(2,1)S(1)}, u32[]{:S(2)}, u32[]{:S(2)}) %collective-permute-start.73) | collective-permute-done | bytes 262176 | tf_op jit(solution)/shard_map/ppermute | solution.py:403
  411.5 1.8 fusion.22
  413.4 2.8 collective-permute-done.55
  418.1 2.9 collective-permute-done.56
  422.1 1.8 fusion.21
  426.7 3.8 collective-permute-done.58
  436.5 1.7 add_convert_fusion.22
  441.4 12.6 %collective-permute-done.63 = bf16[2,10,32,256]{3,2,1,0:T(8,128)(2,1)S(1)} collective-permute-done((bf16[2,10,32,256]{3,2,1,0:T(8,128)(2,1)}, bf16[2,10,32,256]{3,2,1,0:T(8,128)(2,1)S(1)}, u32[]{:S(2)}, u32[]{:S(2)}) %collective-permute-start.63) | collective-permute-done | bytes 327712 | tf_op jit(solution)/shard_map/ppermute | solution.py:403
  454.2 3.9 collective-permute-done.69
  459.4 7.5 %collective-permute-done.64 = bf16[10,32,256]{2,1,0:T(8,128)(2,1)S(1)} collective-permute-done((bf16[10,32,256]{2,1,0:T(8,128)(2,1)S(1)}, bf16[10,32,256]{2,1,0:T(8,128)(2,1)S(1)}, u32[]{:S(2)}, u32[]{:S(2)}) %collective-permute-start.64) | collective-permute-done | bytes 163872 | tf_op jit(solution)/shard_map/ppermute | solution.py:403
  (406 shorter events, 98.2 us)
Async XLA Ops:
  4.0 22.0 %collective-permute-start = (bf16[4,32,512]{2,1,0:T(8,128)(2,1)S(1)}, bf16[4,32,512]{2,1,0:T(8,128)(2,1)S(1)}, u32[]{:S(2)}, u32[]{:S(2)}) collective-permute-start(bf16[4,32,512]{2,1,0:T(8,128)(2,1)S(1)} %bitcast.310), channel_id=1, source_target_pairs={{0,4},{1,5},{2,6},{3,7},{4,0},{5,1},{6,2},{7,3},{8,12},{9,13},{10,... | collective-permute-start | bytes 393224 | tf_op jit(solution)/shard_map/ppermute | solution.py:403
  4.8 14.1 %collective-permute-start.2 = (bf16[208,512]{1,0:T(8,128)(2,1)S(1)}, bf16[208,512]{1,0:T(8,128)(2,1)S(1)}, u32[]{:S(2)}, u32[]{:S(2)}) collective-permute-start(bf16[208,512]{1,0:T(8,128)(2,1)S(1)} %concatenate.94), channel_id=1, source_target_pairs={{0,2},{1,3},{2,0},{3,1},{4,6},{5,7},{6,4},{7,5},{8,10},{9,11},{10,... | collective-permute-start | bytes 638984 | tf_op jit(solution)/shard_map/ppermute | solution.py:403
  20.5 4.0 collective-permute-start.12
  22.2 11.8 %collective-permute-start.3 = (bf16[2,208,512]{2,1,0:T(8,128)(2,1)S(1)}, bf16[2,208,512]{2,1,0:T(8,128)(2,1)S(1)}, u32[]{:S(2)}, u32[]{:S(2)}) collective-permute-start(bf16[2,208,512]{2,1,0:T(8,128)(2,1)S(1)} %pad_maximum_fusion.12), channel_id=1, source_target_pairs={{0,1},{1,0},{2,3},{3,2},{4,5},{5,4},{6,7},{7,6},{8,9},{9,8},{10,11... | collective-permute-start | bytes 1277960 | tf_op jit(solution)/shard_map/ppermute | solution.py:403
  24.5 3.9 collective-permute-start.13
  26.1 26.2 %collective-permute-start.17 = (bf16[2,208,512]{2,1,0:T(8,128)(2,1)S(1)}, bf16[2,208,512]{2,1,0:T(8,128)(2,1)S(1)}, u32[]{:S(2)}, u32[]{:S(2)}) collective-permute-start(bf16[2,208,512]{2,1,0:T(8,128)(2,1)S(1)} %pad_maximum_fusion.12), channel_id=1, source_target_pairs={{0,8},{1,9},{2,10},{3,11},{4,12},{5,13},{6,14},{7,15},{8,0},{9,1},... | collective-permute-start | bytes 1277960 | tf_op jit(solution)/shard_map/ppermute | solution.py:403
  28.4 9.4 %collective-permute-start.14 = (f32[2,1024]{1,0:T(2,128)S(1)}, f32[2,1024]{1,0:T(2,128)S(1)}, u32[]{:S(2)}, u32[]{:S(2)}) collective-permute-start(f32[2,1024]{1,0:T(2,128)S(1)} %slice.665), channel_id=1, source_target_pairs={{0,2},{1,3},{2,0},{3,1},{4,6},{5,7},{6,4},{7,5},{8,10},{9,11},{10,... | collective-permute-start | bytes 24584 | tf_op jit(solution)/shard_map/ppermute | solution.py:403
  34.1 16.6 %collective-permute-start.4 = (bf16[10,32,512]{2,1,0:T(8,128)(2,1)S(1)}, bf16[10,32,512]{2,1,0:T(8,128)(2,1)}, u32[]{:S(2)}, u32[]{:S(2)}) collective-permute-start(bf16[10,32,512]{2,1,0:T(8,128)(2,1)S(1)} %pad_maximum_fusion.13), channel_id=1, source_target_pairs={{0,2},{1,3},{2,0},{3,1},{4,6},{5,7},{6,4},{7,5},{8,10},{9,11},{10,... | collective-permute-start | bytes 983048 | tf_op jit(solution)/shard_map/ppermute | solution.py:403
  36.3 16.1 %collective-permute-start.18 = (bf16[2,208,512]{2,1,0:T(8,128)(2,1)S(1)}, bf16[2,208,512]{2,1,0:T(8,128)(2,1)}, u32[]{:S(2)}, u32[]{:S(2)}) collective-permute-start(bf16[2,208,512]{2,1,0:T(8,128)(2,1)S(1)} %collective-permute-done.3), channel_id=1, source_target_pairs={{0,16},{1,17},{2,18},{3,19},{4,20},{5,21},{6,22},{7,23},{8,24},{9,... | collective-permute-start | bytes 1277960 | tf_op jit(solution)/shard_map/ppermute | solution.py:403
  37.8 15.2 %collective-permute-start.15 = (f32[1,1024]{1,0:T(1,128)S(1)}, f32[1,1024]{1,0:T(1,128)S(1)}, u32[]{:S(2)}, u32[]{:S(2)}) collective-permute-start(f32[1,1024]{1,0:T(1,128)S(1)} %slice.667), channel_id=1, source_target_pairs={{0,1},{1,0},{2,3},{3,2},{4,5},{5,4},{6,7},{7,6},{8,9},{9,8},{10,11... | collective-permute-start | bytes 12296 | tf_op jit(solution)/shard_map/ppermute | solution.py:403
  51.8 15.9 %collective-permute-start.5 = (bf16[2,10,32,512]{3,2,1,0:T(8,128)(2,1)S(1)}, bf16[2,10,32,512]{3,2,1,0:T(8,128)(2,1)}, u32[]{:S(2)}, u32[]{:S(2)}) collective-permute-start(bf16[2,10,32,512]{3,2,1,0:T(8,128)(2,1)S(1)} %pad_maximum_fusion.10), channel_id=1, source_target_pairs={{0,1},{1,0},{2,3},{3,2},{4,5},{5,4},{6,7},{7,6},{8,9},{9,8},{10,11... | collective-permute-start | bytes 1966088 | tf_op jit(solution)/shard_map/ppermute | solution.py:403
  52.5 20.7 %collective-permute-start.20 = (bf16[2,2,208,512]{3,2,1,0:T(8,128)(2,1)S(1)}, bf16[2,2,208,512]{3,2,1,0:T(8,128)(2,1)S(1)}, u32[]{:S(2)}, u32[]{:S(2)}) collective-permute-start(bf16[2,2,208,512]{3,2,1,0:T(8,128)(2,1)S(1)} %pad_maximum_fusion.8.rest_0_), channel_id=1, source_target_pairs={{0,16},{1,17},{2,18},{3,19},{4,20},{5,21},{6,22},{7,23},{8,24},{9,... | collective-permute-start | bytes 2555912 | tf_op jit(solution)/shard_map/ppermute | solution.py:403
  53.6 40.8 %collective-permute-start.23 = (bf16[2,10,32,512]{3,2,1,0:T(8,128)(2,1)S(1)}, bf16[2,10,32,512]{3,2,1,0:T(8,128)(2,1)}, u32[]{:S(2)}, u32[]{:S(2)}) collective-permute-start(bf16[2,10,32,512]{3,2,1,0:T(8,128)(2,1)S(1)} %pad_maximum_fusion.10), channel_id=1, source_target_pairs={{0,8},{1,9},{2,10},{3,11},{4,12},{5,13},{6,14},{7,15},{8,0},{9,1},... | collective-permute-start | bytes 1966088 | tf_op jit(solution)/shard_map/ppermute | solution.py:403
  56.2 31.8 %collective-permute-start.19 = (bf16[2,2,208,512]{3,2,1,0:T(8,128)(2,1)S(1)}, bf16[2,2,208,512]{3,2,1,0:T(8,128)(2,1)S(1)}, u32[]{:S(2)}, u32[]{:S(2)}) collective-permute-start(bf16[2,2,208,512]{3,2,1,0:T(8,128)(2,1)S(1)} %pad_maximum_fusion.9.rest_2_), channel_id=1, source_target_pairs={{0,8},{1,9},{2,10},{3,11},{4,12},{5,13},{6,14},{7,15},{8,0},{9,1},... | collective-permute-start | bytes 2555912 | tf_op jit(solution)/shard_map/ppermute | solution.py:403
  67.8 20.3 %collective-permute-start.6 = (bf16[272,1024]{1,0:T(8,128)(2,1)S(1)}, bf16[272,1024]{1,0:T(8,128)(2,1)S(1)}, u32[]{:S(2)}, u32[]{:S(2)}) collective-permute-start(bf16[272,1024]{1,0:T(8,128)(2,1)S(1)} %get-tuple-element.283), channel_id=1, source_target_pairs={{0,0},{1,1},{2,4},{3,5},{4,2},{5,3},{6,6},{7,7},{8,8},{9,9},{10,12... | collective-permute-start | bytes 1671176 | tf_op jit(solution)/shard_map/ppermute | solution.py:403
  68.5 19.6 %collective-permute-start.7 = (bf16[272,1024]{1,0:T(8,128)(2,1)S(1)}, bf16[272,1024]{1,0:T(8,128)(2,1)S(1)}, u32[]{:S(2)}, u32[]{:S(2)}) collective-permute-start(bf16[272,1024]{1,0:T(8,128)(2,1)S(1)} %get-tuple-element.284), channel_id=1, source_target_pairs={{0,1},{1,0},{2,5},{3,4},{4,3},{5,2},{6,7},{7,6},{8,9},{9,8},{10,13... | collective-permute-start | bytes 1671176 | tf_op jit(solution)/shard_map/ppermute | solution.py:403
  73.1 21.3 %collective-permute-start.24 = (bf16[2,10,32,512]{3,2,1,0:T(8,128)(2,1)}, bf16[2,10,32,512]{3,2,1,0:T(8,128)(2,1)S(1)}, u32[]{:S(2)}, u32[]{:S(2)}) collective-permute-start(bf16[2,10,32,512]{3,2,1,0:T(8,128)(2,1)} %collective-permute-done.5), channel_id=1, source_target_pairs={{0,16},{1,17},{2,18},{3,19},{4,20},{5,21},{6,22},{7,23},{8,24},{9,... | collective-permute-start | bytes 1966088 | tf_op jit(solution)/shard_map/ppermute | solution.py:403
  89.3 9.8 %collective-permute-start.16 = (bf16[2,272,1024]{2,1,0:T(8,128)(2,1)}, bf16[2,272,1024]{2,1,0:T(8,128)(2,1)}, u32[]{:S(2)}, u32[]{:S(2)}) collective-permute-start(bf16[2,272,1024]{2,1,0:T(8,128)(2,1)} %pad_maximum_fusion.2.own_ref.tok_ref), channel_id=1, source_target_pairs={{0,4},{1,5},{2,6},{3,7},{4,0},{5,1},{6,2},{7,3},{8,12},{9,13},{10,... | collective-permute-start | bytes 3342344 | tf_op jit(solution)/shard_map/ppermute | solution.py:403
  95.7 50.3 %collective-permute-start.26 = (bf16[2,2,10,32,512]{4,3,2,1,0:T(8,128)(2,1)S(1)}, bf16[2,2,10,32,512]{4,3,2,1,0:T(8,128)(2,1)}, u32[]{:S(2)}, u32[]{:S(2)}) collective-permute-start(bf16[2,2,10,32,512]{4,3,2,1,0:T(8,128)(2,1)S(1)} %pad_maximum_fusion.1.rest_2_.rest_6_), channel_id=1, source_target_pairs={{0,8},{1,9},{2,10},{3,11},{4,12},{5,13},{6,14},{7,15},{8,0},{9,1},... | collective-permute-start | bytes 3932168 | tf_op jit(solution)/shard_map/ppermute | solution.py:403
  98.5 47.5 %collective-permute-start.25 = (bf16[2,2,10,32,512]{4,3,2,1,0:T(8,128)(2,1)S(1)}, bf16[2,2,10,32,512]{4,3,2,1,0:T(8,128)(2,1)}, u32[]{:S(2)}, u32[]{:S(2)}) collective-permute-start(bf16[2,2,10,32,512]{4,3,2,1,0:T(8,128)(2,1)S(1)} %pad_maximum_fusion.rest_0_.rest_4_), channel_id=1, source_target_pairs={{0,16},{1,17},{2,18},{3,19},{4,20},{5,21},{6,22},{7,23},{8,24},{9,... | collective-permute-start | bytes 3932168 | tf_op jit(solution)/shard_map/ppermute | solution.py:403
  111.4 20.5 %collective-permute-start.21 = (bf16[2,128,512]{2,1,0:T(8,128)(2,1)S(1)}, bf16[2,128,512]{2,1,0:T(8,128)(2,1)S(1)}, u32[]{:S(2)}, u32[]{:S(2)}) collective-permute-start(bf16[2,128,512]{2,1,0:T(8,128)(2,1)S(1)} %bitcast.292), channel_id=1, source_target_pairs={{0,2},{1,3},{2,0},{3,1},{4,6},{5,7},{6,4},{7,5},{8,10},{9,11},{10,... | collective-permute-start | bytes 786440 | tf_op jit(solution)/shard_map/ppermute | solution.py:403
  131.9 14.0 %collective-permute-start.22 = (bf16[2,2,128,512]{3,2,1,0:T(8,128)(2,1)S(1)}, bf16[2,2,128,512]{3,2,1,0:T(8,128)(2,1)}, u32[]{:S(2)}, u32[]{:S(2)}) collective-permute-start(bf16[2,2,128,512]{3,2,1,0:T(8,128)(2,1)S(1)} %pad_maximum_fusion.11), channel_id=1, source_target_pairs={{0,1},{1,0},{2,3},{3,2},{4,5},{5,4},{6,7},{7,6},{8,9},{9,8},{10,11... | collective-permute-start | bytes 1572872 | tf_op jit(solution)/shard_map/ppermute | solution.py:403
  153.6 16.1 %collective-permute-start.29 = (bf16[2,2,128,512]{3,2,1,0:T(8,128)(2,1)S(1)}, bf16[2,2,128,512]{3,2,1,0:T(8,128)(2,1)S(1)}, u32[]{:S(2)}, u32[]{:S(2)}) collective-permute-start(bf16[2,2,128,512]{3,2,1,0:T(8,128)(2,1)S(1)} %pad_maximum_fusion.11), channel_id=1, source_target_pairs={{0,8},{1,9},{2,10},{3,11},{4,12},{5,13},{6,14},{7,15},{8,0},{9,1},... | collective-permute-start | bytes 1572872 | tf_op jit(solution)/shard_map/ppermute | solution.py:403
  154.3 15.3 %collective-permute-start.30 = (bf16[2,2,128,512]{3,2,1,0:T(8,128)(2,1)}, bf16[2,2,128,512]{3,2,1,0:T(8,128)(2,1)S(1)}, u32[]{:S(2)}, u32[]{:S(2)}) collective-permute-start(bf16[2,2,128,512]{3,2,1,0:T(8,128)(2,1)} %collective-permute-done.22), channel_id=1, source_target_pairs={{0,16},{1,17},{2,18},{3,19},{4,20},{5,21},{6,22},{7,23},{8,24},{9,... | collective-permute-start | bytes 1572872 | tf_op jit(solution)/shard_map/ppermute | solution.py:403
  162.8 29.1 %collective-permute-start.28 = (bf16[512,1024]{1,0:T(8,128)(2,1)}, bf16[512,1024]{1,0:T(8,128)(2,1)}, u32[]{:S(2)}, u32[]{:S(2)}) collective-permute-start(bf16[512,1024]{1,0:T(8,128)(2,1)} %get-tuple-element.142.own_ref), channel_id=1, source_target_pairs={{0,4},{1,5},{2,6},{3,7},{4,0},{5,1},{6,2},{7,3},{8,12},{9,13},{10,... | collective-permute-start | bytes 3145736 | tf_op jit(solution)/shard_map/ppermute | solution.py:403
  163.9 11.1 %collective-permute-start.31 = (bf16[256,1024]{1,0:T(8,128)(2,1)}, bf16[256,1024]{1,0:T(8,128)(2,1)}, u32[]{:S(2)}, u32[]{:S(2)}) collective-permute-start(bf16[256,1024]{1,0:T(8,128)(2,1)} %get-tuple-element.297), channel_id=1, source_target_pairs={{0,0},{1,1},{2,4},{3,5},{4,2},{5,3},{6,6},{7,7},{8,8},{9,9},{10,12... | collective-permute-start | bytes 1572872 | tf_op jit(solution)/shard_map/ppermute | solution.py:403
  169.4 20.2 %collective-permute-start.32 = (bf16[256,1024]{1,0:T(8,128)(2,1)}, bf16[256,1024]{1,0:T(8,128)(2,1)}, u32[]{:S(2)}, u32[]{:S(2)}) collective-permute-start(bf16[256,1024]{1,0:T(8,128)(2,1)} %get-tuple-element.298), channel_id=1, source_target_pairs={{0,1},{1,0},{2,5},{3,4},{4,3},{5,2},{6,7},{7,6},{8,9},{9,8},{10,13... | collective-permute-start | bytes 1572872 | tf_op jit(solution)/shard_map/ppermute | solution.py:403
  171.0 34.0 %collective-permute-start.34 = (bf16[2,2,2,128,512]{4,3,2,1,0:T(8,128)(2,1)S(1)}, bf16[2,2,2,128,512]{4,3,2,1,0:T(8,128)(2,1)}, u32[]{:S(2)}, u32[]{:S(2)}) collective-permute-start(bf16[2,2,2,128,512]{4,3,2,1,0:T(8,128)(2,1)S(1)} %pad_maximum_fusion.4.rest_2_), channel_id=1, source_target_pairs={{0,8},{1,9},{2,10},{3,11},{4,12},{5,13},{6,14},{7,15},{8,0},{9,1},... | collective-permute-start | bytes 3145736 | tf_op jit(solution)/shard_map/ppermute | solution.py:403
  173.6 31.4 %collective-permute-start.33 = (bf16[2,2,2,128,512]{4,3,2,1,0:T(8,128)(2,1)S(1)}, bf16[2,2,2,128,512]{4,3,2,1,0:T(8,128)(2,1)}, u32[]{:S(2)}, u32[]{:S(2)}) collective-permute-start(bf16[2,2,2,128,512]{4,3,2,1,0:T(8,128)(2,1)S(1)} %pad_maximum_fusion.3.rest_0_), channel_id=1, source_target_pairs={{0,16},{1,17},{2,18},{3,19},{4,20},{5,21},{6,22},{7,23},{8,24},{9,... | collective-permute-start | bytes 3145736 | tf_op jit(solution)/shard_map/ppermute | solution.py:403
  240.1 30.8 %collective-permute-start.38 = (bf16[2,2,2,128,512]{4,3,2,1,0:T(8,128)(2,1)}, bf16[2,2,2,128,512]{4,3,2,1,0:T(8,128)(2,1)S(1)}, u32[]{:S(2)}, u32[]{:S(2)}) collective-permute-start(bf16[2,2,2,128,512]{4,3,2,1,0:T(8,128)(2,1)} %get-tuple-element.160), channel_id=1, source_target_pairs={{0,8},{1,9},{2,10},{3,11},{4,12},{5,13},{6,14},{7,15},{8,0},{9,1},... | collective-permute-start | bytes 3145736 | tf_op jit(solution)/shard_map/ppermute | solution.py:403
  241.5 30.5 %collective-permute-start.37 = (bf16[2,2,2,128,512]{4,3,2,1,0:T(8,128)(2,1)}, bf16[2,2,2,128,512]{4,3,2,1,0:T(8,128)(2,1)S(1)}, u32[]{:S(2)}, u32[]{:S(2)}) collective-permute-start(bf16[2,2,2,128,512]{4,3,2,1,0:T(8,128)(2,1)} %get-tuple-element.159), channel_id=1, source_target_pairs={{0,16},{1,17},{2,18},{3,19},{4,20},{5,21},{6,22},{7,23},{8,24},{9,... | collective-permute-start | bytes 3145736 | tf_op jit(solution)/shard_map/ppermute | solution.py:403
  261.0 12.3 %collective-permute-start.39 = (bf16[512,1024]{1,0:T(8,128)(2,1)}, bf16[512,1024]{1,0:T(8,128)(2,1)S(1)}, u32[]{:S(2)}, u32[]{:S(2)}) collective-permute-start(bf16[512,1024]{1,0:T(8,128)(2,1)} %get-tuple-element.172), channel_id=1, source_target_pairs={{0,4},{1,5},{2,6},{3,7},{4,0},{5,1},{6,2},{7,3},{8,12},{9,13},{10,... | collective-permute-start | bytes 3145736 | tf_op jit(solution)/shard_map/ppermute | solution.py:403
  280.1 6.5 %collective-permute-start.40 = (bf16[512,1024]{1,0:T(8,128)(2,1)}, bf16[512,1024]{1,0:T(8,128)(2,1)S(1)}, u32[]{:S(2)}, u32[]{:S(2)}) collective-permute-start(bf16[512,1024]{1,0:T(8,128)(2,1)} %get-tuple-element.174.own_ref.rest_2_), channel_id=1, source_target_pairs={{0,4},{1,5},{2,6},{3,7},{4,0},{5,1},{6,2},{7,3},{8,12},{9,13},{10,... | collective-permute-start | bytes 3145736 | tf_op jit(solution)/shard_map/ppermute | solution.py:403
  281.8 14.1 %collective-permute-start.44 = (bf16[2,2,128,512]{3,2,1,0:T(8,128)(2,1)}, bf16[2,2,128,512]{3,2,1,0:T(8,128)(2,1)S(1)}, u32[]{:S(2)}, u32[]{:S(2)}) collective-permute-start(bf16[2,2,128,512]{3,2,1,0:T(8,128)(2,1)} %get-tuple-element.275), channel_id=1, source_target_pairs={{0,16},{1,17},{2,18},{3,19},{4,20},{5,21},{6,22},{7,23},{8,24},{9,... | collective-permute-start | bytes 1572872 | tf_op jit(solution)/shard_map/ppermute | solution.py:403
  284.9 14.9 %collective-permute-start.43 = (bf16[2,2,128,512]{3,2,1,0:T(8,128)(2,1)}, bf16[2,2,128,512]{3,2,1,0:T(8,128)(2,1)S(1)}, u32[]{:S(2)}, u32[]{:S(2)}) collective-permute-start(bf16[2,2,128,512]{3,2,1,0:T(8,128)(2,1)} %get-tuple-element.277), channel_id=1, source_target_pairs={{0,8},{1,9},{2,10},{3,11},{4,12},{5,13},{6,14},{7,15},{8,0},{9,1},... | collective-permute-start | bytes 1572872 | tf_op jit(solution)/shard_map/ppermute | solution.py:403
  296.0 44.1 %collective-permute-start.47 = (bf16[2,2,128,512]{3,2,1,0:T(8,128)(2,1)S(1)}, bf16[2,2,128,512]{3,2,1,0:T(8,128)(2,1)}, u32[]{:S(2)}, u32[]{:S(2)}) collective-permute-start(bf16[2,2,128,512]{3,2,1,0:T(8,128)(2,1)S(1)} %add_convert_fusion.6), channel_id=1, source_target_pairs={{0,1},{1,0},{2,3},{3,2},{4,5},{5,4},{6,7},{7,6},{8,9},{9,8},{10,11... | collective-permute-start | bytes 1572872 | tf_op jit(solution)/shard_map/ppermute | solution.py:403
  300.0 27.9 %collective-permute-start.41 = (bf16[256,1024]{1,0:T(8,128)(2,1)S(1)}, bf16[256,1024]{1,0:T(8,128)(2,1)S(1)}, u32[]{:S(2)}, u32[]{:S(2)}) collective-permute-start(bf16[256,1024]{1,0:T(8,128)(2,1)S(1)} %get-tuple-element.295), channel_id=1, source_target_pairs={{1,0},{0,1},{5,2},{4,3},{3,4},{2,5},{7,6},{6,7},{9,8},{8,9},{13,10... | collective-permute-start | bytes 1572872 | tf_op jit(solution)/shard_map/ppermute | solution.py:403
  302.7 25.3 %collective-permute-start.42 = (bf16[256,1024]{1,0:T(8,128)(2,1)S(1)}, bf16[256,1024]{1,0:T(8,128)(2,1)S(1)}, u32[]{:S(2)}, u32[]{:S(2)}) collective-permute-start(bf16[256,1024]{1,0:T(8,128)(2,1)S(1)} %get-tuple-element.296), channel_id=1, source_target_pairs={{0,0},{1,1},{4,2},{5,3},{2,4},{3,5},{6,6},{7,7},{8,8},{9,9},{12,10... | collective-permute-start | bytes 1572872 | tf_op jit(solution)/shard_map/ppermute | solution.py:403
  303.3 40.6 %collective-permute-start.46 = (bf16[2,2,8,32,512]{4,3,2,1,0:T(8,128)(2,1)}, bf16[2,2,8,32,512]{4,3,2,1,0:T(8,128)(2,1)S(1)}, u32[]{:S(2)}, u32[]{:S(2)}) collective-permute-start(bf16[2,2,8,32,512]{4,3,2,1,0:T(8,128)(2,1)} %get-tuple-element.194), channel_id=1, source_target_pairs={{0,8},{1,9},{2,10},{3,11},{4,12},{5,13},{6,14},{7,15},{8,0},{9,1},... | collective-permute-start | bytes 3145736 | tf_op jit(solution)/shard_map/ppermute | solution.py:403
  304.1 41.9 %collective-permute-start.45 = (bf16[2,2,8,32,512]{4,3,2,1,0:T(8,128)(2,1)}, bf16[2,2,8,32,512]{4,3,2,1,0:T(8,128)(2,1)S(1)}, u32[]{:S(2)}, u32[]{:S(2)}) collective-permute-start(bf16[2,2,8,32,512]{4,3,2,1,0:T(8,128)(2,1)} %get-tuple-element.192), channel_id=1, source_target_pairs={{0,16},{1,17},{2,18},{3,19},{4,20},{5,21},{6,22},{7,23},{8,24},{9,... | collective-permute-start | bytes 3145736 | tf_op jit(solution)/shard_map/ppermute | solution.py:403
  337.8 52.5 %collective-permute-start.59 = (bf16[2,2,10,32,256]{4,3,2,1,0:T(8,128)(2,1)}, bf16[2,2,10,32,256]{4,3,2,1,0:T(8,128)(2,1)S(1)}, u32[]{:S(2)}, u32[]{:S(2)}) collective-permute-start(bf16[2,2,10,32,256]{4,3,2,1,0:T(8,128)(2,1)} %get-tuple-element.188), channel_id=1, source_target_pairs={{0,16},{1,17},{2,18},{3,19},{4,20},{5,21},{6,22},{7,23},{8,24},{9,... | collective-permute-start | bytes 1966088 | tf_op jit(solution)/shard_map/ppermute | solution.py:403
  339.4 52.6 %collective-permute-start.60 = (bf16[2,2,10,32,256]{4,3,2,1,0:T(8,128)(2,1)}, bf16[2,2,10,32,256]{4,3,2,1,0:T(8,128)(2,1)S(1)}, u32[]{:S(2)}, u32[]{:S(2)}) collective-permute-start(bf16[2,2,10,32,256]{4,3,2,1,0:T(8,128)(2,1)} %get-tuple-element.190), channel_id=1, source_target_pairs={{0,8},{1,9},{2,10},{3,11},{4,12},{5,13},{6,14},{7,15},{8,0},{9,1},... | collective-permute-start | bytes 1966088 | tf_op jit(solution)/shard_map/ppermute | solution.py:403
  341.3 25.9 %collective-permute-start.50 = (bf16[2,128,512]{2,1,0:T(8,128)(2,1)S(1)}, bf16[2,128,512]{2,1,0:T(8,128)(2,1)S(1)}, u32[]{:S(2)}, u32[]{:S(2)}) collective-permute-start(bf16[2,128,512]{2,1,0:T(8,128)(2,1)S(1)} %get-tuple-element.291), channel_id=1, source_target_pairs={{0,2},{1,3},{2,0},{3,1},{4,6},{5,7},{6,4},{7,5},{8,10},{9,11},{10,... | collective-permute-start | bytes 786440 | tf_op jit(solution)/shard_map/ppermute | solution.py:403
  345.1 24.3 %collective-permute-start.49 = (bf16[2,8,32,512]{3,2,1,0:T(8,128)(2,1)}, bf16[2,8,32,512]{3,2,1,0:T(8,128)(2,1)}, u32[]{:S(2)}, u32[]{:S(2)}) collective-permute-start(bf16[2,8,32,512]{3,2,1,0:T(8,128)(2,1)} %get-tuple-element.271), channel_id=1, source_target_pairs={{0,16},{1,17},{2,18},{3,19},{4,20},{5,21},{6,22},{7,23},{8,24},{9,... | collective-permute-start | bytes 1572872 | tf_op jit(solution)/shard_map/ppermute | solution.py:403
  347.2 23.5 %collective-permute-start.48 = (bf16[2,8,32,512]{3,2,1,0:T(8,128)(2,1)}, bf16[2,8,32,512]{3,2,1,0:T(8,128)(2,1)}, u32[]{:S(2)}, u32[]{:S(2)}) collective-permute-start(bf16[2,8,32,512]{3,2,1,0:T(8,128)(2,1)} %get-tuple-element.273), channel_id=1, source_target_pairs={{0,8},{1,9},{2,10},{3,11},{4,12},{5,13},{6,14},{7,15},{8,0},{9,1},... | collective-permute-start | bytes 1572872 | tf_op jit(solution)/shard_map/ppermute | solution.py:403
  370.6 23.8 %collective-permute-start.72 = (bf16[2,8,32,512]{3,2,1,0:T(8,128)(2,1)S(1)}, bf16[2,8,32,512]{3,2,1,0:T(8,128)(2,1)S(1)}, u32[]{:S(2)}, u32[]{:S(2)}) collective-permute-start(bf16[2,8,32,512]{3,2,1,0:T(8,128)(2,1)S(1)} %add_convert_fusion), channel_id=1, source_target_pairs={{0,1},{1,0},{2,3},{3,2},{4,5},{5,4},{6,7},{7,6},{8,9},{9,8},{10,11... | collective-permute-start | bytes 1572872 | tf_op jit(solution)/shard_map/ppermute | solution.py:403
  382.1 13.7 %collective-permute-start.51 = (bf16[512,1024]{1,0:T(8,128)(2,1)}, bf16[512,1024]{1,0:T(8,128)(2,1)S(1)}, u32[]{:S(2)}, u32[]{:S(2)}) collective-permute-start(bf16[512,1024]{1,0:T(8,128)(2,1)} %get-tuple-element.210), channel_id=1, source_target_pairs={{0,4},{1,5},{2,6},{3,7},{4,0},{5,1},{6,2},{7,3},{8,12},{9,13},{10,... | collective-permute-start | bytes 3145736 | tf_op jit(solution)/shard_map/ppermute | solution.py:403
  388.8 22.6 %collective-permute-start.65 = (bf16[2,2,6,32,256]{4,3,2,1,0:T(8,128)(2,1)}, bf16[2,2,6,32,256]{4,3,2,1,0:T(8,128)(2,1)}, u32[]{:S(2)}, u32[]{:S(2)}) collective-permute-start(bf16[2,2,6,32,256]{4,3,2,1,0:T(8,128)(2,1)} %get-tuple-element.206), channel_id=1, source_target_pairs={{0,16},{1,17},{2,18},{3,19},{4,20},{5,21},{6,22},{7,23},{8,24},{9,... | collective-permute-start | bytes 1179656 | tf_op jit(solution)/shard_map/ppermute | solution.py:403
  390.3 31.8 %collective-permute-start.66 = (bf16[2,2,6,32,256]{4,3,2,1,0:T(8,128)(2,1)}, bf16[2,2,6,32,256]{4,3,2,1,0:T(8,128)(2,1)}, u32[]{:S(2)}, u32[]{:S(2)}) collective-permute-start(bf16[2,2,6,32,256]{4,3,2,1,0:T(8,128)(2,1)} %get-tuple-element.208), channel_id=1, source_target_pairs={{0,8},{1,9},{2,10},{3,11},{4,12},{5,13},{6,14},{7,15},{8,0},{9,1},... | collective-permute-start | bytes 1179656 | tf_op jit(solution)/shard_map/ppermute | solution.py:403
  392.0 34.0 %collective-permute-start.61 = (bf16[2,10,32,256]{3,2,1,0:T(8,128)(2,1)}, bf16[2,10,32,256]{3,2,1,0:T(8,128)(2,1)S(1)}, u32[]{:S(2)}, u32[]{:S(2)}) collective-permute-start(bf16[2,10,32,256]{3,2,1,0:T(8,128)(2,1)} %get-tuple-element.279), channel_id=1, source_target_pairs={{0,8},{1,9},{2,10},{3,11},{4,12},{5,13},{6,14},{7,15},{8,0},{9,1},... | collective-permute-start | bytes 983048 | tf_op jit(solution)/shard_map/ppermute | solution.py:403
  394.4 22.8 %collective-permute-start.62 = (bf16[2,10,32,256]{3,2,1,0:T(8,128)(2,1)}, bf16[2,10,32,256]{3,2,1,0:T(8,128)(2,1)S(1)}, u32[]{:S(2)}, u32[]{:S(2)}) collective-permute-start(bf16[2,10,32,256]{3,2,1,0:T(8,128)(2,1)} %get-tuple-element.282), channel_id=1, source_target_pairs={{0,16},{1,17},{2,18},{3,19},{4,20},{5,21},{6,22},{7,23},{8,24},{9,... | collective-permute-start | bytes 983048 | tf_op jit(solution)/shard_map/ppermute | solution.py:403
  395.8 14.2 %collective-permute-start.73 = (bf16[8,32,512]{2,1,0:T(8,128)(2,1)}, bf16[8,32,512]{2,1,0:T(8,128)(2,1)S(1)}, u32[]{:S(2)}, u32[]{:S(2)}) collective-permute-start(bf16[8,32,512]{2,1,0:T(8,128)(2,1)} %get-tuple-element.286), channel_id=1, source_target_pairs={{0,2},{1,3},{2,0},{3,1},{4,6},{5,7},{6,4},{7,5},{8,10},{9,11},{10,... | collective-permute-start | bytes 786440 | tf_op jit(solution)/shard_map/ppermute | solution.py:403
  411.2 27.5 %collective-permute-start.74 = (f32[4,32,512]{2,1,0:T(8,128)}, f32[4,32,512]{2,1,0:T(8,128)}, u32[]{:S(2)}, u32[]{:S(2)}) collective-permute-start(f32[4,32,512]{2,1,0:T(8,128)} %get-tuple-element.306), channel_id=1, source_target_pairs={{0,4},{1,5},{2,6},{3,7},{4,0},{5,1},{6,2},{7,3},{8,12},{9,13},{10,... | collective-permute-start | bytes 786440 | tf_op jit(solution)/shard_map/ppermute | solution.py:403
  411.5 4.7 collective-permute-start.55
  416.2 17.8 %collective-permute-start.67 = (bf16[2,6,32,256]{3,2,1,0:T(8,128)(2,1)}, bf16[2,6,32,256]{3,2,1,0:T(8,128)(2,1)}, u32[]{:S(2)}, u32[]{:S(2)}) collective-permute-start(bf16[2,6,32,256]{3,2,1,0:T(8,128)(2,1)} %get-tuple-element.299), channel_id=1, source_target_pairs={{0,8},{1,9},{2,10},{3,11},{4,12},{5,13},{6,14},{7,15},{8,0},{9,1},... | collective-permute-start | bytes 589832 | tf_op jit(solution)/shard_map/ppermute | solution.py:403
  421.0 4.4 collective-permute-start.57
  424.0 12.5 %collective-permute-start.68 = (bf16[2,6,32,256]{3,2,1,0:T(8,128)(2,1)}, bf16[2,6,32,256]{3,2,1,0:T(8,128)(2,1)}, u32[]{:S(2)}, u32[]{:S(2)}) collective-permute-start(bf16[2,6,32,256]{3,2,1,0:T(8,128)(2,1)} %get-tuple-element.302), channel_id=1, source_target_pairs={{0,16},{1,17},{2,18},{3,19},{4,20},{5,21},{6,22},{7,23},{8,24},{9,... | collective-permute-start | bytes 589832 | tf_op jit(solution)/shard_map/ppermute | solution.py:403
  425.4 32.8 %collective-permute-start.52 = (bf16[256,1024]{1,0:T(8,128)(2,1)}, bf16[256,1024]{1,0:T(8,128)(2,1)S(1)}, u32[]{:S(2)}, u32[]{:S(2)}) collective-permute-start(bf16[256,1024]{1,0:T(8,128)(2,1)} %get-tuple-element.289), channel_id=1, source_target_pairs={{1,0},{0,1},{5,2},{4,3},{3,4},{2,5},{7,6},{6,7},{9,8},{8,9},{13,10... | collective-permute-start | bytes 1572872 | tf_op jit(solution)/shard_map/ppermute | solution.py:403
  426.0 4.6 collective-permute-start.58
  430.5 27.7 %collective-permute-start.53 = (bf16[256,1024]{1,0:T(8,128)(2,1)S(1)}, bf16[256,1024]{1,0:T(8,128)(2,1)S(1)}, u32[]{:S(2)}, u32[]{:S(2)}) collective-permute-start(bf16[256,1024]{1,0:T(8,128)(2,1)S(1)} %get-tuple-element.290), channel_id=1, source_target_pairs={{0,0},{1,1},{4,2},{5,3},{2,4},{3,5},{6,6},{7,7},{8,8},{9,9},{12,10... | collective-permute-start | bytes 1572872 | tf_op jit(solution)/shard_map/ppermute | solution.py:403
  434.0 20.1 %collective-permute-start.63 = (bf16[2,10,32,256]{3,2,1,0:T(8,128)(2,1)}, bf16[2,10,32,256]{3,2,1,0:T(8,128)(2,1)S(1)}, u32[]{:S(2)}, u32[]{:S(2)}) collective-permute-start(bf16[2,10,32,256]{3,2,1,0:T(8,128)(2,1)} %add_convert_fusion.12), channel_id=1, source_target_pairs={{0,1},{1,0},{2,3},{3,2},{4,5},{5,4},{6,7},{7,6},{8,9},{9,8},{10,11... | collective-permute-start | bytes 983048 | tf_op jit(solution)/shard_map/ppermute | solution.py:403
  438.1 20.0 %collective-permute-start.69 = (bf16[2,6,32,256]{3,2,1,0:T(8,128)(2,1)}, bf16[2,6,32,256]{3,2,1,0:T(8,128)(2,1)S(1)}, u32[]{:S(2)}, u32[]{:S(2)}) collective-permute-start(bf16[2,6,32,256]{3,2,1,0:T(8,128)(2,1)} %add_convert_fusion.22), channel_id=1, source_target_pairs={{0,1},{1,0},{2,3},{3,2},{4,5},{5,4},{6,7},{7,6},{8,9},{9,8},{10,11... | collective-permute-start | bytes 589832 | tf_op jit(solution)/shard_map/ppermute | solution.py:403
  454.2 12.7 %collective-permute-start.64 = (bf16[10,32,256]{2,1,0:T(8,128)(2,1)S(1)}, bf16[10,32,256]{2,1,0:T(8,128)(2,1)S(1)}, u32[]{:S(2)}, u32[]{:S(2)}) collective-permute-start(bf16[10,32,256]{2,1,0:T(8,128)(2,1)S(1)} %get-tuple-element.304), channel_id=1, source_target_pairs={{0,2},{1,3},{2,0},{3,1},{4,6},{5,7},{6,4},{7,5},{8,10},{9,11},{10,... | collective-permute-start | bytes 491528 | tf_op jit(solution)/shard_map/ppermute | solution.py:403
  459.4 8.5 %collective-permute-start.70 = (bf16[6,32,256]{2,1,0:T(8,128)(2,1)S(1)}, bf16[6,32,256]{2,1,0:T(8,128)(2,1)S(1)}, u32[]{:S(2)}, u32[]{:S(2)}) collective-permute-start(bf16[6,32,256]{2,1,0:T(8,128)(2,1)S(1)} %get-tuple-element.228), channel_id=1, source_target_pairs={{0,2},{1,3},{2,0},{3,1},{4,6},{5,7},{6,4},{7,5},{8,10},{9,11},{10,... | collective-permute-start | bytes 294920 | tf_op jit(solution)/shard_map/ppermute | solution.py:403
  (60 other events, 413.4 us)

commit v4 on v3

--- a/solution.py
+++ b/solution.py
@@ -508,6 +508,24 @@
     return copies
 
 
+def load_out(meta, refs, weight, sem):
+    copies = []
+    for slot, ref in enumerate(refs):
+        for at in range(2):
+            for j in range(2):
+                chip, z = place(meta, slot, at, j)
+                row = pl.multiple_of((chip * 4 + z) * 32, 32)
+                for b in range(2):
+                    copies.append(
+                        pltpu.make_async_copy(
+                            ref.at[at, j, pl.ds(192 + b * 32, 32)],
+                            weight.at[b, pl.ds(row, 32), :],
+                            sem.at[len(copies)],
+                        )
+                    )
+    return copies
+
+
 def load_own_rows(meta, refs, base, blocks, rows, weight, sem):
     copies = []
     for slot, ref in enumerate(refs):
@@ -611,22 +629,18 @@
 
 def attend(meta, part, qkv, seg_column, seg_row):
     def kernel(m, q_ref, k_ref, v_ref, column_ref, row_ref, out_ref, lse_ref):
-        keys, values = k_ref[0], v_ref[0]
-        for block in range(4):
-            rows = pl.ds(block * 256, 256)
-            queries = q_ref[0, rows, :] * jnp.asarray(0.125, BF)
-            allowed = column_ref[rows, :] == row_ref[...]
-            mixed = jnp.zeros((256, 128), F32)
-            for h in range(2):
-                lanes = head_lanes(h, BF)
-                scores = jnp.where(allowed, dot(queries * lanes, keys, NT), -1e30)
-                largest = jnp.max(scores, axis=1, keepdims=True)
-                exponent = jnp.exp(scores - largest)
-                total = jnp.sum(exponent, axis=1, keepdims=True)
-                mixed += dot(exponent.astype(BF), values * lanes) / total
-                lse = jnp.broadcast_to(largest + jnp.log(total), (256, 128))
-                lse_ref[0, h : h + 1, rows] = jnp.transpose(lse)[0:1, :]
-            out_ref[rows, :] = mixed.astype(BF)
+        queries, keys, values = q_ref[0] * jnp.asarray(0.125, BF), k_ref[0], v_ref[0]
+        allowed = column_ref[...] == row_ref[...]
+        mixed = jnp.zeros((128, 1024), F32)
+        for h in range(2):
+            lanes = head_lanes(h, BF)
+            scores = jnp.where(allowed, dot(keys * lanes, queries, NT), -1e30)
+            largest = jnp.max(scores, axis=0, keepdims=True)
+            exponent = jnp.exp(scores - largest)
+            total = jnp.sum(exponent, axis=0, keepdims=True)
+            mixed += dot(values * lanes, exponent.astype(BF), TN) / total
+            lse_ref[0, h : h + 1, :] = largest + jnp.log(total)
+        out_ref[...] = jnp.transpose(mixed).astype(BF)
 
     base = part * 2
     third = lambda t: spec((1, 1024, 128), lambda i, m: (t, 0, base + i))
@@ -645,39 +659,31 @@
 
 
 def attend_back(meta, part, qkv, out, grad, lse, seg_column, seg_row):
-    def kernel(m, q_ref, k_ref, v_ref, out_ref, grad_ref, lse_ref, column_ref, row_ref, d_ref, sum_ref, dq):
+    def kernel(m, q_ref, k_ref, v_ref, out_ref, grad_ref, lse_ref, column_ref, row_ref, d_ref, sum_ref, prob, ds):
         queries, upstream = q_ref[0], grad_ref[...]
         product = out_ref[...].astype(F32) * upstream.astype(F32)
         row = lax.broadcasted_iota(jnp.int32, (8, 128), 0)
         lane = lax.broadcasted_iota(jnp.int32, (8, 128), 1)
         picked = jnp.where(lane // HEAD_DIM == row, 1.0, 0.0).astype(F32)
         center = lax.dot_general(picked, product, NT, precision=lax.Precision.HIGHEST, preferred_element_type=F32)
-        dq[...] = jnp.zeros_like(dq)
-        value_sum = jnp.zeros((1, 128), F32)
-        for block in range(4):
-            rows = pl.ds(block * 256, 256)
-            keys, values = k_ref[0, rows, :], v_ref[0, rows, :]
-            allowed = column_ref[rows, :] == row_ref[...]
-            dk = jnp.zeros((256, 128), F32)
-            dv = jnp.zeros((256, 128), F32)
-            for h in range(2):
-                lanes = head_lanes(h, BF)
-                keys_h = keys * lanes
-                scores = dot(keys_h * jnp.asarray(0.125, BF), queries, NT)
-                prob = jnp.where(allowed, jnp.exp(scores - lse_ref[0, h : h + 1, :]), 0.0)
-                dp = dot(values * lanes, upstream, NT)
-                ds = (prob * (dp - center[h : h + 1, :])).astype(BF)
-                dv += dot(prob.astype(BF), upstream * lanes)
-                dk += dot(ds, queries * lanes)
-                dq[...] += dot(ds, keys_h, TN)
-            dv = dv.astype(BF)
-            d_ref[1, rows, :] = (dk * 0.125).astype(BF)
-            d_ref[2, rows, :] = dv
-            value_sum += jnp.sum(dv.astype(F32), axis=0, keepdims=True)
-        final = (dq[...] * 0.125).astype(BF)
-        d_ref[0] = final
-        sum_ref[0:1, :] = jnp.sum(final.astype(F32), axis=0, keepdims=True)
-        sum_ref[1:2, :] = value_sum
+        dq, dk, dv = (jnp.zeros((1024, 128), F32) for _ in range(3))
+        for h in range(2):
+            lanes = head_lanes(h, BF)
+            for block in range(4):
+                rows = pl.ds(block * 256, 256)
+                allowed = column_ref[rows, :] == row_ref[...]
+                scores = dot(k_ref[0, rows, :] * lanes * jnp.asarray(0.125, BF), queries, NT)
+                p = jnp.where(allowed, jnp.exp(scores - lse_ref[0, h : h + 1, :]), 0.0)
+                dp = dot(v_ref[0, rows, :] * lanes, upstream, NT)
+                prob[rows, :] = p.astype(BF)
+                ds[rows, :] = (p * (dp - center[h : h + 1, :])).astype(BF)
+            dv += dot(prob[...], upstream * lanes)
+            dk += dot(ds[...], queries * lanes)
+            dq += dot(ds[...], k_ref[0] * lanes, TN)
+        dq, dk, dv = (dq * 0.125).astype(BF), (dk * 0.125).astype(BF), dv.astype(BF)
+        d_ref[0], d_ref[1], d_ref[2] = dq, dk, dv
+        sum_ref[0:1, :] = jnp.sum(dq.astype(F32), axis=0, keepdims=True)
+        sum_ref[1:2, :] = jnp.sum(dv.astype(F32), axis=0, keepdims=True)
 
     base = part * 2
     third = lambda t: spec((1, 1024, 128), lambda i, m: (t, 0, base + i))
@@ -689,7 +695,7 @@
         [third(0), third(1), third(2), heads(0), heads(base), spec((1, 8, 1024), lambda i, m: (i, 0, 0)), whole((1024, 1)), whole((1, 1024))],
         [spec((3, 1024, 128), lambda i, m: (0, 0, i)), spec((8, 128), lambda i, m: (0, i))],
         [shaped((3, 1024, 256), BF), shaped((8, 256), F32)],
-        [pltpu.VMEM((1024, 128), F32)],
+        [pltpu.VMEM((1024, 1024), BF), pltpu.VMEM((1024, 1024), BF)],
         grid=(2,),
         flops=8 * 10 * 1024 * 1024 * 256,
         moved=8 << 20,
@@ -704,7 +710,7 @@
 
         @pl.when(i == 0)
         def _():
-            load_all(load_own_rows(m, refs, 0, 2, 32, weight, sem))
+            load_all(load_out(m, refs, weight, sem))
 
         for b in range(2):
             columns = pl.ds(b * 512, 512)
@@ -725,7 +731,7 @@
         [spec((256, 256), lambda i, m: (turned(i), 0))] * 2 + [HBM] * 4,
         [spec((256, 1024), lambda i, m: (low_block(i), 0)), spec((256, 1024), lambda i, m: (high_block(i), 0))],
         [shaped((512, 1024), BF), shaped((512, 1024), F32)],
-        [pltpu.VMEM((2, 512, 512), BF), pltpu.SemaphoreType.DMA((16,))],
+        [pltpu.VMEM((2, 512, 512), BF), pltpu.SemaphoreType.DMA((32,))],
         flops=2 * 1024 * 1024 * 512,
         moved=6 << 20,
     )
@@ -779,7 +785,7 @@
 
         @pl.when(i == 0)
         def _():
-            load_all(load_split_rows(m, refs, 2, 4, weight, sem))
+            load_all(load_split_rows(m, refs, 0, 4, weight, sem))
 
         x = jnp.where(i < 2, own_ref[...].astype(F32), other_ref[...].astype(F32)).astype(BF)
         for b in range(4):
@@ -889,7 +895,7 @@
         def _():
             load_all(
                 load_own_rows(m, down_refs, 0, 2, 128, down, down_sem)
-                + load_split_rows(m, up_refs, 2, 4, up, up_sem)
+                + load_split_rows(m, up_refs, 0, 4, up, up_sem)
             )
             sum_ref[...] = jnp.zeros_like(sum_ref)
 
@@ -970,7 +976,7 @@
 
         @pl.when(i == 0)
         def _():
-            load_all(load_own_rows(m, refs, 0, 2, 32, weight, sem))
+            load_all(load_out(m, refs, weight, sem))
 
         da = jnp.where(i < 2, own_ref[...].astype(F32), other_ref[...].astype(F32)).astype(BF)
         out_ref[...] = (dot(da[:, :512], weight[0], NT) + dot(da[:, 512:], weight[1], NT)).astype(BF)
@@ -986,7 +992,7 @@
         + [HBM] * 4,
         spec((256, 512), BY_ROWS),
         shaped((1024, 512), BF),
-        [pltpu.VMEM((2, 512, 512), BF), pltpu.SemaphoreType.DMA((16,))],
+        [pltpu.VMEM((2, 512, 512), BF), pltpu.SemaphoreType.DMA((32,))],
         flops=2 * 1024 * 1024 * 512,
         moved=4 << 20,
     )
@@ -1258,9 +1264,9 @@
     small = jnp.pad(small[None], ((0, 15), (0, 128)))
     received = send(jnp.concatenate([qkv_half(1 - c), small]), PAIR)
     small = jnp.concatenate([small[:1], received[96:97], small[2:]])
-    qkv_shard = jnp.concatenate([qkv_half(c), received[:96], small])
-    out_shard = out_weight.reshape(32, 2, 512).transpose(1, 0, 2)
-    mid_shard = jnp.concatenate([out_shard, up_half(c), send(up_half(1 - c), PAIR)])
+    out_shard = out_weight.reshape(32, 2, 512).transpose(1, 0, 2).reshape(64, 512)
+    qkv_shard = jnp.concatenate([qkv_half(c), received[:96], out_shard, small])
+    up_shard = jnp.concatenate([up_half(c), send(up_half(1 - c), PAIR)])
     down_shard = down_weight.reshape(128, 2, 512).transpose(1, 0, 2)
     qkv_line = gather_line(qkv_shard)
 
@@ -1283,11 +1289,10 @@
     for width, pairs in ((8, ALONG_Y), (4, ALONG_X), (2, ALONG_Z[2]), (1, ALONG_Z[1])):
         embedded = embedded[:width] + send(embedded[width:], pairs)
 
-    mid_line = gather_line(after(mid_shard, qkv_line))
     qkv_pieces = gather_plane(*qkv_line)
 
-    def take_rows(value):
-        return jnp.stack([send(pick(value, (z + k) % 2, 0), ROW_OUT[k]) for k in range(2)])
+    def take_rows(value, *earlier):
+        return jnp.stack(after([send(pick(value, (z + k) % 2, 0), ROW_OUT[k]) for k in range(2)], earlier))
 
     def give_rows(value):
         parts = [send(value[k * 256 : (k + 1) * 256], ROW_BACK[k]) for k in range(2)]
@@ -1296,17 +1301,17 @@
 
     documents = jnp.concatenate([segment_ids // 32, segment_ids % 32], axis=1).astype(BF)
     documents = jnp.pad(documents[:, None, :], ((0, 0), (0, 15), (0, 512)))
-    own_tokens = take_rows(after(jnp.concatenate([tokens, documents], axis=1), mid_line))
+    own_tokens = take_rows(after(jnp.concatenate([tokens, documents], axis=1), qkv_line))
     other_tokens = send(own_tokens, PAIR)
     codes = jnp.concatenate([own_tokens[:, 256], other_tokens[:, 256]]).astype(F32)
     segments = (codes[:, :256] * 32.0 + codes[:, 256:512]).reshape(1024)
     seg_column, seg_row = segments[:, None], segments[None, :]
 
-    mid_pieces = gather_plane(*mid_line)
+    up_far = send(after(up_shard, own_tokens), ALONG_Z[2])
 
     natural = jnp.arange(32, dtype=jnp.int32)
     order = (natural[:, None] ^ me) == natural[None, :]
-    small = jnp.stack([piece[:, :, 192:194, :384] for piece in qkv_pieces])
+    small = jnp.stack([piece[:, :, 256:258, :384] for piece in qkv_pieces])
     small = jnp.stack(
         [
             small[half * 2 + (x_rel if half else y_rel), y_rel if half else x_rel, j, rel]
@@ -1327,24 +1332,29 @@
     up_shift = pick(up_full.reshape(4, 2, 512), c, 1).reshape(1, 2048)
 
     hidden, qkv = project_qkv(meta, own_tokens, other_tokens, embedded, qkv_shift, qkv_pieces)
-    mixed_one, lse_one = attend(meta, 0, qkv, seg_column, seg_row)
-    down_first = jnp.stack([after(down_shard, mixed_one), send(after(down_shard, qkv), ALONG_Z[2])])
-    mixed_two, lse_two = attend(meta, 1, after(qkv, down_first), seg_column, seg_row)
-    down_second = after(send(down_first, ALONG_Z[1]), mixed_two)
-    mixed = mixed_one, after(mixed_two, down_second)
-    away, mine = project_out(meta, mixed, mid_pieces)
-    own_cotangent = take_rows(after(cotangent, down_second))
-    down_pieces = gather_plane(down_first, down_second, mine)
-    normal_one, inverse_one, normed = first_norm(meta, own_tokens, embedded, mine, send(away, PAIR), vectors)
+    up_first = jnp.stack([after(up_shard, qkv), up_far])
+    mixed_one, lse_one = attend(meta, 0, after(qkv, up_first), seg_column, seg_row)
+    up_second = after(send(up_first, ALONG_Z[1]), mixed_one)
+    mixed_two, lse_two = attend(meta, 1, after(qkv, up_second), seg_column, seg_row)
+    up_pieces = gather_plane(up_first, up_second, mixed_two)
+    down_first = jnp.stack([after(down_shard, mixed_two), send(after(down_shard, up_second), ALONG_Z[2])])
+    mixed = mixed_one, after(mixed_two, down_first, up_pieces[0], up_pieces[2])
+    away, mine = project_out(meta, mixed, qkv_pieces)
+    down_second = after(send(down_first, ALONG_Z[1]), mine)
+    normal_one, inverse_one, normed = first_norm(
+        meta, own_tokens, embedded, after(mine, down_second, up_pieces), send(away, PAIR), vectors
+    )
     normed_other = send(normed, PAIR)
-    activated, slope = expand(meta, normed, after(normed_other, down_pieces[0], down_pieces[2]), up_shift, mid_pieces)
+    down_pieces = gather_plane(down_first, down_second, normed)
+    normed_other = after(normed_other, down_pieces[0], down_pieces[2])
+    activated, slope = expand(meta, normed, normed_other, up_shift, up_pieces)
+    own_cotangent = take_rows(after(cotangent, normed), activated).reshape(512, 1024)
     away, mine = contract(meta, after(activated, own_cotangent), down_pieces)
-    own_cotangent = after(own_cotangent, mine).reshape(512, 1024)
     result, resid_two, df, sums_two = second_norm(meta, normal_one, mine, send(away, PAIR), own_cotangent, vectors)
 
     df_other = send(df, PAIR)
     down_terms = weigh_down(meta, activated, df, df_other)
-    du, away, mine, up_sums = feed_back(meta, after(df, down_terms), df_other, slope, down_pieces, mid_pieces)
+    du, away, mine, up_sums = feed_back(meta, after(df, down_terms), df_other, slope, down_pieces, up_pieces)
     received = send(away, PAIR)
     up_terms = weigh_up(meta, normed, normed_other, du)
     down_sums = add_one(*scatter_one(*down_terms), up_terms)
@@ -1352,7 +1362,7 @@
         meta, after(resid_two, down_sums), mine, received, normal_one, inverse_one, vectors
     )
     da_other = send(da, PAIR)
-    dout = output_back(meta, da, da_other, mid_pieces)
+    dout = output_back(meta, da, da_other, qkv_pieces)
     down_sums = add_two(*scatter_two(*down_sums), dout)
     output = give_rows(after(result, dout))
     grad = after(dout, down_sums)
@@ -1378,7 +1388,7 @@
     qkv_sums_one = add_three(*scatter_three(*qkv_sums_one))
     up_share = scatter_four(*up_sums_three, input_low)
     qkv_sums_two = add_three(*scatter_three(*qkv_sums_two))
-    qkv_share_one = scatter_four(*qkv_sums_one)
+    qkv_share_one = scatter_four(*after(qkv_sums_one, input_grad))
     qkv_share_two = scatter_four(*after(qkv_sums_two, input_grad))
     qkv_share = jnp.concatenate([qkv_share_one[:6], qkv_share_two], axis=2)
     qv_sums = jnp.concatenate([qv_sums_one[0:2], qv_sums_two[0:2]], axis=1)
@@ -1394,6 +1404,7 @@
     grad_qkv = both_halves(split(qkv_share[:3]), split(send(qkv_share[3:], PAIR)))
     grad_qkv = grad_qkv.transpose(1, 0, 2, 3, 4).reshape(32, 3072)
 
+    qv_sums, up_sums, sums_one, sums_two = after((qv_sums, up_sums, sums_one, sums_two), input_low)
     core_lane = (jnp.arange(2) == c).astype(F32)
     spread = lambda sums, width: (sums.reshape(-1, 1, width) * core_lane[None, :, None]).reshape(32, -1)
     grads = jnp.concatenate(
@@ -1409,16 +1420,17 @@
         ],
         axis=1,
     )
-    total = jnp.dot(order.astype(F32), after(grads, embed_sums), precision=lax.Precision.HIGHEST)
-    total = total.reshape(2, 2, 2, 4, 3, 128).transpose(2, 3, 1, 0, 4, 5).reshape(96, 128)
+    total = jnp.dot(order.astype(F32), grads, precision=lax.Precision.HIGHEST)
+    total = total.reshape(4, 2, 4, 3, 128).transpose(1, 0, 2, 3, 4).reshape(96, 128)
     sums = embed_sums[0:1].reshape(8, 128)
     received = send(jnp.concatenate([total[48:], sums]), PAIR)
     total, sums = total[:48] + received[:48], sums + received[48:]
-    for width, pairs in ((24, ALONG_Z[2]), (12, ALONG_Z[1]), (6, ALONG_X), (3, ALONG_Y)):
-        received = send(jnp.concatenate([total[width:], sums]), pairs)
+    for width, pairs in ((24, ALONG_Y), (12, ALONG_X), (6, ALONG_Z[2]), (3, ALONG_Z[1])):
+        message = jnp.concatenate([total[width:], sums])
+        received = send(after(message, input_grad) if width == 6 else message, pairs)
         total, sums = total[:width] + received[:width], jnp.concatenate([sums, received[width:]])
     small_grads = [part.reshape(-1) for part in split_vectors(total.reshape(1, 384))]
-    sums = sums.reshape(2, 2, 2, 2, 1024).transpose(0, 1, 3, 2, 4).reshape(16, 1024)
+    sums = sums.reshape(2, 2, 2, 2, 1024).transpose(3, 2, 1, 0, 4).reshape(16, 1024)
     grad_time = jnp.dot(features.astype(F32).T, sums, precision=lax.Precision.HIGHEST)
 
     return (

time: 479 us -> 462 us (0.965)
  starting transfers between devices: 83.2 us -> 96.6 us
  other arithmetic: 36.6 us -> 25.6 us
  waiting for transfers between devices: 121 us -> 111 us
  Pallas kernels: 194 us -> 189 us
    ppermute x75, starting transfers between devices: 83.2 us -> 96.6 us  [send(): return lax.ppermute(value, AXES, pairs)]
    ppermute x75, waiting for transfers between devices: 121 us -> 111 us  [send(): return lax.ppermute(value, AXES, pairs)]
    pallas_call x19, Pallas kernels: 194 us -> 189 us  [kernel_call(): pl.pallas_call(kernel, grid_spec=pltpu.PrefetchScalarGridSpec(num_scalar_...]
  transfers between devices with their start and end apart: 75 -> 75, of which waited for: 28 -> 31; matrix products, arithmetic and copies ran while one was open for 13% -> 10% of each run, Pallas kernels for 33% -> 34%
where the time goes in v4:
time: 462 us; the launch traced here: 455 us
  Pallas kernels  189 us (41%)
  waiting for transfers between devices  111 us (24%)
  starting transfers between devices  96.6 us (21%)
  local copies, waits for them, and re-layouts  29.3 us (6%)
  other arithmetic  25.6 us (6%)
    pallas_call x19, Pallas kernels, kernel_call(): pl.pallas_call(kernel, grid_spec=pltpu.PrefetchScalarGridSpec(num_scalar_...  189 us
    ppermute x75, waiting for transfers between devices, send(): return lax.ppermute(value, AXES, pairs)  111 us
    ppermute x75, starting transfers between devices, send(): return lax.ppermute(value, AXES, pairs)  96.6 us
    convert_element_type x20, other arithmetic, add_low(): return (a.astype(F32) + b.astype(F32)).astype(BF)  14 us
  transfers between devices with their start and end apart: 75, of which 31 were waited for; matrix products, arithmetic and copies ran while one was open for 10% of the time, Pallas kernels for 34%

profile of v4, /device:TPU:0, one launch (start us, length us, event | category | flops | bytes accessed | tf_op | source)
XLA Modules:
  0.0 455.3 jit_solution(14031069628782187809)
XLA Ops:
  5.6 4.1 collective-permute-start.1
  12.5 2.0 collective-permute-done.6
  16.1 2.0 collective-permute-done.7
  19.2 3.3 collective-permute-done.1
  24.7 1.6 collective-permute-start.9
  28.7 1.6 collective-permute-start.10
  30.9 5.7 %collective-permute-done.2 = bf16[2,272,512]{2,1,0:T(8,128)(2,1)S(1)} collective-permute-done((bf16[2,272,512]{2,1,0:T(8,128)(2,1)S(1)}, bf16[2,272,512]{2,1,0:T(8,128)(2,1)S(1)}, u32[]{:S(2)}, u32[]{:S(2)}) %collective-permute-start.2) | collective-permute-done | bytes 557088 | tf_op jit(solution)/shard_map/ppermute | solution.py:403
  37.9 3.2 collective-permute-start.11
  41.9 1.8 collective-permute-start.4
  44.6 5.1 %collective-permute-done.15 = bf16[2,272,512]{2,1,0:T(8,128)(2,1)S(1)} collective-permute-done((bf16[2,272,512]{2,1,0:T(8,128)(2,1)S(1)}, bf16[2,272,512]{2,1,0:T(8,128)(2,1)S(1)}, u32[]{:S(2)}, u32[]{:S(2)}) %collective-permute-start.15) | collective-permute-done | bytes 557088 | tf_op jit(solution)/shard_map/ppermute | solution.py:403
  50.9 6.0 %collective-permute-done.12 = f32[1,1024]{1,0:T(1,128)S(1)} collective-permute-done((f32[1,1024]{1,0:T(1,128)S(1)}, f32[1,1024]{1,0:T(1,128)S(1)}, u32[]{:S(2)}, u32[]{:S(2)}) %collective-permute-start.12) | collective-permute-done | bytes 4128 | tf_op jit(solution)/shard_map/ppermute | solution.py:403
  57.6 1.6 collective-permute-start.16
  59.3 4.8 %collective-permute-start.13 = (bf16[2,272,1024]{2,1,0:T(8,128)(2,1)S(1)}, bf16[2,272,1024]{2,1,0:T(8,128)(2,1)}, u32[]{:S(2)}, u32[]{:S(2)}) collective-permute-start(bf16[2,272,1024]{2,1,0:T(8,128)(2,1)S(1)} %pad_maximum_fusion.own_ref.tok_ref), channel_id=1, source_target_pairs={{0,4},{1,5},{2,6},{3,7},{4,0},{5,1},{6,2},{7,3},{8,12},{9,13},{10,... | collective-permute-start | bytes 3342344 | tf_op jit(solution)/shard_map/ppermute | solution.py:403
  64.0 7.1 %collective-permute-start.19 = (bf16[8,32,512]{2,1,0:T(8,128)(2,1)S(1)}, bf16[8,32,512]{2,1,0:T(8,128)(2,1)S(1)}, u32[]{:S(2)}, u32[]{:S(2)}) collective-permute-start(bf16[8,32,512]{2,1,0:T(8,128)(2,1)S(1)} %pad_maximum_fusion.13), channel_id=1, source_target_pairs={{0,2},{1,3},{2,0},{3,1},{4,6},{5,7},{6,4},{7,5},{8,10},{9,11},{10,... | collective-permute-start | bytes 786440 | tf_op jit(solution)/shard_map/ppermute | solution.py:403
  71.3 2.8 collective-permute-done.17.rest_1_
  74.1 7.0 %collective-permute-done.16.rest_3_ = bf16[2,2,272,512]{3,2,1,0:T(8,128)(2,1)S(1)} collective-permute-done((bf16[2,2,272,512]{3,2,1,0:T(8,128)(2,1)S(1)}, bf16[2,2,272,512]{3,2,1,0:T(8,128)(2,1)S(1)}, u32[]{:S(2)}, u32[]{:S(2)}) %collective-permute-start.16) | collective-permute-done | bytes 1114144 | tf_op jit(solution)/shard_map/ppermute | solution.py:403
  83.2 10.4 %shard_map.280 = (bf16[1024,1024]{1,0:T(8,128)(2,1)}, bf16[3,1024,512]{2,1,0:T(8,128)(2,1)}) custom-call(s32[4]{0:T(128)} %pad_add_fusion.m, bf16[2,272,1024]{2,1,0:T(8,128)(2,1)} %copy-done.2, bf16[2,272,1024]{2,1,0:T(8,128)(2,1)} %collective-permute-done.13.other_ref, f32[1,1024]{1,0:T(1,128)} %slice_add_fusion.8.emb_ref, ...), custom_call_target="tpu_custom_call" | custom-call | flops 4831838208 | bytes 15728640 | tf_op jit(solution)/shard_map/pallas_call | solution.py:547
  93.7 2.5 collective-permute-start.20
  99.6 9.9 %shard_map.281 = (bf16[1024,256]{1,0:T(8,128)(2,1)}, f32[2,8,1024]{2,1,0:T(8,128)}) custom-call(s32[4]{0:T(128)} %pad_add_fusion.m, bf16[3,1024,512]{2,1,0:T(8,128)(2,1)} %get-tuple-element.151.q_ref.k_ref.v_ref, bf16[3,1024,512]{2,1,0:T(8,128)(2,1)} %get-tuple-element.151.q_ref.k_ref.v_ref, bf16[3,1024,512]{2,1,0:T(8,128)(2,1)} %get-tuple-element.151.q_ref.k_ref.v_ref, ...), custom_call_target="tpu_custom_call" | custom-call | flops 12884901888 | bytes 7864320 | tf_op jit(solution)/shard_map/pallas_call | solution.py:547
  110.1 10.0 %shard_map.282 = (bf16[1024,256]{1,0:T(8,128)(2,1)}, f32[2,8,1024]{2,1,0:T(8,128)}) custom-call(s32[4]{0:T(128)} %pad_add_fusion.m, bf16[3,1024,512]{2,1,0:T(8,128)(2,1)} %get-tuple-element.151.q_ref.k_ref.v_ref, bf16[3,1024,512]{2,1,0:T(8,128)(2,1)} %get-tuple-element.151.q_ref.k_ref.v_ref, bf16[3,1024,512]{2,1,0:T(8,128)(2,1)} %get-tuple-element.151.q_ref.k_ref.v_ref, ...), custom_call_target="tpu_custom_call" | custom-call | flops 12884901888 | bytes 7864320 | tf_op jit(solution)/shard_map/pallas_call | solution.py:547
  120.1 5.1 %collective-permute-done.21 = bf16[2,128,512]{2,1,0:T(8,128)(2,1)S(1)} collective-permute-done((bf16[2,128,512]{2,1,0:T(8,128)(2,1)S(1)}, bf16[2,128,512]{2,1,0:T(8,128)(2,1)S(1)}, u32[]{:S(2)}, u32[]{:S(2)}) %collective-permute-start.21) | collective-permute-done | bytes 262176 | tf_op jit(solution)/shard_map/ppermute | solution.py:403
  127.2 1.6 collective-permute-start.25
  128.8 7.4 %shard_map.283 = (bf16[512,1024]{1,0:T(8,128)(2,1)}, f32[512,1024]{1,0:T(8,128)}) custom-call(s32[4]{0:T(128)} %pad_add_fusion.m, bf16[1024,256]{1,0:T(8,128)(2,1)} %get-tuple-element.149.x_ref.out_ref.rest_0_, bf16[1024,256]{1,0:T(8,128)(2,1)} %get-tuple-element.159.w_ref.rest_1_.out_ref, bf16[2,2,272,512]{3,2,1,0:T(8,128)(2,1)} %copy-done.3, ...), custom_call_target="tpu_custom_call" | custom-call | flops 1610612736 | bytes 9437184 | tf_op jit(solution)/shard_map/pallas_call | solution.py:547
  138.0 12.9 %collective-permute-done.24 = bf16[2,2,128,512]{3,2,1,0:T(8,128)(2,1)} collective-permute-done((bf16[2,2,128,512]{3,2,1,0:T(8,128)(2,1)S(1)}, bf16[2,2,128,512]{3,2,1,0:T(8,128)(2,1)}, u32[]{:S(2)}, u32[]{:S(2)}) %collective-permute-start.24) | collective-permute-done | bytes 524320 | tf_op jit(solution)/shard_map/ppermute | solution.py:403
  152.6 4.6 %shard_map.284 = (f32[512,1024]{1,0:T(8,128)}, f32[512,128]{1,0:T(8,128)}, bf16[512,1024]{1,0:T(8,128)(2,1)}) custom-call(s32[4]{0:T(128)} %pad_add_fusion.m, bf16[2,272,1024]{2,1,0:T(8,128)(2,1)} %copy-done.2, f32[1,1024]{1,0:T(1,128)} %slice_add_fusion.8.emb_ref, f32[512,1024]{1,0:T(8,128)} %get-tuple-element.162.own_ref, ...), custom_call_target="tpu_custom_call" | custom-call | flops 9437184 | bytes 12582912 | tf_op jit(solution)/shard_map/pallas_call | solution.py:547
  157.2 4.7 %collective-permute-done.29 = bf16[2,2,128,512]{3,2,1,0:T(8,128)(2,1)S(1)} collective-permute-done((bf16[2,2,128,512]{3,2,1,0:T(8,128)(2,1)S(1)}, bf16[2,2,128,512]{3,2,1,0:T(8,128)(2,1)S(1)}, u32[]{:S(2)}, u32[]{:S(2)}) %collective-permute-start.29) | collective-permute-done | bytes 524320 | tf_op jit(solution)/shard_map/ppermute | solution.py:403
  161.9 2.7 collective-permute-done.30
  171.4 13.2 %shard_map.285 = (bf16[1024,2048]{1,0:T(8,128)(2,1)}, bf16[1024,2048]{1,0:T(8,128)(2,1)}) custom-call(s32[4]{0:T(128)} %pad_add_fusion.m, bf16[512,1024]{1,0:T(8,128)(2,1)} %get-tuple-element.165.own_ref, bf16[512,1024]{1,0:T(8,128)(2,1)} %collective-permute-done.28.other_ref, f32[1,2048]{1,0:T(1,128)} %bitcast.335, bf16[2,2,8,32,512]{4,3,2,1,0:T(8,128)(2,1)} %copy-done.14, ...), custom_call_target="tpu_custom_call" | custom-call | flops 6442450944 | bytes 22020096 | tf_op jit(solution)/shard_map/pallas_call | solution.py:547
  185.8 4.3 collective-permute-done.34.rest_3_
  191.3 11.5 %shard_map.286 = (bf16[512,1024]{1,0:T(8,128)(2,1)}, f32[512,1024]{1,0:T(8,128)}) custom-call(s32[4]{0:T(128)} %pad_add_fusion.m, bf16[1024,2048]{1,0:T(8,128)(2,1)} %get-tuple-element.175.x_ref, bf16[2,2,2,128,512]{4,3,2,1,0:T(8,128)(2,1)} %copy-done.17, bf16[2,2,2,128,512]{4,3,2,1,0:T(8,128)(2,1)} %collective-permute-done.33.rest_1_, ...), custom_call_target="tpu_custom_call" | custom-call | flops 6442450944 | bytes 17301504 | tf_op jit(solution)/shard_map/pallas_call | solution.py:547
  203.7 2.5 collective-permute-done.35.recv_ref
  207.1 6.5 %shard_map.287 = (bf16[512,1024]{1,0:T(8,128)(2,1)}, f32[512,1024]{1,0:T(8,128)}, bf16[512,1024]{1,0:T(8,128)(2,1)}, f32[8,1024]{1,0:T(8,128)}) custom-call(s32[4]{0:T(128)} %pad_add_fusion.m, f32[512,1024]{1,0:T(8,128)} %get-tuple-element.164.normal_ref, f32[512,1024]{1,0:T(8,128)} %get-tuple-element.176.own_ref, bf16[512,1024]{1,0:T(8,128)(2,1)} %copy-done.11, ...), custom_call_target="tpu_custom_call" | custom-call | flops 23592960 | bytes 15728640 | tf_op jit(solution)/shard_map/pallas_call | solution.py:547
  214.1 2.5 collective-permute-done.36.other_ref
  217.6 9.3 %shard_map.288 = (bf16[2,2,2,128,512]{4,3,2,1,0:T(8,128)(2,1)}, bf16[2,2,2,128,512]{4,3,2,1,0:T(8,128)(2,1)}, bf16[2,2,2,128,512]{4,3,2,1,0:T(8,128)(2,1)}, bf16[2,2,2,128,512]{4,3,2,1,0:T(8,128)(2,1)}) custom-call(s32[4]{0:T(128)} %pad_add_fusion.m, bf16[1024,2048]{1,0:T(8,128)(2,1)} %get-tuple-element.175.x_ref, ...), custom_call_target="tpu_custom_call" | custom-call | flops 6442450944 | bytes 15728640 | tf_op jit(solution)/shard_map/pallas_call | solution.py:547
  229.0 18.9 %shard_map.289 = (bf16[1024,2048]{1,0:T(8,128)(2,1)}, bf16[512,1024]{1,0:T(8,128)(2,1)}, f32[512,1024]{1,0:T(8,128)}, f32[8,2048]{1,0:T(8,128)}) custom-call(s32[4]{0:T(128)} %pad_add_fusion.m, bf16[512,1024]{1,0:T(8,128)(2,1)} %get-tuple-element.185.own_ref, bf16[512,1024]{1,0:T(8,128)(2,1)} %copy-done.45, bf16[1024,2048]{1,0:T(8,128)(2,1)} %get-tuple-element.186.slope_ref, ...), custom_call_target="tpu_custom_call" | custom-call | flops 12884901888 | bytes 34603008 | tf_op jit(solution)/shard_map/pallas_call | solution.py:547
  248.0 9.9 %shard_map.290 = (bf16[2,2,8,32,512]{4,3,2,1,0:T(8,128)(2,1)}, bf16[2,2,8,32,512]{4,3,2,1,0:T(8,128)(2,1)}, bf16[2,2,8,32,512]{4,3,2,1,0:T(8,128)(2,1)}, bf16[2,2,8,32,512]{4,3,2,1,0:T(8,128)(2,1)}) custom-call(s32[4]{0:T(128)} %pad_add_fusion.m, bf16[512,1024]{1,0:T(8,128)(2,1)} %get-tuple-element.165.own_ref, ...), custom_call_target="tpu_custom_call" | custom-call | flops 6442450944 | bytes 23592960 | tf_op jit(solution)/shard_map/pallas_call | solution.py:547
  260.4 6.1 %shard_map.291 = (f32[512,1024]{1,0:T(8,128)}, bf16[512,1024]{1,0:T(8,128)(2,1)}, f32[8,1024]{1,0:T(8,128)}) custom-call(s32[4]{0:T(128)} %pad_add_fusion.m, f32[512,1024]{1,0:T(8,128)} %get-tuple-element.194.resid_ref, f32[512,1024]{1,0:T(8,128)} %get-tuple-element.195.own_ref, bf16[512,1024]{1,0:T(8,128)(2,1)} %copy-done.21, ...), custom_call_target="tpu_custom_call" | custom-call | flops 15728640 | bytes 15728640 | tf_op jit(solution)/shard_map/pallas_call | solution.py:547
  270.5 6.9 %shard_map.292.grad_ref = bf16[1024,512]{1,0:T(8,128)(2,1)} custom-call(s32[4]{0:T(128)} %pad_add_fusion.m, bf16[512,1024]{1,0:T(8,128)(2,1)} %get-tuple-element.198.own_ref.rest_2_, bf16[512,1024]{1,0:T(8,128)(2,1)} %copy-done.19, bf16[2,2,272,512]{3,2,1,0:T(8,128)(2,1)} %copy-done.3, bf16[2,2,272,512]{3,2,1,0:T(8,128)(2,1)} %copy-done.5, ...), custom_call_target="tpu_custom_call" | custom-call | flops 1610612736 | bytes 6291456 | tf_op jit(solution)/shard_map/pallas_call | solution.py:547
  277.4 3.7 collective-permute-done.44
  281.3 6.2 %collective-permute-start.47 = (bf16[2,2,128,512]{3,2,1,0:T(8,128)(2,1)S(1)}, bf16[2,2,128,512]{3,2,1,0:T(8,128)(2,1)S(1)}, u32[]{:S(2)}, u32[]{:S(2)}) collective-permute-start(bf16[2,2,128,512]{3,2,1,0:T(8,128)(2,1)S(1)} %add_convert_fusion.6), channel_id=1, source_target_pairs={{0,1},{1,0},{2,3},{3,2},{4,5},{5,4},{6,7},{7,6},{8,9},{9,8},{10,11... | collective-permute-start | bytes 1572872 | tf_op jit(solution)/shard_map/ppermute | solution.py:403
  291.5 17.2 %shard_map.293 = (bf16[3,1024,256]{2,1,0:T(8,128)(2,1)}, f32[8,256]{1,0:T(8,128)}) custom-call(s32[4]{0:T(128)} %pad_add_fusion.m, bf16[3,1024,512]{2,1,0:T(8,128)(2,1)} %get-tuple-element.151.q_ref.k_ref.v_ref, bf16[3,1024,512]{2,1,0:T(8,128)(2,1)} %get-tuple-element.151.q_ref.k_ref.v_ref, bf16[3,1024,512]{2,1,0:T(8,128)(2,1)} %get-tuple-element.151.q_ref.k_ref.v_ref, ...), custom_call_target="tpu_custom_call" | custom-call | flops 32212254720 | bytes 12582912 | tf_op jit(solution)/shard_map/pallas_call | solution.py:547
  309.4 6.3 %collective-permute-done.41 = bf16[256,1024]{1,0:T(8,128)(2,1)S(1)} collective-permute-done((bf16[256,1024]{1,0:T(8,128)(2,1)S(1)}, bf16[256,1024]{1,0:T(8,128)(2,1)S(1)}, u32[]{:S(2)}, u32[]{:S(2)}) %collective-permute-start.41) | collective-permute-done | bytes 524320 | tf_op jit(solution)/shard_map/ppermute | solution.py:403
  316.9 8.7 %shard_map.294 = (bf16[2,2,10,32,256]{4,3,2,1,0:T(8,128)(2,1)}, bf16[2,2,10,32,256]{4,3,2,1,0:T(8,128)(2,1)}, bf16[2,2,10,32,256]{4,3,2,1,0:T(8,128)(2,1)}, bf16[2,2,10,32,256]{4,3,2,1,0:T(8,128)(2,1)}) custom-call(s32[4]{0:T(128)} %pad_add_fusion.m, bf16[1024,1024]{1,0:T(8,128)(2,1)} %get-tuple-element.209.x_ref, ...), custom_call_target="tpu_custom_call" | custom-call | flops 3221225472 | bytes 12582912 | tf_op jit(solution)/shard_map/pallas_call | solution.py:547
  327.8 2.7 collective-permute-start.50
  331.7 1.5 collective-permute-start.49
  334.4 17.7 %shard_map.295 = (bf16[3,1024,256]{2,1,0:T(8,128)(2,1)}, f32[8,256]{1,0:T(8,128)}) custom-call(s32[4]{0:T(128)} %pad_add_fusion.m, bf16[3,1024,512]{2,1,0:T(8,128)(2,1)} %get-tuple-element.151.q_ref.k_ref.v_ref, bf16[3,1024,512]{2,1,0:T(8,128)(2,1)} %get-tuple-element.151.q_ref.k_ref.v_ref, bf16[3,1024,512]{2,1,0:T(8,128)(2,1)} %get-tuple-element.151.q_ref.k_ref.v_ref, ...), custom_call_target="tpu_custom_call" | custom-call | flops 32212254720 | bytes 12582912 | tf_op jit(solution)/shard_map/pallas_call | solution.py:547
  356.9 5.3 %collective-permute-done.48 = bf16[2,8,32,512]{3,2,1,0:T(8,128)(2,1)} collective-permute-done((bf16[2,8,32,512]{3,2,1,0:T(8,128)(2,1)}, bf16[2,8,32,512]{3,2,1,0:T(8,128)(2,1)}, u32[]{:S(2)}, u32[]{:S(2)}) %collective-permute-start.48) | collective-permute-done | bytes 524320 | tf_op jit(solution)/shard_map/ppermute | solution.py:403
  363.4 10.2 %shard_map.296 = (bf16[512,1024]{1,0:T(8,128)(2,1)}, f32[512,1024]{1,0:T(8,128)}) custom-call(s32[4]{0:T(128)} %pad_add_fusion.m, bf16[3,1024,256]{2,1,0:T(8,128)(2,1)} %get-tuple-element.210.d_ref, bf16[3,1024,256]{2,1,0:T(8,128)(2,1)} %get-tuple-element.228.e_ref.d_ref, bf16[2,2,272,512]{3,2,1,0:T(8,128)(2,1)} %copy-done.3, ...), custom_call_target="tpu_custom_call" | custom-call | flops 4831838208 | bytes 14155776 | tf_op jit(solution)/shard_map/pallas_call | solution.py:547
  373.7 6.5 %shard_map.297 = (bf16[2,2,6,32,256]{4,3,2,1,0:T(8,128)(2,1)}, bf16[2,2,6,32,256]{4,3,2,1,0:T(8,128)(2,1)}, bf16[2,2,6,32,256]{4,3,2,1,0:T(8,128)(2,1)}, bf16[2,2,6,32,256]{4,3,2,1,0:T(8,128)(2,1)}) custom-call(s32[4]{0:T(128)} %pad_add_fusion.m, bf16[1024,1024]{1,0:T(8,128)(2,1)} %get-tuple-element.209.x_ref, ...), custom_call_target="tpu_custom_call" | custom-call | flops 3221225472 | bytes 12582912 | tf_op jit(solution)/shard_map/pallas_call | solution.py:547
  381.9 2.6 collective-permute-start.73
  387.6 1.5 collective-permute-start.62
  389.2 4.1 shard_map.298
  393.2 3.4 collective-permute-done.73
  403.3 1.8 add_convert_fusion.12
  412.2 3.6 collective-permute-done.56
  417.0 2.0 collective-permute-start.63
  419.1 2.9 collective-permute-done.68
  422.8 3.2 collective-permute-start.69
  429.8 2.9 collective-permute-start.57
  432.9 1.7 collective-permute-done.57
  435.1 2.1 collective-permute-start.58
  438.1 3.0 collective-permute-start.70
  444.0 4.8 %collective-permute-done.70 = bf16[6,32,256]{2,1,0:T(8,128)(2,1)S(1)} collective-permute-done((bf16[6,32,256]{2,1,0:T(8,128)(2,1)S(1)}, bf16[6,32,256]{2,1,0:T(8,128)(2,1)S(1)}, u32[]{:S(2)}, u32[]{:S(2)}) %collective-permute-start.70) | collective-permute-done | bytes 98336 | tf_op jit(solution)/shard_map/ppermute | solution.py:403
  448.8 3.1 collective-permute-done.64
  (400 shorter events, 101.0 us)
Async XLA Ops:
  4.0 26.3 %collective-permute-start.18 = (bf16[4,32,512]{2,1,0:T(8,128)(2,1)S(1)}, bf16[4,32,512]{2,1,0:T(8,128)(2,1)S(1)}, u32[]{:S(2)}, u32[]{:S(2)}) collective-permute-start(bf16[4,32,512]{2,1,0:T(8,128)(2,1)S(1)} %bitcast.320), channel_id=1, source_target_pairs={{0,4},{1,5},{2,6},{3,7},{4,0},{5,1},{6,2},{7,3},{8,12},{9,13},{10,... | collective-permute-start | bytes 393224 | tf_op jit(solution)/shard_map/ppermute | solution.py:403
  5.6 16.9 %collective-permute-start.1 = (bf16[272,512]{1,0:T(8,128)(2,1)S(1)}, bf16[272,512]{1,0:T(8,128)(2,1)S(1)}, u32[]{:S(2)}, u32[]{:S(2)}) collective-permute-start(bf16[272,512]{1,0:T(8,128)(2,1)S(1)} %concatenate.93), channel_id=1, source_target_pairs={{0,2},{1,3},{2,0},{3,1},{4,6},{5,7},{6,4},{7,5},{8,10},{9,11},{10,... | collective-permute-start | bytes 835592 | tf_op jit(solution)/shard_map/ppermute | solution.py:403
  22.5 14.1 %collective-permute-start.2 = (bf16[2,272,512]{2,1,0:T(8,128)(2,1)S(1)}, bf16[2,272,512]{2,1,0:T(8,128)(2,1)S(1)}, u32[]{:S(2)}, u32[]{:S(2)}) collective-permute-start(bf16[2,272,512]{2,1,0:T(8,128)(2,1)S(1)} %pad_maximum_fusion.10), channel_id=1, source_target_pairs={{0,1},{1,0},{2,3},{3,2},{4,5},{5,4},{6,7},{7,6},{8,9},{9,8},{10,11... | collective-permute-start | bytes 1671176 | tf_op jit(solution)/shard_map/ppermute | solution.py:403
  28.7 9.2 %collective-permute-start.10 = (f32[4,1024]{1,0:T(4,128)S(1)}, f32[4,1024]{1,0:T(4,128)S(1)}, u32[]{:S(2)}, u32[]{:S(2)}) collective-permute-start(f32[4,1024]{1,0:T(4,128)S(1)} %slice.663), channel_id=1, source_target_pairs={{0,8},{1,9},{2,10},{3,11},{4,12},{5,13},{6,14},{7,15},{8,0},{9,1},... | collective-permute-start | bytes 49160 | tf_op jit(solution)/shard_map/ppermute | solution.py:403
  30.3 14.3 %collective-permute-start.14 = (bf16[2,272,512]{2,1,0:T(8,128)(2,1)S(1)}, bf16[2,272,512]{2,1,0:T(8,128)(2,1)S(1)}, u32[]{:S(2)}, u32[]{:S(2)}) collective-permute-start(bf16[2,272,512]{2,1,0:T(8,128)(2,1)S(1)} %pad_maximum_fusion.10), channel_id=1, source_target_pairs={{0,8},{1,9},{2,10},{3,11},{4,12},{5,13},{6,14},{7,15},{8,0},{9,1},... | collective-permute-start | bytes 1671176 | tf_op jit(solution)/shard_map/ppermute | solution.py:403
  36.6 13.1 %collective-permute-start.15 = (bf16[2,272,512]{2,1,0:T(8,128)(2,1)S(1)}, bf16[2,272,512]{2,1,0:T(8,128)(2,1)S(1)}, u32[]{:S(2)}, u32[]{:S(2)}) collective-permute-start(bf16[2,272,512]{2,1,0:T(8,128)(2,1)S(1)} %collective-permute-done.2), channel_id=1, source_target_pairs={{0,16},{1,17},{2,18},{3,19},{4,20},{5,21},{6,22},{7,23},{8,24},{9,... | collective-permute-start | bytes 1671176 | tf_op jit(solution)/shard_map/ppermute | solution.py:403
  37.9 5.8 %collective-permute-start.11 = (f32[2,1024]{1,0:T(2,128)S(1)}, f32[2,1024]{1,0:T(2,128)S(1)}, u32[]{:S(2)}, u32[]{:S(2)}) collective-permute-start(f32[2,1024]{1,0:T(2,128)S(1)} %slice.665), channel_id=1, source_target_pairs={{0,2},{1,3},{2,0},{3,1},{4,6},{5,7},{6,4},{7,5},{8,10},{9,11},{10,... | collective-permute-start | bytes 24584 | tf_op jit(solution)/shard_map/ppermute | solution.py:403
  41.2 17.9 %collective-permute-start.3 = (bf16[272,1024]{1,0:T(8,128)(2,1)S(1)}, bf16[272,1024]{1,0:T(8,128)(2,1)S(1)}, u32[]{:S(2)}, u32[]{:S(2)}) collective-permute-start(bf16[272,1024]{1,0:T(8,128)(2,1)S(1)} %get-tuple-element.314), channel_id=1, source_target_pairs={{0,0},{1,1},{2,4},{3,5},{4,2},{5,3},{6,6},{7,7},{8,8},{9,9},{10,12... | collective-permute-start | bytes 1671176 | tf_op jit(solution)/shard_map/ppermute | solution.py:403
  41.9 17.2 %collective-permute-start.4 = (bf16[272,1024]{1,0:T(8,128)(2,1)S(1)}, bf16[272,1024]{1,0:T(8,128)(2,1)S(1)}, u32[]{:S(2)}, u32[]{:S(2)}) collective-permute-start(bf16[272,1024]{1,0:T(8,128)(2,1)S(1)} %get-tuple-element.313), channel_id=1, source_target_pairs={{0,1},{1,0},{2,5},{3,4},{4,3},{5,2},{6,7},{7,6},{8,9},{9,8},{10,13... | collective-permute-start | bytes 1671176 | tf_op jit(solution)/shard_map/ppermute | solution.py:403
  43.7 13.1 %collective-permute-start.12 = (f32[1,1024]{1,0:T(1,128)S(1)}, f32[1,1024]{1,0:T(1,128)S(1)}, u32[]{:S(2)}, u32[]{:S(2)}) collective-permute-start(f32[1,1024]{1,0:T(1,128)S(1)} %slice.667), channel_id=1, source_target_pairs={{0,1},{1,0},{2,3},{3,2},{4,5},{5,4},{6,7},{7,6},{8,9},{9,8},{10,11... | collective-permute-start | bytes 12296 | tf_op jit(solution)/shard_map/ppermute | solution.py:403
  49.9 24.2 %collective-permute-start.17 = (bf16[2,2,272,512]{3,2,1,0:T(8,128)(2,1)S(1)}, bf16[2,2,272,512]{3,2,1,0:T(8,128)(2,1)S(1)}, u32[]{:S(2)}, u32[]{:S(2)}) collective-permute-start(bf16[2,2,272,512]{3,2,1,0:T(8,128)(2,1)S(1)} %pad_maximum_fusion.1.rest_0_), channel_id=1, source_target_pairs={{0,16},{1,17},{2,18},{3,19},{4,20},{5,21},{6,22},{7,23},{8,24},{9,... | collective-permute-start | bytes 3342344 | tf_op jit(solution)/shard_map/ppermute | solution.py:403
  57.6 23.5 %collective-permute-start.16 = (bf16[2,2,272,512]{3,2,1,0:T(8,128)(2,1)S(1)}, bf16[2,2,272,512]{3,2,1,0:T(8,128)(2,1)S(1)}, u32[]{:S(2)}, u32[]{:S(2)}) collective-permute-start(bf16[2,2,272,512]{3,2,1,0:T(8,128)(2,1)S(1)} %pad_maximum_fusion.2.rest_2_), channel_id=1, source_target_pairs={{0,8},{1,9},{2,10},{3,11},{4,12},{5,13},{6,14},{7,15},{8,0},{9,1},... | collective-permute-start | bytes 3342344 | tf_op jit(solution)/shard_map/ppermute | solution.py:403
  59.3 24.0 %collective-permute-start.13 = (bf16[2,272,1024]{2,1,0:T(8,128)(2,1)S(1)}, bf16[2,272,1024]{2,1,0:T(8,128)(2,1)}, u32[]{:S(2)}, u32[]{:S(2)}) collective-permute-start(bf16[2,272,1024]{2,1,0:T(8,128)(2,1)S(1)} %pad_maximum_fusion.own_ref.tok_ref), channel_id=1, source_target_pairs={{0,4},{1,5},{2,6},{3,7},{4,0},{5,1},{6,2},{7,3},{8,12},{9,13},{10,... | collective-permute-start | bytes 3342344 | tf_op jit(solution)/shard_map/ppermute | solution.py:403
  64.0 29.6 %collective-permute-start.19 = (bf16[8,32,512]{2,1,0:T(8,128)(2,1)S(1)}, bf16[8,32,512]{2,1,0:T(8,128)(2,1)S(1)}, u32[]{:S(2)}, u32[]{:S(2)}) collective-permute-start(bf16[8,32,512]{2,1,0:T(8,128)(2,1)S(1)} %pad_maximum_fusion.13), channel_id=1, source_target_pairs={{0,2},{1,3},{2,0},{3,1},{4,6},{5,7},{6,4},{7,5},{8,10},{9,11},{10,... | collective-permute-start | bytes 786440 | tf_op jit(solution)/shard_map/ppermute | solution.py:403
  93.7 15.8 %collective-permute-start.20 = (bf16[2,8,32,512]{3,2,1,0:T(8,128)(2,1)S(1)}, bf16[2,8,32,512]{3,2,1,0:T(8,128)(2,1)S(1)}, u32[]{:S(2)}, u32[]{:S(2)}) collective-permute-start(bf16[2,8,32,512]{3,2,1,0:T(8,128)(2,1)S(1)} %pad_maximum_fusion.11), channel_id=1, source_target_pairs={{0,1},{1,0},{2,3},{3,2},{4,5},{5,4},{6,7},{7,6},{8,9},{9,8},{10,11... | collective-permute-start | bytes 1572872 | tf_op jit(solution)/shard_map/ppermute | solution.py:403
  96.3 29.0 %collective-permute-start.22 = (bf16[2,8,32,512]{3,2,1,0:T(8,128)(2,1)S(1)}, bf16[2,8,32,512]{3,2,1,0:T(8,128)(2,1)S(1)}, u32[]{:S(2)}, u32[]{:S(2)}) collective-permute-start(bf16[2,8,32,512]{3,2,1,0:T(8,128)(2,1)S(1)} %pad_maximum_fusion.11), channel_id=1, source_target_pairs={{0,8},{1,9},{2,10},{3,11},{4,12},{5,13},{6,14},{7,15},{8,0},{9,1},... | collective-permute-start | bytes 1572872 | tf_op jit(solution)/shard_map/ppermute | solution.py:403
  109.6 15.8 %collective-permute-start.23 = (bf16[2,8,32,512]{3,2,1,0:T(8,128)(2,1)S(1)}, bf16[2,8,32,512]{3,2,1,0:T(8,128)(2,1)S(1)}, u32[]{:S(2)}, u32[]{:S(2)}) collective-permute-start(bf16[2,8,32,512]{3,2,1,0:T(8,128)(2,1)S(1)} %collective-permute-done.20), channel_id=1, source_target_pairs={{0,16},{1,17},{2,18},{3,19},{4,20},{5,21},{6,22},{7,23},{8,24},{9,... | collective-permute-start | bytes 1572872 | tf_op jit(solution)/shard_map/ppermute | solution.py:403
  110.1 15.1 %collective-permute-start.21 = (bf16[2,128,512]{2,1,0:T(8,128)(2,1)S(1)}, bf16[2,128,512]{2,1,0:T(8,128)(2,1)S(1)}, u32[]{:S(2)}, u32[]{:S(2)}) collective-permute-start(bf16[2,128,512]{2,1,0:T(8,128)(2,1)S(1)} %bitcast.298), channel_id=1, source_target_pairs={{0,2},{1,3},{2,0},{3,1},{4,6},{5,7},{6,4},{7,5},{8,10},{9,11},{10,... | collective-permute-start | bytes 786440 | tf_op jit(solution)/shard_map/ppermute | solution.py:403
  125.4 27.1 %collective-permute-start.26 = (bf16[2,2,8,32,512]{4,3,2,1,0:T(8,128)(2,1)S(1)}, bf16[2,2,8,32,512]{4,3,2,1,0:T(8,128)(2,1)}, u32[]{:S(2)}, u32[]{:S(2)}) collective-permute-start(bf16[2,2,8,32,512]{4,3,2,1,0:T(8,128)(2,1)S(1)} %pad_maximum_fusion.4.rest_2_.rest_6_), channel_id=1, source_target_pairs={{0,8},{1,9},{2,10},{3,11},{4,12},{5,13},{6,14},{7,15},{8,0},{9,1},... | collective-permute-start | bytes 3145736 | tf_op jit(solution)/shard_map/ppermute | solution.py:403
  127.2 25.4 %collective-permute-start.25 = (bf16[2,2,8,32,512]{4,3,2,1,0:T(8,128)(2,1)S(1)}, bf16[2,2,8,32,512]{4,3,2,1,0:T(8,128)(2,1)}, u32[]{:S(2)}, u32[]{:S(2)}) collective-permute-start(bf16[2,2,8,32,512]{4,3,2,1,0:T(8,128)(2,1)S(1)} %pad_maximum_fusion.3.rest_0_.rest_4_), channel_id=1, source_target_pairs={{0,16},{1,17},{2,18},{3,19},{4,20},{5,21},{6,22},{7,23},{8,24},{9,... | collective-permute-start | bytes 3145736 | tf_op jit(solution)/shard_map/ppermute | solution.py:403
  136.3 16.3 %collective-permute-start.27 = (bf16[512,1024]{1,0:T(8,128)(2,1)}, bf16[512,1024]{1,0:T(8,128)(2,1)}, u32[]{:S(2)}, u32[]{:S(2)}) collective-permute-start(bf16[512,1024]{1,0:T(8,128)(2,1)} %get-tuple-element.163), channel_id=1, source_target_pairs={{0,4},{1,5},{2,6},{3,7},{4,0},{5,1},{6,2},{7,3},{8,12},{9,13},{10,... | collective-permute-start | bytes 3145736 | tf_op jit(solution)/shard_map/ppermute | solution.py:403
  136.4 14.4 %collective-permute-start.24 = (bf16[2,2,128,512]{3,2,1,0:T(8,128)(2,1)S(1)}, bf16[2,2,128,512]{3,2,1,0:T(8,128)(2,1)}, u32[]{:S(2)}, u32[]{:S(2)}) collective-permute-start(bf16[2,2,128,512]{3,2,1,0:T(8,128)(2,1)S(1)} %pad_maximum_fusion.12), channel_id=1, source_target_pairs={{0,1},{1,0},{2,3},{3,2},{4,5},{5,4},{6,7},{7,6},{8,9},{9,8},{10,11... | collective-permute-start | bytes 1572872 | tf_op jit(solution)/shard_map/ppermute | solution.py:403
  136.5 25.5 %collective-permute-start.29 = (bf16[2,2,128,512]{3,2,1,0:T(8,128)(2,1)S(1)}, bf16[2,2,128,512]{3,2,1,0:T(8,128)(2,1)S(1)}, u32[]{:S(2)}, u32[]{:S(2)}) collective-permute-start(bf16[2,2,128,512]{3,2,1,0:T(8,128)(2,1)S(1)} %pad_maximum_fusion.12), channel_id=1, source_target_pairs={{0,8},{1,9},{2,10},{3,11},{4,12},{5,13},{6,14},{7,15},{8,0},{9,1},... | collective-permute-start | bytes 1572872 | tf_op jit(solution)/shard_map/ppermute | solution.py:403
  150.8 13.8 %collective-permute-start.30 = (bf16[2,2,128,512]{3,2,1,0:T(8,128)(2,1)}, bf16[2,2,128,512]{3,2,1,0:T(8,128)(2,1)}, u32[]{:S(2)}, u32[]{:S(2)}) collective-permute-start(bf16[2,2,128,512]{3,2,1,0:T(8,128)(2,1)} %collective-permute-done.24), channel_id=1, source_target_pairs={{0,16},{1,17},{2,18},{3,19},{4,20},{5,21},{6,22},{7,23},{8,24},{9,... | collective-permute-start | bytes 1572872 | tf_op jit(solution)/shard_map/ppermute | solution.py:403
  157.2 14.2 %collective-permute-start.28 = (bf16[512,1024]{1,0:T(8,128)(2,1)}, bf16[512,1024]{1,0:T(8,128)(2,1)}, u32[]{:S(2)}, u32[]{:S(2)}) collective-permute-start(bf16[512,1024]{1,0:T(8,128)(2,1)} %get-tuple-element.165.own_ref), channel_id=1, source_target_pairs={{0,4},{1,5},{2,6},{3,7},{4,0},{5,1},{6,2},{7,3},{8,12},{9,13},{10,... | collective-permute-start | bytes 3145736 | tf_op jit(solution)/shard_map/ppermute | solution.py:403
  166.0 24.0 %collective-permute-start.34 = (bf16[2,2,2,128,512]{4,3,2,1,0:T(8,128)(2,1)S(1)}, bf16[2,2,2,128,512]{4,3,2,1,0:T(8,128)(2,1)}, u32[]{:S(2)}, u32[]{:S(2)}) collective-permute-start(bf16[2,2,2,128,512]{4,3,2,1,0:T(8,128)(2,1)S(1)} %pad_maximum_fusion.6.rest_2_), channel_id=1, source_target_pairs={{0,8},{1,9},{2,10},{3,11},{4,12},{5,13},{6,14},{7,15},{8,0},{9,1},... | collective-permute-start | bytes 3145736 | tf_op jit(solution)/shard_map/ppermute | solution.py:403
  167.6 23.7 %collective-permute-start.33 = (bf16[2,2,2,128,512]{4,3,2,1,0:T(8,128)(2,1)S(1)}, bf16[2,2,2,128,512]{4,3,2,1,0:T(8,128)(2,1)}, u32[]{:S(2)}, u32[]{:S(2)}) collective-permute-start(bf16[2,2,2,128,512]{4,3,2,1,0:T(8,128)(2,1)S(1)} %pad_maximum_fusion.5.rest_0_), channel_id=1, source_target_pairs={{0,16},{1,17},{2,18},{3,19},{4,20},{5,21},{6,22},{7,23},{8,24},{9,... | collective-permute-start | bytes 3145736 | tf_op jit(solution)/shard_map/ppermute | solution.py:403
  170.2 14.5 %collective-permute-start.31 = (bf16[256,1024]{1,0:T(8,128)(2,1)S(1)}, bf16[256,1024]{1,0:T(8,128)(2,1)S(1)}, u32[]{:S(2)}, u32[]{:S(2)}) collective-permute-start(bf16[256,1024]{1,0:T(8,128)(2,1)S(1)} %get-tuple-element.328), channel_id=1, source_target_pairs={{0,0},{1,1},{2,4},{3,5},{4,2},{5,3},{6,6},{7,7},{8,8},{9,9},{10,12... | collective-permute-start | bytes 1572872 | tf_op jit(solution)/shard_map/ppermute | solution.py:403
  170.9 13.8 %collective-permute-start.32 = (bf16[256,1024]{1,0:T(8,128)(2,1)S(1)}, bf16[256,1024]{1,0:T(8,128)(2,1)S(1)}, u32[]{:S(2)}, u32[]{:S(2)}) collective-permute-start(bf16[256,1024]{1,0:T(8,128)(2,1)S(1)} %get-tuple-element.327), channel_id=1, source_target_pairs={{0,1},{1,0},{2,5},{3,4},{4,3},{5,2},{6,7},{7,6},{8,9},{9,8},{10,13... | collective-permute-start | bytes 1572872 | tf_op jit(solution)/shard_map/ppermute | solution.py:403
  226.8 31.1 %collective-permute-start.38 = (bf16[2,2,2,128,512]{4,3,2,1,0:T(8,128)(2,1)}, bf16[2,2,2,128,512]{4,3,2,1,0:T(8,128)(2,1)S(1)}, u32[]{:S(2)}, u32[]{:S(2)}) collective-permute-start(bf16[2,2,2,128,512]{4,3,2,1,0:T(8,128)(2,1)} %get-tuple-element.184), channel_id=1, source_target_pairs={{0,8},{1,9},{2,10},{3,11},{4,12},{5,13},{6,14},{7,15},{8,0},{9,1},... | collective-permute-start | bytes 3145736 | tf_op jit(solution)/shard_map/ppermute | solution.py:403
  227.9 31.1 %collective-permute-start.37 = (bf16[2,2,2,128,512]{4,3,2,1,0:T(8,128)(2,1)}, bf16[2,2,2,128,512]{4,3,2,1,0:T(8,128)(2,1)S(1)}, u32[]{:S(2)}, u32[]{:S(2)}) collective-permute-start(bf16[2,2,2,128,512]{4,3,2,1,0:T(8,128)(2,1)} %get-tuple-element.183), channel_id=1, source_target_pairs={{0,16},{1,17},{2,18},{3,19},{4,20},{5,21},{6,22},{7,23},{8,24},{9,... | collective-permute-start | bytes 3145736 | tf_op jit(solution)/shard_map/ppermute | solution.py:403
  248.0 11.5 %collective-permute-start.39 = (bf16[512,1024]{1,0:T(8,128)(2,1)}, bf16[512,1024]{1,0:T(8,128)(2,1)S(1)}, u32[]{:S(2)}, u32[]{:S(2)}) collective-permute-start(bf16[512,1024]{1,0:T(8,128)(2,1)} %get-tuple-element.196), channel_id=1, source_target_pairs={{0,4},{1,5},{2,6},{3,7},{4,0},{5,1},{6,2},{7,3},{8,12},{9,13},{10,... | collective-permute-start | bytes 3145736 | tf_op jit(solution)/shard_map/ppermute | solution.py:403
  267.0 14.1 %collective-permute-start.44 = (bf16[2,2,128,512]{3,2,1,0:T(8,128)(2,1)}, bf16[2,2,128,512]{3,2,1,0:T(8,128)(2,1)S(1)}, u32[]{:S(2)}, u32[]{:S(2)}) collective-permute-start(bf16[2,2,128,512]{3,2,1,0:T(8,128)(2,1)} %get-tuple-element.305), channel_id=1, source_target_pairs={{0,16},{1,17},{2,18},{3,19},{4,20},{5,21},{6,22},{7,23},{8,24},{9,... | collective-permute-start | bytes 1572872 | tf_op jit(solution)/shard_map/ppermute | solution.py:403
  267.9 19.6 %collective-permute-start.43 = (bf16[2,2,128,512]{3,2,1,0:T(8,128)(2,1)S(1)}, bf16[2,2,128,512]{3,2,1,0:T(8,128)(2,1)S(1)}, u32[]{:S(2)}, u32[]{:S(2)}) collective-permute-start(bf16[2,2,128,512]{3,2,1,0:T(8,128)(2,1)S(1)} %get-tuple-element.307), channel_id=1, source_target_pairs={{0,8},{1,9},{2,10},{3,11},{4,12},{5,13},{6,14},{7,15},{8,0},{9,1},... | collective-permute-start | bytes 1572872 | tf_op jit(solution)/shard_map/ppermute | solution.py:403
  281.3 46.3 %collective-permute-start.47 = (bf16[2,2,128,512]{3,2,1,0:T(8,128)(2,1)S(1)}, bf16[2,2,128,512]{3,2,1,0:T(8,128)(2,1)S(1)}, u32[]{:S(2)}, u32[]{:S(2)}) collective-permute-start(bf16[2,2,128,512]{3,2,1,0:T(8,128)(2,1)S(1)} %add_convert_fusion.6), channel_id=1, source_target_pairs={{0,1},{1,0},{2,3},{3,2},{4,5},{5,4},{6,7},{7,6},{8,9},{9,8},{10,11... | collective-permute-start | bytes 1572872 | tf_op jit(solution)/shard_map/ppermute | solution.py:403
  287.8 27.9 %collective-permute-start.41 = (bf16[256,1024]{1,0:T(8,128)(2,1)S(1)}, bf16[256,1024]{1,0:T(8,128)(2,1)S(1)}, u32[]{:S(2)}, u32[]{:S(2)}) collective-permute-start(bf16[256,1024]{1,0:T(8,128)(2,1)S(1)} %get-tuple-element.325), channel_id=1, source_target_pairs={{1,0},{0,1},{5,2},{4,3},{3,4},{2,5},{7,6},{6,7},{9,8},{8,9},{13,10... | collective-permute-start | bytes 1572872 | tf_op jit(solution)/shard_map/ppermute | solution.py:403
  288.8 26.9 %collective-permute-start.42 = (bf16[256,1024]{1,0:T(8,128)(2,1)S(1)}, bf16[256,1024]{1,0:T(8,128)(2,1)S(1)}, u32[]{:S(2)}, u32[]{:S(2)}) collective-permute-start(bf16[256,1024]{1,0:T(8,128)(2,1)S(1)} %get-tuple-element.326), channel_id=1, source_target_pairs={{0,0},{1,1},{4,2},{5,3},{2,4},{3,5},{6,6},{7,7},{8,8},{9,9},{12,10... | collective-permute-start | bytes 1572872 | tf_op jit(solution)/shard_map/ppermute | solution.py:403
  289.5 41.0 %collective-permute-start.46 = (bf16[2,2,8,32,512]{4,3,2,1,0:T(8,128)(2,1)}, bf16[2,2,8,32,512]{4,3,2,1,0:T(8,128)(2,1)S(1)}, u32[]{:S(2)}, u32[]{:S(2)}) collective-permute-start(bf16[2,2,8,32,512]{4,3,2,1,0:T(8,128)(2,1)} %get-tuple-element.218), channel_id=1, source_target_pairs={{0,8},{1,9},{2,10},{3,11},{4,12},{5,13},{6,14},{7,15},{8,0},{9,1},... | collective-permute-start | bytes 3145736 | tf_op jit(solution)/shard_map/ppermute | solution.py:403
  291.0 42.2 %collective-permute-start.45 = (bf16[2,2,8,32,512]{4,3,2,1,0:T(8,128)(2,1)}, bf16[2,2,8,32,512]{4,3,2,1,0:T(8,128)(2,1)S(1)}, u32[]{:S(2)}, u32[]{:S(2)}) collective-permute-start(bf16[2,2,8,32,512]{4,3,2,1,0:T(8,128)(2,1)} %get-tuple-element.216), channel_id=1, source_target_pairs={{0,16},{1,17},{2,18},{3,19},{4,20},{5,21},{6,22},{7,23},{8,24},{9,... | collective-permute-start | bytes 3145736 | tf_op jit(solution)/shard_map/ppermute | solution.py:403
  325.6 56.2 %collective-permute-start.59 = (bf16[2,2,10,32,256]{4,3,2,1,0:T(8,128)(2,1)}, bf16[2,2,10,32,256]{4,3,2,1,0:T(8,128)(2,1)S(1)}, u32[]{:S(2)}, u32[]{:S(2)}) collective-permute-start(bf16[2,2,10,32,256]{4,3,2,1,0:T(8,128)(2,1)} %get-tuple-element.212), channel_id=1, source_target_pairs={{0,16},{1,17},{2,18},{3,19},{4,20},{5,21},{6,22},{7,23},{8,24},{9,... | collective-permute-start | bytes 1966088 | tf_op jit(solution)/shard_map/ppermute | solution.py:403
  326.5 59.0 %collective-permute-start.60 = (bf16[2,2,10,32,256]{4,3,2,1,0:T(8,128)(2,1)}, bf16[2,2,10,32,256]{4,3,2,1,0:T(8,128)(2,1)S(1)}, u32[]{:S(2)}, u32[]{:S(2)}) collective-permute-start(bf16[2,2,10,32,256]{4,3,2,1,0:T(8,128)(2,1)} %get-tuple-element.214), channel_id=1, source_target_pairs={{0,8},{1,9},{2,10},{3,11},{4,12},{5,13},{6,14},{7,15},{8,0},{9,1},... | collective-permute-start | bytes 1966088 | tf_op jit(solution)/shard_map/ppermute | solution.py:403
  327.8 25.0 %collective-permute-start.50 = (bf16[2,128,512]{2,1,0:T(8,128)(2,1)S(1)}, bf16[2,128,512]{2,1,0:T(8,128)(2,1)}, u32[]{:S(2)}, u32[]{:S(2)}) collective-permute-start(bf16[2,128,512]{2,1,0:T(8,128)(2,1)S(1)} %get-tuple-element.321), channel_id=1, source_target_pairs={{0,2},{1,3},{2,0},{3,1},{4,6},{5,7},{6,4},{7,5},{8,10},{9,11},{10,... | collective-permute-start | bytes 786440 | tf_op jit(solution)/shard_map/ppermute | solution.py:403
  331.7 24.0 %collective-permute-start.49 = (bf16[2,8,32,512]{3,2,1,0:T(8,128)(2,1)}, bf16[2,8,32,512]{3,2,1,0:T(8,128)(2,1)}, u32[]{:S(2)}, u32[]{:S(2)}) collective-permute-start(bf16[2,8,32,512]{3,2,1,0:T(8,128)(2,1)} %get-tuple-element.301), channel_id=1, source_target_pairs={{0,16},{1,17},{2,18},{3,19},{4,20},{5,21},{6,22},{7,23},{8,24},{9,... | collective-permute-start | bytes 1572872 | tf_op jit(solution)/shard_map/ppermute | solution.py:403
  352.1 10.1 %collective-permute-start.48 = (bf16[2,8,32,512]{3,2,1,0:T(8,128)(2,1)}, bf16[2,8,32,512]{3,2,1,0:T(8,128)(2,1)}, u32[]{:S(2)}, u32[]{:S(2)}) collective-permute-start(bf16[2,8,32,512]{3,2,1,0:T(8,128)(2,1)} %get-tuple-element.303), channel_id=1, source_target_pairs={{0,8},{1,9},{2,10},{3,11},{4,12},{5,13},{6,14},{7,15},{8,0},{9,1},... | collective-permute-start | bytes 1572872 | tf_op jit(solution)/shard_map/ppermute | solution.py:403
  356.9 24.2 %collective-permute-start.72 = (bf16[2,8,32,512]{3,2,1,0:T(8,128)(2,1)S(1)}, bf16[2,8,32,512]{3,2,1,0:T(8,128)(2,1)S(1)}, u32[]{:S(2)}, u32[]{:S(2)}) collective-permute-start(bf16[2,8,32,512]{3,2,1,0:T(8,128)(2,1)S(1)} %add_convert_fusion), channel_id=1, source_target_pairs={{0,1},{1,0},{2,3},{3,2},{4,5},{5,4},{6,7},{7,6},{8,9},{9,8},{10,11... | collective-permute-start | bytes 1572872 | tf_op jit(solution)/shard_map/ppermute | solution.py:403
  373.6 14.0 %collective-permute-start.51 = (bf16[512,1024]{1,0:T(8,128)(2,1)}, bf16[512,1024]{1,0:T(8,128)(2,1)S(1)}, u32[]{:S(2)}, u32[]{:S(2)}) collective-permute-start(bf16[512,1024]{1,0:T(8,128)(2,1)} %get-tuple-element.234), channel_id=1, source_target_pairs={{0,4},{1,5},{2,6},{3,7},{4,0},{5,1},{6,2},{7,3},{8,12},{9,13},{10,... | collective-permute-start | bytes 3145736 | tf_op jit(solution)/shard_map/ppermute | solution.py:403
  380.2 26.0 %collective-permute-start.65 = (bf16[2,2,6,32,256]{4,3,2,1,0:T(8,128)(2,1)}, bf16[2,2,6,32,256]{4,3,2,1,0:T(8,128)(2,1)}, u32[]{:S(2)}, u32[]{:S(2)}) collective-permute-start(bf16[2,2,6,32,256]{4,3,2,1,0:T(8,128)(2,1)} %get-tuple-element.230), channel_id=1, source_target_pairs={{0,16},{1,17},{2,18},{3,19},{4,20},{5,21},{6,22},{7,23},{8,24},{9,... | collective-permute-start | bytes 1179656 | tf_op jit(solution)/shard_map/ppermute | solution.py:403
  381.1 30.0 %collective-permute-start.66 = (bf16[2,2,6,32,256]{4,3,2,1,0:T(8,128)(2,1)}, bf16[2,2,6,32,256]{4,3,2,1,0:T(8,128)(2,1)S(1)}, u32[]{:S(2)}, u32[]{:S(2)}) collective-permute-start(bf16[2,2,6,32,256]{4,3,2,1,0:T(8,128)(2,1)} %get-tuple-element.232), channel_id=1, source_target_pairs={{0,8},{1,9},{2,10},{3,11},{4,12},{5,13},{6,14},{7,15},{8,0},{9,1},... | collective-permute-start | bytes 1179656 | tf_op jit(solution)/shard_map/ppermute | solution.py:403
  381.9 14.7 %collective-permute-start.73 = (bf16[8,32,512]{2,1,0:T(8,128)(2,1)S(1)}, bf16[8,32,512]{2,1,0:T(8,128)(2,1)S(1)}, u32[]{:S(2)}, u32[]{:S(2)}) collective-permute-start(bf16[8,32,512]{2,1,0:T(8,128)(2,1)S(1)} %get-tuple-element.316), channel_id=1, source_target_pairs={{0,2},{1,3},{2,0},{3,1},{4,6},{5,7},{6,4},{7,5},{8,10},{9,11},{10,... | collective-permute-start | bytes 786440 | tf_op jit(solution)/shard_map/ppermute | solution.py:403
  385.5 15.7 %collective-permute-start.61 = (bf16[2,10,32,256]{3,2,1,0:T(8,128)(2,1)}, bf16[2,10,32,256]{3,2,1,0:T(8,128)(2,1)S(1)}, u32[]{:S(2)}, u32[]{:S(2)}) collective-permute-start(bf16[2,10,32,256]{3,2,1,0:T(8,128)(2,1)} %get-tuple-element.309), channel_id=1, source_target_pairs={{0,8},{1,9},{2,10},{3,11},{4,12},{5,13},{6,14},{7,15},{8,0},{9,1},... | collective-permute-start | bytes 983048 | tf_op jit(solution)/shard_map/ppermute | solution.py:403
  387.6 15.1 %collective-permute-start.62 = (bf16[2,10,32,256]{3,2,1,0:T(8,128)(2,1)}, bf16[2,10,32,256]{3,2,1,0:T(8,128)(2,1)}, u32[]{:S(2)}, u32[]{:S(2)}) collective-permute-start(bf16[2,10,32,256]{3,2,1,0:T(8,128)(2,1)} %get-tuple-element.312), channel_id=1, source_target_pairs={{0,16},{1,17},{2,18},{3,19},{4,20},{5,21},{6,22},{7,23},{8,24},{9,... | collective-permute-start | bytes 983048 | tf_op jit(solution)/shard_map/ppermute | solution.py:403
  397.4 28.5 %collective-permute-start.74 = (f32[4,32,512]{2,1,0:T(8,128)}, f32[4,32,512]{2,1,0:T(8,128)}, u32[]{:S(2)}, u32[]{:S(2)}) collective-permute-start(f32[4,32,512]{2,1,0:T(8,128)} %get-tuple-element.336), channel_id=1, source_target_pairs={{0,4},{1,5},{2,6},{3,7},{4,0},{5,1},{6,2},{7,3},{8,12},{9,13},{10,... | collective-permute-start | bytes 786440 | tf_op jit(solution)/shard_map/ppermute | solution.py:403
  401.2 4.0 collective-permute-start.54
  402.7 26.0 %collective-permute-start.52 = (bf16[256,1024]{1,0:T(8,128)(2,1)}, bf16[256,1024]{1,0:T(8,128)(2,1)S(1)}, u32[]{:S(2)}, u32[]{:S(2)}) collective-permute-start(bf16[256,1024]{1,0:T(8,128)(2,1)} %get-tuple-element.319), channel_id=1, source_target_pairs={{1,0},{0,1},{5,2},{4,3},{3,4},{2,5},{7,6},{6,7},{9,8},{8,9},{13,10... | collective-permute-start | bytes 1572872 | tf_op jit(solution)/shard_map/ppermute | solution.py:403
  405.2 23.5 %collective-permute-start.53 = (bf16[256,1024]{1,0:T(8,128)(2,1)S(1)}, bf16[256,1024]{1,0:T(8,128)(2,1)S(1)}, u32[]{:S(2)}, u32[]{:S(2)}) collective-permute-start(bf16[256,1024]{1,0:T(8,128)(2,1)S(1)} %get-tuple-element.320), channel_id=1, source_target_pairs={{0,0},{1,1},{4,2},{5,3},{2,4},{3,5},{6,6},{7,7},{8,8},{9,9},{12,10... | collective-permute-start | bytes 1572872 | tf_op jit(solution)/shard_map/ppermute | solution.py:403
  409.9 7.1 %collective-permute-start.67 = (bf16[2,6,32,256]{3,2,1,0:T(8,128)(2,1)S(1)}, bf16[2,6,32,256]{3,2,1,0:T(8,128)(2,1)S(1)}, u32[]{:S(2)}, u32[]{:S(2)}) collective-permute-start(bf16[2,6,32,256]{3,2,1,0:T(8,128)(2,1)S(1)} %get-tuple-element.329), channel_id=1, source_target_pairs={{0,8},{1,9},{2,10},{3,11},{4,12},{5,13},{6,14},{7,15},{8,0},{9,1},... | collective-permute-start | bytes 589832 | tf_op jit(solution)/shard_map/ppermute | solution.py:403
  411.1 4.7 %collective-permute-start.56 = (f32[28,128]{1,0:T(8,128)S(1)}, f32[28,128]{1,0:T(8,128)S(1)}, u32[]{:S(2)}, u32[]{:S(2)}) collective-permute-start(f32[28,128]{1,0:T(8,128)S(1)} %pad_maximum_fusion.19), channel_id=1, source_target_pairs={{0,8},{1,9},{2,10},{3,11},{4,12},{5,13},{6,14},{7,15},{8,0},{9,1},... | collective-permute-start | bytes 43016 | tf_op jit(solution)/shard_map/ppermute | solution.py:403
  415.8 6.2 %collective-permute-start.68 = (bf16[2,6,32,256]{3,2,1,0:T(8,128)(2,1)S(1)}, bf16[2,6,32,256]{3,2,1,0:T(8,128)(2,1)S(1)}, u32[]{:S(2)}, u32[]{:S(2)}) collective-permute-start(bf16[2,6,32,256]{3,2,1,0:T(8,128)(2,1)S(1)} %get-tuple-element.332), channel_id=1, source_target_pairs={{0,16},{1,17},{2,18},{3,19},{4,20},{5,21},{6,22},{7,23},{8,24},{9,... | collective-permute-start | bytes 589832 | tf_op jit(solution)/shard_map/ppermute | solution.py:403
  417.0 15.8 %collective-permute-start.63 = (bf16[2,10,32,256]{3,2,1,0:T(8,128)(2,1)}, bf16[2,10,32,256]{3,2,1,0:T(8,128)(2,1)S(1)}, u32[]{:S(2)}, u32[]{:S(2)}) collective-permute-start(bf16[2,10,32,256]{3,2,1,0:T(8,128)(2,1)} %add_convert_fusion.12), channel_id=1, source_target_pairs={{0,1},{1,0},{2,3},{3,2},{4,5},{5,4},{6,7},{7,6},{8,9},{9,8},{10,11... | collective-permute-start | bytes 983048 | tf_op jit(solution)/shard_map/ppermute | solution.py:403
  422.8 14.4 %collective-permute-start.69 = (bf16[2,6,32,256]{3,2,1,0:T(8,128)(2,1)}, bf16[2,6,32,256]{3,2,1,0:T(8,128)(2,1)}, u32[]{:S(2)}, u32[]{:S(2)}) collective-permute-start(bf16[2,6,32,256]{3,2,1,0:T(8,128)(2,1)} %add_convert_fusion.22), channel_id=1, source_target_pairs={{0,1},{1,0},{2,3},{3,2},{4,5},{5,4},{6,7},{7,6},{8,9},{9,8},{10,11... | collective-permute-start | bytes 589832 | tf_op jit(solution)/shard_map/ppermute | solution.py:403
  429.8 4.7 %collective-permute-start.57 = (f32[38,128]{1,0:T(8,128)S(1)}, f32[38,128]{1,0:T(8,128)S(1)}, u32[]{:S(2)}, u32[]{:S(2)}) collective-permute-start(f32[38,128]{1,0:T(8,128)S(1)} %pad_maximum_fusion.17), channel_id=1, source_target_pairs={{0,2},{1,3},{2,0},{3,1},{4,6},{5,7},{6,4},{7,5},{8,10},{9,11},{10,... | collective-permute-start | bytes 58376 | tf_op jit(solution)/shard_map/ppermute | solution.py:403
  435.1 6.1 %collective-permute-start.58 = (f32[67,128]{1,0:T(8,128)S(1)}, f32[67,128]{1,0:T(8,128)S(1)}, u32[]{:S(2)}, u32[]{:S(2)}) collective-permute-start(f32[67,128]{1,0:T(8,128)S(1)} %concatenate.107), channel_id=1, source_target_pairs={{0,1},{1,0},{2,3},{3,2},{4,5},{5,4},{6,7},{7,6},{8,9},{9,8},{10,11... | collective-permute-start | bytes 102920 | tf_op jit(solution)/shard_map/ppermute | solution.py:403
  438.1 10.7 %collective-permute-start.70 = (bf16[6,32,256]{2,1,0:T(8,128)(2,1)S(1)}, bf16[6,32,256]{2,1,0:T(8,128)(2,1)S(1)}, u32[]{:S(2)}, u32[]{:S(2)}) collective-permute-start(bf16[6,32,256]{2,1,0:T(8,128)(2,1)S(1)} %get-tuple-element.258), channel_id=1, source_target_pairs={{0,2},{1,3},{2,0},{3,1},{4,6},{5,7},{6,4},{7,5},{8,10},{9,11},{10,... | collective-permute-start | bytes 294920 | tf_op jit(solution)/shard_map/ppermute | solution.py:403
  441.1 10.8 %collective-permute-start.64 = (bf16[10,32,256]{2,1,0:T(8,128)(2,1)S(1)}, bf16[10,32,256]{2,1,0:T(8,128)(2,1)S(1)}, u32[]{:S(2)}, u32[]{:S(2)}) collective-permute-start(bf16[10,32,256]{2,1,0:T(8,128)(2,1)S(1)} %get-tuple-element.252), channel_id=1, source_target_pairs={{0,2},{1,3},{2,0},{3,1},{4,6},{5,7},{6,4},{7,5},{8,10},{9,11},{10,... | collective-permute-start | bytes 491528 | tf_op jit(solution)/shard_map/ppermute | solution.py:403
  (58 other events, 305.6 us)

commit v5 on v4

--- a/solution.py
+++ b/solution.py
@@ -658,48 +658,91 @@
     )
 
 
-def attend_back(meta, part, qkv, out, grad, lse, seg_column, seg_row):
-    def kernel(m, q_ref, k_ref, v_ref, out_ref, grad_ref, lse_ref, column_ref, row_ref, d_ref, sum_ref, prob, ds):
-        queries, upstream = q_ref[0], grad_ref[...]
-        product = out_ref[...].astype(F32) * upstream.astype(F32)
-        row = lax.broadcasted_iota(jnp.int32, (8, 128), 0)
-        lane = lax.broadcasted_iota(jnp.int32, (8, 128), 1)
-        picked = jnp.where(lane // HEAD_DIM == row, 1.0, 0.0).astype(F32)
-        center = lax.dot_general(picked, product, NT, precision=lax.Precision.HIGHEST, preferred_element_type=F32)
-        dq, dk, dv = (jnp.zeros((1024, 128), F32) for _ in range(3))
-        for h in range(2):
-            lanes = head_lanes(h, BF)
-            for block in range(4):
-                rows = pl.ds(block * 256, 256)
-                allowed = column_ref[rows, :] == row_ref[...]
-                scores = dot(k_ref[0, rows, :] * lanes * jnp.asarray(0.125, BF), queries, NT)
-                p = jnp.where(allowed, jnp.exp(scores - lse_ref[0, h : h + 1, :]), 0.0)
-                dp = dot(v_ref[0, rows, :] * lanes, upstream, NT)
-                prob[rows, :] = p.astype(BF)
-                ds[rows, :] = (p * (dp - center[h : h + 1, :])).astype(BF)
-            dv += dot(prob[...], upstream * lanes)
-            dk += dot(ds[...], queries * lanes)
-            dq += dot(ds[...], k_ref[0] * lanes, TN)
-        dq, dk, dv = (dq * 0.125).astype(BF), (dk * 0.125).astype(BF), dv.astype(BF)
-        d_ref[0], d_ref[1], d_ref[2] = dq, dk, dv
-        sum_ref[0:1, :] = jnp.sum(dq.astype(F32), axis=0, keepdims=True)
-        sum_ref[1:2, :] = jnp.sum(dv.astype(F32), axis=0, keepdims=True)
-
-    base = part * 2
-    third = lambda t: spec((1, 1024, 128), lambda i, m: (t, 0, base + i))
-    heads = lambda first: spec((1024, 128), lambda i, m: (0, first + i))
+def attend_back(i, q_ref, k_ref, v_ref, out_ref, lse_ref, column_ref, row_ref, d_ref, sum_ref, dout, prob, ds):
+    columns = pl.ds(pl.multiple_of(i * 128, 128), 128)
+    queries, upstream = q_ref[0], dout[:, columns]
+    product = out_ref[...].astype(F32) * upstream.astype(F32)
+    row = lax.broadcasted_iota(jnp.int32, (8, 128), 0)
+    lane = lax.broadcasted_iota(jnp.int32, (8, 128), 1)
+    picked = jnp.where(lane // HEAD_DIM == row, 1.0, 0.0).astype(F32)
+    center = lax.dot_general(picked, product, NT, precision=lax.Precision.HIGHEST, preferred_element_type=F32)
+    dq, dk, dv = (jnp.zeros((1024, 128), F32) for _ in range(3))
+    for h in range(2):
+        lanes = head_lanes(h, BF)
+        for block in range(4):
+            rows = pl.ds(block * 256, 256)
+            allowed = column_ref[rows, :] == row_ref[...]
+            scores = dot(k_ref[0, rows, :] * lanes * jnp.asarray(0.125, BF), queries, NT)
+            p = jnp.where(allowed, jnp.exp(scores - lse_ref[0, h : h + 1, :]), 0.0)
+            dp = dot(v_ref[0, rows, :] * lanes, upstream, NT)
+            prob[rows, :] = p.astype(BF)
+            ds[rows, :] = (p * (dp - center[h : h + 1, :])).astype(BF)
+        dv += dot(prob[...], upstream * lanes)
+        dk += dot(ds[...], queries * lanes)
+        dq += dot(ds[...], k_ref[0] * lanes, TN)
+    dq, dk, dv = (dq * 0.125).astype(BF), (dk * 0.125).astype(BF), dv.astype(BF)
+    d_ref[0, :, columns], d_ref[1, :, columns], d_ref[2, :, columns] = dq, dk, dv
+    sum_ref[0:1, columns] = jnp.sum(dq.astype(F32), axis=0, keepdims=True)
+    sum_ref[1:2, columns] = jnp.sum(dv.astype(F32), axis=0, keepdims=True)
+
+
+def heads_out(part, own_ref, other_ref, weight, dout):
+    rows = pl.ds(part * 256, 256)
+    for half, ref in enumerate((own_ref, other_ref)):
+        da = ref[...]
+        result = dot(da[:, :512], weight[0, rows, :], NT) + dot(da[:, 512:], weight[1, rows, :], NT)
+        dout[pl.ds(half * 512, 512), :] = result.astype(BF)
+
+
+def attend_specs(part):
+    pair = lambda i: jnp.minimum(i, 1)
+    third = lambda t: spec((1, 1024, 128), lambda i, m: (t, 0, part * 2 + pair(i)))
+    return [
+        third(0),
+        third(1),
+        third(2),
+        spec((1024, 128), lambda i, m: (0, pair(i))),
+        spec((1, 8, 1024), lambda i, m: (pair(i), 0, 0)),
+        whole((1024, 1)),
+        whole((1, 1024)),
+        whole((512, 1024)),
+        whole((512, 1024)),
+    ]
+
+
+ATTEND_SCRATCH = (
+    pltpu.VMEM((2, 512, 512), BF),
+    pltpu.VMEM((1024, 256), BF),
+    pltpu.VMEM((1024, 1024), BF),
+    pltpu.VMEM((1024, 1024), BF),
+    pltpu.SemaphoreType.DMA((32,)),
+)
+
+
+def attend_back_part(meta, part, qkv, mixed, lse, seg_column, seg_row, da_own, da_other, pieces):
+    def kernel(m, q_ref, k_ref, v_ref, out_ref, lse_ref, column_ref, row_ref, own_ref, other_ref, *rest):
+        refs, (d_ref, sum_ref), (weight, dout, prob, ds, sem) = rest[:4], rest[4:6], rest[6:]
+        i = pl.program_id(0)
+
+        @pl.when(i == 0)
+        def _():
+            load_all(load_out(m, refs, weight, sem))
+            heads_out(part, own_ref, other_ref, weight, dout)
+
+        attend_back(i, q_ref, k_ref, v_ref, out_ref, lse_ref, column_ref, row_ref, d_ref, sum_ref, dout, prob, ds)
+
     return kernel_call(
         kernel,
         meta,
-        (qkv, qkv, qkv, out, grad, lse, seg_column, seg_row),
-        [third(0), third(1), third(2), heads(0), heads(base), spec((1, 8, 1024), lambda i, m: (i, 0, 0)), whole((1024, 1)), whole((1, 1024))],
-        [spec((3, 1024, 128), lambda i, m: (0, 0, i)), spec((8, 128), lambda i, m: (0, i))],
+        (qkv, qkv, qkv, mixed, lse, seg_column, seg_row, da_own, da_other, *pieces),
+        attend_specs(part) + [HBM] * 4,
+        [whole((3, 1024, 256)), whole((8, 256))],
         [shaped((3, 1024, 256), BF), shaped((8, 256), F32)],
-        [pltpu.VMEM((1024, 1024), BF), pltpu.VMEM((1024, 1024), BF)],
+        ATTEND_SCRATCH,
         grid=(2,),
-        flops=8 * 10 * 1024 * 1024 * 256,
-        moved=8 << 20,
-        exps=8 << 20,
+        flops=11 * 10**9,
+        moved=10 << 20,
+        exps=4 << 20,
     )
 
 
@@ -969,35 +1012,6 @@
     )
 
 
-def output_back(meta, own, other, pieces):
-    def kernel(m, own_ref, other_ref, *rest):
-        refs, (out_ref, weight, sem) = rest[:4], rest[4:]
-        i = pl.program_id(0)
-
-        @pl.when(i == 0)
-        def _():
-            load_all(load_out(m, refs, weight, sem))
-
-        da = jnp.where(i < 2, own_ref[...].astype(F32), other_ref[...].astype(F32)).astype(BF)
-        out_ref[...] = (dot(da[:, :512], weight[0], NT) + dot(da[:, 512:], weight[1], NT)).astype(BF)
-
-    return kernel_call(
-        kernel,
-        meta,
-        (own, other, *pieces),
-        [
-            spec((256, 1024), lambda i, m: (low_block(i), 0)),
-            spec((256, 1024), lambda i, m: (high_block(i), 0)),
-        ]
-        + [HBM] * 4,
-        spec((256, 512), BY_ROWS),
-        shaped((1024, 512), BF),
-        [pltpu.VMEM((2, 512, 512), BF), pltpu.SemaphoreType.DMA((32,))],
-        flops=2 * 1024 * 1024 * 512,
-        moved=4 << 20,
-    )
-
-
 def rel_chip(s, m):
     return (m[0] ^ (s // 2)) * 2 + (m[1] ^ lax.rem(s, 2))
 
@@ -1294,8 +1308,8 @@
     def take_rows(value, *earlier):
         return jnp.stack(after([send(pick(value, (z + k) % 2, 0), ROW_OUT[k]) for k in range(2)], earlier))
 
-    def give_rows(value):
-        parts = [send(value[k * 256 : (k + 1) * 256], ROW_BACK[k]) for k in range(2)]
+    def give_rows(value, *earlier):
+        parts = after([send(value[k * 256 : (k + 1) * 256], ROW_BACK[k]) for k in range(2)], earlier)
         swapped = (z % 2) == 1
         return jnp.stack([jnp.where(swapped, parts[1], parts[0]), jnp.where(swapped, parts[0], parts[1])])
 
@@ -1354,41 +1368,43 @@
 
     df_other = send(df, PAIR)
     down_terms = weigh_down(meta, activated, df, df_other)
-    du, away, mine, up_sums = feed_back(meta, after(df, down_terms), df_other, slope, down_pieces, up_pieces)
+    du, away, mine, bias_sums = feed_back(meta, after(df, down_terms), df_other, slope, down_pieces, up_pieces)
     received = send(away, PAIR)
     up_terms = weigh_up(meta, normed, normed_other, du)
+    output = give_rows(after(result, down_terms), up_terms)
     down_sums = add_one(*scatter_one(*down_terms), up_terms)
     resid_one, da, sums_one = first_norm_back(
-        meta, after(resid_two, down_sums), mine, received, normal_one, inverse_one, vectors
+        meta, after(resid_two, down_sums, output), mine, received, normal_one, inverse_one, vectors
     )
     da_other = send(da, PAIR)
-    dout = output_back(meta, da, da_other, qkv_pieces)
-    down_sums = add_two(*scatter_two(*down_sums), dout)
-    output = give_rows(after(result, dout))
-    grad = after(dout, down_sums)
-    dqkv_one, qv_sums_one = attend_back(meta, 0, qkv, mixed_one, grad, lse_one, seg_column, seg_row)
-    output = after(output, dqkv_one)
-    qkv_terms_one = weigh_qkv(meta, hidden, after(dqkv_one, output), (mixed_one, mixed_two, da, da_other))
-    up_sums_one = add_one(*scatter_one(*after(up_terms, dout)), qkv_terms_one)
-    down_sums = add_three(*scatter_three(*down_sums), qkv_terms_one)
-    grad = after(dout, up_sums_one, down_sums)
-    dqkv_two, qv_sums_two = attend_back(meta, 1, qkv, mixed_two, grad, lse_two, seg_column, seg_row)
-    up_sums_two = add_two(*scatter_two(*up_sums_one), dqkv_two)
-    down_share = scatter_four(*down_sums, dqkv_two)
-    away, mine = qkv_back(meta, (dqkv_one, after(dqkv_two, up_sums_two, down_share)), qkv_pieces)
+    down_sums = scatter_two(*down_sums)
+    up_sums = scatter_one(*after(up_terms, da))
+    heads = lambda part, mixed, lse, own: attend_back_part(
+        meta, part, qkv, mixed, lse, seg_column, seg_row, own, da_other, qkv_pieces
+    )
+    dqkv_one, qv_sums_one = heads(0, mixed_one, lse_one, da)
+    down_sums = add_two(*down_sums, dqkv_one)
+    dqkv_one = after(dqkv_one, down_sums)
+    qkv_terms_one = weigh_qkv(meta, hidden, dqkv_one, (mixed_one, mixed_two, da, da_other))
+    up_sums = add_one(*up_sums, qkv_terms_one)
+    dqkv_two, qv_sums_two = heads(1, mixed_two, lse_two, after(da, qkv_terms_one, up_sums))
+    down_sums = add_three(*scatter_three(*down_sums), dqkv_two)
+    up_sums = add_two(*scatter_two(*up_sums), dqkv_two)
+    qkv_sums_one = add_one(*scatter_one(*qkv_terms_one), dqkv_two)
+    dqkv_two = after(dqkv_two, up_sums, qkv_sums_one, down_sums)
+    away, mine = qkv_back(meta, (dqkv_one, dqkv_two), qkv_pieces)
     received = send(away, PAIR)
-    qkv_terms_two = weigh_qkv(meta, hidden, after(dqkv_two, mine))
-    qkv_sums_one = add_one(*scatter_one(*qkv_terms_one), mine)
+    qkv_sums_one = add_two(*scatter_two(*qkv_sums_one), mine)
+    up_sums = add_three(*scatter_three(*up_sums), mine)
+    down_share = scatter_four(*down_sums, mine)
+    qkv_terms_two = weigh_qkv(meta, hidden, after(dqkv_two, mine, qkv_sums_one))
+    qkv_sums_one = add_three(*scatter_three(*qkv_sums_one), qkv_terms_two)
     input_low, embed_sums = last_sum(meta, resid_one, after(mine, qkv_terms_two), received)
     input_grad = give_rows(input_low)
-    up_sums_three = add_three(*scatter_three(*up_sums_two), qkv_terms_two)
-    qkv_sums_one = add_two(*scatter_two(*qkv_sums_one), input_low)
-    qkv_sums_two = add_one(*scatter_one(*qkv_terms_two), input_low)
-    qkv_sums_two = add_two(*scatter_two(*qkv_sums_two))
-    qkv_sums_one = add_three(*scatter_three(*qkv_sums_one))
-    up_share = scatter_four(*up_sums_three, input_low)
+    up_share = scatter_four(*up_sums, input_low)
+    qkv_sums_two = add_two(*scatter_two(*add_one(*scatter_one(*qkv_terms_two), input_low)))
     qkv_sums_two = add_three(*scatter_three(*qkv_sums_two))
-    qkv_share_one = scatter_four(*after(qkv_sums_one, input_grad))
+    qkv_share_one = scatter_four(*qkv_sums_one, input_low)
     qkv_share_two = scatter_four(*after(qkv_sums_two, input_grad))
     qkv_share = jnp.concatenate([qkv_share_one[:6], qkv_share_two], axis=2)
     qv_sums = jnp.concatenate([qv_sums_one[0:2], qv_sums_two[0:2]], axis=1)
@@ -1404,7 +1420,7 @@
     grad_qkv = both_halves(split(qkv_share[:3]), split(send(qkv_share[3:], PAIR)))
     grad_qkv = grad_qkv.transpose(1, 0, 2, 3, 4).reshape(32, 3072)
 
-    qv_sums, up_sums, sums_one, sums_two = after((qv_sums, up_sums, sums_one, sums_two), input_low)
+    qv_sums, bias_sums, sums_one, sums_two = after((qv_sums, bias_sums, sums_one, sums_two), input_low)
     core_lane = (jnp.arange(2) == c).astype(F32)
     spread = lambda sums, width: (sums.reshape(-1, 1, width) * core_lane[None, :, None]).reshape(32, -1)
     grads = jnp.concatenate(
@@ -1413,7 +1429,7 @@
             sums_one[2].reshape(32, 32),
             sums_one[0].reshape(32, 32),
             sums_one[1].reshape(32, 32),
-            spread(up_sums[0:1], 512),
+            spread(bias_sums[0:1], 512),
             sums_two[2].reshape(32, 32),
             sums_two[0].reshape(32, 32),
             sums_two[1].reshape(32, 32),

time: 462 us -> 451 us (0.976)
  waiting for transfers between devices: 111 us -> 95.1 us
    ppermute x75, waiting for transfers between devices: 111 us -> 95.1 us  [send(): return lax.ppermute(value, AXES, pairs)]
    pallas_call x19 -> x18, Pallas kernels: 189 us -> 188 us  [kernel_call(): pl.pallas_call(kernel, grid_spec=pltpu.PrefetchScalarGridSpec(num_scalar_...]
  transfers between devices with their start and end apart: 75 -> 75, of which waited for: 31 -> 29; matrix products, arithmetic and copies ran while one was open for 10% -> 11% of each run, Pallas kernels for 34% -> 35%
where the time goes in v5:
time: 451 us; the launch traced here: 445 us
  Pallas kernels  188 us (42%)
  starting transfers between devices  98.5 us (22%)
  waiting for transfers between devices  95.1 us (21%)
  local copies, waits for them, and re-layouts  29.6 us (7%)
  other arithmetic  29.2 us (6%)
    pallas_call x18, Pallas kernels, kernel_call(): pl.pallas_call(kernel, grid_spec=pltpu.PrefetchScalarGridSpec(num_scalar_...  188 us
    ppermute x75, starting transfers between devices, send(): return lax.ppermute(value, AXES, pairs)  98.5 us
    ppermute x75, waiting for transfers between devices, send(): return lax.ppermute(value, AXES, pairs)  95.1 us
    convert_element_type x20, other arithmetic, add_low(): return (a.astype(F32) + b.astype(F32)).astype(BF)  15.2 us
  transfers between devices with their start and end apart: 75, of which 29 were waited for; matrix products, arithmetic and copies ran while one was open for 11% of the time, Pallas kernels for 35%

profile of v5, /device:TPU:0, one launch (start us, length us, event | category | flops | bytes accessed | tf_op | source)
XLA Modules:
  0.0 444.6 jit_solution(8175208460820747502)
XLA Ops:
  6.2 4.1 collective-permute-start.1
  13.1 2.0 collective-permute-done.6
  15.3 1.5 collective-permute-start.7
  16.8 2.0 collective-permute-done.7
  19.8 3.3 collective-permute-done.1
  25.4 1.6 collective-permute-start.9
  29.4 1.6 collective-permute-start.10
  32.2 5.1 %collective-permute-done.2 = bf16[2,272,512]{2,1,0:T(8,128)(2,1)S(1)} collective-permute-done((bf16[2,272,512]{2,1,0:T(8,128)(2,1)S(1)}, bf16[2,272,512]{2,1,0:T(8,128)(2,1)S(1)}, u32[]{:S(2)}, u32[]{:S(2)}) %collective-permute-start.2) | collective-permute-done | bytes 557088 | tf_op jit(solution)/shard_map/ppermute | solution.py:403
  38.6 3.2 collective-permute-start.11
  42.6 1.8 collective-permute-start.4
  45.3 5.1 %collective-permute-done.15 = bf16[2,272,512]{2,1,0:T(8,128)(2,1)S(1)} collective-permute-done((bf16[2,272,512]{2,1,0:T(8,128)(2,1)S(1)}, bf16[2,272,512]{2,1,0:T(8,128)(2,1)S(1)}, u32[]{:S(2)}, u32[]{:S(2)}) %collective-permute-start.15) | collective-permute-done | bytes 557088 | tf_op jit(solution)/shard_map/ppermute | solution.py:403
  51.5 6.0 %collective-permute-done.12 = f32[1,1024]{1,0:T(1,128)S(1)} collective-permute-done((f32[1,1024]{1,0:T(1,128)S(1)}, f32[1,1024]{1,0:T(1,128)S(1)}, u32[]{:S(2)}, u32[]{:S(2)}) %collective-permute-start.12) | collective-permute-done | bytes 4128 | tf_op jit(solution)/shard_map/ppermute | solution.py:403
  58.2 1.6 collective-permute-start.16
  59.9 4.8 %collective-permute-start.13 = (bf16[2,272,1024]{2,1,0:T(8,128)(2,1)S(1)}, bf16[2,272,1024]{2,1,0:T(8,128)(2,1)}, u32[]{:S(2)}, u32[]{:S(2)}) collective-permute-start(bf16[2,272,1024]{2,1,0:T(8,128)(2,1)S(1)} %pad_maximum_fusion.own_ref.tok_ref), channel_id=1, source_target_pairs={{0,4},{1,5},{2,6},{3,7},{4,0},{5,1},{6,2},{7,3},{8,12},{9,13},{10,... | collective-permute-start | bytes 3342344 | tf_op jit(solution)/shard_map/ppermute | solution.py:403
  64.7 7.1 %collective-permute-start.19 = (bf16[8,32,512]{2,1,0:T(8,128)(2,1)}, bf16[8,32,512]{2,1,0:T(8,128)(2,1)}, u32[]{:S(2)}, u32[]{:S(2)}) collective-permute-start(bf16[8,32,512]{2,1,0:T(8,128)(2,1)} %pad_maximum_fusion.13), channel_id=1, source_target_pairs={{0,2},{1,3},{2,0},{3,1},{4,6},{5,7},{6,4},{7,5},{8,10},{9,11},{10,... | collective-permute-start | bytes 786440 | tf_op jit(solution)/shard_map/ppermute | solution.py:403
  71.9 2.8 collective-permute-done.17.rest_1_
  74.7 7.0 %collective-permute-done.16.rest_3_ = bf16[2,2,272,512]{3,2,1,0:T(8,128)(2,1)S(1)} collective-permute-done((bf16[2,2,272,512]{3,2,1,0:T(8,128)(2,1)S(1)}, bf16[2,2,272,512]{3,2,1,0:T(8,128)(2,1)S(1)}, u32[]{:S(2)}, u32[]{:S(2)}) %collective-permute-start.16) | collective-permute-done | bytes 1114144 | tf_op jit(solution)/shard_map/ppermute | solution.py:403
  83.9 10.4 %shard_map.280 = (bf16[1024,1024]{1,0:T(8,128)(2,1)}, bf16[3,1024,512]{2,1,0:T(8,128)(2,1)}) custom-call(s32[4]{0:T(128)} %pad_add_fusion.m, bf16[2,272,1024]{2,1,0:T(8,128)(2,1)} %copy-done.2, bf16[2,272,1024]{2,1,0:T(8,128)(2,1)} %collective-permute-done.13.other_ref, f32[1,1024]{1,0:T(1,128)} %slice_add_fusion.8.emb_ref, ...), custom_call_target="tpu_custom_call" | custom-call | flops 4831838208 | bytes 15728640 | tf_op jit(solution)/shard_map/pallas_call | solution.py:547
  95.4 2.5 collective-permute-start.20
  101.3 10.1 %shard_map.281 = (bf16[1024,256]{1,0:T(8,128)(2,1)}, f32[2,8,1024]{2,1,0:T(8,128)}) custom-call(s32[4]{0:T(128)} %pad_add_fusion.m, bf16[3,1024,512]{2,1,0:T(8,128)(2,1)} %get-tuple-element.153.q_ref.k_ref.v_ref, bf16[3,1024,512]{2,1,0:T(8,128)(2,1)} %get-tuple-element.153.q_ref.k_ref.v_ref, bf16[3,1024,512]{2,1,0:T(8,128)(2,1)} %get-tuple-element.153.q_ref.k_ref.v_ref, ...), custom_call_target="tpu_custom_call" | custom-call | flops 12884901888 | bytes 7864320 | tf_op jit(solution)/shard_map/pallas_call | solution.py:547
  111.9 10.0 %shard_map.282 = (bf16[1024,256]{1,0:T(8,128)(2,1)}, f32[2,8,1024]{2,1,0:T(8,128)}) custom-call(s32[4]{0:T(128)} %pad_add_fusion.m, bf16[3,1024,512]{2,1,0:T(8,128)(2,1)} %get-tuple-element.153.q_ref.k_ref.v_ref, bf16[3,1024,512]{2,1,0:T(8,128)(2,1)} %get-tuple-element.153.q_ref.k_ref.v_ref, bf16[3,1024,512]{2,1,0:T(8,128)(2,1)} %get-tuple-element.153.q_ref.k_ref.v_ref, ...), custom_call_target="tpu_custom_call" | custom-call | flops 12884901888 | bytes 7864320 | tf_op jit(solution)/shard_map/pallas_call | solution.py:547
  121.9 5.1 %collective-permute-done.21 = bf16[2,128,512]{2,1,0:T(8,128)(2,1)S(1)} collective-permute-done((bf16[2,128,512]{2,1,0:T(8,128)(2,1)S(1)}, bf16[2,128,512]{2,1,0:T(8,128)(2,1)S(1)}, u32[]{:S(2)}, u32[]{:S(2)}) %collective-permute-start.21) | collective-permute-done | bytes 262176 | tf_op jit(solution)/shard_map/ppermute | solution.py:403
  129.1 1.6 collective-permute-start.25
  130.6 7.4 %shard_map.283 = (bf16[512,1024]{1,0:T(8,128)(2,1)}, f32[512,1024]{1,0:T(8,128)}) custom-call(s32[4]{0:T(128)} %pad_add_fusion.m, bf16[1024,256]{1,0:T(8,128)(2,1)} %get-tuple-element.151.x_ref.out_ref.rest_0_, bf16[1024,256]{1,0:T(8,128)(2,1)} %get-tuple-element.161.w_ref.rest_1_.out_ref, bf16[2,2,272,512]{3,2,1,0:T(8,128)(2,1)} %copy-done.4, ...), custom_call_target="tpu_custom_call" | custom-call | flops 1610612736 | bytes 9437184 | tf_op jit(solution)/shard_map/pallas_call | solution.py:547
  138.3 1.5 collective-permute-start.29
  139.8 12.9 %collective-permute-done.24 = bf16[2,2,128,512]{3,2,1,0:T(8,128)(2,1)} collective-permute-done((bf16[2,2,128,512]{3,2,1,0:T(8,128)(2,1)S(1)}, bf16[2,2,128,512]{3,2,1,0:T(8,128)(2,1)}, u32[]{:S(2)}, u32[]{:S(2)}) %collective-permute-start.24) | collective-permute-done | bytes 524320 | tf_op jit(solution)/shard_map/ppermute | solution.py:403
  154.4 4.6 %shard_map.284 = (f32[512,1024]{1,0:T(8,128)}, f32[512,128]{1,0:T(8,128)}, bf16[512,1024]{1,0:T(8,128)(2,1)}) custom-call(s32[4]{0:T(128)} %pad_add_fusion.m, bf16[2,272,1024]{2,1,0:T(8,128)(2,1)} %copy-done.2, f32[1,1024]{1,0:T(1,128)} %slice_add_fusion.8.emb_ref, f32[512,1024]{1,0:T(8,128)} %get-tuple-element.164.own_ref, ...), custom_call_target="tpu_custom_call" | custom-call | flops 9437184 | bytes 12582912 | tf_op jit(solution)/shard_map/pallas_call | solution.py:547
  159.0 4.7 %collective-permute-done.29 = bf16[2,2,128,512]{3,2,1,0:T(8,128)(2,1)S(1)} collective-permute-done((bf16[2,2,128,512]{3,2,1,0:T(8,128)(2,1)S(1)}, bf16[2,2,128,512]{3,2,1,0:T(8,128)(2,1)S(1)}, u32[]{:S(2)}, u32[]{:S(2)}) %collective-permute-start.29) | collective-permute-done | bytes 524320 | tf_op jit(solution)/shard_map/ppermute | solution.py:403
  163.7 2.7 collective-permute-done.30
  173.2 13.2 %shard_map.285 = (bf16[1024,2048]{1,0:T(8,128)(2,1)}, bf16[1024,2048]{1,0:T(8,128)(2,1)}) custom-call(s32[4]{0:T(128)} %pad_add_fusion.m, bf16[512,1024]{1,0:T(8,128)(2,1)} %get-tuple-element.167.own_ref, bf16[512,1024]{1,0:T(8,128)(2,1)} %collective-permute-done.28.other_ref, f32[1,2048]{1,0:T(1,128)} %bitcast.334, bf16[2,2,8,32,512]{4,3,2,1,0:T(8,128)(2,1)} %copy-done.12, ...), custom_call_target="tpu_custom_call" | custom-call | flops 6442450944 | bytes 22020096 | tf_op jit(solution)/shard_map/pallas_call | solution.py:547
  187.5 4.3 collective-permute-done.34.rest_3_
  193.1 11.5 %shard_map.286 = (bf16[512,1024]{1,0:T(8,128)(2,1)}, f32[512,1024]{1,0:T(8,128)}) custom-call(s32[4]{0:T(128)} %pad_add_fusion.m, bf16[1024,2048]{1,0:T(8,128)(2,1)} %get-tuple-element.177.x_ref, bf16[2,2,2,128,512]{4,3,2,1,0:T(8,128)(2,1)} %copy-done.14, bf16[2,2,2,128,512]{4,3,2,1,0:T(8,128)(2,1)} %collective-permute-done.33.rest_1_, ...), custom_call_target="tpu_custom_call" | custom-call | flops 6442450944 | bytes 17301504 | tf_op jit(solution)/shard_map/pallas_call | solution.py:547
  205.5 2.5 collective-permute-done.35.recv_ref
  208.9 6.5 %shard_map.287 = (bf16[512,1024]{1,0:T(8,128)(2,1)}, f32[512,1024]{1,0:T(8,128)}, bf16[512,1024]{1,0:T(8,128)(2,1)}, f32[8,1024]{1,0:T(8,128)}) custom-call(s32[4]{0:T(128)} %pad_add_fusion.m, f32[512,1024]{1,0:T(8,128)} %get-tuple-element.166.normal_ref, f32[512,1024]{1,0:T(8,128)} %get-tuple-element.178.own_ref, bf16[512,1024]{1,0:T(8,128)(2,1)} %copy-done.10, ...), custom_call_target="tpu_custom_call" | custom-call | flops 23592960 | bytes 15728640 | tf_op jit(solution)/shard_map/pallas_call | solution.py:547
  215.8 2.5 collective-permute-done.36.other_ref
  219.4 9.2 %shard_map.288 = (bf16[2,2,2,128,512]{4,3,2,1,0:T(8,128)(2,1)}, bf16[2,2,2,128,512]{4,3,2,1,0:T(8,128)(2,1)}, bf16[2,2,2,128,512]{4,3,2,1,0:T(8,128)(2,1)}, bf16[2,2,2,128,512]{4,3,2,1,0:T(8,128)(2,1)}) custom-call(s32[4]{0:T(128)} %pad_add_fusion.m, bf16[1024,2048]{1,0:T(8,128)(2,1)} %get-tuple-element.177.x_ref, ...), custom_call_target="tpu_custom_call" | custom-call | flops 6442450944 | bytes 15728640 | tf_op jit(solution)/shard_map/pallas_call | solution.py:547
  231.6 6.2 %collective-permute-start.38 = (bf16[256,1024]{1,0:T(8,128)(2,1)S(1)}, bf16[256,1024]{1,0:T(8,128)(2,1)S(1)}, u32[]{:S(2)}, u32[]{:S(2)}) collective-permute-start(bf16[256,1024]{1,0:T(8,128)(2,1)S(1)} %get-tuple-element.329), channel_id=1, source_target_pairs={{1,0},{0,1},{5,2},{4,3},{3,4},{2,5},{7,6},{6,7},{9,8},{8,9},{13,10... | collective-permute-start | bytes 1572872 | tf_op jit(solution)/shard_map/ppermute | solution.py:403
  237.8 18.9 %shard_map.289 = (bf16[1024,2048]{1,0:T(8,128)(2,1)}, bf16[512,1024]{1,0:T(8,128)(2,1)}, f32[512,1024]{1,0:T(8,128)}, f32[8,2048]{1,0:T(8,128)}) custom-call(s32[4]{0:T(128)} %pad_add_fusion.m, bf16[512,1024]{1,0:T(8,128)(2,1)} %get-tuple-element.187.own_ref, bf16[512,1024]{1,0:T(8,128)(2,1)} %copy-done.43, bf16[1024,2048]{1,0:T(8,128)(2,1)} %get-tuple-element.188.slope_ref, ...), custom_call_target="tpu_custom_call" | custom-call | flops 12884901888 | bytes 34603008 | tf_op jit(solution)/shard_map/pallas_call | solution.py:547
  256.7 3.2 collective-permute-start.41
  259.9 9.7 %shard_map.290 = (bf16[2,2,8,32,512]{4,3,2,1,0:T(8,128)(2,1)}, bf16[2,2,8,32,512]{4,3,2,1,0:T(8,128)(2,1)}, bf16[2,2,8,32,512]{4,3,2,1,0:T(8,128)(2,1)}, bf16[2,2,8,32,512]{4,3,2,1,0:T(8,128)(2,1)}) custom-call(s32[4]{0:T(128)} %pad_add_fusion.m, bf16[512,1024]{1,0:T(8,128)(2,1)} %get-tuple-element.167.own_ref, ...), custom_call_target="tpu_custom_call" | custom-call | flops 6442450944 | bytes 23592960 | tf_op jit(solution)/shard_map/pallas_call | solution.py:547
  274.5 6.0 %shard_map.291 = (f32[512,1024]{1,0:T(8,128)}, bf16[512,1024]{1,0:T(8,128)(2,1)}, f32[8,1024]{1,0:T(8,128)}) custom-call(s32[4]{0:T(128)} %pad_add_fusion.m, f32[512,1024]{1,0:T(8,128)} %get-tuple-element.199.resid_ref, f32[512,1024]{1,0:T(8,128)} %get-tuple-element.200.own_ref, bf16[512,1024]{1,0:T(8,128)(2,1)} %copy-done.18, ...), custom_call_target="tpu_custom_call" | custom-call | flops 15728640 | bytes 15728640 | tf_op jit(solution)/shard_map/pallas_call | solution.py:547
  284.7 20.3 %shard_map.292 = (bf16[3,1024,256]{2,1,0:T(8,128)(2,1)}, f32[8,256]{1,0:T(8,128)}) custom-call(s32[4]{0:T(128)} %pad_add_fusion.m, bf16[3,1024,512]{2,1,0:T(8,128)(2,1)} %get-tuple-element.153.q_ref.k_ref.v_ref, bf16[3,1024,512]{2,1,0:T(8,128)(2,1)} %get-tuple-element.153.q_ref.k_ref.v_ref, bf16[3,1024,512]{2,1,0:T(8,128)(2,1)} %get-tuple-element.153.q_ref.k_ref.v_ref, ...), custom_call_target="tpu_custom_call" | custom-call | flops 16499999744 | bytes 15728640 | tf_op jit(solution)/shard_map/pallas_call | solution.py:547
  305.4 9.0 %shard_map.293 = (bf16[2,2,10,32,256]{4,3,2,1,0:T(8,128)(2,1)}, bf16[2,2,10,32,256]{4,3,2,1,0:T(8,128)(2,1)}, bf16[2,2,10,32,256]{4,3,2,1,0:T(8,128)(2,1)}, bf16[2,2,10,32,256]{4,3,2,1,0:T(8,128)(2,1)}) custom-call(s32[4]{0:T(128)} %pad_add_fusion.m, bf16[1024,1024]{1,0:T(8,128)(2,1)} %get-tuple-element.211.x_ref, ...), custom_call_target="tpu_custom_call" | custom-call | flops 3221225472 | bytes 12582912 | tf_op jit(solution)/shard_map/pallas_call | solution.py:547
  314.4 1.5 collective-permute-start.50
  316.4 2.5 collective-permute-done.46
  320.9 1.5 collective-permute-start.47
  322.4 20.7 %shard_map.294 = (bf16[3,1024,256]{2,1,0:T(8,128)(2,1)}, f32[8,256]{1,0:T(8,128)}) custom-call(s32[4]{0:T(128)} %pad_add_fusion.m, bf16[3,1024,512]{2,1,0:T(8,128)(2,1)} %get-tuple-element.153.q_ref.k_ref.v_ref, bf16[3,1024,512]{2,1,0:T(8,128)(2,1)} %get-tuple-element.153.q_ref.k_ref.v_ref, bf16[3,1024,512]{2,1,0:T(8,128)(2,1)} %get-tuple-element.153.q_ref.k_ref.v_ref, ...), custom_call_target="tpu_custom_call" | custom-call | flops 16499999744 | bytes 15728640 | tf_op jit(solution)/shard_map/pallas_call | solution.py:547
  345.7 2.3 collective-permute-start.71
  348.2 2.1 fusion.15
  351.5 2.1 fusion.13
  353.6 10.2 %shard_map.295 = (bf16[512,1024]{1,0:T(8,128)(2,1)}, f32[512,1024]{1,0:T(8,128)}) custom-call(s32[4]{0:T(128)} %pad_add_fusion.m, bf16[3,1024,256]{2,1,0:T(8,128)(2,1)} %get-tuple-element.209.d_ref, bf16[3,1024,256]{2,1,0:T(8,128)(2,1)} %get-tuple-element.233.e_ref.d_ref, bf16[2,2,272,512]{3,2,1,0:T(8,128)(2,1)} %copy-done.4, ...), custom_call_target="tpu_custom_call" | custom-call | flops 4831838208 | bytes 14155776 | tf_op jit(solution)/shard_map/pallas_call | solution.py:547
  367.7 3.5 collective-permute-done.52
  372.3 6.5 %shard_map.296 = (bf16[2,2,6,32,256]{4,3,2,1,0:T(8,128)(2,1)}, bf16[2,2,6,32,256]{4,3,2,1,0:T(8,128)(2,1)}, bf16[2,2,6,32,256]{4,3,2,1,0:T(8,128)(2,1)}, bf16[2,2,6,32,256]{4,3,2,1,0:T(8,128)(2,1)}) custom-call(s32[4]{0:T(128)} %pad_add_fusion.m, bf16[1024,1024]{1,0:T(8,128)(2,1)} %get-tuple-element.211.x_ref, ...), custom_call_target="tpu_custom_call" | custom-call | flops 3221225472 | bytes 12582912 | tf_op jit(solution)/shard_map/pallas_call | solution.py:547
  383.8 1.7 collective-permute-start.63
  386.4 4.2 shard_map.297
  395.7 1.8 collective-permute-done.72
  397.6 2.6 collective-permute-done.63
  410.5 2.5 collective-permute-done.59
  413.0 2.1 collective-permute-start.67
  415.2 5.3 %collective-permute-done.67 = bf16[2,6,32,256]{3,2,1,0:T(8,128)(2,1)S(1)} collective-permute-done((bf16[2,6,32,256]{3,2,1,0:T(8,128)(2,1)S(1)}, bf16[2,6,32,256]{3,2,1,0:T(8,128)(2,1)S(1)}, u32[]{:S(2)}, u32[]{:S(2)}) %collective-permute-start.67) | collective-permute-done | bytes 196640 | tf_op jit(solution)/shard_map/ppermute | solution.py:403
  420.6 2.8 collective-permute-start.68
  424.6 6.1 %collective-permute-start.60 = (f32[38,128]{1,0:T(8,128)S(1)}, f32[38,128]{1,0:T(8,128)S(1)}, u32[]{:S(2)}, u32[]{:S(2)}) collective-permute-start(f32[38,128]{1,0:T(8,128)S(1)} %pad_maximum_fusion.17), channel_id=1, source_target_pairs={{0,2},{1,3},{2,0},{3,1},{4,6},{5,7},{6,4},{7,5},{8,10},{9,11},{10,... | collective-permute-start | bytes 58376 | tf_op jit(solution)/shard_map/ppermute | solution.py:403
  433.1 3.0 collective-permute-start.69
  439.2 1.7 collective-permute-done.69
  (396 shorter events, 98.3 us)
Async XLA Ops:
  4.0 26.9 %collective-permute-start.18 = (bf16[4,32,512]{2,1,0:T(8,128)(2,1)S(1)}, bf16[4,32,512]{2,1,0:T(8,128)(2,1)S(1)}, u32[]{:S(2)}, u32[]{:S(2)}) collective-permute-start(bf16[4,32,512]{2,1,0:T(8,128)(2,1)S(1)} %bitcast.319), channel_id=1, source_target_pairs={{0,4},{1,5},{2,6},{3,7},{4,0},{5,1},{6,2},{7,3},{8,12},{9,13},{10,... | collective-permute-start | bytes 393224 | tf_op jit(solution)/shard_map/ppermute | solution.py:403
  6.2 16.9 %collective-permute-start.1 = (bf16[272,512]{1,0:T(8,128)(2,1)S(1)}, bf16[272,512]{1,0:T(8,128)(2,1)S(1)}, u32[]{:S(2)}, u32[]{:S(2)}) collective-permute-start(bf16[272,512]{1,0:T(8,128)(2,1)S(1)} %concatenate.93), channel_id=1, source_target_pairs={{0,2},{1,3},{2,0},{3,1},{4,6},{5,7},{6,4},{7,5},{8,10},{9,11},{10,... | collective-permute-start | bytes 835592 | tf_op jit(solution)/shard_map/ppermute | solution.py:403
  23.2 14.1 %collective-permute-start.2 = (bf16[2,272,512]{2,1,0:T(8,128)(2,1)S(1)}, bf16[2,272,512]{2,1,0:T(8,128)(2,1)S(1)}, u32[]{:S(2)}, u32[]{:S(2)}) collective-permute-start(bf16[2,272,512]{2,1,0:T(8,128)(2,1)S(1)} %pad_maximum_fusion.10), channel_id=1, source_target_pairs={{0,1},{1,0},{2,3},{3,2},{4,5},{5,4},{6,7},{7,6},{8,9},{9,8},{10,11... | collective-permute-start | bytes 1671176 | tf_op jit(solution)/shard_map/ppermute | solution.py:403
  29.4 9.2 %collective-permute-start.10 = (f32[4,1024]{1,0:T(4,128)S(1)}, f32[4,1024]{1,0:T(4,128)S(1)}, u32[]{:S(2)}, u32[]{:S(2)}) collective-permute-start(f32[4,1024]{1,0:T(4,128)S(1)} %slice.663), channel_id=1, source_target_pairs={{0,8},{1,9},{2,10},{3,11},{4,12},{5,13},{6,14},{7,15},{8,0},{9,1},... | collective-permute-start | bytes 49160 | tf_op jit(solution)/shard_map/ppermute | solution.py:403
  31.7 13.6 %collective-permute-start.14 = (bf16[2,272,512]{2,1,0:T(8,128)(2,1)S(1)}, bf16[2,272,512]{2,1,0:T(8,128)(2,1)S(1)}, u32[]{:S(2)}, u32[]{:S(2)}) collective-permute-start(bf16[2,272,512]{2,1,0:T(8,128)(2,1)S(1)} %pad_maximum_fusion.10), channel_id=1, source_target_pairs={{0,8},{1,9},{2,10},{3,11},{4,12},{5,13},{6,14},{7,15},{8,0},{9,1},... | collective-permute-start | bytes 1671176 | tf_op jit(solution)/shard_map/ppermute | solution.py:403
  37.3 13.1 %collective-permute-start.15 = (bf16[2,272,512]{2,1,0:T(8,128)(2,1)S(1)}, bf16[2,272,512]{2,1,0:T(8,128)(2,1)S(1)}, u32[]{:S(2)}, u32[]{:S(2)}) collective-permute-start(bf16[2,272,512]{2,1,0:T(8,128)(2,1)S(1)} %collective-permute-done.2), channel_id=1, source_target_pairs={{0,16},{1,17},{2,18},{3,19},{4,20},{5,21},{6,22},{7,23},{8,24},{9,... | collective-permute-start | bytes 1671176 | tf_op jit(solution)/shard_map/ppermute | solution.py:403
  38.6 5.8 %collective-permute-start.11 = (f32[2,1024]{1,0:T(2,128)S(1)}, f32[2,1024]{1,0:T(2,128)S(1)}, u32[]{:S(2)}, u32[]{:S(2)}) collective-permute-start(f32[2,1024]{1,0:T(2,128)S(1)} %slice.665), channel_id=1, source_target_pairs={{0,2},{1,3},{2,0},{3,1},{4,6},{5,7},{6,4},{7,5},{8,10},{9,11},{10,... | collective-permute-start | bytes 24584 | tf_op jit(solution)/shard_map/ppermute | solution.py:403
  41.9 17.9 %collective-permute-start.3 = (bf16[272,1024]{1,0:T(8,128)(2,1)S(1)}, bf16[272,1024]{1,0:T(8,128)(2,1)S(1)}, u32[]{:S(2)}, u32[]{:S(2)}) collective-permute-start(bf16[272,1024]{1,0:T(8,128)(2,1)S(1)} %get-tuple-element.318), channel_id=1, source_target_pairs={{0,0},{1,1},{2,4},{3,5},{4,2},{5,3},{6,6},{7,7},{8,8},{9,9},{10,12... | collective-permute-start | bytes 1671176 | tf_op jit(solution)/shard_map/ppermute | solution.py:403
  42.6 17.2 %collective-permute-start.4 = (bf16[272,1024]{1,0:T(8,128)(2,1)S(1)}, bf16[272,1024]{1,0:T(8,128)(2,1)S(1)}, u32[]{:S(2)}, u32[]{:S(2)}) collective-permute-start(bf16[272,1024]{1,0:T(8,128)(2,1)S(1)} %get-tuple-element.317), channel_id=1, source_target_pairs={{0,1},{1,0},{2,5},{3,4},{4,3},{5,2},{6,7},{7,6},{8,9},{9,8},{10,13... | collective-permute-start | bytes 1671176 | tf_op jit(solution)/shard_map/ppermute | solution.py:403
  44.4 13.1 %collective-permute-start.12 = (f32[1,1024]{1,0:T(1,128)S(1)}, f32[1,1024]{1,0:T(1,128)S(1)}, u32[]{:S(2)}, u32[]{:S(2)}) collective-permute-start(f32[1,1024]{1,0:T(1,128)S(1)} %slice.667), channel_id=1, source_target_pairs={{0,1},{1,0},{2,3},{3,2},{4,5},{5,4},{6,7},{7,6},{8,9},{9,8},{10,11... | collective-permute-start | bytes 12296 | tf_op jit(solution)/shard_map/ppermute | solution.py:403
  50.5 24.2 %collective-permute-start.17 = (bf16[2,2,272,512]{3,2,1,0:T(8,128)(2,1)S(1)}, bf16[2,2,272,512]{3,2,1,0:T(8,128)(2,1)S(1)}, u32[]{:S(2)}, u32[]{:S(2)}) collective-permute-start(bf16[2,2,272,512]{3,2,1,0:T(8,128)(2,1)S(1)} %pad_maximum_fusion.1.rest_0_), channel_id=1, source_target_pairs={{0,16},{1,17},{2,18},{3,19},{4,20},{5,21},{6,22},{7,23},{8,24},{9,... | collective-permute-start | bytes 3342344 | tf_op jit(solution)/shard_map/ppermute | solution.py:403
  58.2 23.5 %collective-permute-start.16 = (bf16[2,2,272,512]{3,2,1,0:T(8,128)(2,1)S(1)}, bf16[2,2,272,512]{3,2,1,0:T(8,128)(2,1)S(1)}, u32[]{:S(2)}, u32[]{:S(2)}) collective-permute-start(bf16[2,2,272,512]{3,2,1,0:T(8,128)(2,1)S(1)} %pad_maximum_fusion.2.rest_2_), channel_id=1, source_target_pairs={{0,8},{1,9},{2,10},{3,11},{4,12},{5,13},{6,14},{7,15},{8,0},{9,1},... | collective-permute-start | bytes 3342344 | tf_op jit(solution)/shard_map/ppermute | solution.py:403
  59.9 23.9 %collective-permute-start.13 = (bf16[2,272,1024]{2,1,0:T(8,128)(2,1)S(1)}, bf16[2,272,1024]{2,1,0:T(8,128)(2,1)}, u32[]{:S(2)}, u32[]{:S(2)}) collective-permute-start(bf16[2,272,1024]{2,1,0:T(8,128)(2,1)S(1)} %pad_maximum_fusion.own_ref.tok_ref), channel_id=1, source_target_pairs={{0,4},{1,5},{2,6},{3,7},{4,0},{5,1},{6,2},{7,3},{8,12},{9,13},{10,... | collective-permute-start | bytes 3342344 | tf_op jit(solution)/shard_map/ppermute | solution.py:403
  64.7 29.6 %collective-permute-start.19 = (bf16[8,32,512]{2,1,0:T(8,128)(2,1)}, bf16[8,32,512]{2,1,0:T(8,128)(2,1)}, u32[]{:S(2)}, u32[]{:S(2)}) collective-permute-start(bf16[8,32,512]{2,1,0:T(8,128)(2,1)} %pad_maximum_fusion.13), channel_id=1, source_target_pairs={{0,2},{1,3},{2,0},{3,1},{4,6},{5,7},{6,4},{7,5},{8,10},{9,11},{10,... | collective-permute-start | bytes 786440 | tf_op jit(solution)/shard_map/ppermute | solution.py:403
  95.4 16.0 %collective-permute-start.20 = (bf16[2,8,32,512]{3,2,1,0:T(8,128)(2,1)S(1)}, bf16[2,8,32,512]{3,2,1,0:T(8,128)(2,1)S(1)}, u32[]{:S(2)}, u32[]{:S(2)}) collective-permute-start(bf16[2,8,32,512]{3,2,1,0:T(8,128)(2,1)S(1)} %pad_maximum_fusion.11), channel_id=1, source_target_pairs={{0,1},{1,0},{2,3},{3,2},{4,5},{5,4},{6,7},{7,6},{8,9},{9,8},{10,11... | collective-permute-start | bytes 1572872 | tf_op jit(solution)/shard_map/ppermute | solution.py:403
  97.9 29.2 %collective-permute-start.22 = (bf16[2,8,32,512]{3,2,1,0:T(8,128)(2,1)S(1)}, bf16[2,8,32,512]{3,2,1,0:T(8,128)(2,1)S(1)}, u32[]{:S(2)}, u32[]{:S(2)}) collective-permute-start(bf16[2,8,32,512]{3,2,1,0:T(8,128)(2,1)S(1)} %pad_maximum_fusion.11), channel_id=1, source_target_pairs={{0,8},{1,9},{2,10},{3,11},{4,12},{5,13},{6,14},{7,15},{8,0},{9,1},... | collective-permute-start | bytes 1572872 | tf_op jit(solution)/shard_map/ppermute | solution.py:403
  111.3 15.8 %collective-permute-start.23 = (bf16[2,8,32,512]{3,2,1,0:T(8,128)(2,1)S(1)}, bf16[2,8,32,512]{3,2,1,0:T(8,128)(2,1)S(1)}, u32[]{:S(2)}, u32[]{:S(2)}) collective-permute-start(bf16[2,8,32,512]{3,2,1,0:T(8,128)(2,1)S(1)} %collective-permute-done.20), channel_id=1, source_target_pairs={{0,16},{1,17},{2,18},{3,19},{4,20},{5,21},{6,22},{7,23},{8,24},{9,... | collective-permute-start | bytes 1572872 | tf_op jit(solution)/shard_map/ppermute | solution.py:403
  111.9 15.1 %collective-permute-start.21 = (bf16[2,128,512]{2,1,0:T(8,128)(2,1)S(1)}, bf16[2,128,512]{2,1,0:T(8,128)(2,1)S(1)}, u32[]{:S(2)}, u32[]{:S(2)}) collective-permute-start(bf16[2,128,512]{2,1,0:T(8,128)(2,1)S(1)} %bitcast.298), channel_id=1, source_target_pairs={{0,2},{1,3},{2,0},{3,1},{4,6},{5,7},{6,4},{7,5},{8,10},{9,11},{10,... | collective-permute-start | bytes 786440 | tf_op jit(solution)/shard_map/ppermute | solution.py:403
  127.2 27.1 %collective-permute-start.26 = (bf16[2,2,8,32,512]{4,3,2,1,0:T(8,128)(2,1)S(1)}, bf16[2,2,8,32,512]{4,3,2,1,0:T(8,128)(2,1)}, u32[]{:S(2)}, u32[]{:S(2)}) collective-permute-start(bf16[2,2,8,32,512]{4,3,2,1,0:T(8,128)(2,1)S(1)} %pad_maximum_fusion.4.rest_2_.rest_6_), channel_id=1, source_target_pairs={{0,8},{1,9},{2,10},{3,11},{4,12},{5,13},{6,14},{7,15},{8,0},{9,1},... | collective-permute-start | bytes 3145736 | tf_op jit(solution)/shard_map/ppermute | solution.py:403
  129.1 25.4 %collective-permute-start.25 = (bf16[2,2,8,32,512]{4,3,2,1,0:T(8,128)(2,1)S(1)}, bf16[2,2,8,32,512]{4,3,2,1,0:T(8,128)(2,1)}, u32[]{:S(2)}, u32[]{:S(2)}) collective-permute-start(bf16[2,2,8,32,512]{4,3,2,1,0:T(8,128)(2,1)S(1)} %pad_maximum_fusion.3.rest_0_.rest_4_), channel_id=1, source_target_pairs={{0,16},{1,17},{2,18},{3,19},{4,20},{5,21},{6,22},{7,23},{8,24},{9,... | collective-permute-start | bytes 3145736 | tf_op jit(solution)/shard_map/ppermute | solution.py:403
  138.1 16.3 %collective-permute-start.27 = (bf16[512,1024]{1,0:T(8,128)(2,1)}, bf16[512,1024]{1,0:T(8,128)(2,1)}, u32[]{:S(2)}, u32[]{:S(2)}) collective-permute-start(bf16[512,1024]{1,0:T(8,128)(2,1)} %get-tuple-element.165), channel_id=1, source_target_pairs={{0,4},{1,5},{2,6},{3,7},{4,0},{5,1},{6,2},{7,3},{8,12},{9,13},{10,... | collective-permute-start | bytes 3145736 | tf_op jit(solution)/shard_map/ppermute | solution.py:403
  138.2 14.4 %collective-permute-start.24 = (bf16[2,2,128,512]{3,2,1,0:T(8,128)(2,1)S(1)}, bf16[2,2,128,512]{3,2,1,0:T(8,128)(2,1)}, u32[]{:S(2)}, u32[]{:S(2)}) collective-permute-start(bf16[2,2,128,512]{3,2,1,0:T(8,128)(2,1)S(1)} %pad_maximum_fusion.12), channel_id=1, source_target_pairs={{0,1},{1,0},{2,3},{3,2},{4,5},{5,4},{6,7},{7,6},{8,9},{9,8},{10,11... | collective-permute-start | bytes 1572872 | tf_op jit(solution)/shard_map/ppermute | solution.py:403
  138.3 25.5 %collective-permute-start.29 = (bf16[2,2,128,512]{3,2,1,0:T(8,128)(2,1)S(1)}, bf16[2,2,128,512]{3,2,1,0:T(8,128)(2,1)S(1)}, u32[]{:S(2)}, u32[]{:S(2)}) collective-permute-start(bf16[2,2,128,512]{3,2,1,0:T(8,128)(2,1)S(1)} %pad_maximum_fusion.12), channel_id=1, source_target_pairs={{0,8},{1,9},{2,10},{3,11},{4,12},{5,13},{6,14},{7,15},{8,0},{9,1},... | collective-permute-start | bytes 1572872 | tf_op jit(solution)/shard_map/ppermute | solution.py:403
  152.6 13.8 %collective-permute-start.30 = (bf16[2,2,128,512]{3,2,1,0:T(8,128)(2,1)}, bf16[2,2,128,512]{3,2,1,0:T(8,128)(2,1)}, u32[]{:S(2)}, u32[]{:S(2)}) collective-permute-start(bf16[2,2,128,512]{3,2,1,0:T(8,128)(2,1)} %collective-permute-done.24), channel_id=1, source_target_pairs={{0,16},{1,17},{2,18},{3,19},{4,20},{5,21},{6,22},{7,23},{8,24},{9,... | collective-permute-start | bytes 1572872 | tf_op jit(solution)/shard_map/ppermute | solution.py:403
  159.0 14.2 %collective-permute-start.28 = (bf16[512,1024]{1,0:T(8,128)(2,1)}, bf16[512,1024]{1,0:T(8,128)(2,1)}, u32[]{:S(2)}, u32[]{:S(2)}) collective-permute-start(bf16[512,1024]{1,0:T(8,128)(2,1)} %get-tuple-element.167.own_ref), channel_id=1, source_target_pairs={{0,4},{1,5},{2,6},{3,7},{4,0},{5,1},{6,2},{7,3},{8,12},{9,13},{10,... | collective-permute-start | bytes 3145736 | tf_op jit(solution)/shard_map/ppermute | solution.py:403
  167.8 24.0 %collective-permute-start.34 = (bf16[2,2,2,128,512]{4,3,2,1,0:T(8,128)(2,1)S(1)}, bf16[2,2,2,128,512]{4,3,2,1,0:T(8,128)(2,1)}, u32[]{:S(2)}, u32[]{:S(2)}) collective-permute-start(bf16[2,2,2,128,512]{4,3,2,1,0:T(8,128)(2,1)S(1)} %pad_maximum_fusion.6.rest_2_), channel_id=1, source_target_pairs={{0,8},{1,9},{2,10},{3,11},{4,12},{5,13},{6,14},{7,15},{8,0},{9,1},... | collective-permute-start | bytes 3145736 | tf_op jit(solution)/shard_map/ppermute | solution.py:403
  169.4 23.7 %collective-permute-start.33 = (bf16[2,2,2,128,512]{4,3,2,1,0:T(8,128)(2,1)S(1)}, bf16[2,2,2,128,512]{4,3,2,1,0:T(8,128)(2,1)}, u32[]{:S(2)}, u32[]{:S(2)}) collective-permute-start(bf16[2,2,2,128,512]{4,3,2,1,0:T(8,128)(2,1)S(1)} %pad_maximum_fusion.5.rest_0_), channel_id=1, source_target_pairs={{0,16},{1,17},{2,18},{3,19},{4,20},{5,21},{6,22},{7,23},{8,24},{9,... | collective-permute-start | bytes 3145736 | tf_op jit(solution)/shard_map/ppermute | solution.py:403
  172.0 14.5 %collective-permute-start.31 = (bf16[256,1024]{1,0:T(8,128)(2,1)S(1)}, bf16[256,1024]{1,0:T(8,128)(2,1)S(1)}, u32[]{:S(2)}, u32[]{:S(2)}) collective-permute-start(bf16[256,1024]{1,0:T(8,128)(2,1)S(1)} %get-tuple-element.332), channel_id=1, source_target_pairs={{0,0},{1,1},{2,4},{3,5},{4,2},{5,3},{6,6},{7,7},{8,8},{9,9},{10,12... | collective-permute-start | bytes 1572872 | tf_op jit(solution)/shard_map/ppermute | solution.py:403
  172.7 13.8 %collective-permute-start.32 = (bf16[256,1024]{1,0:T(8,128)(2,1)S(1)}, bf16[256,1024]{1,0:T(8,128)(2,1)S(1)}, u32[]{:S(2)}, u32[]{:S(2)}) collective-permute-start(bf16[256,1024]{1,0:T(8,128)(2,1)S(1)} %get-tuple-element.331), channel_id=1, source_target_pairs={{0,1},{1,0},{2,5},{3,4},{4,3},{5,2},{6,7},{7,6},{8,9},{9,8},{10,13... | collective-permute-start | bytes 1572872 | tf_op jit(solution)/shard_map/ppermute | solution.py:403
  228.6 42.2 %collective-permute-start.40 = (bf16[2,2,2,128,512]{4,3,2,1,0:T(8,128)(2,1)}, bf16[2,2,2,128,512]{4,3,2,1,0:T(8,128)(2,1)S(1)}, u32[]{:S(2)}, u32[]{:S(2)}) collective-permute-start(bf16[2,2,2,128,512]{4,3,2,1,0:T(8,128)(2,1)} %get-tuple-element.185), channel_id=1, source_target_pairs={{0,8},{1,9},{2,10},{3,11},{4,12},{5,13},{6,14},{7,15},{8,0},{9,1},... | collective-permute-start | bytes 3145736 | tf_op jit(solution)/shard_map/ppermute | solution.py:403
  229.7 42.8 %collective-permute-start.39 = (bf16[2,2,2,128,512]{4,3,2,1,0:T(8,128)(2,1)}, bf16[2,2,2,128,512]{4,3,2,1,0:T(8,128)(2,1)S(1)}, u32[]{:S(2)}, u32[]{:S(2)}) collective-permute-start(bf16[2,2,2,128,512]{4,3,2,1,0:T(8,128)(2,1)} %get-tuple-element.183), channel_id=1, source_target_pairs={{0,16},{1,17},{2,18},{3,19},{4,20},{5,21},{6,22},{7,23},{8,24},{9,... | collective-permute-start | bytes 3145736 | tf_op jit(solution)/shard_map/ppermute | solution.py:403
  230.9 38.7 %collective-permute-start.37 = (bf16[256,1024]{1,0:T(8,128)(2,1)S(1)}, bf16[256,1024]{1,0:T(8,128)(2,1)S(1)}, u32[]{:S(2)}, u32[]{:S(2)}) collective-permute-start(bf16[256,1024]{1,0:T(8,128)(2,1)S(1)} %get-tuple-element.330), channel_id=1, source_target_pairs={{0,0},{1,1},{4,2},{5,3},{2,4},{3,5},{6,6},{7,7},{8,8},{9,9},{12,10... | collective-permute-start | bytes 1572872 | tf_op jit(solution)/shard_map/ppermute | solution.py:403
  231.6 38.0 %collective-permute-start.38 = (bf16[256,1024]{1,0:T(8,128)(2,1)S(1)}, bf16[256,1024]{1,0:T(8,128)(2,1)S(1)}, u32[]{:S(2)}, u32[]{:S(2)}) collective-permute-start(bf16[256,1024]{1,0:T(8,128)(2,1)S(1)} %get-tuple-element.329), channel_id=1, source_target_pairs={{1,0},{0,1},{5,2},{4,3},{3,4},{2,5},{7,6},{6,7},{9,8},{8,9},{13,10... | collective-permute-start | bytes 1572872 | tf_op jit(solution)/shard_map/ppermute | solution.py:403
  256.7 16.8 %collective-permute-start.41 = (bf16[512,1024]{1,0:T(8,128)(2,1)}, bf16[512,1024]{1,0:T(8,128)(2,1)S(1)}, u32[]{:S(2)}, u32[]{:S(2)}) collective-permute-start(bf16[512,1024]{1,0:T(8,128)(2,1)} %get-tuple-element.201), channel_id=1, source_target_pairs={{0,4},{1,5},{2,6},{3,7},{4,0},{5,1},{6,2},{7,3},{8,12},{9,13},{10,... | collective-permute-start | bytes 3145736 | tf_op jit(solution)/shard_map/ppermute | solution.py:403
  280.5 4.2 collective-permute-start.42
  280.6 24.5 %collective-permute-start.44 = (bf16[2,2,128,512]{3,2,1,0:T(8,128)(2,1)}, bf16[2,2,128,512]{3,2,1,0:T(8,128)(2,1)S(1)}, u32[]{:S(2)}, u32[]{:S(2)}) collective-permute-start(bf16[2,2,128,512]{3,2,1,0:T(8,128)(2,1)} %get-tuple-element.309), channel_id=1, source_target_pairs={{0,16},{1,17},{2,18},{3,19},{4,20},{5,21},{6,22},{7,23},{8,24},{9,... | collective-permute-start | bytes 1572872 | tf_op jit(solution)/shard_map/ppermute | solution.py:403
  281.5 23.8 %collective-permute-start.43 = (bf16[2,2,128,512]{3,2,1,0:T(8,128)(2,1)}, bf16[2,2,128,512]{3,2,1,0:T(8,128)(2,1)S(1)}, u32[]{:S(2)}, u32[]{:S(2)}) collective-permute-start(bf16[2,2,128,512]{3,2,1,0:T(8,128)(2,1)} %get-tuple-element.311), channel_id=1, source_target_pairs={{0,8},{1,9},{2,10},{3,11},{4,12},{5,13},{6,14},{7,15},{8,0},{9,1},... | collective-permute-start | bytes 1572872 | tf_op jit(solution)/shard_map/ppermute | solution.py:403
  282.6 36.3 %collective-permute-start.46 = (bf16[2,2,8,32,512]{4,3,2,1,0:T(8,128)(2,1)}, bf16[2,2,8,32,512]{4,3,2,1,0:T(8,128)(2,1)S(1)}, u32[]{:S(2)}, u32[]{:S(2)}) collective-permute-start(bf16[2,2,8,32,512]{4,3,2,1,0:T(8,128)(2,1)} %get-tuple-element.221), channel_id=1, source_target_pairs={{0,8},{1,9},{2,10},{3,11},{4,12},{5,13},{6,14},{7,15},{8,0},{9,1},... | collective-permute-start | bytes 3145736 | tf_op jit(solution)/shard_map/ppermute | solution.py:403
  283.5 37.1 %collective-permute-start.45 = (bf16[2,2,8,32,512]{4,3,2,1,0:T(8,128)(2,1)}, bf16[2,2,8,32,512]{4,3,2,1,0:T(8,128)(2,1)S(1)}, u32[]{:S(2)}, u32[]{:S(2)}) collective-permute-start(bf16[2,2,8,32,512]{4,3,2,1,0:T(8,128)(2,1)} %get-tuple-element.219), channel_id=1, source_target_pairs={{0,16},{1,17},{2,18},{3,19},{4,20},{5,21},{6,22},{7,23},{8,24},{9,... | collective-permute-start | bytes 3145736 | tf_op jit(solution)/shard_map/ppermute | solution.py:403
  305.2 39.3 %collective-permute-start.51 = (bf16[2,2,128,512]{3,2,1,0:T(8,128)(2,1)S(1)}, bf16[2,2,128,512]{3,2,1,0:T(8,128)(2,1)S(1)}, u32[]{:S(2)}, u32[]{:S(2)}) collective-permute-start(bf16[2,2,128,512]{3,2,1,0:T(8,128)(2,1)S(1)} %add_convert_fusion.6), channel_id=1, source_target_pairs={{0,1},{1,0},{2,3},{3,2},{4,5},{5,4},{6,7},{7,6},{8,9},{9,8},{10,11... | collective-permute-start | bytes 1572872 | tf_op jit(solution)/shard_map/ppermute | solution.py:403
  314.4 33.7 %collective-permute-start.50 = (bf16[2,2,10,32,256]{4,3,2,1,0:T(8,128)(2,1)}, bf16[2,2,10,32,256]{4,3,2,1,0:T(8,128)(2,1)}, u32[]{:S(2)}, u32[]{:S(2)}) collective-permute-start(bf16[2,2,10,32,256]{4,3,2,1,0:T(8,128)(2,1)} %get-tuple-element.215), channel_id=1, source_target_pairs={{0,8},{1,9},{2,10},{3,11},{4,12},{5,13},{6,14},{7,15},{8,0},{9,1},... | collective-permute-start | bytes 1966088 | tf_op jit(solution)/shard_map/ppermute | solution.py:403
  315.9 35.6 %collective-permute-start.49 = (bf16[2,2,10,32,256]{4,3,2,1,0:T(8,128)(2,1)}, bf16[2,2,10,32,256]{4,3,2,1,0:T(8,128)(2,1)}, u32[]{:S(2)}, u32[]{:S(2)}) collective-permute-start(bf16[2,2,10,32,256]{4,3,2,1,0:T(8,128)(2,1)} %get-tuple-element.213), channel_id=1, source_target_pairs={{0,16},{1,17},{2,18},{3,19},{4,20},{5,21},{6,22},{7,23},{8,24},{9,... | collective-permute-start | bytes 1966088 | tf_op jit(solution)/shard_map/ppermute | solution.py:403
  319.3 25.5 %collective-permute-start.48 = (bf16[2,8,32,512]{3,2,1,0:T(8,128)(2,1)S(1)}, bf16[2,8,32,512]{3,2,1,0:T(8,128)(2,1)S(1)}, u32[]{:S(2)}, u32[]{:S(2)}) collective-permute-start(bf16[2,8,32,512]{3,2,1,0:T(8,128)(2,1)S(1)} %get-tuple-element.305), channel_id=1, source_target_pairs={{0,16},{1,17},{2,18},{3,19},{4,20},{5,21},{6,22},{7,23},{8,24},{9,... | collective-permute-start | bytes 1572872 | tf_op jit(solution)/shard_map/ppermute | solution.py:403
  320.9 27.0 %collective-permute-start.47 = (bf16[2,8,32,512]{3,2,1,0:T(8,128)(2,1)S(1)}, bf16[2,8,32,512]{3,2,1,0:T(8,128)(2,1)S(1)}, u32[]{:S(2)}, u32[]{:S(2)}) collective-permute-start(bf16[2,8,32,512]{3,2,1,0:T(8,128)(2,1)S(1)} %get-tuple-element.307), channel_id=1, source_target_pairs={{0,8},{1,9},{2,10},{3,11},{4,12},{5,13},{6,14},{7,15},{8,0},{9,1},... | collective-permute-start | bytes 1572872 | tf_op jit(solution)/shard_map/ppermute | solution.py:403
  344.7 19.8 %collective-permute-start.74 = (bf16[2,128,512]{2,1,0:T(8,128)(2,1)S(1)}, bf16[2,128,512]{2,1,0:T(8,128)(2,1)S(1)}, u32[]{:S(2)}, u32[]{:S(2)}) collective-permute-start(bf16[2,128,512]{2,1,0:T(8,128)(2,1)S(1)} %get-tuple-element.325), channel_id=1, source_target_pairs={{0,2},{1,3},{2,0},{3,1},{4,6},{5,7},{6,4},{7,5},{8,10},{9,11},{10,... | collective-permute-start | bytes 786440 | tf_op jit(solution)/shard_map/ppermute | solution.py:403
  345.7 34.8 %collective-permute-start.71 = (bf16[2,8,32,512]{3,2,1,0:T(8,128)(2,1)}, bf16[2,8,32,512]{3,2,1,0:T(8,128)(2,1)}, u32[]{:S(2)}, u32[]{:S(2)}) collective-permute-start(bf16[2,8,32,512]{3,2,1,0:T(8,128)(2,1)} %add_convert_fusion), channel_id=1, source_target_pairs={{0,1},{1,0},{2,3},{3,2},{4,5},{5,4},{6,7},{7,6},{8,9},{9,8},{10,11... | collective-permute-start | bytes 1572872 | tf_op jit(solution)/shard_map/ppermute | solution.py:403
  350.3 15.5 %collective-permute-start.53 = (bf16[2,10,32,256]{3,2,1,0:T(8,128)(2,1)}, bf16[2,10,32,256]{3,2,1,0:T(8,128)(2,1)}, u32[]{:S(2)}, u32[]{:S(2)}) collective-permute-start(bf16[2,10,32,256]{3,2,1,0:T(8,128)(2,1)} %get-tuple-element.313), channel_id=1, source_target_pairs={{0,16},{1,17},{2,18},{3,19},{4,20},{5,21},{6,22},{7,23},{8,24},{9,... | collective-permute-start | bytes 983048 | tf_op jit(solution)/shard_map/ppermute | solution.py:403
  363.8 7.5 %collective-permute-start.52 = (bf16[2,10,32,256]{3,2,1,0:T(8,128)(2,1)}, bf16[2,10,32,256]{3,2,1,0:T(8,128)(2,1)}, u32[]{:S(2)}, u32[]{:S(2)}) collective-permute-start(bf16[2,10,32,256]{3,2,1,0:T(8,128)(2,1)} %get-tuple-element.315), channel_id=1, source_target_pairs={{0,8},{1,9},{2,10},{3,11},{4,12},{5,13},{6,14},{7,15},{8,0},{9,1},... | collective-permute-start | bytes 983048 | tf_op jit(solution)/shard_map/ppermute | solution.py:403
  364.5 21.0 %collective-permute-start.54 = (bf16[512,1024]{1,0:T(8,128)(2,1)}, bf16[512,1024]{1,0:T(8,128)(2,1)S(1)}, u32[]{:S(2)}, u32[]{:S(2)}) collective-permute-start(bf16[512,1024]{1,0:T(8,128)(2,1)} %get-tuple-element.239), channel_id=1, source_target_pairs={{0,4},{1,5},{2,6},{3,7},{4,0},{5,1},{6,2},{7,3},{8,12},{9,13},{10,... | collective-permute-start | bytes 3145736 | tf_op jit(solution)/shard_map/ppermute | solution.py:403
  366.8 16.2 %collective-permute-start.62 = (bf16[2,10,32,256]{3,2,1,0:T(8,128)(2,1)S(1)}, bf16[2,10,32,256]{3,2,1,0:T(8,128)(2,1)S(1)}, u32[]{:S(2)}, u32[]{:S(2)}) collective-permute-start(bf16[2,10,32,256]{3,2,1,0:T(8,128)(2,1)S(1)} %add_convert_fusion.12), channel_id=1, source_target_pairs={{0,1},{1,0},{2,3},{3,2},{4,5},{5,4},{6,7},{7,6},{8,9},{9,8},{10,11... | collective-permute-start | bytes 983048 | tf_op jit(solution)/shard_map/ppermute | solution.py:403
  378.8 23.9 %collective-permute-start.64 = (bf16[2,2,6,32,256]{4,3,2,1,0:T(8,128)(2,1)}, bf16[2,2,6,32,256]{4,3,2,1,0:T(8,128)(2,1)}, u32[]{:S(2)}, u32[]{:S(2)}) collective-permute-start(bf16[2,2,6,32,256]{4,3,2,1,0:T(8,128)(2,1)} %get-tuple-element.235), channel_id=1, source_target_pairs={{0,16},{1,17},{2,18},{3,19},{4,20},{5,21},{6,22},{7,23},{8,24},{9,... | collective-permute-start | bytes 1179656 | tf_op jit(solution)/shard_map/ppermute | solution.py:403
  379.7 27.7 %collective-permute-start.65 = (bf16[2,2,6,32,256]{4,3,2,1,0:T(8,128)(2,1)}, bf16[2,2,6,32,256]{4,3,2,1,0:T(8,128)(2,1)}, u32[]{:S(2)}, u32[]{:S(2)}) collective-permute-start(bf16[2,2,6,32,256]{4,3,2,1,0:T(8,128)(2,1)} %get-tuple-element.237), channel_id=1, source_target_pairs={{0,8},{1,9},{2,10},{3,11},{4,12},{5,13},{6,14},{7,15},{8,0},{9,1},... | collective-permute-start | bytes 1179656 | tf_op jit(solution)/shard_map/ppermute | solution.py:403
  381.7 15.8 %collective-permute-start.72 = (bf16[8,32,512]{2,1,0:T(8,128)(2,1)S(1)}, bf16[8,32,512]{2,1,0:T(8,128)(2,1)S(1)}, u32[]{:S(2)}, u32[]{:S(2)}) collective-permute-start(bf16[8,32,512]{2,1,0:T(8,128)(2,1)S(1)} %get-tuple-element.320), channel_id=1, source_target_pairs={{0,2},{1,3},{2,0},{3,1},{4,6},{5,7},{6,4},{7,5},{8,10},{9,11},{10,... | collective-permute-start | bytes 786440 | tf_op jit(solution)/shard_map/ppermute | solution.py:403
  383.8 16.5 %collective-permute-start.63 = (bf16[10,32,256]{2,1,0:T(8,128)(2,1)}, bf16[10,32,256]{2,1,0:T(8,128)(2,1)S(1)}, u32[]{:S(2)}, u32[]{:S(2)}) collective-permute-start(bf16[10,32,256]{2,1,0:T(8,128)(2,1)} %get-tuple-element.338), channel_id=1, source_target_pairs={{0,2},{1,3},{2,0},{3,1},{4,6},{5,7},{6,4},{7,5},{8,10},{9,11},{10,... | collective-permute-start | bytes 491528 | tf_op jit(solution)/shard_map/ppermute | solution.py:403
  394.4 6.8 %collective-permute-start.57 = (f32[56,128]{1,0:T(8,128)S(1)}, f32[56,128]{1,0:T(8,128)}, u32[]{:S(2)}, u32[]{:S(2)}) collective-permute-start(f32[56,128]{1,0:T(8,128)S(1)} %pad_maximum_fusion.16), channel_id=1, source_target_pairs={{0,4},{1,5},{2,6},{3,7},{4,0},{5,1},{6,2},{7,3},{8,12},{9,13},{10,... | collective-permute-start | bytes 86024 | tf_op jit(solution)/shard_map/ppermute | solution.py:403
  400.3 30.4 %collective-permute-start.73 = (f32[4,32,512]{2,1,0:T(8,128)S(1)}, f32[4,32,512]{2,1,0:T(8,128)S(1)}, u32[]{:S(2)}, u32[]{:S(2)}) collective-permute-start(f32[4,32,512]{2,1,0:T(8,128)S(1)} %get-tuple-element.340), channel_id=1, source_target_pairs={{0,4},{1,5},{2,6},{3,7},{4,0},{5,1},{6,2},{7,3},{8,12},{9,13},{10,... | collective-permute-start | bytes 786440 | tf_op jit(solution)/shard_map/ppermute | solution.py:403
  400.4 23.0 %collective-permute-start.55 = (bf16[256,1024]{1,0:T(8,128)(2,1)S(1)}, bf16[256,1024]{1,0:T(8,128)(2,1)S(1)}, u32[]{:S(2)}, u32[]{:S(2)}) collective-permute-start(bf16[256,1024]{1,0:T(8,128)(2,1)S(1)} %get-tuple-element.324), channel_id=1, source_target_pairs={{0,0},{1,1},{4,2},{5,3},{2,4},{3,5},{6,6},{7,7},{8,8},{9,9},{12,10... | collective-permute-start | bytes 1572872 | tf_op jit(solution)/shard_map/ppermute | solution.py:403
  401.3 22.2 %collective-permute-start.56 = (bf16[256,1024]{1,0:T(8,128)(2,1)S(1)}, bf16[256,1024]{1,0:T(8,128)(2,1)S(1)}, u32[]{:S(2)}, u32[]{:S(2)}) collective-permute-start(bf16[256,1024]{1,0:T(8,128)(2,1)S(1)} %get-tuple-element.323), channel_id=1, source_target_pairs={{1,0},{0,1},{5,2},{4,3},{3,4},{2,5},{7,6},{6,7},{9,8},{8,9},{13,10... | collective-permute-start | bytes 1572872 | tf_op jit(solution)/shard_map/ppermute | solution.py:403
  406.5 8.6 %collective-permute-start.66 = (bf16[2,6,32,256]{3,2,1,0:T(8,128)(2,1)S(1)}, bf16[2,6,32,256]{3,2,1,0:T(8,128)(2,1)S(1)}, u32[]{:S(2)}, u32[]{:S(2)}) collective-permute-start(bf16[2,6,32,256]{3,2,1,0:T(8,128)(2,1)S(1)} %get-tuple-element.333), channel_id=1, source_target_pairs={{0,8},{1,9},{2,10},{3,11},{4,12},{5,13},{6,14},{7,15},{8,0},{9,1},... | collective-permute-start | bytes 589832 | tf_op jit(solution)/shard_map/ppermute | solution.py:403
  407.4 5.6 %collective-permute-start.59 = (f32[28,128]{1,0:T(8,128)S(1)}, f32[28,128]{1,0:T(8,128)S(1)}, u32[]{:S(2)}, u32[]{:S(2)}) collective-permute-start(f32[28,128]{1,0:T(8,128)S(1)} %pad_maximum_fusion.19), channel_id=1, source_target_pairs={{0,8},{1,9},{2,10},{3,11},{4,12},{5,13},{6,14},{7,15},{8,0},{9,1},... | collective-permute-start | bytes 43016 | tf_op jit(solution)/shard_map/ppermute | solution.py:403
  413.0 7.5 %collective-permute-start.67 = (bf16[2,6,32,256]{3,2,1,0:T(8,128)(2,1)S(1)}, bf16[2,6,32,256]{3,2,1,0:T(8,128)(2,1)S(1)}, u32[]{:S(2)}, u32[]{:S(2)}) collective-permute-start(bf16[2,6,32,256]{3,2,1,0:T(8,128)(2,1)S(1)} %get-tuple-element.336), channel_id=1, source_target_pairs={{0,16},{1,17},{2,18},{3,19},{4,20},{5,21},{6,22},{7,23},{8,24},{9,... | collective-permute-start | bytes 589832 | tf_op jit(solution)/shard_map/ppermute | solution.py:403
  420.6 12.5 %collective-permute-start.68 = (bf16[2,6,32,256]{3,2,1,0:T(8,128)(2,1)S(1)}, bf16[2,6,32,256]{3,2,1,0:T(8,128)(2,1)S(1)}, u32[]{:S(2)}, u32[]{:S(2)}) collective-permute-start(bf16[2,6,32,256]{3,2,1,0:T(8,128)(2,1)S(1)} %add_convert_fusion.22), channel_id=1, source_target_pairs={{0,1},{1,0},{2,3},{3,2},{4,5},{5,4},{6,7},{7,6},{8,9},{9,8},{10,11... | collective-permute-start | bytes 589832 | tf_op jit(solution)/shard_map/ppermute | solution.py:403
  424.6 7.9 %collective-permute-start.60 = (f32[38,128]{1,0:T(8,128)S(1)}, f32[38,128]{1,0:T(8,128)S(1)}, u32[]{:S(2)}, u32[]{:S(2)}) collective-permute-start(f32[38,128]{1,0:T(8,128)S(1)} %pad_maximum_fusion.17), channel_id=1, source_target_pairs={{0,2},{1,3},{2,0},{3,1},{4,6},{5,7},{6,4},{7,5},{8,10},{9,11},{10,... | collective-permute-start | bytes 58376 | tf_op jit(solution)/shard_map/ppermute | solution.py:403
  433.1 7.9 %collective-permute-start.69 = (bf16[6,32,256]{2,1,0:T(8,128)(2,1)S(1)}, bf16[6,32,256]{2,1,0:T(8,128)(2,1)S(1)}, u32[]{:S(2)}, u32[]{:S(2)}) collective-permute-start(bf16[6,32,256]{2,1,0:T(8,128)(2,1)S(1)} %get-tuple-element.261), channel_id=1, source_target_pairs={{0,2},{1,3},{2,0},{3,1},{4,6},{5,7},{6,4},{7,5},{8,10},{9,11},{10,... | collective-permute-start | bytes 294920 | tf_op jit(solution)/shard_map/ppermute | solution.py:403
  (57 other events, 268.0 us)

commit v6 on v5

--- a/solution.py
+++ b/solution.py
@@ -418,6 +418,15 @@
     return [first, send(first, ALONG_Y), second, send(second, ALONG_X)]
 
 
+def gather_near(half):
+    return send(half, ALONG_X), send(half, ALONG_Y)
+
+
+def gather_far(first, first_near, second, second_near):
+    first_far, second_far = send(first_near[0], ALONG_Y), send(second_near[1], ALONG_X)
+    return [first, *first_near, first_far, second, second_near[1], second_near[0], second_far]
+
+
 def add_low(a, b):
     return (a.astype(F32) + b.astype(F32)).astype(BF)
 
@@ -492,19 +501,18 @@
 
 def load_split_rows(meta, refs, base, blocks, weight, sem):
     copies = []
-    for slot, ref in enumerate(refs):
-        for at in range(2):
-            for j in range(2):
-                chip, z = place(meta, slot, at, j)
-                for other in range(2):
-                    row = pl.multiple_of((chip * 2 + (meta[2] ^ other)) * 128 + z * 32, 32)
-                    copies.append(
-                        pltpu.make_async_copy(
-                            ref.at[at, j, pl.ds(base + other * blocks, blocks)],
-                            weight.at[:, pl.ds(row, 32), :],
-                            sem.at[len(copies)],
-                        )
+    for n, ref in enumerate(refs):
+        for j in range(2):
+            chip, z = place(meta, n // 2, n % 2, j)
+            for other in range(2):
+                row = pl.multiple_of((chip * 2 + (meta[2] ^ other)) * 128 + z * 32, 32)
+                copies.append(
+                    pltpu.make_async_copy(
+                        ref.at[j, pl.ds(base + other * blocks, blocks)],
+                        weight.at[:, pl.ds(row, 32), :],
+                        sem.at[len(copies)],
                     )
+                )
     return copies
 
 
@@ -823,7 +831,7 @@
 
 def expand(meta, own, other, shift, pieces):
     def kernel(m, own_ref, other_ref, shift_ref, *rest):
-        refs, (act_ref, slope_ref, weight, sem) = rest[:4], rest[4:]
+        refs, (act_ref, slope_ref, weight, sem) = rest[:8], rest[8:]
         i = pl.program_id(0)
 
         @pl.when(i == 0)
@@ -848,7 +856,7 @@
             spec((256, 1024), lambda i, m: (high_block(i), 0)),
             whole((1, 2048)),
         ]
-        + [HBM] * 4,
+        + [HBM] * 8,
         [spec((256, 2048), BY_ROWS), spec((256, 2048), BY_ROWS)],
         [shaped((1024, 2048), BF), shaped((1024, 2048), BF)],
         [pltpu.VMEM((4, 1024, 512), BF), pltpu.SemaphoreType.DMA((32,))],
@@ -930,8 +938,8 @@
 
 def feed_back(meta, own, other, slope, down_pieces, up_pieces):
     def kernel(m, own_ref, other_ref, slope_ref, *rest):
-        down_refs, up_refs = rest[:4], rest[4:8]
-        du_ref, send_ref, mine_ref, sum_ref, down, up, down_sem, up_sem = rest[8:]
+        down_refs, up_refs = rest[:4], rest[4:12]
+        du_ref, send_ref, mine_ref, sum_ref, down, up, down_sem, up_sem = rest[12:]
         i = pl.program_id(0)
 
         @pl.when(i == 0)
@@ -969,7 +977,7 @@
             spec((256, 1024), lambda i, m: (low_block(i), 0)),
             spec((256, 2048), lambda i, m: (turned(i), 0)),
         ]
-        + [HBM] * 8,
+        + [HBM] * 12,
         [
             spec((256, 2048), lambda i, m: (turned(i), 0)),
             spec((256, 1024), lambda i, m: (low_block(i), 0)),
@@ -1349,17 +1357,18 @@
     up_first = jnp.stack([after(up_shard, qkv), up_far])
     mixed_one, lse_one = attend(meta, 0, after(qkv, up_first), seg_column, seg_row)
     up_second = after(send(up_first, ALONG_Z[1]), mixed_one)
-    mixed_two, lse_two = attend(meta, 1, after(qkv, up_second), seg_column, seg_row)
-    up_pieces = gather_plane(up_first, up_second, mixed_two)
+    up_near = after(gather_near(up_first), mixed_one)
+    mixed_two, lse_two = attend(meta, 1, after(qkv, up_second, up_near), seg_column, seg_row)
+    up_more = after(gather_near(up_second), mixed_two)
     down_first = jnp.stack([after(down_shard, mixed_two), send(after(down_shard, up_second), ALONG_Z[2])])
-    mixed = mixed_one, after(mixed_two, down_first, up_pieces[0], up_pieces[2])
+    down_second = send(down_first, ALONG_Z[1])
+    up_pieces = gather_far(up_first, up_near, up_second, up_more)
+    mixed = mixed_one, after(mixed_two, down_second, up_pieces)
     away, mine = project_out(meta, mixed, qkv_pieces)
-    down_second = after(send(down_first, ALONG_Z[1]), mine)
-    normal_one, inverse_one, normed = first_norm(
-        meta, own_tokens, embedded, after(mine, down_second, up_pieces), send(away, PAIR), vectors
-    )
+    down_pieces = gather_plane(down_first, down_second, mine)
+    away = after(away, down_pieces[0], down_pieces[2])
+    normal_one, inverse_one, normed = first_norm(meta, own_tokens, embedded, mine, send(away, PAIR), vectors)
     normed_other = send(normed, PAIR)
-    down_pieces = gather_plane(down_first, down_second, normed)
     normed_other = after(normed_other, down_pieces[0], down_pieces[2])
     activated, slope = expand(meta, normed, normed_other, up_shift, up_pieces)
     own_cotangent = take_rows(after(cotangent, normed), activated).reshape(512, 1024)
@@ -1404,7 +1413,7 @@
     up_share = scatter_four(*up_sums, input_low)
     qkv_sums_two = add_two(*scatter_two(*add_one(*scatter_one(*qkv_terms_two), input_low)))
     qkv_sums_two = add_three(*scatter_three(*qkv_sums_two))
-    qkv_share_one = scatter_four(*qkv_sums_one, input_low)
+    qkv_share_one = scatter_four(*after(qkv_sums_one, input_grad))
     qkv_share_two = scatter_four(*after(qkv_sums_two, input_grad))
     qkv_share = jnp.concatenate([qkv_share_one[:6], qkv_share_two], axis=2)
     qv_sums = jnp.concatenate([qv_sums_one[0:2], qv_sums_two[0:2]], axis=1)

time: 451 us -> 446 us (0.989)
  other arithmetic: 29.2 us -> 20.9 us
  waiting for transfers between devices: 95.1 us -> 102 us
    ppermute x75 -> x77, waiting for transfers between devices: 95.1 us -> 102 us  [send(): return lax.ppermute(value, AXES, pairs)]
    ppermute x75 -> x77, starting transfers between devices: 98.5 us -> 96.3 us  [send(): return lax.ppermute(value, AXES, pairs)]
    unnamed x101 -> x103, local copies, waits for them, and re-layouts: 8.06 us -> 9.06 us
  transfers between devices with their start and end apart: 75 -> 77, of which waited for: 29 -> 31; matrix products, arithmetic and copies ran while one was open for 11% -> 9% of each run, Pallas kernels for 35% -> 34%
where the time goes in v6:
time: 446 us; the launch traced here: 440 us
  Pallas kernels  188 us (42%)
  waiting for transfers between devices  102 us (23%)
  starting transfers between devices  96.3 us (22%)
  local copies, waits for them, and re-layouts  28.6 us (6%)
  other arithmetic  20.9 us (5%)
    pallas_call x18, Pallas kernels, kernel_call(): pl.pallas_call(kernel, grid_spec=pltpu.PrefetchScalarGridSpec(num_scalar_...  188 us
    ppermute x77, waiting for transfers between devices, send(): return lax.ppermute(value, AXES, pairs)  102 us
    ppermute x77, starting transfers between devices, send(): return lax.ppermute(value, AXES, pairs)  96.3 us
    convert_element_type x20, other arithmetic, add_low(): return (a.astype(F32) + b.astype(F32)).astype(BF)  13.8 us
    unnamed x103, local copies, waits for them, and re-layouts  9.06 us
  transfers between devices with their start and end apart: 77, of which 31 were waited for; matrix products, arithmetic and copies ran while one was open for 9% of the time, Pallas kernels for 34%

profile of v6, /device:TPU:0, one launch (start us, length us, event | category | flops | bytes accessed | tf_op | source)
XLA Modules:
  0.0 440.1 jit_solution(9571984301529165613)
XLA Ops:
  5.6 4.1 collective-permute-start.1
  12.5 2.0 collective-permute-done.6
  14.6 1.5 collective-permute-start.7
  16.1 2.0 collective-permute-done.7
  19.1 3.3 collective-permute-done.1
  24.7 1.6 collective-permute-start.9
  28.7 1.6 collective-permute-start.10
  30.9 5.7 %collective-permute-done.2 = bf16[2,272,512]{2,1,0:T(8,128)(2,1)S(1)} collective-permute-done((bf16[2,272,512]{2,1,0:T(8,128)(2,1)S(1)}, bf16[2,272,512]{2,1,0:T(8,128)(2,1)S(1)}, u32[]{:S(2)}, u32[]{:S(2)}) %collective-permute-start.2) | collective-permute-done | bytes 557088 | tf_op jit(solution)/shard_map/ppermute | solution.py:403
  37.9 3.2 collective-permute-start.11
  41.9 1.8 collective-permute-start.4
  44.6 5.1 %collective-permute-done.15 = bf16[2,272,512]{2,1,0:T(8,128)(2,1)S(1)} collective-permute-done((bf16[2,272,512]{2,1,0:T(8,128)(2,1)S(1)}, bf16[2,272,512]{2,1,0:T(8,128)(2,1)S(1)}, u32[]{:S(2)}, u32[]{:S(2)}) %collective-permute-start.15) | collective-permute-done | bytes 557088 | tf_op jit(solution)/shard_map/ppermute | solution.py:403
  50.9 6.0 %collective-permute-done.12 = f32[1,1024]{1,0:T(1,128)S(1)} collective-permute-done((f32[1,1024]{1,0:T(1,128)S(1)}, f32[1,1024]{1,0:T(1,128)S(1)}, u32[]{:S(2)}, u32[]{:S(2)}) %collective-permute-start.12) | collective-permute-done | bytes 4128 | tf_op jit(solution)/shard_map/ppermute | solution.py:403
  57.6 1.6 collective-permute-start.16
  59.3 4.8 %collective-permute-start.13 = (bf16[2,272,1024]{2,1,0:T(8,128)(2,1)S(1)}, bf16[2,272,1024]{2,1,0:T(8,128)(2,1)}, u32[]{:S(2)}, u32[]{:S(2)}) collective-permute-start(bf16[2,272,1024]{2,1,0:T(8,128)(2,1)S(1)} %pad_maximum_fusion.own_ref.tok_ref), channel_id=1, source_target_pairs={{0,4},{1,5},{2,6},{3,7},{4,0},{5,1},{6,2},{7,3},{8,12},{9,13},{10,... | collective-permute-start | bytes 3342344 | tf_op jit(solution)/shard_map/ppermute | solution.py:403
  64.0 7.1 %collective-permute-start.19 = (bf16[8,32,512]{2,1,0:T(8,128)(2,1)S(1)}, bf16[8,32,512]{2,1,0:T(8,128)(2,1)S(1)}, u32[]{:S(2)}, u32[]{:S(2)}) collective-permute-start(bf16[8,32,512]{2,1,0:T(8,128)(2,1)S(1)} %pad_maximum_fusion.11), channel_id=1, source_target_pairs={{0,2},{1,3},{2,0},{3,1},{4,6},{5,7},{6,4},{7,5},{8,10},{9,11},{10,... | collective-permute-start | bytes 786440 | tf_op jit(solution)/shard_map/ppermute | solution.py:403
  71.3 2.8 collective-permute-done.17.rest_1_
  74.1 7.0 %collective-permute-done.16.rest_3_ = bf16[2,2,272,512]{3,2,1,0:T(8,128)(2,1)S(1)} collective-permute-done((bf16[2,2,272,512]{3,2,1,0:T(8,128)(2,1)S(1)}, bf16[2,2,272,512]{3,2,1,0:T(8,128)(2,1)S(1)}, u32[]{:S(2)}, u32[]{:S(2)}) %collective-permute-start.16) | collective-permute-done | bytes 1114144 | tf_op jit(solution)/shard_map/ppermute | solution.py:403
  83.2 10.4 %shard_map.280 = (bf16[1024,1024]{1,0:T(8,128)(2,1)}, bf16[3,1024,512]{2,1,0:T(8,128)(2,1)}) custom-call(s32[4]{0:T(128)} %pad_add_fusion.m, bf16[2,272,1024]{2,1,0:T(8,128)(2,1)} %copy-done.2, bf16[2,272,1024]{2,1,0:T(8,128)(2,1)} %collective-permute-done.13.other_ref, f32[1,1024]{1,0:T(1,128)} %slice_add_fusion.8.emb_ref, ...), custom_call_target="tpu_custom_call" | custom-call | flops 4831838208 | bytes 15728640 | tf_op jit(solution)/shard_map/pallas_call | solution.py:555
  93.7 1.6 collective-permute-start.21
  95.8 2.5 collective-permute-start.20
  100.1 9.9 %shard_map.281 = (bf16[1024,256]{1,0:T(8,128)(2,1)}, f32[2,8,1024]{2,1,0:T(8,128)}) custom-call(s32[4]{0:T(128)} %pad_add_fusion.m, bf16[3,1024,512]{2,1,0:T(8,128)(2,1)} %get-tuple-element.155.q_ref.k_ref.v_ref, bf16[3,1024,512]{2,1,0:T(8,128)(2,1)} %get-tuple-element.155.q_ref.k_ref.v_ref, bf16[3,1024,512]{2,1,0:T(8,128)(2,1)} %get-tuple-element.155.q_ref.k_ref.v_ref, ...), custom_call_target="tpu_custom_call" | custom-call | flops 12884901888 | bytes 7864320 | tf_op jit(solution)/shard_map/pallas_call | solution.py:555
  112.3 10.0 %shard_map.282 = (bf16[1024,256]{1,0:T(8,128)(2,1)}, f32[2,8,1024]{2,1,0:T(8,128)}) custom-call(s32[4]{0:T(128)} %pad_add_fusion.m, bf16[3,1024,512]{2,1,0:T(8,128)(2,1)} %get-tuple-element.155.q_ref.k_ref.v_ref, bf16[3,1024,512]{2,1,0:T(8,128)(2,1)} %get-tuple-element.155.q_ref.k_ref.v_ref, bf16[3,1024,512]{2,1,0:T(8,128)(2,1)} %get-tuple-element.155.q_ref.k_ref.v_ref, ...), custom_call_target="tpu_custom_call" | custom-call | flops 12884901888 | bytes 7864320 | tf_op jit(solution)/shard_map/pallas_call | solution.py:555
  122.3 5.6 %collective-permute-done.23 = bf16[2,128,512]{2,1,0:T(8,128)(2,1)S(1)} collective-permute-done((bf16[2,128,512]{2,1,0:T(8,128)(2,1)S(1)}, bf16[2,128,512]{2,1,0:T(8,128)(2,1)S(1)}, u32[]{:S(2)}, u32[]{:S(2)}) %collective-permute-start.23) | collective-permute-done | bytes 262176 | tf_op jit(solution)/shard_map/ppermute | solution.py:403
  128.6 1.6 collective-permute-start.28
  130.7 11.2 %collective-permute-done.24 = bf16[2,2,128,512]{3,2,1,0:T(8,128)(2,1)S(1)} collective-permute-done((bf16[2,2,128,512]{3,2,1,0:T(8,128)(2,1)S(1)}, bf16[2,2,128,512]{3,2,1,0:T(8,128)(2,1)S(1)}, u32[]{:S(2)}, u32[]{:S(2)}) %collective-permute-start.24) | collective-permute-done | bytes 524320 | tf_op jit(solution)/shard_map/ppermute | solution.py:403
  143.5 7.4 %shard_map.283 = (bf16[512,1024]{1,0:T(8,128)(2,1)}, f32[512,1024]{1,0:T(8,128)}) custom-call(s32[4]{0:T(128)} %pad_add_fusion.m, bf16[1024,256]{1,0:T(8,128)(2,1)} %get-tuple-element.151.x_ref.out_ref.rest_0_, bf16[1024,256]{1,0:T(8,128)(2,1)} %get-tuple-element.161.w_ref.rest_1_.out_ref, bf16[2,2,272,512]{3,2,1,0:T(8,128)(2,1)} %copy-done.3, ...), custom_call_target="tpu_custom_call" | custom-call | flops 1610612736 | bytes 9437184 | tf_op jit(solution)/shard_map/pallas_call | solution.py:555
  151.0 2.6 collective-permute-done.29
  156.6 1.7 collective-permute-done.31.recv_ref
  158.3 4.6 %shard_map.284 = (f32[512,1024]{1,0:T(8,128)}, f32[512,128]{1,0:T(8,128)}, bf16[512,1024]{1,0:T(8,128)(2,1)}) custom-call(s32[4]{0:T(128)} %pad_add_fusion.m, bf16[2,272,1024]{2,1,0:T(8,128)(2,1)} %copy-done.2, f32[1,1024]{1,0:T(1,128)} %slice_add_fusion.8.emb_ref, f32[512,1024]{1,0:T(8,128)} %get-tuple-element.162.own_ref, ...), custom_call_target="tpu_custom_call" | custom-call | flops 9437184 | bytes 12582912 | tf_op jit(solution)/shard_map/pallas_call | solution.py:555
  163.1 1.5 collective-permute-start.36
  167.9 13.2 %shard_map.285 = (bf16[1024,2048]{1,0:T(8,128)(2,1)}, bf16[1024,2048]{1,0:T(8,128)(2,1)}) custom-call(s32[4]{0:T(128)} %pad_add_fusion.m, bf16[512,1024]{1,0:T(8,128)(2,1)} %get-tuple-element.170.own_ref, bf16[512,1024]{1,0:T(8,128)(2,1)} %collective-permute-done.32.other_ref, f32[1,2048]{1,0:T(1,128)} %bitcast.330, bf16[2,8,32,512]{3,2,1,0:T(8,128)(2,1)} %copy-done.19, ...), custom_call_target="tpu_custom_call" | custom-call | flops 6442450944 | bytes 22020096 | tf_op jit(solution)/shard_map/pallas_call | solution.py:555
  182.2 6.5 %collective-permute-done.36.rest_3_ = bf16[2,2,2,128,512]{4,3,2,1,0:T(8,128)(2,1)} collective-permute-done((bf16[2,2,2,128,512]{4,3,2,1,0:T(8,128)(2,1)S(1)}, bf16[2,2,2,128,512]{4,3,2,1,0:T(8,128)(2,1)}, u32[]{:S(2)}, u32[]{:S(2)}) %collective-permute-start.36) | collective-permute-done | bytes 1048608 | tf_op jit(solution)/shard_map/ppermute | solution.py:403
  189.9 11.5 %shard_map.286 = (bf16[512,1024]{1,0:T(8,128)(2,1)}, f32[512,1024]{1,0:T(8,128)}) custom-call(s32[4]{0:T(128)} %pad_add_fusion.m, bf16[1024,2048]{1,0:T(8,128)(2,1)} %get-tuple-element.176.x_ref, bf16[2,2,2,128,512]{4,3,2,1,0:T(8,128)(2,1)} %copy-done.12, bf16[2,2,2,128,512]{4,3,2,1,0:T(8,128)(2,1)} %collective-permute-done.35.rest_1_, ...), custom_call_target="tpu_custom_call" | custom-call | flops 6442450944 | bytes 17301504 | tf_op jit(solution)/shard_map/pallas_call | solution.py:555
  201.5 2.9 collective-permute-done.37.recv_ref
  205.3 6.4 %shard_map.287 = (bf16[512,1024]{1,0:T(8,128)(2,1)}, f32[512,1024]{1,0:T(8,128)}, bf16[512,1024]{1,0:T(8,128)(2,1)}, f32[8,1024]{1,0:T(8,128)}) custom-call(s32[4]{0:T(128)} %pad_add_fusion.m, f32[512,1024]{1,0:T(8,128)} %get-tuple-element.169.normal_ref, f32[512,1024]{1,0:T(8,128)} %get-tuple-element.177.own_ref, bf16[512,1024]{1,0:T(8,128)(2,1)} %copy-done.9, ...), custom_call_target="tpu_custom_call" | custom-call | flops 23592960 | bytes 15728640 | tf_op jit(solution)/shard_map/pallas_call | solution.py:555
  211.9 2.7 collective-permute-done.38.other_ref
  215.6 9.3 %shard_map.288 = (bf16[2,2,2,128,512]{4,3,2,1,0:T(8,128)(2,1)}, bf16[2,2,2,128,512]{4,3,2,1,0:T(8,128)(2,1)}, bf16[2,2,2,128,512]{4,3,2,1,0:T(8,128)(2,1)}, bf16[2,2,2,128,512]{4,3,2,1,0:T(8,128)(2,1)}) custom-call(s32[4]{0:T(128)} %pad_add_fusion.m, bf16[1024,2048]{1,0:T(8,128)(2,1)} %get-tuple-element.176.x_ref, ...), custom_call_target="tpu_custom_call" | custom-call | flops 6442450944 | bytes 15728640 | tf_op jit(solution)/shard_map/pallas_call | solution.py:555
  227.0 6.2 %collective-permute-start.40 = (bf16[256,1024]{1,0:T(8,128)(2,1)S(1)}, bf16[256,1024]{1,0:T(8,128)(2,1)S(1)}, u32[]{:S(2)}, u32[]{:S(2)}) collective-permute-start(bf16[256,1024]{1,0:T(8,128)(2,1)S(1)} %get-tuple-element.329), channel_id=1, source_target_pairs={{1,0},{0,1},{5,2},{4,3},{3,4},{2,5},{7,6},{6,7},{9,8},{8,9},{13,10... | collective-permute-start | bytes 1572872 | tf_op jit(solution)/shard_map/ppermute | solution.py:403
  233.3 19.0 %shard_map.289 = (bf16[1024,2048]{1,0:T(8,128)(2,1)}, bf16[512,1024]{1,0:T(8,128)(2,1)}, f32[512,1024]{1,0:T(8,128)}, f32[8,2048]{1,0:T(8,128)}) custom-call(s32[4]{0:T(128)} %pad_add_fusion.m, bf16[512,1024]{1,0:T(8,128)(2,1)} %get-tuple-element.186.own_ref, bf16[512,1024]{1,0:T(8,128)(2,1)} %copy-done.37, bf16[1024,2048]{1,0:T(8,128)(2,1)} %get-tuple-element.187.slope_ref, ...), custom_call_target="tpu_custom_call" | custom-call | flops 12884901888 | bytes 34603008 | tf_op jit(solution)/shard_map/pallas_call | solution.py:555
  252.3 3.1 collective-permute-start.43
  255.4 9.7 %shard_map.290 = (bf16[2,2,8,32,512]{4,3,2,1,0:T(8,128)(2,1)}, bf16[2,2,8,32,512]{4,3,2,1,0:T(8,128)(2,1)}, bf16[2,2,8,32,512]{4,3,2,1,0:T(8,128)(2,1)}, bf16[2,2,8,32,512]{4,3,2,1,0:T(8,128)(2,1)}) custom-call(s32[4]{0:T(128)} %pad_add_fusion.m, bf16[512,1024]{1,0:T(8,128)(2,1)} %get-tuple-element.170.own_ref, ...), custom_call_target="tpu_custom_call" | custom-call | flops 6442450944 | bytes 23592960 | tf_op jit(solution)/shard_map/pallas_call | solution.py:555
  268.9 6.0 %shard_map.291 = (f32[512,1024]{1,0:T(8,128)}, bf16[512,1024]{1,0:T(8,128)(2,1)}, f32[8,1024]{1,0:T(8,128)}) custom-call(s32[4]{0:T(128)} %pad_add_fusion.m, f32[512,1024]{1,0:T(8,128)} %get-tuple-element.198.resid_ref, f32[512,1024]{1,0:T(8,128)} %get-tuple-element.199.own_ref, bf16[512,1024]{1,0:T(8,128)(2,1)} %copy-done.16, ...), custom_call_target="tpu_custom_call" | custom-call | flops 15728640 | bytes 15728640 | tf_op jit(solution)/shard_map/pallas_call | solution.py:555
  279.1 20.3 %shard_map.292 = (bf16[3,1024,256]{2,1,0:T(8,128)(2,1)}, f32[8,256]{1,0:T(8,128)}) custom-call(s32[4]{0:T(128)} %pad_add_fusion.m, bf16[3,1024,512]{2,1,0:T(8,128)(2,1)} %get-tuple-element.155.q_ref.k_ref.v_ref, bf16[3,1024,512]{2,1,0:T(8,128)(2,1)} %get-tuple-element.155.q_ref.k_ref.v_ref, bf16[3,1024,512]{2,1,0:T(8,128)(2,1)} %get-tuple-element.155.q_ref.k_ref.v_ref, ...), custom_call_target="tpu_custom_call" | custom-call | flops 16499999744 | bytes 15728640 | tf_op jit(solution)/shard_map/pallas_call | solution.py:555
  300.5 8.9 %shard_map.293 = (bf16[2,2,10,32,256]{4,3,2,1,0:T(8,128)(2,1)}, bf16[2,2,10,32,256]{4,3,2,1,0:T(8,128)(2,1)}, bf16[2,2,10,32,256]{4,3,2,1,0:T(8,128)(2,1)}, bf16[2,2,10,32,256]{4,3,2,1,0:T(8,128)(2,1)}) custom-call(s32[4]{0:T(128)} %pad_add_fusion.m, bf16[1024,1024]{1,0:T(8,128)(2,1)} %get-tuple-element.210.x_ref, ...), custom_call_target="tpu_custom_call" | custom-call | flops 3221225472 | bytes 12582912 | tf_op jit(solution)/shard_map/pallas_call | solution.py:555
  309.4 1.6 collective-permute-start.52
  313.5 2.0 collective-permute-start.50
  316.7 1.5 collective-permute-start.49
  318.2 20.7 %shard_map.294 = (bf16[3,1024,256]{2,1,0:T(8,128)(2,1)}, f32[8,256]{1,0:T(8,128)}) custom-call(s32[4]{0:T(128)} %pad_add_fusion.m, bf16[3,1024,512]{2,1,0:T(8,128)(2,1)} %get-tuple-element.155.q_ref.k_ref.v_ref, bf16[3,1024,512]{2,1,0:T(8,128)(2,1)} %get-tuple-element.155.q_ref.k_ref.v_ref, bf16[3,1024,512]{2,1,0:T(8,128)(2,1)} %get-tuple-element.155.q_ref.k_ref.v_ref, ...), custom_call_target="tpu_custom_call" | custom-call | flops 16499999744 | bytes 15728640 | tf_op jit(solution)/shard_map/pallas_call | solution.py:555
  341.5 2.3 collective-permute-start.73
  346.0 10.2 %shard_map.295 = (bf16[512,1024]{1,0:T(8,128)(2,1)}, f32[512,1024]{1,0:T(8,128)}) custom-call(s32[4]{0:T(128)} %pad_add_fusion.m, bf16[3,1024,256]{2,1,0:T(8,128)(2,1)} %get-tuple-element.208.d_ref, bf16[3,1024,256]{2,1,0:T(8,128)(2,1)} %get-tuple-element.232.e_ref.d_ref, bf16[2,2,272,512]{3,2,1,0:T(8,128)(2,1)} %copy-done.3, ...), custom_call_target="tpu_custom_call" | custom-call | flops 4831838208 | bytes 14155776 | tf_op jit(solution)/shard_map/pallas_call | solution.py:555
  360.4 3.3 collective-permute-done.54
  364.7 6.5 %shard_map.296 = (bf16[2,2,6,32,256]{4,3,2,1,0:T(8,128)(2,1)}, bf16[2,2,6,32,256]{4,3,2,1,0:T(8,128)(2,1)}, bf16[2,2,6,32,256]{4,3,2,1,0:T(8,128)(2,1)}, bf16[2,2,6,32,256]{4,3,2,1,0:T(8,128)(2,1)}) custom-call(s32[4]{0:T(128)} %pad_add_fusion.m, bf16[1024,1024]{1,0:T(8,128)(2,1)} %get-tuple-element.210.x_ref, ...), custom_call_target="tpu_custom_call" | custom-call | flops 3221225472 | bytes 12582912 | tf_op jit(solution)/shard_map/pallas_call | solution.py:555
  371.3 2.0 collective-permute-start.66
  373.8 1.9 fusion.18
  378.3 4.2 shard_map.297
  391.6 2.4 collective-permute-done.60
  393.9 1.5 collective-permute-start.68
  397.2 3.3 collective-permute-done.61
  400.7 7.1 %collective-permute-done.69 = bf16[2,6,32,256]{3,2,1,0:T(8,128)(2,1)S(1)} collective-permute-done((bf16[2,6,32,256]{3,2,1,0:T(8,128)(2,1)S(1)}, bf16[2,6,32,256]{3,2,1,0:T(8,128)(2,1)S(1)}, u32[]{:S(2)}, u32[]{:S(2)}) %collective-permute-start.69) | collective-permute-done | bytes 196640 | tf_op jit(solution)/shard_map/ppermute | solution.py:403
  407.9 2.1 collective-permute-start.70
  411.2 7.7 %collective-permute-start.62 = (f32[38,128]{1,0:T(8,128)S(1)}, f32[38,128]{1,0:T(8,128)S(1)}, u32[]{:S(2)}, u32[]{:S(2)}) collective-permute-start(f32[38,128]{1,0:T(8,128)S(1)} %pad_maximum_fusion.15), channel_id=1, source_target_pairs={{0,2},{1,3},{2,0},{3,1},{4,6},{5,7},{6,4},{7,5},{8,10},{9,11},{10,... | collective-permute-start | bytes 58376 | tf_op jit(solution)/shard_map/ppermute | solution.py:403
  421.3 3.0 collective-permute-start.71
  427.9 5.3 %collective-permute-done.71 = bf16[6,32,256]{2,1,0:T(8,128)(2,1)S(1)} collective-permute-done((bf16[6,32,256]{2,1,0:T(8,128)(2,1)S(1)}, bf16[6,32,256]{2,1,0:T(8,128)(2,1)S(1)}, u32[]{:S(2)}, u32[]{:S(2)}) %collective-permute-start.71) | collective-permute-done | bytes 98336 | tf_op jit(solution)/shard_map/ppermute | solution.py:403
  433.3 3.5 collective-permute-done.65
  (399 shorter events, 87.8 us)
Async XLA Ops:
  4.0 26.3 %collective-permute-start.18 = (bf16[4,32,512]{2,1,0:T(8,128)(2,1)S(1)}, bf16[4,32,512]{2,1,0:T(8,128)(2,1)S(1)}, u32[]{:S(2)}, u32[]{:S(2)}) collective-permute-start(bf16[4,32,512]{2,1,0:T(8,128)(2,1)S(1)} %bitcast.315), channel_id=1, source_target_pairs={{0,4},{1,5},{2,6},{3,7},{4,0},{5,1},{6,2},{7,3},{8,12},{9,13},{10,... | collective-permute-start | bytes 393224 | tf_op jit(solution)/shard_map/ppermute | solution.py:403
  5.6 16.9 %collective-permute-start.1 = (bf16[272,512]{1,0:T(8,128)(2,1)S(1)}, bf16[272,512]{1,0:T(8,128)(2,1)S(1)}, u32[]{:S(2)}, u32[]{:S(2)}) collective-permute-start(bf16[272,512]{1,0:T(8,128)(2,1)S(1)} %concatenate.93), channel_id=1, source_target_pairs={{0,2},{1,3},{2,0},{3,1},{4,6},{5,7},{6,4},{7,5},{8,10},{9,11},{10,... | collective-permute-start | bytes 835592 | tf_op jit(solution)/shard_map/ppermute | solution.py:403
  22.5 14.1 %collective-permute-start.2 = (bf16[2,272,512]{2,1,0:T(8,128)(2,1)S(1)}, bf16[2,272,512]{2,1,0:T(8,128)(2,1)S(1)}, u32[]{:S(2)}, u32[]{:S(2)}) collective-permute-start(bf16[2,272,512]{2,1,0:T(8,128)(2,1)S(1)} %pad_maximum_fusion.8), channel_id=1, source_target_pairs={{0,1},{1,0},{2,3},{3,2},{4,5},{5,4},{6,7},{7,6},{8,9},{9,8},{10,11... | collective-permute-start | bytes 1671176 | tf_op jit(solution)/shard_map/ppermute | solution.py:403
  28.7 9.2 %collective-permute-start.10 = (f32[4,1024]{1,0:T(4,128)S(1)}, f32[4,1024]{1,0:T(4,128)S(1)}, u32[]{:S(2)}, u32[]{:S(2)}) collective-permute-start(f32[4,1024]{1,0:T(4,128)S(1)} %slice.663), channel_id=1, source_target_pairs={{0,8},{1,9},{2,10},{3,11},{4,12},{5,13},{6,14},{7,15},{8,0},{9,1},... | collective-permute-start | bytes 49160 | tf_op jit(solution)/shard_map/ppermute | solution.py:403
  30.3 14.3 %collective-permute-start.14 = (bf16[2,272,512]{2,1,0:T(8,128)(2,1)S(1)}, bf16[2,272,512]{2,1,0:T(8,128)(2,1)S(1)}, u32[]{:S(2)}, u32[]{:S(2)}) collective-permute-start(bf16[2,272,512]{2,1,0:T(8,128)(2,1)S(1)} %pad_maximum_fusion.8), channel_id=1, source_target_pairs={{0,8},{1,9},{2,10},{3,11},{4,12},{5,13},{6,14},{7,15},{8,0},{9,1},... | collective-permute-start | bytes 1671176 | tf_op jit(solution)/shard_map/ppermute | solution.py:403
  36.6 13.1 %collective-permute-start.15 = (bf16[2,272,512]{2,1,0:T(8,128)(2,1)S(1)}, bf16[2,272,512]{2,1,0:T(8,128)(2,1)S(1)}, u32[]{:S(2)}, u32[]{:S(2)}) collective-permute-start(bf16[2,272,512]{2,1,0:T(8,128)(2,1)S(1)} %collective-permute-done.2), channel_id=1, source_target_pairs={{0,16},{1,17},{2,18},{3,19},{4,20},{5,21},{6,22},{7,23},{8,24},{9,... | collective-permute-start | bytes 1671176 | tf_op jit(solution)/shard_map/ppermute | solution.py:403
  37.9 5.8 %collective-permute-start.11 = (f32[2,1024]{1,0:T(2,128)S(1)}, f32[2,1024]{1,0:T(2,128)S(1)}, u32[]{:S(2)}, u32[]{:S(2)}) collective-permute-start(f32[2,1024]{1,0:T(2,128)S(1)} %slice.665), channel_id=1, source_target_pairs={{0,2},{1,3},{2,0},{3,1},{4,6},{5,7},{6,4},{7,5},{8,10},{9,11},{10,... | collective-permute-start | bytes 24584 | tf_op jit(solution)/shard_map/ppermute | solution.py:403
  41.2 17.9 %collective-permute-start.3 = (bf16[272,1024]{1,0:T(8,128)(2,1)S(1)}, bf16[272,1024]{1,0:T(8,128)(2,1)S(1)}, u32[]{:S(2)}, u32[]{:S(2)}) collective-permute-start(bf16[272,1024]{1,0:T(8,128)(2,1)S(1)} %get-tuple-element.318), channel_id=1, source_target_pairs={{0,0},{1,1},{2,4},{3,5},{4,2},{5,3},{6,6},{7,7},{8,8},{9,9},{10,12... | collective-permute-start | bytes 1671176 | tf_op jit(solution)/shard_map/ppermute | solution.py:403
  41.9 17.2 %collective-permute-start.4 = (bf16[272,1024]{1,0:T(8,128)(2,1)S(1)}, bf16[272,1024]{1,0:T(8,128)(2,1)S(1)}, u32[]{:S(2)}, u32[]{:S(2)}) collective-permute-start(bf16[272,1024]{1,0:T(8,128)(2,1)S(1)} %get-tuple-element.317), channel_id=1, source_target_pairs={{0,1},{1,0},{2,5},{3,4},{4,3},{5,2},{6,7},{7,6},{8,9},{9,8},{10,13... | collective-permute-start | bytes 1671176 | tf_op jit(solution)/shard_map/ppermute | solution.py:403
  43.7 13.1 %collective-permute-start.12 = (f32[1,1024]{1,0:T(1,128)S(1)}, f32[1,1024]{1,0:T(1,128)S(1)}, u32[]{:S(2)}, u32[]{:S(2)}) collective-permute-start(f32[1,1024]{1,0:T(1,128)S(1)} %slice.667), channel_id=1, source_target_pairs={{0,1},{1,0},{2,3},{3,2},{4,5},{5,4},{6,7},{7,6},{8,9},{9,8},{10,11... | collective-permute-start | bytes 12296 | tf_op jit(solution)/shard_map/ppermute | solution.py:403
  49.9 24.2 %collective-permute-start.17 = (bf16[2,2,272,512]{3,2,1,0:T(8,128)(2,1)S(1)}, bf16[2,2,272,512]{3,2,1,0:T(8,128)(2,1)S(1)}, u32[]{:S(2)}, u32[]{:S(2)}) collective-permute-start(bf16[2,2,272,512]{3,2,1,0:T(8,128)(2,1)S(1)} %pad_maximum_fusion.1.rest_0_), channel_id=1, source_target_pairs={{0,16},{1,17},{2,18},{3,19},{4,20},{5,21},{6,22},{7,23},{8,24},{9,... | collective-permute-start | bytes 3342344 | tf_op jit(solution)/shard_map/ppermute | solution.py:403
  57.6 23.5 %collective-permute-start.16 = (bf16[2,2,272,512]{3,2,1,0:T(8,128)(2,1)S(1)}, bf16[2,2,272,512]{3,2,1,0:T(8,128)(2,1)S(1)}, u32[]{:S(2)}, u32[]{:S(2)}) collective-permute-start(bf16[2,2,272,512]{3,2,1,0:T(8,128)(2,1)S(1)} %pad_maximum_fusion.2.rest_2_), channel_id=1, source_target_pairs={{0,8},{1,9},{2,10},{3,11},{4,12},{5,13},{6,14},{7,15},{8,0},{9,1},... | collective-permute-start | bytes 3342344 | tf_op jit(solution)/shard_map/ppermute | solution.py:403
  59.3 23.9 %collective-permute-start.13 = (bf16[2,272,1024]{2,1,0:T(8,128)(2,1)S(1)}, bf16[2,272,1024]{2,1,0:T(8,128)(2,1)}, u32[]{:S(2)}, u32[]{:S(2)}) collective-permute-start(bf16[2,272,1024]{2,1,0:T(8,128)(2,1)S(1)} %pad_maximum_fusion.own_ref.tok_ref), channel_id=1, source_target_pairs={{0,4},{1,5},{2,6},{3,7},{4,0},{5,1},{6,2},{7,3},{8,12},{9,13},{10,... | collective-permute-start | bytes 3342344 | tf_op jit(solution)/shard_map/ppermute | solution.py:403
  64.0 29.6 %collective-permute-start.19 = (bf16[8,32,512]{2,1,0:T(8,128)(2,1)S(1)}, bf16[8,32,512]{2,1,0:T(8,128)(2,1)S(1)}, u32[]{:S(2)}, u32[]{:S(2)}) collective-permute-start(bf16[8,32,512]{2,1,0:T(8,128)(2,1)S(1)} %pad_maximum_fusion.11), channel_id=1, source_target_pairs={{0,2},{1,3},{2,0},{3,1},{4,6},{5,7},{6,4},{7,5},{8,10},{9,11},{10,... | collective-permute-start | bytes 786440 | tf_op jit(solution)/shard_map/ppermute | solution.py:403
  93.7 18.5 %collective-permute-start.21 = (bf16[2,8,32,512]{3,2,1,0:T(8,128)(2,1)S(1)}, bf16[2,8,32,512]{3,2,1,0:T(8,128)(2,1)S(1)}, u32[]{:S(2)}, u32[]{:S(2)}) collective-permute-start(bf16[2,8,32,512]{3,2,1,0:T(8,128)(2,1)S(1)} %pad_maximum_fusion.9.rest_0_.rest_4_), channel_id=1, source_target_pairs={{0,8},{1,9},{2,10},{3,11},{4,12},{5,13},{6,14},{7,15},{8,0},{9,1},... | collective-permute-start | bytes 1572872 | tf_op jit(solution)/shard_map/ppermute | solution.py:403
  95.3 16.9 %collective-permute-start.22 = (bf16[2,8,32,512]{3,2,1,0:T(8,128)(2,1)S(1)}, bf16[2,8,32,512]{3,2,1,0:T(8,128)(2,1)S(1)}, u32[]{:S(2)}, u32[]{:S(2)}) collective-permute-start(bf16[2,8,32,512]{3,2,1,0:T(8,128)(2,1)S(1)} %pad_maximum_fusion.9.rest_0_.rest_4_), channel_id=1, source_target_pairs={{0,16},{1,17},{2,18},{3,19},{4,20},{5,21},{6,22},{7,23},{8,24},{9,... | collective-permute-start | bytes 1572872 | tf_op jit(solution)/shard_map/ppermute | solution.py:403
  95.8 14.3 %collective-permute-start.20 = (bf16[2,8,32,512]{3,2,1,0:T(8,128)(2,1)S(1)}, bf16[2,8,32,512]{3,2,1,0:T(8,128)(2,1)S(1)}, u32[]{:S(2)}, u32[]{:S(2)}) collective-permute-start(bf16[2,8,32,512]{3,2,1,0:T(8,128)(2,1)S(1)} %pad_maximum_fusion.9.rest_0_.rest_4_), channel_id=1, source_target_pairs={{0,1},{1,0},{2,3},{3,2},{4,5},{5,4},{6,7},{7,6},{8,9},{9,8},{10,11... | collective-permute-start | bytes 1572872 | tf_op jit(solution)/shard_map/ppermute | solution.py:403
  110.1 18.5 %collective-permute-start.26 = (bf16[2,8,32,512]{3,2,1,0:T(8,128)(2,1)S(1)}, bf16[2,8,32,512]{3,2,1,0:T(8,128)(2,1)S(1)}, u32[]{:S(2)}, u32[]{:S(2)}) collective-permute-start(bf16[2,8,32,512]{3,2,1,0:T(8,128)(2,1)S(1)} %collective-permute-done.20.rest_4_.rest_8_), channel_id=1, source_target_pairs={{0,8},{1,9},{2,10},{3,11},{4,12},{5,13},{6,14},{7,15},{8,0},{9,1},... | collective-permute-start | bytes 1572872 | tf_op jit(solution)/shard_map/ppermute | solution.py:403
  110.7 17.9 %collective-permute-start.27 = (bf16[2,8,32,512]{3,2,1,0:T(8,128)(2,1)S(1)}, bf16[2,8,32,512]{3,2,1,0:T(8,128)(2,1)S(1)}, u32[]{:S(2)}, u32[]{:S(2)}) collective-permute-start(bf16[2,8,32,512]{3,2,1,0:T(8,128)(2,1)S(1)} %collective-permute-done.20.rest_4_.rest_8_), channel_id=1, source_target_pairs={{0,16},{1,17},{2,18},{3,19},{4,20},{5,21},{6,22},{7,23},{8,24},{9,... | collective-permute-start | bytes 1572872 | tf_op jit(solution)/shard_map/ppermute | solution.py:403
  112.2 15.7 %collective-permute-start.23 = (bf16[2,128,512]{2,1,0:T(8,128)(2,1)S(1)}, bf16[2,128,512]{2,1,0:T(8,128)(2,1)S(1)}, u32[]{:S(2)}, u32[]{:S(2)}) collective-permute-start(bf16[2,128,512]{2,1,0:T(8,128)(2,1)S(1)} %bitcast.293), channel_id=1, source_target_pairs={{0,2},{1,3},{2,0},{3,1},{4,6},{5,7},{6,4},{7,5},{8,10},{9,11},{10,... | collective-permute-start | bytes 786440 | tf_op jit(solution)/shard_map/ppermute | solution.py:403
  127.9 14.0 %collective-permute-start.24 = (bf16[2,2,128,512]{3,2,1,0:T(8,128)(2,1)S(1)}, bf16[2,2,128,512]{3,2,1,0:T(8,128)(2,1)S(1)}, u32[]{:S(2)}, u32[]{:S(2)}) collective-permute-start(bf16[2,2,128,512]{3,2,1,0:T(8,128)(2,1)S(1)} %pad_maximum_fusion.10), channel_id=1, source_target_pairs={{0,1},{1,0},{2,3},{3,2},{4,5},{5,4},{6,7},{7,6},{8,9},{9,8},{10,11... | collective-permute-start | bytes 1572872 | tf_op jit(solution)/shard_map/ppermute | solution.py:403
  128.0 14.4 %collective-permute-start.25 = (bf16[2,8,32,512]{3,2,1,0:T(8,128)(2,1)S(1)}, bf16[2,8,32,512]{3,2,1,0:T(8,128)(2,1)S(1)}, u32[]{:S(2)}, u32[]{:S(2)}) collective-permute-start(bf16[2,8,32,512]{3,2,1,0:T(8,128)(2,1)S(1)} %collective-permute-done.21.rest_1_.rest_5_), channel_id=1, source_target_pairs={{0,16},{1,17},{2,18},{3,19},{4,20},{5,21},{6,22},{7,23},{8,24},{9,... | collective-permute-start | bytes 1572872 | tf_op jit(solution)/shard_map/ppermute | solution.py:403
  128.6 14.9 %collective-permute-start.28 = (bf16[2,8,32,512]{3,2,1,0:T(8,128)(2,1)S(1)}, bf16[2,8,32,512]{3,2,1,0:T(8,128)(2,1)S(1)}, u32[]{:S(2)}, u32[]{:S(2)}) collective-permute-start(bf16[2,8,32,512]{3,2,1,0:T(8,128)(2,1)S(1)} %collective-permute-done.27.rest_5_.rest_9_), channel_id=1, source_target_pairs={{0,8},{1,9},{2,10},{3,11},{4,12},{5,13},{6,14},{7,15},{8,0},{9,1},... | collective-permute-start | bytes 1572872 | tf_op jit(solution)/shard_map/ppermute | solution.py:403
  130.2 23.4 %collective-permute-start.29 = (bf16[2,2,128,512]{3,2,1,0:T(8,128)(2,1)S(1)}, bf16[2,2,128,512]{3,2,1,0:T(8,128)(2,1)S(1)}, u32[]{:S(2)}, u32[]{:S(2)}) collective-permute-start(bf16[2,2,128,512]{3,2,1,0:T(8,128)(2,1)S(1)} %pad_maximum_fusion.10), channel_id=1, source_target_pairs={{0,8},{1,9},{2,10},{3,11},{4,12},{5,13},{6,14},{7,15},{8,0},{9,1},... | collective-permute-start | bytes 1572872 | tf_op jit(solution)/shard_map/ppermute | solution.py:403
  141.9 13.1 %collective-permute-start.30 = (bf16[2,2,128,512]{3,2,1,0:T(8,128)(2,1)S(1)}, bf16[2,2,128,512]{3,2,1,0:T(8,128)(2,1)S(1)}, u32[]{:S(2)}, u32[]{:S(2)}) collective-permute-start(bf16[2,2,128,512]{3,2,1,0:T(8,128)(2,1)S(1)} %collective-permute-done.24), channel_id=1, source_target_pairs={{0,16},{1,17},{2,18},{3,19},{4,20},{5,21},{6,22},{7,23},{8,24},{9,... | collective-permute-start | bytes 1572872 | tf_op jit(solution)/shard_map/ppermute | solution.py:403
  163.0 4.9 %collective-permute-start.32 = (bf16[512,1024]{1,0:T(8,128)(2,1)}, bf16[512,1024]{1,0:T(8,128)(2,1)}, u32[]{:S(2)}, u32[]{:S(2)}) collective-permute-start(bf16[512,1024]{1,0:T(8,128)(2,1)} %get-tuple-element.170.own_ref), channel_id=1, source_target_pairs={{0,4},{1,5},{2,6},{3,7},{4,0},{5,1},{6,2},{7,3},{8,12},{9,13},{10,... | collective-permute-start | bytes 3145736 | tf_op jit(solution)/shard_map/ppermute | solution.py:403
  163.1 25.5 %collective-permute-start.36 = (bf16[2,2,2,128,512]{4,3,2,1,0:T(8,128)(2,1)S(1)}, bf16[2,2,2,128,512]{4,3,2,1,0:T(8,128)(2,1)}, u32[]{:S(2)}, u32[]{:S(2)}) collective-permute-start(bf16[2,2,2,128,512]{4,3,2,1,0:T(8,128)(2,1)S(1)} %pad_maximum_fusion.4.rest_2_), channel_id=1, source_target_pairs={{0,8},{1,9},{2,10},{3,11},{4,12},{5,13},{6,14},{7,15},{8,0},{9,1},... | collective-permute-start | bytes 3145736 | tf_op jit(solution)/shard_map/ppermute | solution.py:403
  164.6 25.2 %collective-permute-start.35 = (bf16[2,2,2,128,512]{4,3,2,1,0:T(8,128)(2,1)S(1)}, bf16[2,2,2,128,512]{4,3,2,1,0:T(8,128)(2,1)}, u32[]{:S(2)}, u32[]{:S(2)}) collective-permute-start(bf16[2,2,2,128,512]{4,3,2,1,0:T(8,128)(2,1)S(1)} %pad_maximum_fusion.3.rest_0_), channel_id=1, source_target_pairs={{0,16},{1,17},{2,18},{3,19},{4,20},{5,21},{6,22},{7,23},{8,24},{9,... | collective-permute-start | bytes 3145736 | tf_op jit(solution)/shard_map/ppermute | solution.py:403
  165.9 15.2 %collective-permute-start.33 = (bf16[256,1024]{1,0:T(8,128)(2,1)S(1)}, bf16[256,1024]{1,0:T(8,128)(2,1)S(1)}, u32[]{:S(2)}, u32[]{:S(2)}) collective-permute-start(bf16[256,1024]{1,0:T(8,128)(2,1)S(1)} %get-tuple-element.332), channel_id=1, source_target_pairs={{0,0},{1,1},{2,4},{3,5},{4,2},{5,3},{6,6},{7,7},{8,8},{9,9},{10,12... | collective-permute-start | bytes 1572872 | tf_op jit(solution)/shard_map/ppermute | solution.py:403
  166.6 14.5 %collective-permute-start.34 = (bf16[256,1024]{1,0:T(8,128)(2,1)S(1)}, bf16[256,1024]{1,0:T(8,128)(2,1)S(1)}, u32[]{:S(2)}, u32[]{:S(2)}) collective-permute-start(bf16[256,1024]{1,0:T(8,128)(2,1)S(1)} %get-tuple-element.331), channel_id=1, source_target_pairs={{0,1},{1,0},{2,5},{3,4},{4,3},{5,2},{6,7},{7,6},{8,9},{9,8},{10,13... | collective-permute-start | bytes 1572872 | tf_op jit(solution)/shard_map/ppermute | solution.py:403
  225.0 41.3 %collective-permute-start.42 = (bf16[2,2,2,128,512]{4,3,2,1,0:T(8,128)(2,1)}, bf16[2,2,2,128,512]{4,3,2,1,0:T(8,128)(2,1)S(1)}, u32[]{:S(2)}, u32[]{:S(2)}) collective-permute-start(bf16[2,2,2,128,512]{4,3,2,1,0:T(8,128)(2,1)} %get-tuple-element.184), channel_id=1, source_target_pairs={{0,8},{1,9},{2,10},{3,11},{4,12},{5,13},{6,14},{7,15},{8,0},{9,1},... | collective-permute-start | bytes 3145736 | tf_op jit(solution)/shard_map/ppermute | solution.py:403
  225.6 41.6 %collective-permute-start.41 = (bf16[2,2,2,128,512]{4,3,2,1,0:T(8,128)(2,1)}, bf16[2,2,2,128,512]{4,3,2,1,0:T(8,128)(2,1)S(1)}, u32[]{:S(2)}, u32[]{:S(2)}) collective-permute-start(bf16[2,2,2,128,512]{4,3,2,1,0:T(8,128)(2,1)} %get-tuple-element.182), channel_id=1, source_target_pairs={{0,16},{1,17},{2,18},{3,19},{4,20},{5,21},{6,22},{7,23},{8,24},{9,... | collective-permute-start | bytes 3145736 | tf_op jit(solution)/shard_map/ppermute | solution.py:403
  226.3 38.8 %collective-permute-start.39 = (bf16[256,1024]{1,0:T(8,128)(2,1)S(1)}, bf16[256,1024]{1,0:T(8,128)(2,1)S(1)}, u32[]{:S(2)}, u32[]{:S(2)}) collective-permute-start(bf16[256,1024]{1,0:T(8,128)(2,1)S(1)} %get-tuple-element.330), channel_id=1, source_target_pairs={{0,0},{1,1},{4,2},{5,3},{2,4},{3,5},{6,6},{7,7},{8,8},{9,9},{12,10... | collective-permute-start | bytes 1572872 | tf_op jit(solution)/shard_map/ppermute | solution.py:403
  227.0 38.1 %collective-permute-start.40 = (bf16[256,1024]{1,0:T(8,128)(2,1)S(1)}, bf16[256,1024]{1,0:T(8,128)(2,1)S(1)}, u32[]{:S(2)}, u32[]{:S(2)}) collective-permute-start(bf16[256,1024]{1,0:T(8,128)(2,1)S(1)} %get-tuple-element.329), channel_id=1, source_target_pairs={{1,0},{0,1},{5,2},{4,3},{3,4},{2,5},{7,6},{6,7},{9,8},{8,9},{13,10... | collective-permute-start | bytes 1572872 | tf_op jit(solution)/shard_map/ppermute | solution.py:403
  252.3 15.6 %collective-permute-start.43 = (bf16[512,1024]{1,0:T(8,128)(2,1)}, bf16[512,1024]{1,0:T(8,128)(2,1)S(1)}, u32[]{:S(2)}, u32[]{:S(2)}) collective-permute-start(bf16[512,1024]{1,0:T(8,128)(2,1)} %get-tuple-element.200), channel_id=1, source_target_pairs={{0,4},{1,5},{2,6},{3,7},{4,0},{5,1},{6,2},{7,3},{8,12},{9,13},{10,... | collective-permute-start | bytes 3145736 | tf_op jit(solution)/shard_map/ppermute | solution.py:403
  274.9 4.2 collective-permute-start.44
  275.0 24.5 %collective-permute-start.46 = (bf16[2,2,128,512]{3,2,1,0:T(8,128)(2,1)S(1)}, bf16[2,2,128,512]{3,2,1,0:T(8,128)(2,1)S(1)}, u32[]{:S(2)}, u32[]{:S(2)}) collective-permute-start(bf16[2,2,128,512]{3,2,1,0:T(8,128)(2,1)S(1)} %get-tuple-element.309), channel_id=1, source_target_pairs={{0,16},{1,17},{2,18},{3,19},{4,20},{5,21},{6,22},{7,23},{8,24},{9,... | collective-permute-start | bytes 1572872 | tf_op jit(solution)/shard_map/ppermute | solution.py:403
  275.6 24.8 %collective-permute-start.45 = (bf16[2,2,128,512]{3,2,1,0:T(8,128)(2,1)S(1)}, bf16[2,2,128,512]{3,2,1,0:T(8,128)(2,1)S(1)}, u32[]{:S(2)}, u32[]{:S(2)}) collective-permute-start(bf16[2,2,128,512]{3,2,1,0:T(8,128)(2,1)S(1)} %get-tuple-element.311), channel_id=1, source_target_pairs={{0,8},{1,9},{2,10},{3,11},{4,12},{5,13},{6,14},{7,15},{8,0},{9,1},... | collective-permute-start | bytes 1572872 | tf_op jit(solution)/shard_map/ppermute | solution.py:403
  277.0 35.3 %collective-permute-start.48 = (bf16[2,2,8,32,512]{4,3,2,1,0:T(8,128)(2,1)}, bf16[2,2,8,32,512]{4,3,2,1,0:T(8,128)(2,1)S(1)}, u32[]{:S(2)}, u32[]{:S(2)}) collective-permute-start(bf16[2,2,8,32,512]{4,3,2,1,0:T(8,128)(2,1)} %get-tuple-element.220), channel_id=1, source_target_pairs={{0,8},{1,9},{2,10},{3,11},{4,12},{5,13},{6,14},{7,15},{8,0},{9,1},... | collective-permute-start | bytes 3145736 | tf_op jit(solution)/shard_map/ppermute | solution.py:403
  277.6 37.9 %collective-permute-start.47 = (bf16[2,2,8,32,512]{4,3,2,1,0:T(8,128)(2,1)}, bf16[2,2,8,32,512]{4,3,2,1,0:T(8,128)(2,1)S(1)}, u32[]{:S(2)}, u32[]{:S(2)}) collective-permute-start(bf16[2,2,8,32,512]{4,3,2,1,0:T(8,128)(2,1)} %get-tuple-element.218), channel_id=1, source_target_pairs={{0,16},{1,17},{2,18},{3,19},{4,20},{5,21},{6,22},{7,23},{8,24},{9,... | collective-permute-start | bytes 3145736 | tf_op jit(solution)/shard_map/ppermute | solution.py:403
  300.3 40.0 %collective-permute-start.53 = (bf16[2,2,128,512]{3,2,1,0:T(8,128)(2,1)}, bf16[2,2,128,512]{3,2,1,0:T(8,128)(2,1)S(1)}, u32[]{:S(2)}, u32[]{:S(2)}) collective-permute-start(bf16[2,2,128,512]{3,2,1,0:T(8,128)(2,1)} %add_convert_fusion.6), channel_id=1, source_target_pairs={{0,1},{1,0},{2,3},{3,2},{4,5},{5,4},{6,7},{7,6},{8,9},{9,8},{10,11... | collective-permute-start | bytes 1572872 | tf_op jit(solution)/shard_map/ppermute | solution.py:403
  309.4 34.6 %collective-permute-start.52 = (bf16[2,2,10,32,256]{4,3,2,1,0:T(8,128)(2,1)}, bf16[2,2,10,32,256]{4,3,2,1,0:T(8,128)(2,1)S(1)}, u32[]{:S(2)}, u32[]{:S(2)}) collective-permute-start(bf16[2,2,10,32,256]{4,3,2,1,0:T(8,128)(2,1)} %get-tuple-element.214), channel_id=1, source_target_pairs={{0,8},{1,9},{2,10},{3,11},{4,12},{5,13},{6,14},{7,15},{8,0},{9,1},... | collective-permute-start | bytes 1966088 | tf_op jit(solution)/shard_map/ppermute | solution.py:403
  311.0 33.9 %collective-permute-start.51 = (bf16[2,2,10,32,256]{4,3,2,1,0:T(8,128)(2,1)}, bf16[2,2,10,32,256]{4,3,2,1,0:T(8,128)(2,1)S(1)}, u32[]{:S(2)}, u32[]{:S(2)}) collective-permute-start(bf16[2,2,10,32,256]{4,3,2,1,0:T(8,128)(2,1)} %get-tuple-element.212), channel_id=1, source_target_pairs={{0,16},{1,17},{2,18},{3,19},{4,20},{5,21},{6,22},{7,23},{8,24},{9,... | collective-permute-start | bytes 1966088 | tf_op jit(solution)/shard_map/ppermute | solution.py:403
  313.5 27.0 %collective-permute-start.50 = (bf16[2,8,32,512]{3,2,1,0:T(8,128)(2,1)}, bf16[2,8,32,512]{3,2,1,0:T(8,128)(2,1)S(1)}, u32[]{:S(2)}, u32[]{:S(2)}) collective-permute-start(bf16[2,8,32,512]{3,2,1,0:T(8,128)(2,1)} %get-tuple-element.305), channel_id=1, source_target_pairs={{0,16},{1,17},{2,18},{3,19},{4,20},{5,21},{6,22},{7,23},{8,24},{9,... | collective-permute-start | bytes 1572872 | tf_op jit(solution)/shard_map/ppermute | solution.py:403
  316.7 27.1 %collective-permute-start.49 = (bf16[2,8,32,512]{3,2,1,0:T(8,128)(2,1)}, bf16[2,8,32,512]{3,2,1,0:T(8,128)(2,1)S(1)}, u32[]{:S(2)}, u32[]{:S(2)}) collective-permute-start(bf16[2,8,32,512]{3,2,1,0:T(8,128)(2,1)} %get-tuple-element.307), channel_id=1, source_target_pairs={{0,8},{1,9},{2,10},{3,11},{4,12},{5,13},{6,14},{7,15},{8,0},{9,1},... | collective-permute-start | bytes 1572872 | tf_op jit(solution)/shard_map/ppermute | solution.py:403
  340.4 16.4 %collective-permute-start.76 = (bf16[2,128,512]{2,1,0:T(8,128)(2,1)S(1)}, bf16[2,128,512]{2,1,0:T(8,128)(2,1)S(1)}, u32[]{:S(2)}, u32[]{:S(2)}) collective-permute-start(bf16[2,128,512]{2,1,0:T(8,128)(2,1)S(1)} %get-tuple-element.325), channel_id=1, source_target_pairs={{0,2},{1,3},{2,0},{3,1},{4,6},{5,7},{6,4},{7,5},{8,10},{9,11},{10,... | collective-permute-start | bytes 786440 | tf_op jit(solution)/shard_map/ppermute | solution.py:403
  341.5 32.3 %collective-permute-start.73 = (bf16[2,8,32,512]{3,2,1,0:T(8,128)(2,1)}, bf16[2,8,32,512]{3,2,1,0:T(8,128)(2,1)}, u32[]{:S(2)}, u32[]{:S(2)}) collective-permute-start(bf16[2,8,32,512]{3,2,1,0:T(8,128)(2,1)} %add_convert_fusion), channel_id=1, source_target_pairs={{0,1},{1,0},{2,3},{3,2},{4,5},{5,4},{6,7},{7,6},{8,9},{9,8},{10,11... | collective-permute-start | bytes 1572872 | tf_op jit(solution)/shard_map/ppermute | solution.py:403
  345.0 13.1 %collective-permute-start.55 = (bf16[2,10,32,256]{3,2,1,0:T(8,128)(2,1)}, bf16[2,10,32,256]{3,2,1,0:T(8,128)(2,1)}, u32[]{:S(2)}, u32[]{:S(2)}) collective-permute-start(bf16[2,10,32,256]{3,2,1,0:T(8,128)(2,1)} %get-tuple-element.313), channel_id=1, source_target_pairs={{0,16},{1,17},{2,18},{3,19},{4,20},{5,21},{6,22},{7,23},{8,24},{9,... | collective-permute-start | bytes 983048 | tf_op jit(solution)/shard_map/ppermute | solution.py:403
  356.2 7.5 %collective-permute-start.54 = (bf16[2,10,32,256]{3,2,1,0:T(8,128)(2,1)}, bf16[2,10,32,256]{3,2,1,0:T(8,128)(2,1)}, u32[]{:S(2)}, u32[]{:S(2)}) collective-permute-start(bf16[2,10,32,256]{3,2,1,0:T(8,128)(2,1)} %get-tuple-element.315), channel_id=1, source_target_pairs={{0,8},{1,9},{2,10},{3,11},{4,12},{5,13},{6,14},{7,15},{8,0},{9,1},... | collective-permute-start | bytes 983048 | tf_op jit(solution)/shard_map/ppermute | solution.py:403
  356.8 20.5 %collective-permute-start.56 = (bf16[512,1024]{1,0:T(8,128)(2,1)}, bf16[512,1024]{1,0:T(8,128)(2,1)S(1)}, u32[]{:S(2)}, u32[]{:S(2)}) collective-permute-start(bf16[512,1024]{1,0:T(8,128)(2,1)} %get-tuple-element.238), channel_id=1, source_target_pairs={{0,4},{1,5},{2,6},{3,7},{4,0},{5,1},{6,2},{7,3},{8,12},{9,13},{10,... | collective-permute-start | bytes 3145736 | tf_op jit(solution)/shard_map/ppermute | solution.py:403
  359.2 18.0 %collective-permute-start.64 = (bf16[2,10,32,256]{3,2,1,0:T(8,128)(2,1)S(1)}, bf16[2,10,32,256]{3,2,1,0:T(8,128)(2,1)S(1)}, u32[]{:S(2)}, u32[]{:S(2)}) collective-permute-start(bf16[2,10,32,256]{3,2,1,0:T(8,128)(2,1)S(1)} %add_convert_fusion.12), channel_id=1, source_target_pairs={{0,1},{1,0},{2,3},{3,2},{4,5},{5,4},{6,7},{7,6},{8,9},{9,8},{10,11... | collective-permute-start | bytes 983048 | tf_op jit(solution)/shard_map/ppermute | solution.py:403
  371.3 18.8 %collective-permute-start.66 = (bf16[2,2,6,32,256]{4,3,2,1,0:T(8,128)(2,1)}, bf16[2,2,6,32,256]{4,3,2,1,0:T(8,128)(2,1)}, u32[]{:S(2)}, u32[]{:S(2)}) collective-permute-start(bf16[2,2,6,32,256]{4,3,2,1,0:T(8,128)(2,1)} %get-tuple-element.234), channel_id=1, source_target_pairs={{0,16},{1,17},{2,18},{3,19},{4,20},{5,21},{6,22},{7,23},{8,24},{9,... | collective-permute-start | bytes 1179656 | tf_op jit(solution)/shard_map/ppermute | solution.py:403
  373.3 22.2 %collective-permute-start.67 = (bf16[2,2,6,32,256]{4,3,2,1,0:T(8,128)(2,1)}, bf16[2,2,6,32,256]{4,3,2,1,0:T(8,128)(2,1)}, u32[]{:S(2)}, u32[]{:S(2)}) collective-permute-start(bf16[2,2,6,32,256]{4,3,2,1,0:T(8,128)(2,1)} %get-tuple-element.236), channel_id=1, source_target_pairs={{0,8},{1,9},{2,10},{3,11},{4,12},{5,13},{6,14},{7,15},{8,0},{9,1},... | collective-permute-start | bytes 1179656 | tf_op jit(solution)/shard_map/ppermute | solution.py:403
  375.7 12.0 %collective-permute-start.74 = (bf16[8,32,512]{2,1,0:T(8,128)(2,1)}, bf16[8,32,512]{2,1,0:T(8,128)(2,1)S(1)}, u32[]{:S(2)}, u32[]{:S(2)}) collective-permute-start(bf16[8,32,512]{2,1,0:T(8,128)(2,1)} %get-tuple-element.320), channel_id=1, source_target_pairs={{0,2},{1,3},{2,0},{3,1},{4,6},{5,7},{6,4},{7,5},{8,10},{9,11},{10,... | collective-permute-start | bytes 786440 | tf_op jit(solution)/shard_map/ppermute | solution.py:403
  387.9 31.0 %collective-permute-start.75 = (f32[4,32,512]{2,1,0:T(8,128)S(1)}, f32[4,32,512]{2,1,0:T(8,128)S(1)}, u32[]{:S(2)}, u32[]{:S(2)}) collective-permute-start(f32[4,32,512]{2,1,0:T(8,128)S(1)} %get-tuple-element.340), channel_id=1, source_target_pairs={{0,4},{1,5},{2,6},{3,7},{4,0},{5,1},{6,2},{7,3},{8,12},{9,13},{10,... | collective-permute-start | bytes 786440 | tf_op jit(solution)/shard_map/ppermute | solution.py:403
  388.2 21.8 %collective-permute-start.57 = (bf16[256,1024]{1,0:T(8,128)(2,1)S(1)}, bf16[256,1024]{1,0:T(8,128)(2,1)S(1)}, u32[]{:S(2)}, u32[]{:S(2)}) collective-permute-start(bf16[256,1024]{1,0:T(8,128)(2,1)S(1)} %get-tuple-element.324), channel_id=1, source_target_pairs={{0,0},{1,1},{4,2},{5,3},{2,4},{3,5},{6,6},{7,7},{8,8},{9,9},{12,10... | collective-permute-start | bytes 1572872 | tf_op jit(solution)/shard_map/ppermute | solution.py:403
  388.9 21.1 %collective-permute-start.58 = (bf16[256,1024]{1,0:T(8,128)(2,1)S(1)}, bf16[256,1024]{1,0:T(8,128)(2,1)S(1)}, u32[]{:S(2)}, u32[]{:S(2)}) collective-permute-start(bf16[256,1024]{1,0:T(8,128)(2,1)S(1)} %get-tuple-element.323), channel_id=1, source_target_pairs={{1,0},{0,1},{5,2},{4,3},{3,4},{2,5},{7,6},{6,7},{9,8},{8,9},{13,10... | collective-permute-start | bytes 1572872 | tf_op jit(solution)/shard_map/ppermute | solution.py:403
  393.9 6.7 %collective-permute-start.68 = (bf16[2,6,32,256]{3,2,1,0:T(8,128)(2,1)S(1)}, bf16[2,6,32,256]{3,2,1,0:T(8,128)(2,1)S(1)}, u32[]{:S(2)}, u32[]{:S(2)}) collective-permute-start(bf16[2,6,32,256]{3,2,1,0:T(8,128)(2,1)S(1)} %get-tuple-element.333), channel_id=1, source_target_pairs={{0,8},{1,9},{2,10},{3,11},{4,12},{5,13},{6,14},{7,15},{8,0},{9,1},... | collective-permute-start | bytes 589832 | tf_op jit(solution)/shard_map/ppermute | solution.py:403
  395.5 5.0 %collective-permute-start.61 = (f32[28,128]{1,0:T(8,128)S(1)}, f32[28,128]{1,0:T(8,128)S(1)}, u32[]{:S(2)}, u32[]{:S(2)}) collective-permute-start(f32[28,128]{1,0:T(8,128)S(1)} %pad_maximum_fusion.17), channel_id=1, source_target_pairs={{0,8},{1,9},{2,10},{3,11},{4,12},{5,13},{6,14},{7,15},{8,0},{9,1},... | collective-permute-start | bytes 43016 | tf_op jit(solution)/shard_map/ppermute | solution.py:403
  400.5 7.3 %collective-permute-start.69 = (bf16[2,6,32,256]{3,2,1,0:T(8,128)(2,1)S(1)}, bf16[2,6,32,256]{3,2,1,0:T(8,128)(2,1)S(1)}, u32[]{:S(2)}, u32[]{:S(2)}) collective-permute-start(bf16[2,6,32,256]{3,2,1,0:T(8,128)(2,1)S(1)} %get-tuple-element.336), channel_id=1, source_target_pairs={{0,16},{1,17},{2,18},{3,19},{4,20},{5,21},{6,22},{7,23},{8,24},{9,... | collective-permute-start | bytes 589832 | tf_op jit(solution)/shard_map/ppermute | solution.py:403
  407.9 13.4 %collective-permute-start.70 = (bf16[2,6,32,256]{3,2,1,0:T(8,128)(2,1)S(1)}, bf16[2,6,32,256]{3,2,1,0:T(8,128)(2,1)S(1)}, u32[]{:S(2)}, u32[]{:S(2)}) collective-permute-start(bf16[2,6,32,256]{3,2,1,0:T(8,128)(2,1)S(1)} %add_convert_fusion.22), channel_id=1, source_target_pairs={{0,1},{1,0},{2,3},{3,2},{4,5},{5,4},{6,7},{7,6},{8,9},{9,8},{10,11... | collective-permute-start | bytes 589832 | tf_op jit(solution)/shard_map/ppermute | solution.py:403
  411.2 9.5 %collective-permute-start.62 = (f32[38,128]{1,0:T(8,128)S(1)}, f32[38,128]{1,0:T(8,128)S(1)}, u32[]{:S(2)}, u32[]{:S(2)}) collective-permute-start(f32[38,128]{1,0:T(8,128)S(1)} %pad_maximum_fusion.15), channel_id=1, source_target_pairs={{0,2},{1,3},{2,0},{3,1},{4,6},{5,7},{6,4},{7,5},{8,10},{9,11},{10,... | collective-permute-start | bytes 58376 | tf_op jit(solution)/shard_map/ppermute | solution.py:403
  421.3 11.9 %collective-permute-start.71 = (bf16[6,32,256]{2,1,0:T(8,128)(2,1)S(1)}, bf16[6,32,256]{2,1,0:T(8,128)(2,1)S(1)}, u32[]{:S(2)}, u32[]{:S(2)}) collective-permute-start(bf16[6,32,256]{2,1,0:T(8,128)(2,1)S(1)} %get-tuple-element.261), channel_id=1, source_target_pairs={{0,2},{1,3},{2,0},{3,1},{4,6},{5,7},{6,4},{7,5},{8,10},{9,11},{10,... | collective-permute-start | bytes 294920 | tf_op jit(solution)/shard_map/ppermute | solution.py:403
  424.3 12.5 %collective-permute-start.65 = (bf16[10,32,256]{2,1,0:T(8,128)(2,1)S(1)}, bf16[10,32,256]{2,1,0:T(8,128)(2,1)S(1)}, u32[]{:S(2)}, u32[]{:S(2)}) collective-permute-start(bf16[10,32,256]{2,1,0:T(8,128)(2,1)S(1)} %get-tuple-element.255), channel_id=1, source_target_pairs={{0,2},{1,3},{2,0},{3,1},{4,6},{5,7},{6,4},{7,5},{8,10},{9,11},{10,... | collective-permute-start | bytes 491528 | tf_op jit(solution)/shard_map/ppermute | solution.py:403
  (59 other events, 319.4 us)
